TPU v7x, 32 devices: a whole 2x2x4 slice. The times are simulated.
32 devices in a mesh: dp: 16 (over z, x, core), head: 2 (over y).
Axes of the slice: x: 2, y: 2, z: 4, core: 2. Of those that a mesh axis runs over, the one named last changes fastest.
Arguments:
- tokens: bfloat16 [32, 392, 768], P('dp', 'head'), may hold values from -6 to 6
- ln1_gain: float32 [768], replicated, may hold values from 0.5 to 1.5
- ln1_bias: float32 [768], replicated, may hold values from -1.75 to 1.75
- w_qkv: bfloat16 [768, 3, 768], P(None, None, 'head'), may hold values from -0.21875 to 0.21875
- pool_q: float32 [27, 96], replicated, may hold values from -1.25 to 1.25
- pool_k: float32 [27, 96], replicated, may hold values from -1.25 to 1.25
- pool_v: float32 [27, 96], replicated, may hold values from -1.25 to 1.25
- squeeze_k: float32 [27, 96], replicated, may hold values from -1.25 to 1.25
- squeeze_v: float32 [27, 96], replicated, may hold values from -1.25 to 1.25
- rel_t: float32 [15, 96], replicated, may hold values from -0.375 to 0.375
- rel_h: float32 [13, 96], replicated, may hold values from -0.375 to 0.375
- rel_w: float32 [13, 96], replicated, may hold values from -0.375 to 0.375
- w_proj: bfloat16 [768, 768], P('head'), may hold values from -0.21875 to 0.21875
- proj_bias: float32 [768], replicated, may hold values from -1.75 to 1.75
- ln2_gain: float32 [768], replicated, may hold values from 0.5 to 1.5
- ln2_bias: float32 [768], replicated, may hold values from -1.75 to 1.75
- w_fc1: bfloat16 [768, 3072], P(None, 'head'), may hold values from -0.21875 to 0.21875
- fc1_bias: float32 [3072], P('head'), may hold values from -1.75 to 1.75
- w_fc2: bfloat16 [3072, 768], P('head'), may hold values from -0.109375 to 0.109375
- fc2_bias: float32 [768], replicated, may hold values from -1.75 to 1.75
- memory_valid: int32 [32, 2], P('dp'), may hold values from 0 to 1, as said below
- cotangent: bfloat16 [32, 392, 768], P('dp', 'head'), may hold values from -6 to 6
Outputs:
- output: bfloat16 [32, 392, 768], P('dp', 'head')
- grad_tokens: float32 [32, 392, 768], P('dp', 'head')
- grad_ln1_gain: float32 [768], replicated
- grad_ln1_bias: float32 [768], replicated
- grad_w_qkv: float32 [768, 3, 768], P(None, None, 'head')
- grad_pool_q: float32 [27, 96], replicated
- grad_pool_k: float32 [27, 96], replicated
- grad_pool_v: float32 [27, 96], replicated
- grad_squeeze_k: float32 [27, 96], replicated
- grad_squeeze_v: float32 [27, 96], replicated
- grad_rel_t: float32 [15, 96], replicated
- grad_rel_h: float32 [13, 96], replicated
- grad_rel_w: float32 [13, 96], replicated
- grad_w_proj: float32 [768, 768], P('head')
- grad_proj_bias: float32 [768], replicated
- grad_ln2_gain: float32 [768], replicated
- grad_ln2_bias: float32 [768], replicated
- grad_w_fc1: float32 [768, 3072], P(None, 'head')
- grad_fc1_bias: float32 [3072], P('head')
- grad_w_fc2: float32 [3072, 768], P('head')
- grad_fc2_bias: float32 [768], replicated
Inputs may be any that keep to these rules, and one draw needn't show every extreme that they name: Videos are runs of 1 to 12 consecutive clips starting at clip 0; memory_valid[c, s] is 1 exactly when clip c - 1 - s exists and belongs to the same video as clip c.
All inputs are finite; a program needn't handle non-finite values.
Results may differ from a plain program's by a relative error of at most 0.012.
The roundings to bfloat16 on the way count: a program that leaves them out, or rounds other values in their place, can miss the bound.
Values may be sent and summed in bfloat16 or wider, within the bound.
A program may use at most 320 MiB of HBM per device.

v0:
```python
from functools import partial

import jax
import jax.numpy as jnp
from jax import lax
from jax.sharding import PartitionSpec as P

HEAD_DIM = 96
T_LEN = 8
HGT = 7
WID = 7
L = 392
TM = 4
M = 196


EPSILON = 1e-06
HIGHEST = lax.Precision.HIGHEST


def from_behind(x, axis, by):
    count = lax.axis_size(axis)
    pairs = [(i, i + by) for i in range(count) if 0 <= i + by < count]
    return lax.ppermute(x, axis, pairs)


def layer_norm(values, scaling, offset):
    average = jnp.mean(values, axis=-1, keepdims=True)
    centred = values - average
    variance = jnp.mean(centred * centred, axis=-1, keepdims=True)
    return centred * lax.rsqrt(variance + EPSILON) * scaling + offset


def depthwise(volume, kernel, stride):
    channels = volume.shape[-1]
    tiled = jnp.tile(kernel, (1, channels // kernel.shape[-1])).reshape(3, 3, 3, 1, channels)
    return lax.conv_general_dilated(
        volume,
        tiled,
        window_strides=(stride, 1, 1),
        padding=((1, 1), (1, 1), (1, 1)),
        dimension_numbers=("NDHWC", "DHWIO", "NDHWC"),
        feature_group_count=channels,
        precision=HIGHEST,
    )


def offsets(length):
    places = jnp.arange(length, dtype=jnp.int32)
    distance = places[:, None] - places[None, :] + length - 1
    entries = jnp.arange(2 * length - 1, dtype=jnp.int32)
    return (distance[:, :, None] == entries[None, None, :]).astype(jnp.float32)


def relative_bias(queries, rel_t, rel_h, rel_w):
    clip_count = queries.shape[0]
    head_count = queries.shape[2]
    gridded = queries.reshape(clip_count, T_LEN, HGT, WID, head_count, HEAD_DIM)
    along_t = jnp.einsum("athwnd,jd->athwnj", gridded, rel_t, precision=HIGHEST)
    along_t = jnp.einsum("athwnj,tsj->anthws", along_t, offsets(T_LEN), precision=HIGHEST)
    along_h = jnp.einsum("athwnd,jd->athwnj", gridded, rel_h, precision=HIGHEST)
    along_h = jnp.einsum("athwnj,hsj->anthws", along_h, offsets(HGT), precision=HIGHEST)
    along_w = jnp.einsum("athwnd,jd->athwnj", gridded, rel_w, precision=HIGHEST)
    along_w = jnp.einsum("athwnj,wsj->anthws", along_w, offsets(WID), precision=HIGHEST)
    summed = along_t[..., :, None, None] + along_h[..., None, :, None] + along_w[..., None, None, :]
    return summed.reshape(clip_count, head_count, L, L)


def on_device(
    tokens,
    ln1_gain,
    ln1_bias,
    w_qkv,
    pool_q,
    pool_k,
    pool_v,
    squeeze_k,
    squeeze_v,
    rel_t,
    rel_h,
    rel_w,
    w_proj,
    proj_bias,
    ln2_gain,
    ln2_bias,
    w_fc1,
    fc1_bias,
    w_fc2,
    fc2_bias,
    memory_valid,
    cotangent,
):
    clip_count = tokens.shape[0]
    local_width = w_qkv.shape[2]
    head_count = local_width // HEAD_DIM
    score_scale = HEAD_DIM ** (-0.5)
    grid_shape = (clip_count, T_LEN, HGT, WID, local_width)
    conv_one = partial(depthwise, stride=1)
    conv_two = partial(depthwise, stride=2)
    inputs = tokens.astype(jnp.float32)
    first_normed, first_pull = jax.vjp(layer_norm, inputs, ln1_gain, ln1_bias)
    first_rows = lax.all_gather(first_normed.astype(jnp.bfloat16), "head", axis=1, tiled=True)
    qkv_out = jnp.einsum("ald,dke->alke", first_rows, w_qkv, preferred_element_type=jnp.float32)
    queries, query_pull = jax.vjp(conv_one, qkv_out[:, :, 0].reshape(grid_shape), pool_q)
    key_field, key_pull = jax.vjp(conv_one, qkv_out[:, :, 1].reshape(grid_shape), pool_k)
    value_field, value_pull = jax.vjp(conv_one, qkv_out[:, :, 2].reshape(grid_shape), pool_v)
    memory_k, squeeze_k_pull = jax.vjp(conv_two, key_field, squeeze_k)
    memory_v, squeeze_v_pull = jax.vjp(conv_two, value_field, squeeze_v)
    memory_k = memory_k.astype(jnp.bfloat16).reshape(clip_count, M, local_width)
    memory_v = memory_v.astype(jnp.bfloat16).reshape(clip_count, M, local_width)
    before_k, before_v = from_behind((memory_k[-2:], memory_v[-2:]), "dp", 1)
    extended_k = jnp.concatenate([before_k, memory_k], axis=0)
    extended_v = jnp.concatenate([before_v, memory_v], axis=0)
    slot_keys = jnp.concatenate([extended_k[1:-1], extended_k[:-2]], axis=1)
    slot_values = jnp.concatenate([extended_v[1:-1], extended_v[:-2]], axis=1)
    heads_q = queries.astype(jnp.bfloat16).reshape(clip_count, L, head_count, HEAD_DIM)
    own_keys = key_field.astype(jnp.bfloat16).reshape(clip_count, L, local_width)
    own_values = value_field.astype(jnp.bfloat16).reshape(clip_count, L, local_width)
    all_keys = jnp.concatenate([own_keys, slot_keys], axis=1).reshape(
        clip_count, L + 2 * M, head_count, HEAD_DIM
    )
    all_values = jnp.concatenate([own_values, slot_values], axis=1).reshape(
        clip_count, L + 2 * M, head_count, HEAD_DIM
    )
    key_valid = jnp.concatenate(
        [jnp.ones((clip_count, L), dtype=bool), jnp.repeat(memory_valid > 0, M, axis=1)], axis=1
    )
    position_bias, bias_pull = jax.vjp(
        relative_bias, heads_q.astype(jnp.float32), rel_t, rel_h, rel_w
    )
    padding = jnp.zeros((clip_count, head_count, L, 2 * M), jnp.float32)
    full_bias = jnp.concatenate([position_bias, padding], axis=-1)

    def score_block():
        raw_scores = jnp.einsum(
            "alnd,amnd->anlm", heads_q, all_keys, preferred_element_type=jnp.float32
        )
        return jnp.where(key_valid[:, None, None, :], raw_scores * score_scale + full_bias, -1e30)

    scores = score_block()
    row_peak = jnp.max(scores, axis=-1, keepdims=True)
    log_total = row_peak + jnp.log(jnp.sum(jnp.exp(scores - row_peak), axis=-1, keepdims=True))
    weights = jnp.exp(scores - log_total).astype(jnp.bfloat16)
    attended = jnp.einsum(
        "anlm,amnd->alnd", weights, all_values, preferred_element_type=jnp.float32
    ) + heads_q.astype(jnp.float32)
    branch = attended.reshape(clip_count, L, local_width).astype(jnp.bfloat16)
    partial_z = jnp.einsum("ale,ef->alf", branch, w_proj, preferred_element_type=jnp.float32)
    middle = (
        inputs + lax.psum_scatter(partial_z, "head", scatter_dimension=1, tiled=True) + proj_bias
    )
    second_normed, second_pull = jax.vjp(layer_norm, middle, ln2_gain, ln2_bias)
    second_rows = lax.all_gather(second_normed.astype(jnp.bfloat16), "head", axis=1, tiled=True)
    hidden = (
        jnp.einsum("ald,df->alf", second_rows, w_fc1, preferred_element_type=jnp.float32) + fc1_bias
    )
    active, gelu_pull = jax.vjp(partial(jax.nn.gelu, approximate=True), hidden)
    active_low = active.astype(jnp.bfloat16)
    partial_m = jnp.einsum("alf,fd->ald", active_low, w_fc2, preferred_element_type=jnp.float32)
    output = (
        middle + lax.psum_scatter(partial_m, "head", scatter_dimension=1, tiled=True) + fc2_bias
    ).astype(jnp.bfloat16)
    upstream = cotangent.astype(jnp.float32)
    fc2_bias_grad = jnp.sum(upstream, axis=(0, 1))
    upstream_rows = lax.all_gather(cotangent, "head", axis=1, tiled=True)
    w_fc2_grad = jnp.einsum(
        "alf,ald->fd", active_low, upstream_rows, preferred_element_type=jnp.float32
    )
    (hidden_grad,) = gelu_pull(
        jnp.einsum("ald,fd->alf", upstream_rows, w_fc2, preferred_element_type=jnp.float32)
    )
    fc1_bias_grad = jnp.sum(hidden_grad, axis=(0, 1))
    hidden_low = hidden_grad.astype(jnp.bfloat16)
    w_fc1_grad = jnp.einsum(
        "ald,alf->df", second_rows, hidden_low, preferred_element_type=jnp.float32
    )
    partial_second = jnp.einsum(
        "alf,df->ald", hidden_low, w_fc1, preferred_element_type=jnp.float32
    )
    second_grad = lax.psum_scatter(partial_second, "head", scatter_dimension=1, tiled=True)
    middle_part, ln2_gain_grad, ln2_bias_grad = second_pull(second_grad)
    middle_grad = middle_part + upstream
    proj_bias_grad = jnp.sum(middle_grad, axis=(0, 1))
    middle_rows = lax.all_gather(middle_grad.astype(jnp.bfloat16), "head", axis=1, tiled=True)
    w_proj_grad = jnp.einsum("ale,alf->ef", branch, middle_rows, preferred_element_type=jnp.float32)
    branch_grad = jnp.einsum(
        "alf,ef->ale", middle_rows, w_proj, preferred_element_type=jnp.float32
    ).astype(jnp.bfloat16)
    branch_grad = branch_grad.reshape(clip_count, L, head_count, HEAD_DIM)
    scores = score_block()
    soft_scores = jnp.exp(scores - log_total)
    weights = soft_scores.astype(jnp.bfloat16)
    values_grad = jnp.einsum(
        "anlm,alnd->amnd", weights, branch_grad, preferred_element_type=jnp.float32
    )
    weights_grad = jnp.einsum(
        "alnd,amnd->anlm", branch_grad, all_values, preferred_element_type=jnp.float32
    )
    score_grad = (
        soft_scores * (weights_grad - jnp.sum(weights_grad * soft_scores, axis=-1, keepdims=True))
    ).astype(jnp.bfloat16)
    query_grad = (
        jnp.einsum("anlm,amnd->alnd", score_grad, all_keys, preferred_element_type=jnp.float32)
        * score_scale
    )
    keys_grad = (
        jnp.einsum("anlm,alnd->amnd", score_grad, heads_q, preferred_element_type=jnp.float32)
        * score_scale
    )
    bias_query_grad, rel_t_grad, rel_h_grad, rel_w_grad = bias_pull(
        score_grad[..., :L].astype(jnp.float32)
    )
    query_grad = query_grad + bias_query_grad + branch_grad.astype(jnp.float32)
    keys_grad = keys_grad.reshape(clip_count, L + 2 * M, local_width)
    values_grad = values_grad.reshape(clip_count, L + 2 * M, local_width)

    def spread_slots(slot_grad):
        zero_rows = jnp.zeros((1, M, local_width), jnp.float32)
        return jnp.concatenate([zero_rows, slot_grad[:, :M], zero_rows], axis=0) + jnp.concatenate(
            [slot_grad[:, M:], zero_rows, zero_rows], axis=0
        )

    memory_k_grad = spread_slots(keys_grad[:, L:])
    memory_v_grad = spread_slots(values_grad[:, L:])
    later_k, later_v = (
        from_behind(memory_k_grad[:2].astype(jnp.bfloat16), "dp", -1).astype(jnp.float32),
        from_behind(memory_v_grad[:2].astype(jnp.bfloat16), "dp", -1).astype(jnp.float32),
    )
    leading_zeros = jnp.zeros((clip_count - 2, M, local_width), jnp.float32)
    memory_k_grad = memory_k_grad[2:] + jnp.concatenate([leading_zeros, later_k], axis=0)
    memory_v_grad = memory_v_grad[2:] + jnp.concatenate([leading_zeros, later_v], axis=0)
    key_from_memory, squeeze_k_grad = squeeze_k_pull(
        memory_k_grad.reshape(clip_count, TM, HGT, WID, local_width)
    )
    value_from_memory, squeeze_v_grad = squeeze_v_pull(
        memory_v_grad.reshape(clip_count, TM, HGT, WID, local_width)
    )
    query_conv_grad, pool_q_grad = query_pull(query_grad.reshape(grid_shape))
    key_conv_grad, pool_k_grad = key_pull(keys_grad[:, :L].reshape(grid_shape) + key_from_memory)
    value_conv_grad, pool_v_grad = value_pull(
        values_grad[:, :L].reshape(grid_shape) + value_from_memory
    )
    qkv_grad = (
        jnp.stack([query_conv_grad, key_conv_grad, value_conv_grad], axis=4)
        .reshape(clip_count, L, 3, local_width)
        .astype(jnp.bfloat16)
    )
    w_qkv_grad = jnp.einsum(
        "ald,alke->dke", first_rows, qkv_grad, preferred_element_type=jnp.float32
    )
    partial_first = jnp.einsum("alke,dke->ald", qkv_grad, w_qkv, preferred_element_type=jnp.float32)
    first_grad = lax.psum_scatter(partial_first, "head", scatter_dimension=1, tiled=True)
    input_part, ln1_gain_grad, ln1_bias_grad = first_pull(first_grad)
    input_grad = middle_grad + input_part
    shared = lax.psum(
        (
            ln1_gain_grad,
            ln1_bias_grad,
            pool_q_grad,
            pool_k_grad,
            pool_v_grad,
            squeeze_k_grad,
            squeeze_v_grad,
            rel_t_grad,
            rel_h_grad,
            rel_w_grad,
            proj_bias_grad,
            ln2_gain_grad,
            ln2_bias_grad,
            fc2_bias_grad,
        ),
        ("dp", "head"),
    )
    w_qkv_grad, w_proj_grad, w_fc1_grad, fc1_bias_grad, w_fc2_grad = lax.psum(
        (w_qkv_grad, w_proj_grad, w_fc1_grad, fc1_bias_grad, w_fc2_grad), "dp"
    )
    return (
        output,
        input_grad,
        shared[0],
        shared[1],
        w_qkv_grad,
        shared[2],
        shared[3],
        shared[4],
        shared[5],
        shared[6],
        shared[7],
        shared[8],
        shared[9],
        w_proj_grad,
        shared[10],
        shared[11],
        shared[12],
        w_fc1_grad,
        fc1_bias_grad,
        w_fc2_grad,
        shared[13],
    )


def solution(mesh):
    return jax.shard_map(
        on_device,
        mesh=mesh,
        in_specs=(
            P("dp", "head", None),
            P(),
            P(),
            P(None, None, "head"),
            P(),
            P(),
            P(),
            P(),
            P(),
            P(),
            P(),
            P(),
            P("head", None),
            P(),
            P(),
            P(),
            P(None, "head"),
            P("head"),
            P("head", None),
            P(),
            P("dp", None),
            P("dp", "head", None),
        ),
        out_specs=(
            P("dp", "head", None),
            P("dp", "head", None),
            P(),
            P(),
            P(None, None, "head"),
            P(),
            P(),
            P(),
            P(),
            P(),
            P(),
            P(),
            P(),
            P("head", None),
            P(),
            P(),
            P(),
            P(None, "head"),
            P("head"),
            P("head", None),
            P(),
        ),
        check_vma=False,
    )
```

profile of v0, /device:TPU:0, one launch (start us, length us, event | category | flops | bytes accessed | tf_op | source)
XLA Modules:
  0.0 1378.0 jit_solution(2418120352101920512)
XLA Ops:
  16.2 23.3 %all-gather.5.cloned.1.call-done = bf16[2,392,768]{2,0,1:T(2,128)(2,1)} async-done(((bf16[2,196,768]{2,0,1:T(2,128)(2,1)}), bf16[2,392,768]{2,0,1:T(2,128)(2,1)}) %all-gather.5.cloned.1.call-update) | async-done | bytes 1204240 | tf_op jit(solution)/shard_map/all_gather | solution.py:102
  57.9 11.9 convolution_bitcast_fusion.4
  75.3 11.9 convolution_bitcast_fusion.5
  119.6 13.4 convolution_bitcast_fusion.3
  143.6 32.6 %broadcast_add_fusion = f32[2,4,8,7,7,8,7,7]{7,6,5,4,3,2,1,0:T(8,128)} fusion(f32[2,4,8,7,7,7]{5,4,3,2,1,0:T(8,128)S(1)} %copy-done.23, f32[2,4,8,7,7,8,7]{6,5,4,3,2,1,0:T(8,128)S(1)} %broadcast_add_fusion.1), kind=kLoop, calls=%fused_computation | loop fusion | flops 1229312 | bytes 5707520 | tf_op jit(solution)/shard_map/jvp()/add | solution.py:65
  190.7 68.7 %add.234 = f32[2,4,392,392]{3,2,1,0:T(8,128)} reshape(f32[2,4,8,7,7,8,7,7]{7,6,5,4,3,2,1,0:T(8,128)} %broadcast_add_fusion) | data formatting | bytes 9834496 | tf_op jit(solution)/shard_map/jvp()/add | solution.py:65
  295.3 66.4 %all-reduce.17.cloned.1.call-done = f32[2,392,768]{2,0,1:T(2,128)} async-done(((f32[2,392,768]{2,0,1:T(2,128)}), f32[2,392,768]{2,0,1:T(2,128)}) %all-reduce.17.cloned.1.call-update) | async-done | bytes 2408464
  369.9 22.6 %all-gather.7.cloned.1.call-done = bf16[2,392,768]{2,0,1:T(2,128)(2,1)} async-done(((bf16[2,196,768]{2,0,1:T(2,128)(2,1)}), bf16[2,392,768]{2,0,1:T(2,128)(2,1)}) %all-gather.7.cloned.1.call-update) | async-done | bytes 1204240 | tf_op jit(solution)/shard_map/all_gather | solution.py:153
  398.7 18.4 %all-gather.9.cloned.1.call-done = bf16[2,392,768]{2,0,1:T(2,128)(2,1)} async-done(((bf16[2,196,768]{2,0,1:T(2,128)(2,1)}), bf16[2,392,768]{2,0,1:T(2,128)(2,1)}) %all-gather.9.cloned.1.call-update) | async-done | bytes 1204240 | tf_op jit(solution)/shard_map/all_gather | solution.py:165
  429.5 69.8 %all-reduce.19.cloned.1.call-done = f32[2,392,768]{2,0,1:T(2,128)} async-done(((f32[2,392,768]{2,0,1:T(2,128)}), f32[2,392,768]{2,0,1:T(2,128)}) %all-reduce.19.cloned.1.call-update) | async-done | bytes 2408464
  522.1 11.1 all-gather.11.cloned.1.call-done
  541.3 9.7 multiply_reduce_fusion
  569.0 97.0 %reshape.335 = f32[2,4,8,7,7,8,7,7]{7,6,5,4,3,2,1,0:T(8,128)} reshape(f32[2,4,392,392]{3,2,1,0:T(8,128)} %slice_convert_fusion) | data formatting | bytes 9834496 | tf_op jit(solution)/shard_map/transpose(jvp())/reshape | solution.py:66
  666.0 59.4 %fusion.127 = (f32[2,4,8,7,7,7]{5,4,3,2,1,0:T(8,128)S(1)}, f32[2,4,8,7,7,8]{5,4,3,2,1,0:T(8,128)}, f32[2,4,8,7,7,7]{5,4,3,2,1,0:T(8,128)}) fusion(f32[2,4,8,7,7,8,7,7]{7,6,5,4,3,2,1,0:T(8,128)} %reshape.335), kind=kLoop, calls=%fused_computation.186 | loop fusion | flops 3618944 | bytes 5193216 | tf_op jit(solution)/shard_map/transpose(jvp())/reduce_sum | solution.py:65
  803.1 8.9 convolution_bitcast_fusion
  811.9 14.3 %convolution_reduce_fusion.2 = f32[3,3,3,384]{3,2,1,0:T(4,128)S(1)} fusion(f32[2,8,7,7,384]{4,0,3,2,1:T(2,128)S(1)} %bitcast.240, f32[2,8,7,7,384]{4,0,3,2,1:T(2,128)S(1)} %copy-done.48), kind=kOutput, calls=%fused_computation.113 | convolution fusion | flops 73193472 | bytes 2449920 | tf_op jit(solution)/shard_map/transpose(jvp())/conv_general_dilated | solution.py:37
  838.1 14.4 %convolution_reduce_fusion.1 = f32[3,3,3,384]{3,2,1,0:T(4,128)S(1)} fusion(f32[2,8,7,7,384]{4,0,3,2,1:T(2,128)S(1)} %bitcast.238, f32[2,8,7,7,384]{4,0,3,2,1:T(2,128)S(1)} %copy-done.124), kind=kOutput, calls=%fused_computation.112 | convolution fusion | flops 73193472 | bytes 2449920 | tf_op jit(solution)/shard_map/transpose(jvp())/conv_general_dilated | solution.py:37
  853.3 8.9 convolution_reduce_fusion.4
  862.9 14.1 %convolution_reduce_fusion = f32[3,3,3,384]{3,2,1,0:T(4,128)S(1)} fusion(f32[2,8,7,7,384]{4,0,3,2,1:T(2,128)S(1)} %bitcast.236, f32[2,8,7,7,384]{4,0,3,2,1:T(2,128)} %copy-done.122), kind=kOutput, calls=%fused_computation.111 | convolution fusion | flops 73193472 | bytes 2449920 | tf_op jit(solution)/shard_map/transpose(jvp())/conv_general_dilated | solution.py:37
  877.8 8.2 convolution_reduce_fusion.3
  886.8 32.9 %all-reduce.25.cloned.1.call-done = (f32[2,392,768]{2,0,1:T(2,128)}, f32[2,392,768]{2,0,1:T(2,128)}) async-done(((f32[2,392,768]{2,0,1:T(2,128)}, f32[2,392,768]{2,0,1:T(2,128)}), (f32[2,392,768]{2,0,1:T(2,128)}, f32[2,392,768]{2,0,1:T(2,128)})) %all-reduce.25.cloned.1.call-update) | async-done | bytes 4816912
  937.6 34.2 %psum.149 = f32[1536]{0:T(1024)} all-reduce(f32[1536]{0:T(1024)S(1)} %copy-done.99), channel_id=1, replica_groups=mesh['dp'=16,'head'=2] {'dp'}, use_global_device_ids=true, to_apply=%region_45.46 | all-reduce | flops 1536 | bytes 12288 | tf_op jit(solution)/shard_map/psum | solution.py:274
  974.5 109.2 %all-reduce.21.cloned.1.call-done = (f32[768]{0:T(1024)}, f32[768]{0:T(1024)}, f32[27,96]{1,0:T(8,128)}, f32[27,96]{1,0:T(8,128)}, f32[27,96]{1,0:T(8,128)}, /*i...) async-done(((f32[768]{0:T(1024)}, f32[768]{0:T(1024)}, ...) | async-done | bytes 86032 | tf_op jit(solution)/shard_map/psum | solution.py:255
  1083.7 267.3 %all-reduce.23.cloned.1.call-done = (f32[768,3,384]{2,0,1:T(8,128)}, f32[384,768]{1,0:T(8,128)}, f32[768,1536]{1,0:T(8,128)}, f32[1536,768]{1,0:T(8,128)}) async-done(((f32[768,3,384]{2,0,1:T(8,128)}, f32[384,768]{1,0:T(8,128)}, f32[768,1536]{1,0:T(8,128)}, f32[1536,768]{1,0:T(8,128)}), (f32[768,3,384]{2,0,1:T(8,128)}, f32[384,768]{1,0:T(8,128)}, f32[768,1536]{1,0:T(8,128)}, ...) | async-done | bytes 14155792 | tf_op jit(solution)/shard_map/psum | solution.py:274
  (462 shorter events, 333.0 us)
Async XLA Ops:
  7.2 409.9 %copy-start = (bf16[1536,768]{1,0:T(8,128)(2,1)S(1)}, bf16[1536,768]{1,0:T(8,128)(2,1)}, u32[]{:S(2)}) copy-start(bf16[1536,768]{1,0:T(8,128)(2,1)} %param.40) | copy-start | bytes 7077892
  7.2 32.3 %all-gather.5.cloned.1.call-start = ((), (), s32[]{:S(2)}) async-start(), calls=%async_computation | async-start | bytes 1806336 | tf_op jit(solution)/shard_map/all_gather | solution.py:102
  13.6 348.1 %all-reduce.17.cloned.1.call-start = ((), (), s32[]{:S(2)}) async-start(), calls=%async_computation.4 | async-start | bytes 4816896
  15.6 59.7 %copy-start.68 = (s32[7,7]{1,0:T(8,128)}, s32[7,7]{1,0:T(8,128)S(1)}, u32[]{:S(2)}) copy-start(s32[7,7]{1,0:T(8,128)S(1)} %subtract_add_fusion) | copy-start | bytes 592
  57.2 61.2 %copy-start.6 = (bf16[2,8,7,7,4,96]{5,4,0,3,2,1:T(4,128)(2,1)}, bf16[2,8,7,7,4,96]{5,4,0,3,2,1:T(4,128)(2,1)S(1)}, u32[]{:S(2)}) copy-start(bf16[2,8,7,7,4,96]{5,4,0,3,2,1:T(4,128)(2,1)S(1)} %reshape.317) | copy-start | bytes 1806340
  101.3 158.1 %collective-permute-start.1 = (bf16[2,196,384]{2,0,1:T(2,128)(2,1)}, bf16[2,196,384]{2,0,1:T(2,128)(2,1)S(1)}, u32[]{:S(2)}, u32[]{:S(2)}) collective-permute-start(bf16[2,196,384]{2,0,1:T(2,128)(2,1)} %bitcast.8), channel_id=1, source_target_pairs={{0,2},{2,4},{4,6},{6,8},{8,10},{10,12},{12,14},{14,16},{16,18},{18... | collective-permute-start | bytes 903176 | tf_op jit(solution)/shard_map/ppermute | solution.py:24
  113.9 150.0 %collective-permute-start = (bf16[2,196,384]{2,0,1:T(2,128)(2,1)}, bf16[2,196,384]{2,0,1:T(2,128)(2,1)}, u32[]{:S(2)}, u32[]{:S(2)}) collective-permute-start(bf16[2,196,384]{2,0,1:T(2,128)(2,1)} %bitcast.3), channel_id=1, source_target_pairs={{0,2},{2,4},{4,6},{6,8},{8,10},{10,12},{12,14},{14,16},{16,18},{18... | collective-permute-start | bytes 903176 | tf_op jit(solution)/shard_map/ppermute | solution.py:24
  179.3 103.7 %copy-start.19 = (bf16[2,392,4,96]{1,3,2,0:T(8,128)(2,1)}, bf16[2,392,4,96]{1,3,2,0:T(8,128)(2,1)S(1)}, u32[]{:S(2)}) copy-start(bf16[2,392,4,96]{1,3,2,0:T(8,128)(2,1)S(1)} %copy.274) | copy-start | bytes 1806340
  293.4 68.3 %copy-start.9 = (bf16[2,196,768]{2,0,1:T(2,128)(2,1)S(1)}, bf16[2,196,768]{2,0,1:T(2,128)(2,1)}, u32[]{:S(2)}) copy-start(bf16[2,196,768]{2,0,1:T(2,128)(2,1)} %param.22) | copy-start | bytes 1806340
  293.4 68.3 %copy-start.104 = (f32[768]{0:T(1024)S(1)}, f32[768]{0:T(1024)}, u32[]{:S(2)}) copy-start(f32[768]{0:T(1024)} %param.35) | copy-start | bytes 9220
  293.4 99.1 %all-gather.7.cloned.1.call-start = ((), (), s32[]{:S(2)}) async-start(), calls=%async_computation.1 | async-start | bytes 1806336 | tf_op jit(solution)/shard_map/all_gather | solution.py:153
  369.3 47.8 %all-gather.9.cloned.1.call-start = ((), (), s32[]{:S(2)}) async-start(), calls=%async_computation.2 | async-start | bytes 1806336 | tf_op jit(solution)/shard_map/all_gather | solution.py:165
  369.9 47.2 %copy-start.116 = (f32[1536]{0:T(1024)S(1)}, f32[1536]{0:T(1024)}, u32[]{:S(2)}) copy-start(f32[1536]{0:T(1024)} %param.39) | copy-start | bytes 18436
  369.9 129.4 %all-reduce.19.cloned.1.call-start = ((), (), s32[]{:S(2)}) async-start(), calls=%async_computation.5 | async-start | bytes 4816896
  429.5 103.7 %all-gather.11.cloned.1.call-start = ((), (), s32[]{:S(2)}) async-start(), calls=%async_computation.3 | async-start | bytes 1806336 | tf_op jit(solution)/shard_map/all_gather | solution.py:184
  510.0 409.7 %all-reduce.25.cloned.1.call-start = ((), (), s32[]{:S(2)}) async-start(), calls=%async_computation.8 | async-start | bytes 9633792
  566.4 198.7 %collective-permute-start.2 = (bf16[2,196,384]{1,2,0:T(8,128)(2,1)}, bf16[2,196,384]{1,2,0:T(8,128)(2,1)}, u32[]{:S(2)}, u32[]{:S(2)}) collective-permute-start(bf16[2,196,384]{1,2,0:T(8,128)(2,1)} %slice.92), channel_id=1, source_target_pairs={{2,0},{4,2},{6,4},{8,6},{10,8},{12,10},{14,12},{16,14},{18,16},{20... | collective-permute-start | bytes 903176 | tf_op jit(solution)/shard_map/ppermute | solution.py:24
  567.7 199.9 %collective-permute-start.3 = (bf16[2,196,384]{1,2,0:T(8,128)(2,1)}, bf16[2,196,384]{1,2,0:T(8,128)(2,1)}, u32[]{:S(2)}, u32[]{:S(2)}) collective-permute-start(bf16[2,196,384]{1,2,0:T(8,128)(2,1)} %slice.91), channel_id=1, source_target_pairs={{2,0},{4,2},{6,4},{8,6},{10,8},{12,10},{14,12},{16,14},{18,16},{20... | collective-permute-start | bytes 903176 | tf_op jit(solution)/shard_map/ppermute | solution.py:24
  666.0 59.4 %copy-start.69 = (s32[7,7]{1,0:T(8,128)S(1)}, s32[7,7]{1,0:T(8,128)}, u32[]{:S(2)}) copy-start(s32[7,7]{1,0:T(8,128)} %copy-done.68) | copy-start | bytes 592
  795.6 288.1 %all-reduce.21.cloned.1.call-start = ((), (), s32[]{:S(2)}) async-start(), calls=%async_computation.6 | async-start | bytes 262144 | tf_op jit(solution)/shard_map/psum | solution.py:255
  877.8 41.9 %copy-start.38 = (f32[2,196]{0,1:T(8,128)S(1)}, f32[2,196]{0,1:T(8,128)}, u32[]{:S(2)}) copy-start(f32[2,196]{0,1:T(8,128)} %copy-done.37) | copy-start | bytes 4708
  877.8 41.9 %copy-start.41 = (f32[2,196]{0,1:T(8,128)S(1)}, f32[2,196]{0,1:T(8,128)}, u32[]{:S(2)}) copy-start(f32[2,196]{0,1:T(8,128)} %copy-done.40) | copy-start | bytes 4708
  877.8 41.9 %copy-start.77 = (f32[768]{0:T(1024)S(1)}, f32[768]{0:T(1024)}, u32[]{:S(2)}) copy-start(f32[768]{0:T(1024)} %param.23) | copy-start | bytes 9220
  931.0 420.1 %all-reduce.23.cloned.1.call-start = ((), (), s32[]{:S(2)}) async-start(), calls=%async_computation.7 | async-start | bytes 28311552 | tf_op jit(solution)/shard_map/psum | solution.py:274
  (122 other events, 910.5 us)
Sparse Core Ops, SparseCore 0:
  13.7 25.7 all-gather.4
  293.6 68.0 all-reduce.16
  369.4 23.0 all-gather.6
  394.0 23.0 all-gather.8
  429.6 69.6 all-reduce.18
  510.1 23.0 all-gather.10
  795.7 123.9 all-reduce.24
  931.1 152.5 all-reduce.20
  1093.2 257.7 all-reduce.22
where the time goes:
time: 1380 us
  waiting for transfers between devices  622 us (45%)
  local copies, waits for them, and re-layouts  283 us (21%)
  matrix products  257 us (19%)
  other arithmetic  156 us (11%)
  blocking collectives  34.2 us (2%)
  between operations  16.5 us (1%)
    psum x1, waiting for transfers between devices, on_device(): lax.psum((w_qkv_grad, w_proj_grad, w_fc1_grad, fc1_bias_grad, w_fc2_grad)...  267 us
    unnamed x12, waiting for transfers between devices  170 us
    conv_general_dilated x15, matrix products, depthwise(): lax.conv_general_dilated(volume, tiled, window_strides=(stride, 1, 1), pa...  111 us
    psum x1, waiting for transfers between devices, on_device(): lax.psum((ln1_gain_grad, ln1_bias_grad, pool_q_grad, pool_k_grad, pool_v_...  109 us
    reshape x1, local copies, waits for them, and re-layouts, relative_bias(): return summed.reshape(clip_count, head_count, L, L)  97 us
    add x1, local copies, waits for them, and re-layouts, relative_bias(): along_t[..., :, None, None] + along_h[..., None, :, None]  68.7 us
    reduce_sum x1, other arithmetic, relative_bias(): along_t[..., :, None, None] + along_h[..., None, :, None]  59.4 us
    add x2, other arithmetic, relative_bias(): along_t[..., :, None, None] + along_h[..., None, :, None]  37.8 us
  transfers between devices with their start and end apart: 13, of which 9 were waited for; matrix products, arithmetic and copies ran while one was open for 34% of the time, Pallas kernels for 0%

commit v1 on v0

v1 whole, which is shorter than its diff:
```python
from functools import partial

import jax
import jax.numpy as jnp
import numpy as np
from jax import lax
from jax.experimental import pallas as pl
from jax.experimental.pallas import tpu as pltpu
from jax.sharding import PartitionSpec as P

HEAD_DIM = 96
T_LEN = 8
HGT = 7
WID = 7
PADW = 8
L = 392
ROWS = T_LEN * HGT * PADW
TM = 4
MROWS = TM * HGT * PADW
KEYS = ROWS + 2 * MROWS
LH = 4
LW = LH * HEAD_DIM
WIN = 256
BLOCK = 128
NBLOCK = KEYS // BLOCK

EPSILON = 1e-06
HIGHEST = lax.Precision.HIGHEST
SCALE = HEAD_DIM ** (-0.5)
LOG2E = 1.4426950408889634
F32 = jnp.float32
BF16 = jnp.bfloat16
VMEM_LIMIT = 56 * 1024 * 1024

NB = T_LEN + HGT + WID
NREL = 2 * T_LEN - 1 + 2 * HGT - 1 + 2 * WID - 1
NPAIR = T_LEN * T_LEN + HGT * HGT + WID * WID


def params(**extra):
    return pltpu.CompilerParams(vmem_limit_bytes=VMEM_LIMIT, **extra)


def window_of(head):
    return 0 if head < 2 else BLOCK


def slot_of(head):
    return 192 if head < 2 else 0


def position_constants():
    t, h, w = np.meshgrid(np.arange(T_LEN), np.arange(HGT), np.arange(PADW), indexing="ij")
    t, h, w = t.ravel(), h.ravel(), w.ravel()
    valid = w < WID
    own = np.zeros((256, ROWS), np.float32)
    pick = np.zeros((256, NREL), np.float32)
    fold = np.zeros((256, 32), np.float32)
    ekey = np.zeros((32, KEYS), np.float32)
    row = 0
    base_entry = 0
    base_bias = 0
    for places, length in ((t, T_LEN), (h, HGT), (w, WID)):
        for a in range(length):
            for b in range(length):
                own[row] = (places == a) & valid
                pick[row, base_entry + a - b + length - 1] = 1
                fold[row, base_bias + b] = 1
                row += 1
        for b in range(length):
            ekey[base_bias + b, :ROWS] = (places == b) & valid
        base_entry += 2 * length - 1
        base_bias += length
    return own, pick, fold, ekey, valid


OWN_T, PICK, FOLD, EKEY, ROW_VALID = position_constants()


def fold_constants():
    out = np.zeros((2, 2, 256, WIN), np.float32)
    for variant, slot in enumerate((192, 0)):
        out[variant, 0, :, slot : slot + 32] = FOLD
        out[variant, 1, :, slot + 32 : slot + 64] = FOLD
    return out


def one_lane():
    out = np.zeros((2, 8, WIN), np.float32)
    for variant, slot in enumerate((192, 0)):
        out[variant, :, slot + NB] = 1
    return out


def head_lanes():
    out = np.zeros((LH, ROWS, WIN), np.float32)
    for head in range(LH):
        first = head * HEAD_DIM - window_of(head)
        out[head, :, first : first + HEAD_DIM] = 1
    return out


def key_constants(memory_valid):
    clip_count = memory_valid.shape[0]
    base = np.zeros((2, KEYS, WIN), np.float32)
    lane = np.zeros((2, 1, WIN), np.float32)
    for variant, slot in enumerate((192, 0)):
        base[variant, :, slot : slot + 32] = EKEY.T
        base[variant, :, slot + 32 : slot + 64] = EKEY.T
        lane[variant, :, slot + NB] = 1
    pads = np.concatenate([ROW_VALID, ROW_VALID[:MROWS], ROW_VALID[:MROWS]])
    use = jnp.concatenate(
        [jnp.ones((clip_count, ROWS), bool), jnp.repeat(memory_valid > 0, MROWS, axis=1)], axis=1
    )
    drop = jnp.where(use & jnp.asarray(pads)[None], 0.0, -1e30).astype(F32)
    return (jnp.asarray(base)[None] + drop[:, None, :, None] * jnp.asarray(lane)[None]).astype(BF16)


def nt(a, b):
    return lax.dot_general(a, b, (((1,), (1,)), ((), ())), preferred_element_type=F32)


def nn(a, b):
    return jnp.dot(a, b, preferred_element_type=F32)


def keep_rows(block):
    place = lax.broadcasted_iota(jnp.int32, block.shape, block.ndim - 2)
    return jnp.where(place < WID, block, 0.0)


def spread(dst, first, value):
    n, _, _, c = value.shape
    flat = value.reshape(n * HGT, PADW, c)
    dst[0, pl.ds(first, n), 1 : HGT + 1] = pltpu.roll(flat, 1, axis=1).reshape(n, HGT, PADW, c)
    dst[1, pl.ds(first, n), 1 : HGT + 1] = value
    dst[2, pl.ds(first, n), 1 : HGT + 1] = pltpu.roll(flat, PADW - 1, axis=1).reshape(n, HGT, PADW, c)


def pool_forward(squeeze, *refs):
    if squeeze:
        a_ref, w_ref, k_ref, s_ref, x0_ref, xp_ref, xf_ref, m_ref, xs, ys = refs
    else:
        a_ref, w_ref, k_ref, x0_ref, xp_ref, xs = refs

    @pl.when((pl.program_id(0) == 0) & (pl.program_id(1) == 0))
    def _():
        xs[...] = jnp.zeros_like(xs)
        if squeeze:
            ys[...] = jnp.zeros_like(ys)

    x = nn(a_ref[0], w_ref[0])
    x0_ref[0, 0] = x
    spread(xs, 1, x.reshape(T_LEN, HGT, PADW, LW))
    for tile in range(LW // 128):
        lanes = slice(tile * 128, tile * 128 + 128)

        def step(pair, _):
            acc = [jnp.zeros((HGT, PADW, 128), F32) for _ in range(2)]
            for a in range(3):
                for c in range(3):
                    for d in range(2):
                        block = xs[c, 2 * pair + d + a, :, :, lanes]
                        for b in range(3):
                            acc[d] = acc[d] + k_ref[0, a * 9 + b * 3 + c, :, lanes][None] * block[b : b + HGT]
            both = keep_rows(jnp.stack(acc))
            rows = pl.ds(pl.multiple_of(pair * 112, 112), 112)
            flat = both.reshape(112, 128)
            xp_ref[0, 0, rows, lanes] = flat.astype(BF16)
            if squeeze:
                xf_ref[0, 0, rows, lanes] = flat
                both = both.reshape(2 * HGT, PADW, 128)
                for c, shift in ((0, 1), (1, 0), (2, PADW - 1)):
                    moved = pltpu.roll(both, shift, axis=1) if shift else both
                    ys[c, pl.ds(2 * pair + 1, 2), 1 : HGT + 1, :, lanes] = moved.reshape(2, HGT, PADW, 128)
            return 0

        lax.fori_loop(0, T_LEN // 2, step, 0)
        if squeeze:

            def squeeze_step(pair, _):
                acc = [jnp.zeros((HGT, PADW, 128), F32) for _ in range(2)]
                for a in range(3):
                    for c in range(3):
                        for d in range(2):
                            block = ys[c, 4 * pair + 2 * d + a, :, :, lanes]
                            for b in range(3):
                                acc[d] = acc[d] + s_ref[0, a * 9 + b * 3 + c, :, lanes][None] * block[b : b + HGT]
                rows = pl.ds(pl.multiple_of(pair * 112, 112), 112)
                m_ref[0, 0, rows, lanes] = keep_rows(jnp.stack(acc)).reshape(112, 128).astype(BF16)
                return 0

            lax.fori_loop(0, TM // 2, squeeze_step, 0)


def call_pool_forward(rows, weights, kernels, squeezes=None):
    clips = rows.shape[0]
    count = weights.shape[0]
    squeeze = squeezes is not None
    tap = pl.BlockSpec((1, 27, 8, LW), lambda j, i: (j, 0, 0, 0))

    def out(n):
        return pl.BlockSpec((1, 1, n, LW), lambda j, i: (i, j, 0, 0))

    frame = pltpu.VMEM((3, T_LEN + 2, HGT + 2, PADW, LW), F32)
    shapes = [
        jax.ShapeDtypeStruct((clips, count, ROWS, LW), F32),
        jax.ShapeDtypeStruct((clips, count, ROWS, LW), BF16),
    ]
    specs = [out(ROWS), out(ROWS)]
    if squeeze:
        shapes += [
            jax.ShapeDtypeStruct((clips, count, ROWS, LW), F32),
            jax.ShapeDtypeStruct((clips, count, MROWS, LW), BF16),
        ]
        specs += [out(ROWS), out(MROWS)]
    return pl.pallas_call(
        partial(pool_forward, squeeze),
        grid=(count, clips),
        in_specs=[
            pl.BlockSpec((1, ROWS, rows.shape[2]), lambda j, i: (i, 0, 0)),
            pl.BlockSpec((1, weights.shape[1], LW), lambda j, i: (j, 0, 0)),
            tap,
        ]
        + ([tap] if squeeze else []),
        out_specs=specs,
        out_shape=shapes,
        scratch_shapes=[frame] * (2 if squeeze else 1),
        compiler_params=params(),
        cost_estimate=pl.CostEstimate(
            flops=60_000_000_000 * count // 10, bytes_accessed=4_000_000 * count, transcendentals=0
        ),
    )(rows, weights, kernels, *([squeezes] if squeeze else []))


def pool_backward(squeeze, *refs):
    if squeeze:
        u_ref, x0_ref, k_ref, m_ref, xf_ref, s_ref, dx_ref, dk_ref, ds_ref, us, ms = refs
    else:
        u_ref, x0_ref, k_ref, dx_ref, dk_ref, us = refs

    @pl.when((pl.program_id(0) == 0) & (pl.program_id(1) == 0))
    def _():
        us[...] = jnp.zeros_like(us)
        if squeeze:
            ms[...] = jnp.zeros_like(ms)

    @pl.when(pl.program_id(1) == 0)
    def _():
        dk_ref[...] = jnp.zeros_like(dk_ref)
        if squeeze:
            ds_ref[...] = jnp.zeros_like(ds_ref)

    if squeeze:
        spread(ms, 0, m_ref[0, 0].reshape(TM, HGT, PADW, LW))
    else:
        spread(us, 1, u_ref[0].reshape(T_LEN, HGT, PADW, LW))
    for tile in range(LW // 128):
        lanes = slice(tile * 128, tile * 128 + 128)
        if squeeze:

            def squeeze_step(pair, _):
                rows = pl.ds(pl.multiple_of(pair * 112, 112), 112)
                own = u_ref[0, rows, lanes].reshape(2, HGT, PADW, 128)
                fields = xf_ref[0, 0, rows, lanes].reshape(2, HGT, PADW, 128)
                acc = [own[0], own[1]]
                for a, d, frame in ((1, 0, 0), (0, 1, 1), (2, 1, 0)):
                    for c in range(3):
                        block = ms[2 - c, pair + frame, :, :, lanes]
                        for b in range(3):
                            at = block[2 - b : 2 - b + HGT]
                            number = a * 9 + b * 3 + c
                            acc[d] = acc[d] + s_ref[0, number, :, lanes][None] * at
                            ds_ref[0, number, :, lanes] += jnp.sum(fields[d] * at, axis=0)
                both = keep_rows(jnp.stack(acc)).reshape(2 * HGT, PADW, 128)
                for c, shift in ((0, 1), (1, 0), (2, PADW - 1)):
                    moved = pltpu.roll(both, shift, axis=1) if shift else both
                    us[c, pl.ds(2 * pair + 1, 2), 1 : HGT + 1, :, lanes] = moved.reshape(2, HGT, PADW, 128)
                return 0

            lax.fori_loop(0, TM, squeeze_step, 0)

        def step(pair, _):
            rows = pl.ds(pl.multiple_of(pair * 112, 112), 112)
            fields = x0_ref[0, 0, rows, lanes].reshape(2, HGT, PADW, 128)
            acc = [jnp.zeros((HGT, PADW, 128), F32) for _ in range(2)]
            for a in range(3):
                for c in range(3):
                    sums = [jnp.zeros((PADW, 128), F32) for _ in range(3)]
                    for d in range(2):
                        block = us[2 - c, 2 * pair + d + 2 - a, :, :, lanes]
                        for b in range(3):
                            at = block[2 - b : 2 - b + HGT]
                            acc[d] = acc[d] + k_ref[0, a * 9 + b * 3 + c, :, lanes][None] * at
                            sums[b] = sums[b] + jnp.sum(fields[d] * at, axis=0)
                    for b in range(3):
                        dk_ref[0, a * 9 + b * 3 + c, :, lanes] += sums[b]
            both = keep_rows(jnp.stack(acc))
            dx_ref[0, 0, rows, lanes] = both.reshape(112, 128).astype(BF16)
            return 0

        lax.fori_loop(0, T_LEN // 2, step, 0)


def call_pool_backward(upstream, fields, kernels, memory=None, pooled=None, squeezes=None):
    clips, count = fields.shape[:2]
    squeeze = memory is not None
    tap = pl.BlockSpec((1, 27, 8, LW), lambda j, i: (j, 0, 0, 0))

    def block(n):
        return pl.BlockSpec((1, 1, n, LW), lambda j, i: (i, j, 0, 0))

    grads = jax.ShapeDtypeStruct((count, 27, 8, LW), F32)
    frame = pltpu.VMEM((3, T_LEN + 2, HGT + 2, PADW, LW), F32)
    in_specs = [
        pl.BlockSpec((1, ROWS, LW), lambda j, i: (i, 0, j)),
        block(ROWS),
        tap,
    ]
    args = [upstream, fields, kernels]
    shapes = [jax.ShapeDtypeStruct((clips, count, ROWS, LW), BF16), grads]
    specs = [block(ROWS), tap]
    scratch = [frame]
    if squeeze:
        in_specs += [block(MROWS), block(ROWS), tap]
        args += [memory, pooled, squeezes]
        shapes.append(grads)
        specs.append(tap)
        scratch += [
            pltpu.VMEM((3, TM + 1, HGT + 2, PADW, LW), F32),
        ]
    return pl.pallas_call(
        partial(pool_backward, squeeze),
        grid=(count, clips),
        in_specs=in_specs,
        out_specs=specs,
        out_shape=shapes,
        scratch_shapes=scratch,
        compiler_params=params(),
        cost_estimate=pl.CostEstimate(
            flops=12_000_000_000 * count, bytes_accessed=6_000_000 * count, transcendentals=0
        ),
    )(*args)


def attention_forward(
    q_ref, kv_ref, m1_ref, m2_ref, ke_ref, tab_ref, fold_ref, one_ref, own_ref, lanes_ref,
    branch_ref, qa_ref, at_ref, lse_ref, keys, vt, scores, expo,
):
    keys[0:ROWS] = kv_ref[0, 0]
    keys[ROWS : ROWS + MROWS] = m1_ref[0, 0]
    keys[ROWS + MROWS :] = m2_ref[0, 0]
    vt[:, 0:ROWS] = kv_ref[0, 1].T
    memory = jnp.concatenate([m1_ref[0, 1], m2_ref[0, 1]], axis=0).T
    vt[:, ROWS:] = memory
    for head in range(LH):
        first = window_of(head)
        variant = head // 2
        win = slice(first, first + WIN)
        heads = lanes_ref[head]
        qm = q_ref[0, 0, :, win] * heads
        raw = nn(qm, tab_ref[head, 0]) + nn(qm, tab_ref[head, 1])
        raw = raw * own_ref[...]
        high = raw.astype(BF16)
        rest = (raw - high.astype(F32)).astype(BF16)
        placed = nn(high, fold_ref[variant, 0]) + nn(rest, fold_ref[variant, 1]) + one_ref[variant, 0:1]
        qa = qm + placed.astype(BF16)
        qa_ref[0, head] = qa

        def score(number, peak):
            rows = pl.ds(pl.multiple_of(number * BLOCK, BLOCK), BLOCK)
            ka = keys[rows, win] * heads[0:BLOCK] + ke_ref[0, variant, rows]
            s = nt(ka, qa)
            scores[rows] = s
            return jnp.maximum(peak, jnp.max(s, axis=0, keepdims=True))

        peak = lax.fori_loop(0, NBLOCK, score, jnp.full((1, ROWS), -3e38, F32))
        shift = peak * (SCALE * LOG2E)

        def soften(number, total):
            rows = pl.ds(pl.multiple_of(number * BLOCK, BLOCK), BLOCK)
            e = jnp.exp2(scores[rows] * (SCALE * LOG2E) - shift)
            expo[rows] = e.astype(BF16)
            return total + jnp.sum(e, axis=0, keepdims=True)

        total = lax.fori_loop(0, NBLOCK, soften, jnp.zeros((1, ROWS), F32))
        out = nn(vt[head * HEAD_DIM : (head + 1) * HEAD_DIM], expo[...]) * (1.0 / total)
        at_ref[0, head * HEAD_DIM : (head + 1) * HEAD_DIM] = out
        lse_ref[0, head : head + 1] = shift + jnp.log2(total)
    branch_ref[0] = (at_ref[0].T + q_ref[0, 0].astype(F32)).astype(BF16)


def whole(shape):
    return pl.BlockSpec(shape, lambda i: (0,) * len(shape))


def clip_block(*shape):
    return pl.BlockSpec((1,) + shape, lambda i: (i,) + (0,) * len(shape))


def call_attention_forward(q, kv, memory, keys_extra, tables, consts):
    clips = q.shape[0]
    return pl.pallas_call(
        attention_forward,
        grid=(clips,),
        in_specs=[
            clip_block(1, ROWS, LW),
            clip_block(2, ROWS, LW),
            pl.BlockSpec((1, 2, MROWS, LW), lambda i: (i + 1, 0, 0, 0)),
            pl.BlockSpec((1, 2, MROWS, LW), lambda i: (i, 0, 0, 0)),
            clip_block(2, KEYS, WIN),
            whole((LH, 2, WIN, 256)),
            whole((2, 2, 256, WIN)),
            whole((2, 8, WIN)),
            whole((ROWS, 256)),
            whole((LH, ROWS, WIN)),
        ],
        out_specs=[
            clip_block(ROWS, LW),
            clip_block(LH, ROWS, WIN),
            clip_block(LW, ROWS),
            clip_block(8, ROWS),
        ],
        out_shape=[
            jax.ShapeDtypeStruct((clips, ROWS, LW), BF16),
            jax.ShapeDtypeStruct((clips, LH, ROWS, WIN), BF16),
            jax.ShapeDtypeStruct((clips, LW, ROWS), F32),
            jax.ShapeDtypeStruct((clips, 8, ROWS), F32),
        ],
        scratch_shapes=[
            pltpu.VMEM((KEYS, LW), BF16),
            pltpu.VMEM((LW, KEYS), BF16),
            pltpu.VMEM((KEYS, ROWS), F32),
            pltpu.VMEM((KEYS, ROWS), BF16),
        ],
        compiler_params=params(),
        cost_estimate=pl.CostEstimate(
            flops=20_000_000_000, bytes_accessed=10_000_000, transcendentals=3_000_000
        ),
    )(q, kv, memory, memory, keys_extra, tables, consts["fold"], consts["one"], consts["own"], consts["lanes"])


def attention_backward(
    q_ref, kv_ref, m1_ref, m2_ref, ke_ref, qa_ref, dm_ref, at_ref, lse_ref, rt_ref, grow_ref, ownt_ref, ekey_ref,
    lanes_ref, dq_ref, dkv_ref, dr_ref, keys, values, kt, dmt, qms, dms, dqt,
):
    @pl.when(pl.program_id(0) == 0)
    def _():
        dr_ref[...] = jnp.zeros_like(dr_ref)

    keys[0:ROWS] = kv_ref[0, 0]
    keys[ROWS : ROWS + MROWS] = m1_ref[0, 0]
    keys[ROWS + MROWS :] = m2_ref[0, 0]
    values[0:ROWS] = kv_ref[0, 1]
    values[ROWS : ROWS + MROWS] = m1_ref[0, 1]
    values[ROWS + MROWS :] = m2_ref[0, 1]
    kt[0:LW] = keys[...].T
    kt[LW:] = ekey_ref[...]
    dmt[...] = dm_ref[0].astype(F32).T
    dqt[...] = jnp.zeros_like(dqt)
    deltas = []
    for head in range(LH):
        first = window_of(head)
        win = slice(first, first + WIN)
        span = slice(head * HEAD_DIM, (head + 1) * HEAD_DIM)
        qms[head] = q_ref[0, 0, :, win] * lanes_ref[head]
        dms[head] = dm_ref[0, :, win] * lanes_ref[head]
        deltas.append(jnp.sum(dmt[span] * at_ref[0, span], axis=0, keepdims=True))

    def step(number, _):
        rows = pl.ds(pl.multiple_of(number * BLOCK, BLOCK), BLOCK)
        dk_parts, dv_parts = [], []
        for head in range(LH):
            first = window_of(head)
            variant = head // 2
            win = slice(first, first + WIN)
            ka = keys[rows, win] * lanes_ref[head, 0:BLOCK] + ke_ref[0, variant, rows]
            s = nt(ka, qa_ref[0, head])
            p = jnp.exp2(s * (SCALE * LOG2E) - lse_ref[0, head : head + 1])
            dp = nt(values[rows, win], dms[head])
            ds = (p * (dp - deltas[head])).astype(BF16)
            dv_parts.append(nn(p.astype(BF16), dms[head]))
            dk_parts.append(nn(ds, qms[head]) * SCALE)
            kts = jnp.concatenate(
                [kt[head * HEAD_DIM : (head + 1) * HEAD_DIM, rows], kt[LW:, rows]], axis=0
            )
            dqt[head] += nn(kts, ds)
        for which, parts in ((0, dk_parts), (1, dv_parts)):
            full = jnp.concatenate(
                [
                    parts[0][:, 0:128] + parts[1][:, 0:128],
                    parts[1][:, 128:256] + parts[2][:, 0:128],
                    parts[2][:, 128:256] + parts[3][:, 128:256],
                ],
                axis=1,
            )
            both[which, rows] = full
        return 0

    both = dkv_ref.at[0]
    lax.fori_loop(0, NBLOCK, step, 0)
    for head in range(LH):
        first = window_of(head)
        span = slice(head * HEAD_DIM, (head + 1) * HEAD_DIM)
        total = dqt[head]
        grown = nn(grow_ref[...], total[HEAD_DIM:].astype(BF16)) * ownt_ref[...]
        grown = grown.astype(BF16)
        dmt[span] = dmt[span] + total[0:HEAD_DIM] * SCALE + nn(rt_ref[...], grown)
        dr_ref[:, first : first + WIN] += nn(grown, qms[head])
    dq_ref[0] = dmt[...].T


def call_attention_backward(q, kv, memory, keys_extra, qa, dmix, at, lse, rt, consts):
    clips = q.shape[0]
    return pl.pallas_call(
        attention_backward,
        grid=(clips,),
        in_specs=[
            clip_block(1, ROWS, LW),
            clip_block(2, ROWS, LW),
            pl.BlockSpec((1, 2, MROWS, LW), lambda i: (i + 1, 0, 0, 0)),
            pl.BlockSpec((1, 2, MROWS, LW), lambda i: (i, 0, 0, 0)),
            clip_block(2, KEYS, WIN),
            clip_block(LH, ROWS, WIN),
            clip_block(ROWS, LW),
            clip_block(LW, ROWS),
            clip_block(8, ROWS),
            whole((HEAD_DIM, 256)),
            whole((256, 32)),
            whole((256, ROWS)),
            whole((32, KEYS)),
            whole((LH, ROWS, WIN)),
        ],
        out_specs=[
            clip_block(ROWS, LW),
            clip_block(2, KEYS, LW),
            whole((256, LW)),
        ],
        out_shape=[
            jax.ShapeDtypeStruct((clips, ROWS, LW), F32),
            jax.ShapeDtypeStruct((clips, 2, KEYS, LW), F32),
            jax.ShapeDtypeStruct((256, LW), F32),
        ],
        scratch_shapes=[
            pltpu.VMEM((KEYS, LW), BF16),
            pltpu.VMEM((KEYS, LW), BF16),
            pltpu.VMEM((LW + 32, KEYS), BF16),
            pltpu.VMEM((LW, ROWS), F32),
            pltpu.VMEM((LH, ROWS, WIN), BF16),
            pltpu.VMEM((LH, ROWS, WIN), BF16),
            pltpu.VMEM((LH, HEAD_DIM + 32, ROWS), F32),
        ],
        compiler_params=params(),
        cost_estimate=pl.CostEstimate(
            flops=40_000_000_000, bytes_accessed=20_000_000, transcendentals=3_000_000
        ),
    )(
        q, kv, memory, memory, keys_extra, qa, dmix, at, lse, rt,
        consts["grow"], consts["ownt"], consts["ekey"], consts["lanes"],
    )


def from_behind(x, axis, by):
    count = lax.axis_size(axis)
    pairs = [(i, i + by) for i in range(count) if 0 <= i + by < count]
    return lax.ppermute(x, axis, pairs)


def layer_norm(values, scaling, offset):
    average = jnp.mean(values, axis=-1, keepdims=True)
    centred = values - average
    variance = jnp.mean(centred * centred, axis=-1, keepdims=True)
    return centred * lax.rsqrt(variance + EPSILON) * scaling + offset


def pad_rows(x):
    lead = x.shape[0]
    frames = x.shape[1] // (HGT * WID)
    grid = x.reshape(lead, frames, HGT, WID, x.shape[-1])
    grid = jnp.pad(grid, ((0, 0), (0, 0), (0, 0), (0, PADW - WID), (0, 0)))
    return grid.reshape(lead, frames * HGT * PADW, x.shape[-1])


def drop_rows(x):
    lead = x.shape[0]
    frames = x.shape[1] // (HGT * PADW)
    grid = x.reshape(lead, frames, HGT, PADW, x.shape[-1])[:, :, :, :WID]
    return grid.reshape(lead, frames * HGT * WID, x.shape[-1])


def swap(x):
    return lax.ppermute(x, "head", [(0, 1), (1, 0)])


def gather_rows(x):
    return lax.all_gather(x, "head", axis=1, tiled=True)


def scatter_sum(x):
    half = x.shape[1] // 2
    mine = lax.axis_index("head") * half
    theirs = half - mine
    sent = lax.dynamic_slice_in_dim(x, theirs, half, axis=1).astype(BF16)
    kept = lax.dynamic_slice_in_dim(x, mine, half, axis=1)
    return kept + swap(sent).astype(F32)


def taps(kernel):
    return jnp.broadcast_to(jnp.tile(kernel, (1, LH))[:, None, :], (27, 8, LW))


def on_device(
    tokens,
    ln1_gain,
    ln1_bias,
    w_qkv,
    pool_q,
    pool_k,
    pool_v,
    squeeze_k,
    squeeze_v,
    rel_t,
    rel_h,
    rel_w,
    w_proj,
    proj_bias,
    ln2_gain,
    ln2_bias,
    w_fc1,
    fc1_bias,
    w_fc2,
    fc2_bias,
    memory_valid,
    cotangent,
):
    clip_count = tokens.shape[0]
    consts = {
        "fold": jnp.asarray(fold_constants(), BF16),
        "one": jnp.asarray(one_lane(), F32),
        "own": jnp.asarray(OWN_T.T, F32),
        "ownt": jnp.asarray(OWN_T, F32),
        "lanes": jnp.asarray(head_lanes(), BF16),
        "grow": jnp.asarray(FOLD, BF16),
        "ekey": jnp.asarray(EKEY, BF16),
    }
    keys_extra = key_constants(memory_valid)
    rel_all = jnp.concatenate([rel_t, rel_h, rel_w], axis=0)
    pairs = jnp.dot(jnp.asarray(PICK), rel_all, precision=HIGHEST)
    pair_table = (pairs * HEAD_DIM**0.5).T
    table_high = pair_table.astype(BF16)
    table_rest = (pair_table - table_high.astype(F32)).astype(BF16)
    tables = jnp.stack(
        [
            jnp.stack(
                [
                    jnp.pad(
                        part,
                        (
                            (head * HEAD_DIM - window_of(head), WIN - HEAD_DIM - head * HEAD_DIM + window_of(head)),
                            (0, 0),
                        ),
                    )
                    for part in (table_high, table_rest)
                ]
            )
            for head in range(LH)
        ]
    )
    rel_rows = pairs.T.astype(BF16)
    tap_q, tap_kv = taps(pool_q)[None], jnp.stack([taps(pool_k), taps(pool_v)])
    tap_s = jnp.stack([taps(squeeze_k), taps(squeeze_v)])

    inputs = pad_rows(tokens).astype(F32)
    upstream_low = pad_rows(cotangent)
    real = (jnp.arange(inputs.shape[1]) % PADW < WID)[None, :, None]
    first_normed, first_pull = jax.vjp(layer_norm, inputs, ln1_gain, ln1_bias)
    first_rows = gather_rows(jnp.where(real, first_normed, 0.0).astype(BF16))
    w_heads = w_qkv.transpose(1, 0, 2)
    kv0, kv, kvf, mem = call_pool_forward(first_rows, w_heads[1:], tap_kv, tap_s)
    before = from_behind(mem[-2:], "dp", 1)
    q0, q = call_pool_forward(first_rows, w_heads[:1], tap_q)
    memory = jnp.concatenate([before, mem], axis=0)
    branch, qa, at, lse = call_attention_forward(q, kv, memory, keys_extra, tables, consts)
    partial_z = jnp.einsum("ale,ef->alf", branch, w_proj, preferred_element_type=F32)
    middle = inputs + scatter_sum(partial_z) + proj_bias
    second_normed, second_pull = jax.vjp(layer_norm, middle, ln2_gain, ln2_bias)
    second_rows = gather_rows(second_normed.astype(BF16))
    hidden = jnp.einsum("ald,df->alf", second_rows, w_fc1, preferred_element_type=F32) + fc1_bias
    active, gelu_pull = jax.vjp(partial(jax.nn.gelu, approximate=True), hidden)
    active_low = active.astype(BF16)
    partial_m = jnp.einsum("alf,fd->ald", active_low, w_fc2, preferred_element_type=F32)
    output = drop_rows((middle + scatter_sum(partial_m) + fc2_bias).astype(BF16))
    upstream = upstream_low.astype(F32)
    fc2_bias_grad = jnp.sum(upstream, axis=(0, 1))
    upstream_rows = gather_rows(upstream_low)
    w_fc2_grad = jnp.einsum("alf,ald->fd", active_low, upstream_rows, preferred_element_type=F32)
    (hidden_grad,) = gelu_pull(
        jnp.einsum("ald,fd->alf", upstream_rows, w_fc2, preferred_element_type=F32)
    )
    fc1_bias_grad = jnp.sum(hidden_grad, axis=(0, 1))
    hidden_low = hidden_grad.astype(BF16)
    w_fc1_grad = jnp.einsum("ald,alf->df", second_rows, hidden_low, preferred_element_type=F32)
    partial_second = jnp.einsum("alf,df->ald", hidden_low, w_fc1, preferred_element_type=F32)
    middle_part, ln2_gain_grad, ln2_bias_grad = second_pull(scatter_sum(partial_second))
    middle_grad = middle_part + upstream
    proj_bias_grad = jnp.sum(middle_grad, axis=(0, 1))
    middle_rows = gather_rows(middle_grad.astype(BF16))
    w_proj_grad = jnp.einsum("ale,alf->ef", branch, middle_rows, preferred_element_type=F32)
    dmix = jnp.einsum("alf,ef->ale", middle_rows, w_proj, preferred_element_type=F32).astype(BF16)

    w_fc2_grad, w_fc1_grad, w_proj_grad = lax.psum(
        (w_fc2_grad.astype(BF16), w_fc1_grad.astype(BF16), w_proj_grad.astype(BF16)), "dp"
    )
    dq, dkv, dr = call_attention_backward(
        q, kv, memory, keys_extra, qa, dmix, at, lse, rel_rows, consts
    )
    slots = dkv[:, :, ROWS:]
    near, far = slots[:, :, :MROWS], slots[:, :, MROWS:]
    zero = jnp.zeros((1,) + near.shape[1:], F32)
    spread_out = jnp.concatenate([zero, near, zero], axis=0) + jnp.concatenate([far, zero, zero], axis=0)
    later = from_behind(spread_out[:2].astype(BF16), "dp", -1).astype(F32)
    dq0, pool_q_grad = call_pool_backward(dq, q0, tap_q)
    leading = jnp.zeros((clip_count - 2,) + near.shape[1:], F32)
    dmem = spread_out[2:] + jnp.concatenate([leading, later], axis=0)
    own = dkv[:, :, :ROWS].transpose(0, 2, 1, 3).reshape(clip_count, ROWS, 2 * LW)
    dkv0, pool_kv_grad, squeeze_grad = call_pool_backward(own, kv0, tap_kv, dmem, kvf, tap_s)
    qkv_grad = jnp.concatenate([dq0, dkv0], axis=1)
    w_qkv_grad = jnp.einsum("ald,akle->dke", first_rows, qkv_grad, preferred_element_type=F32)
    w_qkv_grad = lax.psum(w_qkv_grad.astype(BF16), "dp")
    partial_first = jnp.einsum("akle,dke->ald", qkv_grad, w_qkv, preferred_element_type=F32)
    input_part, ln1_gain_grad, ln1_bias_grad = first_pull(scatter_sum(partial_first))
    input_grad = drop_rows(middle_grad + input_part)

    def tap_grad(g):
        return jnp.sum(jnp.sum(g, axis=1).reshape(27, LH, HEAD_DIM), axis=1)

    pair_grad = jnp.sum(dr.reshape(256, LH, HEAD_DIM), axis=1)
    rel_grad = jnp.dot(jnp.asarray(PICK.T), pair_grad, precision=HIGHEST)
    shared = lax.psum(
        (
            ln1_gain_grad,
            ln1_bias_grad,
            tap_grad(pool_q_grad[0]),
            tap_grad(pool_kv_grad[0]),
            tap_grad(pool_kv_grad[1]),
            tap_grad(squeeze_grad[0]),
            tap_grad(squeeze_grad[1]),
            rel_grad[: 2 * T_LEN - 1],
            rel_grad[2 * T_LEN - 1 : 2 * T_LEN + 2 * HGT - 2],
            rel_grad[2 * T_LEN + 2 * HGT - 2 :],
            proj_bias_grad,
            ln2_gain_grad,
            ln2_bias_grad,
            fc2_bias_grad,
        ),
        ("dp", "head"),
    )
    fc1_bias_grad = lax.psum(fc1_bias_grad, "dp")
    return (
        output,
        input_grad,
        shared[0],
        shared[1],
        w_qkv_grad.astype(F32),
        shared[2],
        shared[3],
        shared[4],
        shared[5],
        shared[6],
        shared[7],
        shared[8],
        shared[9],
        w_proj_grad.astype(F32),
        shared[10],
        shared[11],
        shared[12],
        w_fc1_grad.astype(F32),
        fc1_bias_grad,
        w_fc2_grad.astype(F32),
        shared[13],
    )


def solution(mesh):
    return jax.shard_map(
        on_device,
        mesh=mesh,
        in_specs=(
            P("dp", "head", None),
            P(),
            P(),
            P(None, None, "head"),
            P(),
            P(),
            P(),
            P(),
            P(),
            P(),
            P(),
            P(),
            P("head", None),
            P(),
            P(),
            P(),
            P(None, "head"),
            P("head"),
            P("head", None),
            P(),
            P("dp", None),
            P("dp", "head", None),
        ),
        out_specs=(
            P("dp", "head", None),
            P("dp", "head", None),
            P(),
            P(),
            P(None, None, "head"),
            P(),
            P(),
            P(),
            P(),
            P(),
            P(),
            P(),
            P(),
            P("head", None),
            P(),
            P(),
            P(),
            P(None, "head"),
            P("head"),
            P("head", None),
            P(),
        ),
        check_vma=False,
    )
```

time: 1380 us -> 666 us (0.48)
  waiting for transfers between devices: 622 us -> 344 us
  local copies, waits for them, and re-layouts: 283 us -> 57.3 us
  matrix products: 257 us -> 55.1 us
  other arithmetic: 156 us -> 38.7 us
  Pallas kernels: 0 us -> 105 us
    unnamed x12 -> x6, waiting for transfers between devices: 170 us -> 0.1 us
    psum x2, waiting for transfers between devices: 377 us -> 231 us  [the longest x1 150 us: on_device(): lax.psum((ln1_gain_grad, ln1_bias_grad, tap_grad(pool_q_grad[0]), tap_gra...]
    conv_general_dilated x15 -> x0, matrix products: 111 us -> none  [depthwise(): lax.conv_general_dilated(volume, tiled, window_strides=(stride, 1, 1), pa...]
    pallas_call x0 -> x6, Pallas kernels: none -> 105 us  [the longest x1 28.6 us: call_attention_backward(): pl.pallas_call(attention_backward, grid=(clips,), in_specs=[clip_block(1,...]
    reshape x13 -> x9, local copies, waits for them, and re-layouts: 108 us -> 5.85 us  [the longest x5 2.05 us: tap_grad(): return jnp.sum(jnp.sum(g, axis=1).reshape(27, LH, HEAD_DIM), axis=1)]
    dot_general x31 -> x13, matrix products: 131 us -> 40.6 us  [the longest x1 7.71 us: on_device(): jnp.einsum('ald,fd->alf', upstream_rows, w_fc2, preferred_element_type=F32)]
    add x4 -> x1, local copies, waits for them, and re-layouts: 72.7 us -> 0.09 us  [layer_norm(): return centred * lax.rsqrt(variance + EPSILON) * scaling + offset]
    reduce_sum x7 -> x10, other arithmetic: 65.3 us -> 7.62 us  [the longest x8 5.88 us: tap_grad(): return jnp.sum(jnp.sum(g, axis=1).reshape(27, LH, HEAD_DIM), axis=1)]
  transfers between devices with their start and end apart: 13 -> 12, of which waited for: 9 -> 10; matrix products, arithmetic and copies ran while one was open for 34% -> 13% of each run, Pallas kernels for 0% -> 2%
where the time goes in v1:
time: 666 us; the launch traced here: 660 us
  waiting for transfers between devices  344 us (52%)
  Pallas kernels  105 us (16%)
  local copies, waits for them, and re-layouts  57.3 us (9%)
  matrix products  55.1 us (8%)
  other arithmetic  38.7 us (6%)
  blocking collectives  38.1 us (6%)
  between operations  15.2 us (2%)
  starting transfers between devices  6.92 us (1%)
    psum x1, waiting for transfers between devices, on_device(): lax.psum((ln1_gain_grad, ln1_bias_grad, tap_grad(pool_q_grad[0]), tap_gra...  150 us
    psum x1, waiting for transfers between devices, on_device(): w_qkv_grad = lax.psum(w_qkv_grad.astype(BF16), 'dp')  81.7 us
    all_gather x4, waiting for transfers between devices, gather_rows(): return lax.all_gather(x, 'head', axis=1, tiled=True)  66.3 us
    ppermute x4, waiting for transfers between devices, swap(): return lax.ppermute(x, 'head', [(0, 1), (1, 0)])  45.8 us
    psum x1, blocking collectives, on_device(): fc1_bias_grad = lax.psum(fc1_bias_grad, 'dp')  38.1 us
    unnamed x145, local copies, waits for them, and re-layouts  30.9 us
    pallas_call x1, Pallas kernels, call_attention_backward(): pl.pallas_call(attention_backward, grid=(clips,), in_specs=[clip_block(1,...  28.6 us
    pallas_call x2, Pallas kernels, call_pool_backward(): pl.pallas_call(partial(pool_backward, squeeze), grid=(count, clips), in_s...  27.8 us
  transfers between devices with their start and end apart: 12, of which 10 were waited for; matrix products, arithmetic and copies ran while one was open for 13% of the time, Pallas kernels for 2%

profile of v1, /device:TPU:0, one launch (start us, length us, event | category | flops | bytes accessed | tf_op | source)
XLA Modules:
  0.0 659.9 jit_solution(2065216858020974694)
XLA Ops:
  25.9 13.0 %all-gather.5.cloned.1.call-done.refs_0_ = bf16[2,448,768]{2,1,0:T(8,128)(2,1)} async-done(((bf16[2,224,768]{2,1,0:T(8,128)(2,1)}), bf16[2,448,768]{2,1,0:T(8,128)(2,1)}) %all-gather.5.cloned.1.call-update) | async-done | bytes 1376272 | tf_op jit(solution)/shard_map/all_gather | solution.py:596
  38.9 14.9 %shard_map.482 = (f32[2,2,448,384]{3,2,1,0:T(8,128)}, bf16[2,2,448,384]{3,2,1,0:T(8,128)(2,1)}, f32[2,2,448,384]{3,2,1,0:T(8,128)}, bf16[2,2,224,384]{3,2,1,0:T(8,128)(2,1)}) custom-call(bf16[2,448,768]{2,1,0:T(8,128)(2,1)} %all-gather.5.cloned.1.call-done.refs_0_, bf16[2,768,384]{2,1,0:T(8,128)(2,1)} %slice.72.refs_1_, ...), custom_call_target="tpu_custom_call" | custom-call | flops 12000000000 | bytes 8000000 | tf_op jit(solution)/shard_map/pallas_call | solution.py:217
  57.8 6.7 %shard_map.481 = (f32[2,1,448,384]{3,2,1,0:T(8,128)}, bf16[2,1,448,384]{3,2,1,0:T(8,128)(2,1)}) custom-call(bf16[2,448,768]{2,1,0:T(8,128)(2,1)} %all-gather.5.cloned.1.call-done.refs_0_, bf16[1,768,384]{2,1,0:T(8,128)(2,1)} %slice.71.refs_1_, f32[1,27,8,384]{3,2,1,0:T(8,128)} %broadcast_in_dim_broadcast_in_dim.2.refs_2_), custom_call_target="tpu_custom_call" | custom-call | flops 6000000000 | bytes 4000000 | tf_op jit(solution)/shard_map/pallas_call | solution.py:217
  66.8 26.9 %shard_map.483 = (bf16[2,448,384]{2,1,0:T(8,128)(2,1)}, bf16[2,4,448,256]{3,2,1,0:T(8,128)(2,1)}, f32[2,384,448]{2,1,0:T(8,128)}, f32[2,8,448]{2,1,0:T(8,128)}) custom-call(bf16[2,1,448,384]{3,2,1,0:T(8,128)(2,1)} %get-tuple-element.39.q_ref, bf16[2,2,448,384]{3,2,1,0:T(8,128)(2,1)} %get-tuple-element.40.kv_ref, bf16[4,2,224,384]{3,2,1,0:T(8,128)(2,1)} %copy-done.26, ...), custom_call_target="tpu_custom_call" | custom-call | flops 20000000000 | bytes 10000000 | tf_op jit(solution)/shard_map/pallas_call | solution.py:403
  93.7 3.5 fusion.21
  99.9 17.4 %collective-permute-done.1 = bf16[2,224,768]{2,1,0:T(8,128)(2,1)} collective-permute-done((bf16[2,224,768]{2,1,0:T(8,128)(2,1)}, bf16[2,224,768]{2,1,0:T(8,128)(2,1)}, u32[]{:S(2)}, u32[]{:S(2)}) %collective-permute-start.1) | collective-permute-done | bytes 688160 | tf_op jit(solution)/shard_map/ppermute | solution.py:592
  123.8 23.4 %all-gather.7.cloned.1.call-done = bf16[2,448,768]{2,1,0:T(8,128)(2,1)} async-done(((bf16[2,224,768]{2,1,0:T(8,128)(2,1)}), bf16[2,448,768]{2,1,0:T(8,128)(2,1)}) %all-gather.7.cloned.1.call-update) | async-done | bytes 1376272 | tf_op jit(solution)/shard_map/all_gather | solution.py:596
  147.2 6.8 %fusion.11 = f32[2,448,1536]{2,1,0:T(8,128)} fusion(bf16[2,448,768]{2,1,0:T(8,128)(2,1)} %all-gather.7.cloned.1.call-done, bf16[768,1536]{1,0:T(8,128)(2,1)} %param.50), kind=kOutput, calls=%fused_computation.20 | convolution fusion | flops 2113929216 | bytes 9240576 | tf_op jit(solution)/shard_map/ald,df->alf/dot_general | solution.py:688
  153.9 19.8 %all-gather.9.cloned.1.call-done = bf16[2,448,768]{2,1,0:T(8,128)(2,1)} async-done(((bf16[2,224,768]{2,1,0:T(8,128)(2,1)}), bf16[2,448,768]{2,1,0:T(8,128)(2,1)}) %all-gather.9.cloned.1.call-update) | async-done | bytes 1376272 | tf_op jit(solution)/shard_map/all_gather | solution.py:596
  173.8 7.7 %fusion.33 = (f32[1536]{0:T(1024)S(1)}, bf16[2,448,1536]{2,1,0:T(8,128)(2,1)S(1)}) fusion(f32[2,448,1536]{2,1,0:T(8,128)} %fusion.11, f32[1536]{0:T(1024)S(1)} %copy-done.60, bf16[2,448,768]{2,1,0:T(8,128)(2,1)} %all-gather.9.cloned.1.call-done, bf16[1536,768]{1,0:T(8,128)(2,1)S(1)} %copy-done), kind=kOutput, calls=%fused_computation.111 | convolution fusion | flops 2144205312 | bytes 12005376 | tf_op jit(solution)/shard_map/ald,fd->alf/dot_general | solution.py:698
  185.1 3.5 fusion.7
  189.7 12.6 %collective-permute-done.3 = bf16[2,224,768]{2,1,0:T(8,128)(2,1)S(1)} collective-permute-done((bf16[2,224,768]{2,1,0:T(8,128)(2,1)S(1)}, bf16[2,224,768]{2,1,0:T(8,128)(2,1)S(1)}, u32[]{:S(2)}, u32[]{:S(2)}) %collective-permute-start.3) | collective-permute-done | bytes 688160 | tf_op jit(solution)/shard_map/ppermute | solution.py:592
  203.5 12.4 %collective-permute-done.2 = bf16[2,224,768]{2,1,0:T(8,128)(2,1)S(1)} collective-permute-done((bf16[2,224,768]{2,1,0:T(8,128)(2,1)S(1)}, bf16[2,224,768]{2,1,0:T(8,128)(2,1)S(1)}, u32[]{:S(2)}, u32[]{:S(2)}) %collective-permute-start.2) | collective-permute-done | bytes 688160 | tf_op jit(solution)/shard_map/ppermute | solution.py:592
  219.0 6.4 bitcast_convert_fusion.1
  225.4 8.1 %bitcast_convert_fusion = bf16[1536,768]{1,0:T(8,128)(2,1)} fusion(bf16[2,448,768]{2,1,0:T(8,128)(2,1)S(1)} %copy-done.58, f32[2,448,1536]{2,1,0:T(8,128)} %fusion.11, f32[1536]{0:T(1024)S(1)} %copy-done.60), kind=kOutput, calls=%fused_computation.9 | convolution fusion | flops 2128871424 | bytes 9246720 | tf_op jit(solution)/shard_map/alf,ald->fd/dot_general | solution.py:696
  233.5 10.1 %all-gather.11.cloned.1.call-done = bf16[2,448,768]{2,1,0:T(8,128)(2,1)} async-done(((bf16[2,224,768]{2,1,0:T(8,128)(2,1)}), bf16[2,448,768]{2,1,0:T(8,128)(2,1)}) %all-gather.11.cloned.1.call-update) | async-done | bytes 1376272 | tf_op jit(solution)/shard_map/all_gather | solution.py:596
  246.7 28.6 %shard_map.484 = (f32[2,448,384]{2,1,0:T(8,128)}, f32[2,2,896,384]{3,2,1,0:T(8,128)}, f32[256,384]{1,0:T(8,128)}) custom-call(bf16[2,1,448,384]{3,2,1,0:T(8,128)(2,1)} %get-tuple-element.39.q_ref, bf16[2,2,448,384]{3,2,1,0:T(8,128)(2,1)} %get-tuple-element.40.kv_ref, bf16[4,2,224,384]{3,2,1,0:T(8,128)(2,1)} %copy-done.26, ...), custom_call_target="tpu_custom_call" | custom-call | flops 40000000000 | bytes 20000000 | tf_op jit(solution)/shard_map/pallas_call | solution.py:515
  279.1 8.0 %shard_map.485 = (bf16[2,1,448,384]{3,2,1,0:T(8,128)(2,1)}, f32[1,27,8,384]{3,2,1,0:T(8,128)}) custom-call(f32[2,448,384]{2,1,0:T(8,128)} %get-tuple-element.46.refs_0_, f32[2,1,448,384]{3,2,1,0:T(8,128)} %get-tuple-element.47.refs_1_, f32[1,27,8,384]{3,2,1,0:T(8,128)} %broadcast_in_dim_broadcast_in_dim.2.refs_2_), custom_call_target="tpu_custom_call" | custom-call | flops 12000000000 | bytes 6000000 | tf_op jit(solution)/shard_map/pallas_call | solution.py:332
  295.2 19.8 %shard_map.486 = (bf16[2,2,448,384]{3,2,1,0:T(8,128)(2,1)}, f32[2,27,8,384]{3,2,1,0:T(8,128)}, f32[2,27,8,384]{3,2,1,0:T(8,128)}) custom-call(f32[2,448,768]{2,1,0:T(8,128)} %bitcast.123, f32[2,2,448,384]{3,2,1,0:T(8,128)} %get-tuple-element.50.refs_1_, f32[2,27,8,384]{3,2,1,0:T(8,128)} %get-tuple-element.110.refs_2_, ...), custom_call_target="tpu_custom_call" | custom-call | flops 24000000000 | bytes 12000000 | tf_op jit(solution)/shard_map/pallas_call | solution.py:332
  318.1 3.4 bitcast_convert_fusion.2
  323.3 38.1 %psum.149 = f32[1536]{0:T(1024)} all-reduce(f32[1536]{0:T(1024)S(1)} %get-tuple-element.108), channel_id=1, replica_groups=mesh['dp'=16,'head'=2] {'dp'}, use_global_device_ids=true, to_apply=%region_41.42 | all-reduce | flops 1536 | bytes 12288 | tf_op jit(solution)/shard_map/psum | solution.py:758
  364.0 5.7 convolution_bitcast_fusion
  392.9 81.7 %all-reduce.19.cloned.1.call-done = (bf16[768,3,384]{2,0,1:T(8,128)(2,1)}, bf16[384,768]{1,0:T(8,128)(2,1)}, bf16[768,1536]{1,0:T(8,128)(2,1)}, bf16[1536,768]{1,0:T(8,128)(2,1)}) async-done(((bf16[768,3,384]{2,0,1:T(8,128)(2,1)}, bf16[384,768]{1,0:T(8,128)(2,1)}, bf16[768,1536]{1,0:T(8,128)(2,1)}, bf16[1536,768]{1,0:T(8,128)(2,1)}), (bf16[768,3,384]{2,0,1:T(8,128)(2,1)}, bf16[384,768]{1,0:T(8,128)(2,1)}, ...) | async-done | bytes 7077904 | tf_op jit(solution)/shard_map/psum | solution.py:729
  485.0 149.7 %all-reduce.17.cloned.1.call-done = (f32[768]{0:T(1024)}, f32[768]{0:T(1024)}, f32[27,96]{1,0:T(8,128)}, f32[27,96]{1,0:T(8,128)}, f32[27,96]{1,0:T(8,128)}, /*i...) async-done(((f32[768]{0:T(1024)}, f32[768]{0:T(1024)}, ...) | async-done | bytes 86032 | tf_op jit(solution)/shard_map/psum | solution.py:739
  (267 shorter events, 116.4 us)
Async XLA Ops:
  7.2 166.6 %copy-start = (bf16[1536,768]{1,0:T(8,128)(2,1)S(1)}, bf16[1536,768]{1,0:T(8,128)(2,1)}, u32[]{:S(2)}) copy-start(bf16[1536,768]{1,0:T(8,128)(2,1)} %param.52) | copy-start | bytes 7077892
  7.2 31.7 %all-gather.5.cloned.1.call-start = ((), (), s32[]{:S(2)}) async-start(), calls=%async_computation | async-start | bytes 2064384 | tf_op jit(solution)/shard_map/all_gather | solution.py:596
  8.6 108.8 %copy-start.4 = (bf16[2,4,7,7,768]{4,3,2,1,0:T(8,128)(2,1)}, bf16[2,4,7,7,768]{4,3,2,1,0:T(8,128)(2,1)S(1)}, u32[]{:S(2)}) copy-start(bf16[2,4,7,7,768]{4,3,2,1,0:T(8,128)(2,1)S(1)} %copy.75) | copy-start | bytes 1806340
  11.1 136.1 %all-gather.7.cloned.1.call-start = ((), (), s32[]{:S(2)}) async-start(), calls=%async_computation.1 | async-start | bytes 2064384 | tf_op jit(solution)/shard_map/all_gather | solution.py:596
  38.9 16.9 %copy-start.17 = (bf16[1,2,256,256]{3,2,1,0:T(8,128)(2,1)S(1)}, bf16[1,2,256,256]{3,2,1,0:T(8,128)(2,1)}, u32[]{:S(2)}) copy-start(bf16[1,2,256,256]{3,2,1,0:T(8,128)(2,1)} %get-tuple-element.115) | copy-start | bytes 786436
  53.9 10.6 %collective-permute-start = (bf16[2,2,224,384]{3,2,1,0:T(8,128)(2,1)}, bf16[2,2,224,384]{3,2,1,0:T(8,128)(2,1)S(1)}, u32[]{:S(2)}, u32[]{:S(2)}) collective-permute-start(bf16[2,2,224,384]{3,2,1,0:T(8,128)(2,1)} %get-tuple-element.41), channel_id=1, source_target_pairs={{0,2},{2,4},{4,6},{6,8},{8,10},{10,12},{12,14},{14,16},{16,18},{18... | collective-permute-start | bytes 2064392 | tf_op jit(solution)/shard_map/ppermute | solution.py:566
  66.8 26.9 %copy-start.23 = (bf16[384,768]{1,0:T(8,128)(2,1)S(1)}, bf16[384,768]{1,0:T(8,128)(2,1)}, u32[]{:S(2)}) copy-start(bf16[384,768]{1,0:T(8,128)(2,1)} %param.46) | copy-start | bytes 1769476
  99.4 17.9 %collective-permute-start.1 = (bf16[2,224,768]{2,1,0:T(8,128)(2,1)}, bf16[2,224,768]{2,1,0:T(8,128)(2,1)}, u32[]{:S(2)}, u32[]{:S(2)}) collective-permute-start(bf16[2,224,768]{2,1,0:T(8,128)(2,1)} %dynamic-slice_convert_fusion.3), channel_id=1, source_target_pairs={{0,1},{1,0},{2,3},{3,2},{4,5},{5,4},{6,7},{7,6},{8,9},{9,8},{10,11... | collective-permute-start | bytes 2064392 | tf_op jit(solution)/shard_map/ppermute | solution.py:592
  99.9 19.2 %copy-start.31 = (f32[768]{0:T(1024)S(1)}, f32[768]{0:T(1024)}, u32[]{:S(2)}) copy-start(f32[768]{0:T(1024)} %param.47) | copy-start | bytes 9220
  121.5 52.3 %all-gather.9.cloned.1.call-start = ((), (), s32[]{:S(2)}) async-start(), calls=%async_computation.2 | async-start | bytes 2064384 | tf_op jit(solution)/shard_map/all_gather | solution.py:596
  123.5 50.3 %copy-start.60 = (f32[1536]{0:T(1024)S(1)}, f32[1536]{0:T(1024)}, u32[]{:S(2)}) copy-start(f32[1536]{0:T(1024)} %param.51) | copy-start | bytes 18436
  123.5 120.1 %all-gather.11.cloned.1.call-start = ((), (), s32[]{:S(2)}) async-start(), calls=%async_computation.3 | async-start | bytes 2064384 | tf_op jit(solution)/shard_map/all_gather | solution.py:596
  183.9 18.4 %collective-permute-start.3 = (bf16[2,224,768]{2,1,0:T(8,128)(2,1)S(1)}, bf16[2,224,768]{2,1,0:T(8,128)(2,1)S(1)}, u32[]{:S(2)}, u32[]{:S(2)}) collective-permute-start(bf16[2,224,768]{2,1,0:T(8,128)(2,1)S(1)} %dynamic-slice_convert_fusion.1), channel_id=1, source_target_pairs={{0,1},{1,0},{2,3},{3,2},{4,5},{5,4},{6,7},{7,6},{8,9},{9,8},{10,11... | collective-permute-start | bytes 2064392 | tf_op jit(solution)/shard_map/ppermute | solution.py:592
  188.6 27.3 %copy-start.51 = (f32[768]{0:T(1024)S(1)}, f32[768]{0:T(1024)}, u32[]{:S(2)}) copy-start(f32[768]{0:T(1024)} %param.53) | copy-start | bytes 9220
  188.7 27.3 %collective-permute-start.2 = (bf16[2,224,768]{2,1,0:T(8,128)(2,1)S(1)}, bf16[2,224,768]{2,1,0:T(8,128)(2,1)S(1)}, u32[]{:S(2)}, u32[]{:S(2)}) collective-permute-start(bf16[2,224,768]{2,1,0:T(8,128)(2,1)S(1)} %dynamic-slice_convert_fusion.2), channel_id=1, source_target_pairs={{0,1},{1,0},{2,3},{3,2},{4,5},{5,4},{6,7},{7,6},{8,9},{9,8},{10,11... | collective-permute-start | bytes 2064392 | tf_op jit(solution)/shard_map/ppermute | solution.py:592
  218.5 256.1 %all-reduce.19.cloned.1.call-start = ((), (), s32[]{:S(2)}) async-start(), calls=%async_computation.5 | async-start | bytes 14155776 | tf_op jit(solution)/shard_map/psum | solution.py:729
  225.4 18.3 %copy-start.24 = (bf16[384,768]{1,0:T(8,128)(2,1)S(1)}, bf16[384,768]{1,0:T(8,128)(2,1)}, u32[]{:S(2)}) copy-start(bf16[384,768]{1,0:T(8,128)(2,1)} %param.46) | copy-start | bytes 1769476
  277.6 16.3 %collective-permute-start.4 = (bf16[2,2,224,384]{3,2,1,0:T(8,128)(2,1)S(1)}, bf16[2,2,224,384]{3,2,1,0:T(8,128)(2,1)S(1)}, u32[]{:S(2)}, u32[]{:S(2)}) collective-permute-start(bf16[2,2,224,384]{3,2,1,0:T(8,128)(2,1)S(1)} %slice.87), channel_id=1, source_target_pairs={{2,0},{4,2},{6,4},{8,6},{10,8},{12,10},{14,12},{16,14},{18,16},{20... | collective-permute-start | bytes 2064392 | tf_op jit(solution)/shard_map/ppermute | solution.py:566
  295.2 19.8 %copy-start.28 = (bf16[2,3,448,384]{3,2,1,0:T(8,128)(2,1)S(1)}, bf16[2,3,448,384]{3,2,1,0:T(8,128)(2,1)}, u32[]{:S(2)}) copy-start(bf16[2,3,448,384]{3,2,1,0:T(8,128)(2,1)} %constant_dynamic-update-slice_fusion.3) | copy-start | bytes 6193156
  321.5 41.4 %copy-start.27 = (f32[1,27,8,384]{3,2,1,0:T(8,128)S(1)}, f32[1,27,8,384]{3,2,1,0:T(8,128)}, u32[]{:S(2)}) copy-start(f32[1,27,8,384]{3,2,1,0:T(8,128)} %get-tuple-element.53) | copy-start | bytes 995332
  321.5 42.3 %copy-start.25 = (f32[256,384]{1,0:T(8,128)S(1)}, f32[256,384]{1,0:T(8,128)}, u32[]{:S(2)}) copy-start(f32[256,384]{1,0:T(8,128)} %get-tuple-element.56) | copy-start | bytes 1179652
  321.5 313.2 %all-reduce.17.cloned.1.call-start = ((), (), s32[]{:S(2)}) async-start(), calls=%async_computation.4 | async-start | bytes 262144 | tf_op jit(solution)/shard_map/psum | solution.py:739
  372.0 12.5 %collective-permute-start.5 = (bf16[2,224,768]{2,1,0:T(8,128)(2,1)}, bf16[2,224,768]{2,1,0:T(8,128)(2,1)}, u32[]{:S(2)}, u32[]{:S(2)}) collective-permute-start(bf16[2,224,768]{2,1,0:T(8,128)(2,1)} %dynamic-slice_convert_fusion), channel_id=1, source_target_pairs={{0,1},{1,0},{2,3},{3,2},{4,5},{5,4},{6,7},{7,6},{8,9},{9,8},{10,11... | collective-permute-start | bytes 2064392 | tf_op jit(solution)/shard_map/ppermute | solution.py:592
  482.5 170.4 %copy-start.1 = (bf16[1536,768]{1,0:T(8,128)(2,1)S(1)}, bf16[1536,768]{1,0:T(8,128)(2,1)}, u32[]{:S(2)}) copy-start(bf16[1536,768]{1,0:T(8,128)(2,1)} %param.52) | copy-start | bytes 7077892
  (52 other events, 224.3 us)
Sparse Core Ops, SparseCore 0:
  11.2 27.6 all-gather.4
  121.6 25.5 all-gather.6
  148.7 24.9 all-gather.8
  218.6 24.9 all-gather.10
  321.6 152.8 all-reduce.18
  482.6 152.1 all-reduce.16

commit v2 on v1

--- a/solution.py
+++ b/solution.py
@@ -318,8 +318,8 @@
         tap,
     ]
     args = [upstream, fields, kernels]
-    shapes = [jax.ShapeDtypeStruct((clips, count, ROWS, LW), BF16), grads]
-    specs = [block(ROWS), tap]
+    shapes = [jax.ShapeDtypeStruct((count, clips, ROWS, LW), BF16), grads]
+    specs = [pl.BlockSpec((1, 1, ROWS, LW), lambda j, i: (j, i, 0, 0)), tap]
     scratch = [frame]
     if squeeze:
         in_specs += [block(MROWS), block(ROWS), tap]
@@ -560,6 +560,297 @@
     )
 
 
+EARLY = 40
+HEAD_EARLY = 32
+LATE = 8
+
+
+def tail_kernel(
+    groups,
+    rows_a, rows_x, branch, dq, dkv, w_ref, tokens, middle, gain, early,
+    out, grad, early_out, late_out,
+    acc, send_a, recv_a, send_b, recv_b, send_c, recv_c, result,
+    send_y, recv_y, ebuf, e_y, e_core, e_x, e_z, lbuf, l_y, l_core, l_x, l_z,
+    sems_send, sems_recv, small_send, small_recv,
+):
+    dp = lax.axis_index("dp")
+    head = lax.axis_index("head")
+    core = lax.rem(dp, 2)
+    xbit = lax.rem(lax.div(dp, 2), 2)
+    group = lax.div(dp, 4)
+    to_core = (dp + 1 - 2 * core, head)
+    to_x = (dp + 2 - 4 * xbit, head)
+    to_y = (dp, 1 - head)
+    peers = [
+        (lax.rem(group + o, groups) * 4 + lax.rem(dp, 4), head) for o in range(1, groups)
+    ]
+    barrier = pltpu.get_barrier_semaphore()
+    everyone = [to_core, to_x, to_y] + peers
+    for peer in everyone:
+        pl.semaphore_signal(barrier, inc=1, device_id=peer, device_id_type=pl.DeviceIdType.MESH)
+    pl.semaphore_wait(barrier, len(everyone))
+
+    total = out.shape[1]
+    half, quarter, chunk = total // 2, total // 4, total // 4 // groups
+    depth = rows_a.shape[1]
+
+    def copy(src, dst, send, recv, peer):
+        made = pltpu.make_async_remote_copy(
+            src_ref=src, dst_ref=dst, send_sem=send, recv_sem=recv,
+            device_id=peer, device_id_type=pl.DeviceIdType.MESH,
+        )
+        made.start()
+        return made
+
+    pieces = ((rows_x, branch), (rows_a, dq), (rows_a, dkv.at[0]), (rows_a, dkv.at[1]))
+
+    def product(number, first):
+        left, right = pieces[number]
+        return lax.dot_general(
+            left[:, pl.ds(pl.multiple_of(first, 128), half)], right[...], (((0,), (0,)), ((), ())),
+            preferred_element_type=F32,
+        )
+
+    flights = {}
+
+    def phase_a(number):
+        send_a[number] = product(number, (1 - core) * half).astype(BF16)
+        flights[number, "a"] = copy(
+            send_a.at[number], recv_a.at[number], sems_send.at[number, 0], sems_recv.at[number, 0], to_core
+        )
+        acc[number] = product(number, core * half)
+
+    def phase_b(number):
+        flights[number, "a"].wait()
+        theirs = pl.ds(pl.multiple_of((1 - xbit) * quarter, 16), quarter)
+        send_b[number] = (acc[number, theirs] + recv_a[number, theirs].astype(F32)).astype(BF16)
+        flights[number, "b"] = copy(
+            send_b.at[number], recv_b.at[number], sems_send.at[number, 1], sems_recv.at[number, 1], to_x
+        )
+
+    def phase_c(number):
+        mine = pl.ds(pl.multiple_of(xbit * quarter, 16), quarter)
+        flights[number, "b"].wait()
+        both = acc[number, mine] + recv_a[number, mine].astype(F32) + recv_b[number].astype(F32)
+        acc[number, 0:quarter] = both
+        send_c[number] = both.astype(BF16)
+        for o in range(1, groups):
+            rows = pl.ds(pl.multiple_of(lax.rem(group + o, groups) * chunk, 16), chunk)
+            flights[number, "c", o] = copy(
+                send_c.at[number, rows], recv_c.at[number, o - 1],
+                sems_send.at[number, 1 + o], sems_recv.at[number, 1 + o], peers[o - 1],
+            )
+
+    def place(g):
+        return core * half + xbit * quarter + g * chunk
+
+    def phase_d(number):
+        own = acc[number, pl.ds(pl.multiple_of(group * chunk, 16), chunk)]
+        for o in range(1, groups):
+            flights[number, "c", o].wait()
+            own = own + recv_c[number, o - 1].astype(F32)
+        rows = pl.ds(pl.multiple_of(place(group), 16), chunk)
+        result[number, rows] = own.astype(BF16)
+        for o in range(1, groups):
+            flights[number, "d", o] = copy(
+                result.at[number, rows], result.at[number, rows],
+                sems_send.at[number, groups + o], sems_recv.at[number, groups + o], peers[o - 1],
+            )
+
+    def phase_e(number):
+        for o in range(1, groups):
+            flights[number, "d", o].wait()
+        rows = pl.ds(pl.multiple_of(place(0), 16), quarter)
+        flights[number, "e"] = copy(
+            result.at[number, rows], result.at[number, rows],
+            sems_send.at[number, 2 * groups], sems_recv.at[number, 2 * groups], to_x,
+        )
+
+    def phase_f(number):
+        flights[number, "e"].wait()
+        rows = pl.ds(pl.multiple_of(core * half, 16), half)
+        flights[number, "f"] = copy(
+            result.at[number, rows], result.at[number, rows],
+            sems_send.at[number, 2 * groups + 1], sems_recv.at[number, 2 * groups + 1], to_core,
+        )
+
+    def phase_g(number):
+        flights[number, "f"].wait()
+        out[number] = result[number]
+
+    def small(buffer, slots, rows_y, base):
+        slot_y, slot_core, slot_x, slot_z = slots
+
+        def one():
+            flights[base, 0] = copy(
+                buffer.at[0, 0:rows_y], slot_y, small_send.at[base], small_recv.at[base], to_y
+            )
+
+        def two():
+            flights[base, 0].wait()
+            buffer[1] = buffer[0]
+            buffer[1, 0:rows_y] = buffer[0, 0:rows_y] + slot_y[...]
+            flights[base, 1] = copy(
+                buffer.at[1], slot_core, small_send.at[base + 1], small_recv.at[base + 1], to_core
+            )
+
+        def three():
+            flights[base, 1].wait()
+            buffer[2] = buffer[1] + slot_core[...]
+            flights[base, 2] = copy(
+                buffer.at[2], slot_x, small_send.at[base + 2], small_recv.at[base + 2], to_x
+            )
+
+        def four():
+            flights[base, 2].wait()
+            buffer[3] = buffer[2] + slot_x[...]
+            for o in range(1, groups):
+                flights[base, 2 + o] = copy(
+                    buffer.at[3], slot_z.at[o - 1],
+                    small_send.at[base + 2 + o], small_recv.at[base + 2 + o], peers[o - 1],
+                )
+
+        def five(target):
+            added = buffer[3]
+            for o in range(1, groups):
+                flights[base, 2 + o].wait()
+                added = added + slot_z[o - 1]
+            target[...] = added
+
+        return one, two, three, four, five
+
+    local = tokens.shape[1]
+    clips = tokens.shape[0]
+
+    def input_gradient(clip, side):
+        rows = pl.ds(pl.multiple_of(clip * 2 * local + side * local, 16), local)
+        return nt(dq[rows], w_ref[0]) + nt(dkv[0, rows], w_ref[1]) + nt(dkv[1, rows], w_ref[2])
+
+    ebuf[0] = early[...]
+    e1, e2, e3, e4, e5 = small(ebuf, (e_y, e_core, e_x, e_z), HEAD_EARLY, 0)
+    l1, l2, l3, l4, l5 = small(lbuf, (l_y, l_core, l_x, l_z), LATE, 2 + groups)
+    e1()
+    for clip in range(clips):
+        send_y[clip] = input_gradient(clip, 1 - head).astype(BF16)
+    across = copy(send_y, recv_y, small_send.at[4 + 2 * groups], small_recv.at[4 + 2 * groups], to_y)
+    phase_a(0)
+    e2()
+    phase_a(1)
+    phase_b(0)
+    e3()
+    phase_a(2)
+    phase_b(1)
+    phase_c(0)
+    phase_a(3)
+    phase_b(2)
+    phase_c(1)
+    phase_d(0)
+    e4()
+    mine = [input_gradient(clip, head) for clip in range(clips)]
+    across.wait()
+    bias_sum = jnp.zeros((8, gain.shape[1]), F32)
+    gain_sum = jnp.zeros((8, gain.shape[1]), F32)
+    for clip in range(clips):
+        u = mine[clip] + recv_y[clip].astype(F32)
+        v = tokens[clip]
+        centred = v - jnp.mean(v, axis=-1, keepdims=True)
+        scale = lax.rsqrt(jnp.mean(centred * centred, axis=-1, keepdims=True) + EPSILON)
+        xhat = centred * scale
+        w = u * gain[0:1]
+        dv = scale * (
+            w - jnp.mean(w, axis=-1, keepdims=True) - xhat * jnp.mean(w * xhat, axis=-1, keepdims=True)
+        )
+        grad[clip] = middle[clip] + dv
+        gain_sum = gain_sum + jnp.sum((u * xhat).reshape(-1, 8, u.shape[1]), axis=0)
+        bias_sum = bias_sum + jnp.sum(u.reshape(-1, 8, u.shape[1]), axis=0)
+    lbuf[0, 0:1] = jnp.sum(gain_sum, axis=0, keepdims=True)
+    lbuf[0, 1:2] = jnp.sum(bias_sum, axis=0, keepdims=True)
+    lbuf[0, 2:8] = jnp.zeros((6, gain.shape[1]), F32)
+    l1()
+    phase_b(3)
+    phase_c(2)
+    phase_d(1)
+    phase_e(0)
+    l2()
+    phase_c(3)
+    phase_d(2)
+    phase_e(1)
+    phase_f(0)
+    l3()
+    phase_d(3)
+    phase_e(2)
+    phase_f(1)
+    l4()
+    phase_g(0)
+    phase_e(3)
+    phase_f(2)
+    phase_g(1)
+    e5(early_out)
+    l5(late_out)
+    phase_f(3)
+    phase_g(2)
+    phase_g(3)
+
+
+def call_tail(rows_a, rows_x, branch, dq, dkv, weights, tokens, middle, gain, early):
+    groups = lax.axis_size("dp") // 4
+    width = tokens.shape[2]
+    chunk = -(-width // (4 * groups) // 16) * 16
+    total = chunk * 4 * groups
+    clips, local = tokens.shape[:2]
+    if total != width:
+        extra = ((0, 0), (0, total - width))
+        rows_a, rows_x = jnp.pad(rows_a, extra), jnp.pad(rows_x, extra)
+    half, quarter = total // 2, total // 4
+    vmem = pl.BlockSpec(memory_space=pltpu.VMEM)
+    smalls = 5 + 2 * groups
+
+    def slots(n):
+        return [
+            pltpu.VMEM((n, width), F32),
+            pltpu.VMEM((n, width), F32),
+            pltpu.VMEM((groups - 1, n, width), F32),
+        ]
+
+    return pl.pallas_call(
+        partial(tail_kernel, groups),
+        in_specs=[vmem] * 10,
+        out_specs=[vmem] * 4,
+        out_shape=[
+            jax.ShapeDtypeStruct((4, total, LW), BF16),
+            jax.ShapeDtypeStruct(tokens.shape, F32),
+            jax.ShapeDtypeStruct((EARLY, width), F32),
+            jax.ShapeDtypeStruct((LATE, width), F32),
+        ],
+        scratch_shapes=[
+            pltpu.VMEM((4, half, LW), F32),
+            pltpu.VMEM((4, half, LW), BF16),
+            pltpu.VMEM((4, half, LW), BF16),
+            pltpu.VMEM((4, quarter, LW), BF16),
+            pltpu.VMEM((4, quarter, LW), BF16),
+            pltpu.VMEM((4, quarter, LW), BF16),
+            pltpu.VMEM((4, groups - 1, chunk, LW), BF16),
+            pltpu.VMEM((4, total, LW), BF16),
+            pltpu.VMEM((clips, local, width), BF16),
+            pltpu.VMEM((clips, local, width), BF16),
+            pltpu.VMEM((4, EARLY, width), F32),
+            pltpu.VMEM((HEAD_EARLY, width), F32),
+            *slots(EARLY),
+            pltpu.VMEM((4, LATE, width), F32),
+            pltpu.VMEM((LATE, width), F32),
+            *slots(LATE),
+            pltpu.SemaphoreType.DMA((4, 2 * groups + 2)),
+            pltpu.SemaphoreType.DMA((4, 2 * groups + 2)),
+            pltpu.SemaphoreType.DMA((smalls,)),
+            pltpu.SemaphoreType.DMA((smalls,)),
+        ],
+        compiler_params=params(collective_id=0, has_side_effects=True),
+        cost_estimate=pl.CostEstimate(
+            flops=30_000_000_000, bytes_accessed=20_000_000, transcendentals=0
+        ),
+    )(rows_a, rows_x, branch, dq, dkv, weights, tokens, middle, gain, early)
+
+
 def from_behind(x, axis, by):
     count = lax.axis_size(axis)
     pairs = [(i, i + by) for i in range(count) if 0 <= i + by < count]
@@ -593,7 +884,10 @@
 
 
 def gather_rows(x):
-    return lax.all_gather(x, "head", axis=1, tiled=True)
+    half = x.shape[1]
+    mine = lax.axis_index("head") * half
+    both = jnp.concatenate([x, x], axis=1)
+    return lax.dynamic_update_slice_in_dim(both, swap(x), half - mine, axis=1)
 
 
 def scatter_sum(x):
@@ -673,9 +967,10 @@
     inputs = pad_rows(tokens).astype(F32)
     upstream_low = pad_rows(cotangent)
     real = (jnp.arange(inputs.shape[1]) % PADW < WID)[None, :, None]
-    first_normed, first_pull = jax.vjp(layer_norm, inputs, ln1_gain, ln1_bias)
+    first_normed = layer_norm(inputs, ln1_gain, ln1_bias)
     first_rows = gather_rows(jnp.where(real, first_normed, 0.0).astype(BF16))
     w_heads = w_qkv.transpose(1, 0, 2)
+    upstream_rows = gather_rows(lax.optimization_barrier((upstream_low, first_rows))[0])
     kv0, kv, kvf, mem = call_pool_forward(first_rows, w_heads[1:], tap_kv, tap_s)
     before = from_behind(mem[-2:], "dp", 1)
     q0, q = call_pool_forward(first_rows, w_heads[:1], tap_q)
@@ -692,7 +987,6 @@
     output = drop_rows((middle + scatter_sum(partial_m) + fc2_bias).astype(BF16))
     upstream = upstream_low.astype(F32)
     fc2_bias_grad = jnp.sum(upstream, axis=(0, 1))
-    upstream_rows = gather_rows(upstream_low)
     w_fc2_grad = jnp.einsum("alf,ald->fd", active_low, upstream_rows, preferred_element_type=F32)
     (hidden_grad,) = gelu_pull(
         jnp.einsum("ald,fd->alf", upstream_rows, w_fc2, preferred_element_type=F32)
@@ -705,12 +999,9 @@
     middle_grad = middle_part + upstream
     proj_bias_grad = jnp.sum(middle_grad, axis=(0, 1))
     middle_rows = gather_rows(middle_grad.astype(BF16))
-    w_proj_grad = jnp.einsum("ale,alf->ef", branch, middle_rows, preferred_element_type=F32)
     dmix = jnp.einsum("alf,ef->ale", middle_rows, w_proj, preferred_element_type=F32).astype(BF16)
 
-    w_fc2_grad, w_fc1_grad, w_proj_grad = lax.psum(
-        (w_fc2_grad.astype(BF16), w_fc1_grad.astype(BF16), w_proj_grad.astype(BF16)), "dp"
-    )
+    w_fc2_grad, w_fc1_grad = lax.psum((w_fc2_grad.astype(BF16), w_fc1_grad.astype(BF16)), "dp")
     dq, dkv, dr = call_attention_backward(
         q, kv, memory, keys_extra, qa, dmix, at, lse, rel_rows, consts
     )
@@ -724,44 +1015,65 @@
     dmem = spread_out[2:] + jnp.concatenate([leading, later], axis=0)
     own = dkv[:, :, :ROWS].transpose(0, 2, 1, 3).reshape(clip_count, ROWS, 2 * LW)
     dkv0, pool_kv_grad, squeeze_grad = call_pool_backward(own, kv0, tap_kv, dmem, kvf, tap_s)
-    qkv_grad = jnp.concatenate([dq0, dkv0], axis=1)
-    w_qkv_grad = jnp.einsum("ald,akle->dke", first_rows, qkv_grad, preferred_element_type=F32)
-    w_qkv_grad = lax.psum(w_qkv_grad.astype(BF16), "dp")
-    partial_first = jnp.einsum("akle,dke->ald", qkv_grad, w_qkv, preferred_element_type=F32)
-    input_part, ln1_gain_grad, ln1_bias_grad = first_pull(scatter_sum(partial_first))
-    input_grad = drop_rows(middle_grad + input_part)
-
     def tap_grad(g):
         return jnp.sum(jnp.sum(g, axis=1).reshape(27, LH, HEAD_DIM), axis=1)
 
     pair_grad = jnp.sum(dr.reshape(256, LH, HEAD_DIM), axis=1)
     rel_grad = jnp.dot(jnp.asarray(PICK.T), pair_grad, precision=HIGHEST)
-    shared = lax.psum(
-        (
-            ln1_gain_grad,
-            ln1_bias_grad,
-            tap_grad(pool_q_grad[0]),
-            tap_grad(pool_kv_grad[0]),
-            tap_grad(pool_kv_grad[1]),
-            tap_grad(squeeze_grad[0]),
-            tap_grad(squeeze_grad[1]),
-            rel_grad[: 2 * T_LEN - 1],
-            rel_grad[2 * T_LEN - 1 : 2 * T_LEN + 2 * HGT - 2],
-            rel_grad[2 * T_LEN + 2 * HGT - 2 :],
-            proj_bias_grad,
-            ln2_gain_grad,
-            ln2_bias_grad,
-            fc2_bias_grad,
-        ),
-        ("dp", "head"),
+    parts = (
+        tap_grad(pool_q_grad[0]),
+        tap_grad(pool_kv_grad[0]),
+        tap_grad(pool_kv_grad[1]),
+        tap_grad(squeeze_grad[0]),
+        tap_grad(squeeze_grad[1]),
+        rel_grad,
+        proj_bias_grad,
+        ln2_gain_grad,
+        ln2_bias_grad,
+        fc2_bias_grad,
     )
-    fc1_bias_grad = lax.psum(fc1_bias_grad, "dp")
+    flat = jnp.concatenate([part.reshape(-1) for part in parts])
+    width = tokens.shape[2]
+    early = jnp.concatenate(
+        [
+            jnp.pad(flat, (0, HEAD_EARLY * width - flat.size)).reshape(HEAD_EARLY, width),
+            jnp.pad(fc1_bias_grad, (0, (EARLY - HEAD_EARLY) * width - fc1_bias_grad.size)).reshape(-1, width),
+        ]
+    )
+    tail, input_grad, early, late = call_tail(
+        first_rows.reshape(-1, width),
+        middle_rows.reshape(-1, width),
+        branch.reshape(-1, LW),
+        dq0.reshape(-1, LW),
+        dkv0.reshape(2, -1, LW),
+        w_heads,
+        inputs,
+        middle_grad,
+        ln1_gain.reshape(1, -1),
+        early,
+    )
+    input_grad = drop_rows(input_grad)
+    flat = early[:HEAD_EARLY].reshape(-1)
+    shared = [late[0], late[1]]
+    for part in parts:
+        shared.append(flat[: part.size].reshape(part.shape))
+        flat = flat[part.size :]
+    rel_grad = shared.pop(7)
+    shared[7:7] = [
+        rel_grad[: 2 * T_LEN - 1],
+        rel_grad[2 * T_LEN - 1 : 2 * T_LEN + 2 * HGT - 2],
+        rel_grad[2 * T_LEN + 2 * HGT - 2 :],
+    ]
+    fc1_bias_grad = early[HEAD_EARLY:].reshape(-1)[: fc1_bias_grad.size]
+    tail = tail[:, :width].astype(F32)
+    w_proj_grad = tail[0].T
+    w_qkv_grad = tail[1:].transpose(1, 0, 2)
     return (
         output,
         input_grad,
         shared[0],
         shared[1],
-        w_qkv_grad.astype(F32),
+        w_qkv_grad,
         shared[2],
         shared[3],
         shared[4],
@@ -770,7 +1082,7 @@
         shared[7],
         shared[8],
         shared[9],
-        w_proj_grad.astype(F32),
+        w_proj_grad,
         shared[10],
         shared[11],
         shared[12],

time: 666 us -> 403 us (0.61)
  waiting for transfers between devices: 344 us -> 62.9 us
  Pallas kernels: 105 us -> 182 us
  blocking collectives: 38.1 us -> 0 us
  matrix products: 55.1 us -> 33.7 us
    psum x2 -> x1, waiting for transfers between devices: 231 us -> 0.01 us  [on_device(): lax.psum((w_fc2_grad.astype(BF16), w_fc1_grad.astype(BF16)), 'dp')]
    pallas_call x0 -> x1, Pallas kernels: none -> 76.2 us  [call_tail(): pl.pallas_call(partial(tail_kernel, groups), in_specs=[vmem] * 10, out_sp...]
    all_gather x4 -> x0, waiting for transfers between devices: 66.3 us -> none  [gather_rows(): return lax.all_gather(x, 'head', axis=1, tiled=True)]
    psum x1 -> x0, blocking collectives: 38.1 us -> none  [on_device(): fc1_bias_grad = lax.psum(fc1_bias_grad, 'dp')]
    ppermute x4 -> x7, waiting for transfers between devices: 45.8 us -> 62.9 us  [swap(): return lax.ppermute(x, 'head', [(0, 1), (1, 0)])]
    unnamed x145 -> x115, local copies, waits for them, and re-layouts: 30.9 us -> 17.7 us
    dot_general x3 -> x0, matrix products: 10.8 us -> none  [the longest x1 5.72 us: on_device(): jnp.einsum('akle,dke->ald', qkv_grad, w_qkv, preferred_element_type=F32)]
    ppermute x4 -> x7, starting transfers between devices: 2.51 us -> 9.95 us  [swap(): return lax.ppermute(x, 'head', [(0, 1), (1, 0)])]
  transfers between devices with their start and end apart: 12 -> 10, of which waited for: 10 -> 5; matrix products, arithmetic and copies ran while one was open for 13% -> 19% of each run, Pallas kernels for 2% -> 35%
where the time goes in v2:
time: 403 us; the launch traced here: 397 us
  Pallas kernels  182 us (45%)
  waiting for transfers between devices  62.9 us (16%)
  local copies, waits for them, and re-layouts  57.5 us (14%)
  matrix products  33.7 us (8%)
  other arithmetic  33.2 us (8%)
  between operations  15.2 us (4%)
  starting transfers between devices  12.9 us (3%)
    pallas_call x1, Pallas kernels, call_tail(): pl.pallas_call(partial(tail_kernel, groups), in_specs=[vmem] * 10, out_sp...  76.2 us
    ppermute x7, waiting for transfers between devices, swap(): return lax.ppermute(x, 'head', [(0, 1), (1, 0)])  62.9 us
    pallas_call x1, Pallas kernels, call_attention_backward(): pl.pallas_call(attention_backward, grid=(clips,), in_specs=[clip_block(1,...  29.1 us
    pallas_call x2, Pallas kernels, call_pool_backward(): pl.pallas_call(partial(pool_backward, squeeze), grid=(count, clips), in_s...  27.9 us
    pallas_call x1, Pallas kernels, call_attention_forward(): pl.pallas_call(attention_forward, grid=(clips,), in_specs=[clip_block(1,...  26.9 us
    pallas_call x2, Pallas kernels, call_pool_forward(): pl.pallas_call(partial(pool_forward, squeeze), grid=(count, clips), in_sp...  21.5 us
    unnamed x115, local copies, waits for them, and re-layouts  17.7 us
    ppermute x7, starting transfers between devices, swap(): return lax.ppermute(x, 'head', [(0, 1), (1, 0)])  9.95 us
  transfers between devices with their start and end apart: 10, of which 5 were waited for; matrix products, arithmetic and copies ran while one was open for 19% of the time, Pallas kernels for 35%

profile of v2, /device:TPU:0, one launch (start us, length us, event | category | flops | bytes accessed | tf_op | source)
XLA Modules:
  0.0 397.1 jit_solution(9930257777046868955)
XLA Ops:
  12.4 3.0 collective-permute-start
  33.4 14.9 %shard_map.482 = (f32[2,2,448,384]{3,2,1,0:T(8,128)}, bf16[2,2,448,384]{3,2,1,0:T(8,128)(2,1)}, f32[2,2,448,384]{3,2,1,0:T(8,128)}, bf16[2,2,224,384]{3,2,1,0:T(8,128)(2,1)}) custom-call(bf16[2,448,768]{2,1,0:T(8,128)(2,1)} %copy-done.15, bf16[2,768,384]{2,1,0:T(8,128)(2,1)} %slice.207.refs_1_, f32[2,27,8,384]{3,2,1,0:T(8,128)} %get-tuple-element.194.refs_2_, ...), custom_call_target="tpu_custom_call" | custom-call | flops 12000000000 | bytes 8000000 | tf_op jit(solution)/shard_map/pallas_call | solution.py:217
  51.7 6.7 %shard_map.481 = (f32[2,1,448,384]{3,2,1,0:T(8,128)}, bf16[2,1,448,384]{3,2,1,0:T(8,128)(2,1)}) custom-call(bf16[2,448,768]{2,1,0:T(8,128)(2,1)} %copy-done.15, bf16[1,768,384]{2,1,0:T(8,128)(2,1)} %slice.206.refs_1_, f32[1,27,8,384]{3,2,1,0:T(8,128)} %broadcast_in_dim_broadcast_in_dim.2.refs_2_), custom_call_target="tpu_custom_call" | custom-call | flops 6000000000 | bytes 4000000 | tf_op jit(solution)/shard_map/pallas_call | solution.py:217
  60.8 26.9 %shard_map.483 = (bf16[2,448,384]{2,1,0:T(8,128)(2,1)}, bf16[2,4,448,256]{3,2,1,0:T(8,128)(2,1)}, f32[2,384,448]{2,1,0:T(8,128)}, f32[2,8,448]{2,1,0:T(8,128)}) custom-call(bf16[2,1,448,384]{3,2,1,0:T(8,128)(2,1)} %get-tuple-element.44.q_ref, bf16[2,2,448,384]{3,2,1,0:T(8,128)(2,1)} %get-tuple-element.45.kv_ref, bf16[4,2,224,384]{3,2,1,0:T(8,128)(2,1)} %copy-done.30, ...), custom_call_target="tpu_custom_call" | custom-call | flops 20000000000 | bytes 10000000 | tf_op jit(solution)/shard_map/pallas_call | solution.py:403
  96.3 13.3 %collective-permute-done.2 = bf16[2,224,768]{2,1,0:T(8,128)(2,1)} collective-permute-done((bf16[2,224,768]{2,1,0:T(8,128)(2,1)}, bf16[2,224,768]{2,1,0:T(8,128)(2,1)}, u32[]{:S(2)}, u32[]{:S(2)}) %collective-permute-start.2) | collective-permute-done | bytes 688160 | tf_op jit(solution)/shard_map/ppermute | solution.py:883
  109.7 2.9 add_add_fusion.1
  119.8 4.6 %collective-permute-done.5 = bf16[2,224,768]{2,1,0:T(8,128)(2,1)} collective-permute-done((bf16[2,224,768]{2,1,0:T(8,128)(2,1)}, bf16[2,224,768]{2,1,0:T(8,128)(2,1)}, u32[]{:S(2)}, u32[]{:S(2)}) %collective-permute-start.5) | collective-permute-done | bytes 688160 | tf_op jit(solution)/shard_map/ppermute | solution.py:883
  125.7 13.4 %collective-permute-done.3 = bf16[2,224,768]{2,1,0:T(8,128)(2,1)S(1)} collective-permute-done((bf16[2,224,768]{2,1,0:T(8,128)(2,1)S(1)}, bf16[2,224,768]{2,1,0:T(8,128)(2,1)S(1)}, u32[]{:S(2)}, u32[]{:S(2)}) %collective-permute-start.3) | collective-permute-done | bytes 688160 | tf_op jit(solution)/shard_map/ppermute | solution.py:883
  140.3 2.3 fusion.11
  142.6 5.1 %fusion.7 = f32[2,448,768]{2,1,0:T(8,128)} fusion(bf16[1536,768]{1,0:T(8,128)(2,1)S(1)} %copy-done, f32[2,448,1536]{2,1,0:T(8,128)S(1)} %fusion.11, f32[1536]{0:T(1024)S(1)} %copy-done.50), kind=kOutput, calls=%fused_computation.16 | convolution fusion | flops 2127691776 | bytes 10622976 | tf_op jit(solution)/shard_map/alf,fd->ald/dot_general | solution.py:986
  147.7 6.7 %fusion.27 = (f32[1536]{0:T(1024)S(1)}, bf16[2,448,1536]{2,1,0:T(8,128)(2,1)}) fusion(f32[2,448,1536]{2,1,0:T(8,128)S(1)} %fusion.11, f32[1536]{0:T(1024)S(1)} %copy-done.50, bf16[2,448,768]{2,1,0:T(8,128)(2,1)S(1)} %constant_dynamic-update-slice_fusion.3, bf16[1536,768]{1,0:T(8,128)(2,1)S(1)} %copy-done), kind=kOutput, calls=%fused_computation.107 | convolution fusion | flops 2144205312 | bytes 12005376 | tf_op jit(solution)/shard_map/ald,fd->alf/dot_general | solution.py:992
  157.4 5.0 %fusion.9 = f32[2,448,768]{2,1,0:T(8,128)S(1)} fusion(bf16[768,1536]{1,0:T(8,128)(2,1)} %param.50, bf16[2,448,1536]{2,1,0:T(8,128)(2,1)} %get-tuple-element.193), kind=kOutput, calls=%fused_computation.18 | convolution fusion | flops 2113929216 | bytes 7864320 | tf_op jit(solution)/shard_map/alf,df->ald/dot_general | solution.py:997
  163.2 4.9 %bitcast_convert_fusion = bf16[1536,768]{1,0:T(8,128)(2,1)} fusion(bf16[2,448,768]{2,1,0:T(8,128)(2,1)S(1)} %copy-done.20, f32[2,448,1536]{2,1,0:T(8,128)S(1)} %bitcast.119, f32[1536]{0:T(1024)S(1)} %copy-done.50), kind=kOutput, calls=%fused_computation.9 | convolution fusion | flops 2128871424 | bytes 9246720 | tf_op jit(solution)/shard_map/alf,ald->fd/dot_general | solution.py:990
  168.1 21.0 %collective-permute-done.6 = bf16[2,224,768]{2,1,0:T(8,128)(2,1)S(1)} collective-permute-done((bf16[2,224,768]{2,1,0:T(8,128)(2,1)S(1)}, bf16[2,224,768]{2,1,0:T(8,128)(2,1)S(1)}, u32[]{:S(2)}, u32[]{:S(2)}) %collective-permute-start.6) | collective-permute-done | bytes 688160 | tf_op jit(solution)/shard_map/ppermute | solution.py:883
  195.8 4.0 %bitcast_convert_fusion.1 = bf16[768,1536]{1,0:T(8,128)(2,1)} fusion(bf16[2,448,768]{2,1,0:T(8,128)(2,1)S(1)} %copy-done.18, bf16[2,448,1536]{2,1,0:T(8,128)(2,1)S(1)} %copy-done.53), kind=kOutput, calls=%fused_computation.10 | convolution fusion | flops 2115108864 | bytes 6488064 | tf_op jit(solution)/shard_map/ald,alf->df/dot_general | solution.py:996
  201.4 10.5 %collective-permute-done.7 = bf16[2,224,768]{2,1,0:T(8,128)(2,1)S(1)} collective-permute-done((bf16[2,224,768]{2,1,0:T(8,128)(2,1)S(1)}, bf16[2,224,768]{2,1,0:T(8,128)(2,1)S(1)}, u32[]{:S(2)}, u32[]{:S(2)}) %collective-permute-start.7) | collective-permute-done | bytes 688160 | tf_op jit(solution)/shard_map/ppermute | solution.py:883
  213.8 29.1 %shard_map.484 = (f32[2,448,384]{2,1,0:T(8,128)}, f32[2,2,896,384]{3,2,1,0:T(8,128)}, f32[256,384]{1,0:T(8,128)}) custom-call(bf16[2,1,448,384]{3,2,1,0:T(8,128)(2,1)} %get-tuple-element.44.q_ref, bf16[2,2,448,384]{3,2,1,0:T(8,128)(2,1)} %get-tuple-element.45.kv_ref, bf16[4,2,224,384]{3,2,1,0:T(8,128)(2,1)} %copy-done.30, ...), custom_call_target="tpu_custom_call" | custom-call | flops 40000000000 | bytes 20000000 | tf_op jit(solution)/shard_map/pallas_call | solution.py:515
  248.2 8.1 %shard_map.485 = (bf16[1,2,448,384]{3,2,1,0:T(8,128)(2,1)}, f32[1,27,8,384]{3,2,1,0:T(8,128)}) custom-call(f32[2,448,384]{2,1,0:T(8,128)} %get-tuple-element.52.refs_0_, f32[2,1,448,384]{3,2,1,0:T(8,128)} %get-tuple-element.53.refs_1_, f32[1,27,8,384]{3,2,1,0:T(8,128)} %broadcast_in_dim_broadcast_in_dim.2.refs_2_), custom_call_target="tpu_custom_call" | custom-call | flops 12000000000 | bytes 6000000 | tf_op jit(solution)/shard_map/pallas_call | solution.py:332
  264.0 19.8 %shard_map.486 = (bf16[2,2,448,384]{3,2,1,0:T(8,128)(2,1)}, f32[2,27,8,384]{3,2,1,0:T(8,128)}, f32[2,27,8,384]{3,2,1,0:T(8,128)}) custom-call(f32[2,448,768]{2,1,0:T(8,128)} %bitcast.102, f32[2,2,448,384]{3,2,1,0:T(8,128)} %get-tuple-element.56.refs_1_, f32[2,27,8,384]{3,2,1,0:T(8,128)} %get-tuple-element.194.refs_2_, ...), custom_call_target="tpu_custom_call" | custom-call | flops 24000000000 | bytes 12000000 | tf_op jit(solution)/shard_map/pallas_call | solution.py:332
  288.1 76.2 %shard_map.487 = (bf16[4,768,384]{2,1,0:T(8,128)(2,1)}, f32[2,224,768]{2,1,0:T(8,128)}, f32[40,768]{1,0:T(8,128)}, f32[8,768]{1,0:T(8,128)}) custom-call(bf16[896,768]{1,0:T(8,128)(2,1)} %bitcast.109, bf16[896,768]{1,0:T(8,128)(2,1)} %bitcast.110, bf16[896,384]{1,0:T(8,128)(2,1)} %bitcast.112, bf16[896,384]{1,0:T(8,128)(2,1)} %bitcast.117, ...), custom_call_target="tpu_custom_call" | custom-call | flops 30000001024 | bytes 20000000 | tf_op jit(solution)/shard_map/pallas_call | solution.py:815
  366.1 3.3 copy.80
  378.8 4.0 %slice_bitcast_fusion = f32[768,3,384]{2,0,1:T(8,128)} fusion(f32[4,768,384]{2,1,0:T(8,128)} %copy-done.4), kind=kLoop, calls=%fused_computation.12 | loop fusion | bytes 7077888 | tf_op jit(solution)/shard_map/transpose | solution.py:1070
  382.8 4.6 %convert_element_type.131 = f32[768,1536]{1,0:T(8,128)} convert(bf16[768,1536]{1,0:T(8,128)(2,1)} %get-tuple-element.165) | non-fusion elementwise | flops 1179648 | bytes 7077888 | tf_op jit(solution)/shard_map/convert_element_type | solution.py:1089
  387.5 2.5 convert_element_type.133
  (248 shorter events, 89.0 us)
Async XLA Ops:
  7.2 135.4 %copy-start = (bf16[1536,768]{1,0:T(8,128)(2,1)S(1)}, bf16[1536,768]{1,0:T(8,128)(2,1)}, u32[]{:S(2)}) copy-start(bf16[1536,768]{1,0:T(8,128)(2,1)} %param.52) | copy-start | bytes 7077892
  7.2 375.6 %all-reduce.17.cloned.1.call-start = ((), (), s32[]{:S(2)}) async-start(), calls=%async_computation | async-start | bytes 9437184 | tf_op jit(solution)/shard_map/psum | solution.py:1004
  12.4 18.7 %collective-permute-start = (bf16[2,224,768]{2,1,0:T(8,128)(2,1)S(1)}, bf16[2,224,768]{2,1,0:T(8,128)(2,1)}, u32[]{:S(2)}, u32[]{:S(2)}) collective-permute-start(bf16[2,224,768]{2,1,0:T(8,128)(2,1)S(1)} %select_convert_fusion), channel_id=1, source_target_pairs={{0,1},{1,0},{2,3},{3,2},{4,5},{5,4},{6,7},{7,6},{8,9},{9,8},{10,11... | collective-permute-start | bytes 2064392 | tf_op jit(solution)/shard_map/ppermute | solution.py:883
  48.2 10.2 %collective-permute-start.1 = (bf16[2,2,224,384]{3,2,1,0:T(8,128)(2,1)}, bf16[2,2,224,384]{3,2,1,0:T(8,128)(2,1)S(1)}, u32[]{:S(2)}, u32[]{:S(2)}) collective-permute-start(bf16[2,2,224,384]{3,2,1,0:T(8,128)(2,1)} %get-tuple-element.46), channel_id=1, source_target_pairs={{0,2},{2,4},{4,6},{6,8},{8,10},{10,12},{12,14},{14,16},{16,18},{18... | collective-permute-start | bytes 2064392 | tf_op jit(solution)/shard_map/ppermute | solution.py:857
  60.8 26.9 %copy-start.22 = (bf16[384,768]{1,0:T(8,128)(2,1)S(1)}, bf16[384,768]{1,0:T(8,128)(2,1)}, u32[]{:S(2)}) copy-start(bf16[384,768]{1,0:T(8,128)(2,1)} %param.46) | copy-start | bytes 1769476
  91.2 18.4 %copy-start.46 = (f32[768]{0:T(1024)S(1)}, f32[768]{0:T(1024)}, u32[]{:S(2)}) copy-start(f32[768]{0:T(1024)} %param.47) | copy-start | bytes 9220
  92.2 17.5 %collective-permute-start.2 = (bf16[2,224,768]{2,1,0:T(8,128)(2,1)}, bf16[2,224,768]{2,1,0:T(8,128)(2,1)}, u32[]{:S(2)}, u32[]{:S(2)}) collective-permute-start(bf16[2,224,768]{2,1,0:T(8,128)(2,1)} %dynamic-slice_convert_fusion.2), channel_id=1, source_target_pairs={{0,1},{1,0},{2,3},{3,2},{4,5},{5,4},{6,7},{7,6},{8,9},{9,8},{10,11... | collective-permute-start | bytes 2064392 | tf_op jit(solution)/shard_map/ppermute | solution.py:883
  94.8 14.9 %copy-start.5 = (f32[2,4,7,8,768]{4,3,2,1,0:T(8,128)S(1)}, f32[2,4,7,8,768]{4,3,2,1,0:T(8,128)}, u32[]{:S(2)}) copy-start(f32[2,4,7,8,768]{4,3,2,1,0:T(8,128)} %pad_convert_fusion) | copy-start | bytes 4128772
  95.7 28.7 %collective-permute-start.5 = (bf16[2,224,768]{2,1,0:T(8,128)(2,1)}, bf16[2,224,768]{2,1,0:T(8,128)(2,1)}, u32[]{:S(2)}, u32[]{:S(2)}) collective-permute-start(bf16[2,224,768]{2,1,0:T(8,128)(2,1)} %bitcast.23), channel_id=1, source_target_pairs={{0,1},{1,0},{2,3},{3,2},{4,5},{5,4},{6,7},{7,6},{8,9},{9,8},{10,11... | collective-permute-start | bytes 2064392 | tf_op jit(solution)/shard_map/ppermute | solution.py:883
  116.1 22.9 %collective-permute-start.3 = (bf16[2,224,768]{2,1,0:T(8,128)(2,1)S(1)}, bf16[2,224,768]{2,1,0:T(8,128)(2,1)S(1)}, u32[]{:S(2)}, u32[]{:S(2)}) collective-permute-start(bf16[2,224,768]{2,1,0:T(8,128)(2,1)S(1)} %add_convert_fusion.2), channel_id=1, source_target_pairs={{0,1},{1,0},{2,3},{3,2},{4,5},{5,4},{6,7},{7,6},{8,9},{9,8},{10,11... | collective-permute-start | bytes 2064392 | tf_op jit(solution)/shard_map/ppermute | solution.py:883
  125.6 22.2 %copy-start.19 = (bf16[2,448,768]{2,1,0:T(8,128)(2,1)}, bf16[2,448,768]{2,1,0:T(8,128)(2,1)S(1)}, u32[]{:S(2)}) copy-start(bf16[2,448,768]{2,1,0:T(8,128)(2,1)S(1)} %constant_dynamic-update-slice_fusion.3) | copy-start | bytes 4128772
  125.6 14.7 %copy-start.49 = (bf16[768,1536]{1,0:T(8,128)(2,1)S(1)}, bf16[768,1536]{1,0:T(8,128)(2,1)}, u32[]{:S(2)}) copy-start(bf16[768,1536]{1,0:T(8,128)(2,1)} %param.50) | copy-start | bytes 7077892
  154.4 8.8 %slice-start = ((s8[5505024]{0:T(1024)(128)(4,1)}), s8[4194304]{0:T(1024)(128)(4,1)S(1)}, s32[]{:S(2)}) async-start(s8[5505024]{0:T(1024)(128)(4,1)} %bitcast.118), calls=%async_computation.1 | async-start | bytes 8388608
  156.0 34.2 %collective-permute-start.4 = (bf16[2,224,768]{2,1,0:T(8,128)(2,1)S(1)}, bf16[2,224,768]{2,1,0:T(8,128)(2,1)S(1)}, u32[]{:S(2)}, u32[]{:S(2)}) collective-permute-start(bf16[2,224,768]{2,1,0:T(8,128)(2,1)S(1)} %dynamic-slice_convert_fusion.1), channel_id=1, source_target_pairs={{0,1},{1,0},{2,3},{3,2},{4,5},{5,4},{6,7},{7,6},{8,9},{9,8},{10,11... | collective-permute-start | bytes 2064392 | tf_op jit(solution)/shard_map/ppermute | solution.py:883
  157.4 5.8 %copy-start.20 = (bf16[2,448,768]{2,1,0:T(8,128)(2,1)S(1)}, bf16[2,448,768]{2,1,0:T(8,128)(2,1)}, u32[]{:S(2)}) copy-start(bf16[2,448,768]{2,1,0:T(8,128)(2,1)} %copy-done.19) | copy-start | bytes 4128772
  157.4 5.8 %slice-start.1 = ((s8[5505024]{0:T(1024)(128)(4,1)}), s8[1310720]{0:T(1024)(128)(4,1)S(1)}, s32[]{:S(2)}) async-start(s8[5505024]{0:T(1024)(128)(4,1)} %bitcast.118), calls=%async_computation.2 | async-start | bytes 2621440
  162.4 26.6 %copy-start.3 = (f32[2,224,768]{2,1,0:T(8,128)S(1)}, f32[2,224,768]{2,1,0:T(8,128)}, u32[]{:S(2)}) copy-start(f32[2,224,768]{2,1,0:T(8,128)} %add_add_fusion.1) | copy-start | bytes 4128772
  162.5 26.6 %collective-permute-start.6 = (bf16[2,224,768]{2,1,0:T(8,128)(2,1)S(1)}, bf16[2,224,768]{2,1,0:T(8,128)(2,1)S(1)}, u32[]{:S(2)}, u32[]{:S(2)}) collective-permute-start(bf16[2,224,768]{2,1,0:T(8,128)(2,1)S(1)} %dynamic-slice_convert_fusion), channel_id=1, source_target_pairs={{0,1},{1,0},{2,3},{3,2},{4,5},{5,4},{6,7},{7,6},{8,9},{9,8},{10,11... | collective-permute-start | bytes 2064392 | tf_op jit(solution)/shard_map/ppermute | solution.py:883
  194.5 17.5 %collective-permute-start.7 = (bf16[2,224,768]{2,1,0:T(8,128)(2,1)S(1)}, bf16[2,224,768]{2,1,0:T(8,128)(2,1)S(1)}, u32[]{:S(2)}, u32[]{:S(2)}) collective-permute-start(bf16[2,224,768]{2,1,0:T(8,128)(2,1)S(1)} %convert_element_type.124), channel_id=1, source_target_pairs={{0,1},{1,0},{2,3},{3,2},{4,5},{5,4},{6,7},{7,6},{8,9},{9,8},{10,11... | collective-permute-start | bytes 2064392 | tf_op jit(solution)/shard_map/ppermute | solution.py:883
  201.3 10.7 %copy-start.23 = (bf16[384,768]{1,0:T(8,128)(2,1)S(1)}, bf16[384,768]{1,0:T(8,128)(2,1)}, u32[]{:S(2)}) copy-start(bf16[384,768]{1,0:T(8,128)(2,1)} %param.46) | copy-start | bytes 1769476
  212.0 30.9 %copy-start.16 = (bf16[2,448,768]{2,1,0:T(8,128)(2,1)}, bf16[2,448,768]{2,1,0:T(8,128)(2,1)S(1)}, u32[]{:S(2)}) copy-start(bf16[2,448,768]{2,1,0:T(8,128)(2,1)S(1)} %constant_dynamic-update-slice_fusion.2) | copy-start | bytes 4128772
  246.9 14.9 %collective-permute-start.8 = (bf16[2,2,224,384]{3,2,1,0:T(8,128)(2,1)S(1)}, bf16[2,2,224,384]{3,2,1,0:T(8,128)(2,1)S(1)}, u32[]{:S(2)}, u32[]{:S(2)}) collective-permute-start(bf16[2,2,224,384]{3,2,1,0:T(8,128)(2,1)S(1)} %slice.237), channel_id=1, source_target_pairs={{2,0},{4,2},{6,4},{8,6},{10,8},{12,10},{14,12},{16,14},{18,16},{20... | collective-permute-start | bytes 2064392 | tf_op jit(solution)/shard_map/ppermute | solution.py:857
  248.2 9.4 %copy-start.29 = (f32[256,384]{1,0:T(8,128)S(1)}, f32[256,384]{1,0:T(8,128)}, u32[]{:S(2)}) copy-start(f32[256,384]{1,0:T(8,128)} %get-tuple-element.62) | copy-start | bytes 1179652
  364.3 6.4 %copy-start.11 = (bf16[4,768,384]{2,1,0:T(8,128)(2,1)S(1)}, bf16[4,768,384]{2,1,0:T(8,128)(2,1)}, u32[]{:S(2)}) copy-start(bf16[4,768,384]{2,1,0:T(8,128)(2,1)} %get-tuple-element.65) | copy-start | bytes 7077892
  (42 other events, 114.2 us)
Sparse Core Ops, SparseCore 0:
  200.0 134.2 all-reduce.16

commit v3 on v1

--- a/solution.py
+++ b/solution.py
@@ -30,7 +30,7 @@
 LOG2E = 1.4426950408889634
 F32 = jnp.float32
 BF16 = jnp.bfloat16
-VMEM_LIMIT = 56 * 1024 * 1024
+VMEM_LIMIT = 58 * 1024 * 1024
 
 NB = T_LEN + HGT + WID
 NREL = 2 * T_LEN - 1 + 2 * HGT - 1 + 2 * WID - 1
@@ -150,7 +150,7 @@
             ys[...] = jnp.zeros_like(ys)
 
     x = nn(a_ref[0], w_ref[0])
-    x0_ref[0, 0] = x
+    x0_ref[0, 0] = x.astype(BF16)
     spread(xs, 1, x.reshape(T_LEN, HGT, PADW, LW))
     for tile in range(LW // 128):
         lanes = slice(tile * 128, tile * 128 + 128)
@@ -168,7 +168,7 @@
             flat = both.reshape(112, 128)
             xp_ref[0, 0, rows, lanes] = flat.astype(BF16)
             if squeeze:
-                xf_ref[0, 0, rows, lanes] = flat
+                xf_ref[0, 0, rows, lanes] = flat.astype(BF16)
                 both = both.reshape(2 * HGT, PADW, 128)
                 for c, shift in ((0, 1), (1, 0), (2, PADW - 1)):
                     moved = pltpu.roll(both, shift, axis=1) if shift else both
@@ -204,13 +204,13 @@
 
     frame = pltpu.VMEM((3, T_LEN + 2, HGT + 2, PADW, LW), F32)
     shapes = [
-        jax.ShapeDtypeStruct((clips, count, ROWS, LW), F32),
+        jax.ShapeDtypeStruct((clips, count, ROWS, LW), BF16),
         jax.ShapeDtypeStruct((clips, count, ROWS, LW), BF16),
     ]
     specs = [out(ROWS), out(ROWS)]
     if squeeze:
         shapes += [
-            jax.ShapeDtypeStruct((clips, count, ROWS, LW), F32),
+            jax.ShapeDtypeStruct((clips, count, ROWS, LW), BF16),
             jax.ShapeDtypeStruct((clips, count, MROWS, LW), BF16),
         ]
         specs += [out(ROWS), out(MROWS)]
@@ -231,116 +231,6 @@
             flops=60_000_000_000 * count // 10, bytes_accessed=4_000_000 * count, transcendentals=0
         ),
     )(rows, weights, kernels, *([squeezes] if squeeze else []))
-
-
-def pool_backward(squeeze, *refs):
-    if squeeze:
-        u_ref, x0_ref, k_ref, m_ref, xf_ref, s_ref, dx_ref, dk_ref, ds_ref, us, ms = refs
-    else:
-        u_ref, x0_ref, k_ref, dx_ref, dk_ref, us = refs
-
-    @pl.when((pl.program_id(0) == 0) & (pl.program_id(1) == 0))
-    def _():
-        us[...] = jnp.zeros_like(us)
-        if squeeze:
-            ms[...] = jnp.zeros_like(ms)
-
-    @pl.when(pl.program_id(1) == 0)
-    def _():
-        dk_ref[...] = jnp.zeros_like(dk_ref)
-        if squeeze:
-            ds_ref[...] = jnp.zeros_like(ds_ref)
-
-    if squeeze:
-        spread(ms, 0, m_ref[0, 0].reshape(TM, HGT, PADW, LW))
-    else:
-        spread(us, 1, u_ref[0].reshape(T_LEN, HGT, PADW, LW))
-    for tile in range(LW // 128):
-        lanes = slice(tile * 128, tile * 128 + 128)
-        if squeeze:
-
-            def squeeze_step(pair, _):
-                rows = pl.ds(pl.multiple_of(pair * 112, 112), 112)
-                own = u_ref[0, rows, lanes].reshape(2, HGT, PADW, 128)
-                fields = xf_ref[0, 0, rows, lanes].reshape(2, HGT, PADW, 128)
-                acc = [own[0], own[1]]
-                for a, d, frame in ((1, 0, 0), (0, 1, 1), (2, 1, 0)):
-                    for c in range(3):
-                        block = ms[2 - c, pair + frame, :, :, lanes]
-                        for b in range(3):
-                            at = block[2 - b : 2 - b + HGT]
-                            number = a * 9 + b * 3 + c
-                            acc[d] = acc[d] + s_ref[0, number, :, lanes][None] * at
-                            ds_ref[0, number, :, lanes] += jnp.sum(fields[d] * at, axis=0)
-                both = keep_rows(jnp.stack(acc)).reshape(2 * HGT, PADW, 128)
-                for c, shift in ((0, 1), (1, 0), (2, PADW - 1)):
-                    moved = pltpu.roll(both, shift, axis=1) if shift else both
-                    us[c, pl.ds(2 * pair + 1, 2), 1 : HGT + 1, :, lanes] = moved.reshape(2, HGT, PADW, 128)
-                return 0
-
-            lax.fori_loop(0, TM, squeeze_step, 0)
-
-        def step(pair, _):
-            rows = pl.ds(pl.multiple_of(pair * 112, 112), 112)
-            fields = x0_ref[0, 0, rows, lanes].reshape(2, HGT, PADW, 128)
-            acc = [jnp.zeros((HGT, PADW, 128), F32) for _ in range(2)]
-            for a in range(3):
-                for c in range(3):
-                    sums = [jnp.zeros((PADW, 128), F32) for _ in range(3)]
-                    for d in range(2):
-                        block = us[2 - c, 2 * pair + d + 2 - a, :, :, lanes]
-                        for b in range(3):
-                            at = block[2 - b : 2 - b + HGT]
-                            acc[d] = acc[d] + k_ref[0, a * 9 + b * 3 + c, :, lanes][None] * at
-                            sums[b] = sums[b] + jnp.sum(fields[d] * at, axis=0)
-                    for b in range(3):
-                        dk_ref[0, a * 9 + b * 3 + c, :, lanes] += sums[b]
-            both = keep_rows(jnp.stack(acc))
-            dx_ref[0, 0, rows, lanes] = both.reshape(112, 128).astype(BF16)
-            return 0
-
-        lax.fori_loop(0, T_LEN // 2, step, 0)
-
-
-def call_pool_backward(upstream, fields, kernels, memory=None, pooled=None, squeezes=None):
-    clips, count = fields.shape[:2]
-    squeeze = memory is not None
-    tap = pl.BlockSpec((1, 27, 8, LW), lambda j, i: (j, 0, 0, 0))
-
-    def block(n):
-        return pl.BlockSpec((1, 1, n, LW), lambda j, i: (i, j, 0, 0))
-
-    grads = jax.ShapeDtypeStruct((count, 27, 8, LW), F32)
-    frame = pltpu.VMEM((3, T_LEN + 2, HGT + 2, PADW, LW), F32)
-    in_specs = [
-        pl.BlockSpec((1, ROWS, LW), lambda j, i: (i, 0, j)),
-        block(ROWS),
-        tap,
-    ]
-    args = [upstream, fields, kernels]
-    shapes = [jax.ShapeDtypeStruct((clips, count, ROWS, LW), BF16), grads]
-    specs = [block(ROWS), tap]
-    scratch = [frame]
-    if squeeze:
-        in_specs += [block(MROWS), block(ROWS), tap]
-        args += [memory, pooled, squeezes]
-        shapes.append(grads)
-        specs.append(tap)
-        scratch += [
-            pltpu.VMEM((3, TM + 1, HGT + 2, PADW, LW), F32),
-        ]
-    return pl.pallas_call(
-        partial(pool_backward, squeeze),
-        grid=(count, clips),
-        in_specs=in_specs,
-        out_specs=specs,
-        out_shape=shapes,
-        scratch_shapes=scratch,
-        compiler_params=params(),
-        cost_estimate=pl.CostEstimate(
-            flops=12_000_000_000 * count, bytes_accessed=6_000_000 * count, transcendentals=0
-        ),
-    )(*args)
 
 
 def attention_forward(
@@ -440,108 +330,343 @@
     )(q, kv, memory, memory, keys_extra, tables, consts["fold"], consts["one"], consts["own"], consts["lanes"])
 
 
+EARLY = 16
+HEAD_EARLY = 8
+LATE = 8
+MESH = pl.DeviceIdType.MESH
+
+
+def remote(src, dst, send, recv, peer):
+    made = pltpu.make_async_remote_copy(
+        src_ref=src, dst_ref=dst, send_sem=send, recv_sem=recv, device_id=peer, device_id_type=MESH
+    )
+    made.start()
+    return made
+
+
+def local(src, dst, sem):
+    made = pltpu.make_async_copy(src, dst, sem)
+    made.start()
+    return made
+
+
+class Place:
+    def __init__(self, groups):
+        dp = lax.axis_index("dp")
+        head = lax.axis_index("head")
+        self.groups = groups
+        self.dp, self.head = dp, head
+        self.core = lax.rem(dp, 2)
+        self.xbit = lax.rem(lax.div(dp, 2), 2)
+        self.group = lax.div(dp, 4)
+        self.to_core = (dp + 1 - 2 * self.core, head)
+        self.to_x = (dp + 2 - 4 * self.xbit, head)
+        self.to_y = (dp, 1 - head)
+        self.peers = [
+            (lax.rem(self.group + o, groups) * 4 + lax.rem(dp, 4), head) for o in range(1, groups)
+        ]
+
+    def greet(self, more=()):
+        barrier = pltpu.get_barrier_semaphore()
+        signalled = [self.to_core, self.to_x, self.to_y] + self.peers + list(more)
+        for peer in signalled:
+            pl.semaphore_signal(barrier, inc=1, device_id=peer, device_id_type=MESH)
+        pl.semaphore_wait(barrier, len(signalled))
+
+
+class Piece:
+    def __init__(self, place, rows, source, result, reduce_refs, send, recv):
+        self.at = place
+        self.half, self.quarter = rows // 2, rows // 4
+        self.chunk = rows // 4 // place.groups
+        self.source, self.result = source, result
+        self.refs = reduce_refs
+        self.send, self.recv = send, recv
+        self.tile = 16 if reduce_refs is None or reduce_refs[0].dtype == BF16 else 8
+        self.flights = {}
+
+    def start(self, key, number, src, dst, peer):
+        self.flights[key] = remote(src, dst, self.send.at[number], self.recv.at[number], peer)
+
+    def base(self, g):
+        at = self.at
+        return pl.multiple_of(at.core * self.half + at.xbit * self.quarter + g * self.chunk, self.tile)
+
+    def a(self):
+        theirs = pl.multiple_of((1 - self.at.core) * self.half, self.tile)
+        self.start("a", 0, self.source(theirs, self.half), self.refs[0], self.at.to_core)
+
+    def sum_rows(self, which):
+        recv_a = self.refs[0]
+        first = pl.multiple_of(which * self.quarter, self.tile)
+        own = self.source(pl.multiple_of(self.at.core * self.half + which * self.quarter, self.tile), self.quarter)
+        return own[...].astype(F32) + recv_a[pl.ds(first, self.quarter)].astype(F32)
+
+    def b(self):
+        _, send_b, recv_b, _, _ = self.refs
+        self.flights["a"].wait()
+        send_b[...] = self.sum_rows(1 - self.at.xbit).astype(send_b.dtype)
+        self.start("b", 1, send_b, recv_b, self.at.to_x)
+
+    def c(self):
+        _, _, recv_b, send_c, recv_c = self.refs
+        self.flights["b"].wait()
+        send_c[...] = (self.sum_rows(self.at.xbit) + recv_b[...].astype(F32)).astype(send_c.dtype)
+        for o in range(1, self.at.groups):
+            first = pl.multiple_of(lax.rem(self.at.group + o, self.at.groups) * self.chunk, self.tile)
+            self.start(
+                ("c", o), 1 + o, send_c.at[pl.ds(first, self.chunk)], recv_c.at[o - 1], self.at.peers[o - 1]
+            )
+
+    def total(self):
+        _, _, _, send_c, recv_c = self.refs
+        own = send_c[pl.ds(pl.multiple_of(self.at.group * self.chunk, self.tile), self.chunk)].astype(F32)
+        for o in range(1, self.at.groups):
+            self.flights["c", o].wait()
+            own = own + recv_c[o - 1].astype(F32)
+        return own
+
+    def d(self, own=None):
+        own = self.total() if own is None else own
+        mine = self.result(self.base(self.at.group), self.chunk)
+        mine[...] = own.astype(mine.dtype)
+        for o in range(1, self.at.groups):
+            number = self.at.groups + o
+            self.start(("d", o), number, mine, mine, self.at.peers[o - 1])
+
+    def e(self):
+        for o in range(1, self.at.groups):
+            self.flights["d", o].wait()
+        mine = self.result(self.base(0), self.quarter)
+        self.start("e", 2 * self.at.groups, mine, mine, self.at.to_x)
+
+    def f(self):
+        self.flights["e"].wait()
+        mine = self.result(pl.multiple_of(self.at.core * self.half, self.tile), self.half)
+        self.start("f", 2 * self.at.groups + 1, mine, mine, self.at.to_core)
+
+    def g(self):
+        self.flights["f"].wait()
+
+
+def piece_scratch(rows, groups, width, dtype, count):
+    half, quarter = rows // 2, rows // 4
+    return [
+        pltpu.VMEM((count, half, width), dtype),
+        pltpu.VMEM((count, quarter, width), dtype),
+        pltpu.VMEM((count, quarter, width), dtype),
+        pltpu.VMEM((count, quarter, width), dtype),
+        pltpu.VMEM((count, groups - 1, quarter // groups, width), dtype),
+    ]
+
+
+class Small:
+    def __init__(self, place, buffer, slots, rows_y, send, recv, base):
+        self.at, self.buffer, self.slots, self.rows_y = place, buffer, slots, rows_y
+        self.send, self.recv, self.base = send, recv, base
+        self.flights = {}
+
+    def start(self, number, src, dst, peer):
+        self.flights[number] = remote(
+            src, dst, self.send.at[self.base + number], self.recv.at[self.base + number], peer
+        )
+
+    def one(self):
+        self.start(0, self.buffer.at[0, 0 : self.rows_y], self.slots[0], self.at.to_y)
+
+    def two(self):
+        self.flights[0].wait()
+        if self.rows_y < self.buffer.shape[1]:
+            self.buffer[1, self.rows_y :] = self.buffer[0, self.rows_y :]
+        self.buffer[1, 0 : self.rows_y] = self.buffer[0, 0 : self.rows_y] + self.slots[0][...]
+        self.start(1, self.buffer.at[1], self.slots[1], self.at.to_core)
+
+    def three(self):
+        self.flights[1].wait()
+        self.buffer[2] = self.buffer[1] + self.slots[1][...]
+        self.start(2, self.buffer.at[2], self.slots[2], self.at.to_x)
+
+    def four(self):
+        self.flights[2].wait()
+        self.buffer[3] = self.buffer[2] + self.slots[2][...]
+        for o in range(1, self.at.groups):
+            self.start(2 + o, self.buffer.at[3], self.slots[3].at[o - 1], self.at.peers[o - 1])
+
+    def five(self, target):
+        added = self.buffer[3]
+        for o in range(1, self.at.groups):
+            self.flights[2 + o].wait()
+            added = added + self.slots[3][o - 1]
+        target[...] = added
+
+
+def small_scratch(rows, rows_y, groups, width):
+    return [
+        pltpu.VMEM((4, rows, width), F32),
+        pltpu.VMEM((rows_y, width), F32),
+        pltpu.VMEM((rows, width), F32),
+        pltpu.VMEM((rows, width), F32),
+        pltpu.VMEM((groups - 1, rows, width), F32),
+    ]
+
+
 def attention_backward(
-    q_ref, kv_ref, m1_ref, m2_ref, ke_ref, qa_ref, dm_ref, at_ref, lse_ref, rt_ref, grow_ref, ownt_ref, ekey_ref,
-    lanes_ref, dq_ref, dkv_ref, dr_ref, keys, values, kt, dmt, qms, dms, dqt,
+    groups,
+    q_ref, kv_ref, mem_ref, ke_hbm, qa_hbm, dm_ref, at_hbm, lse_ref, rt_ref, grow_ref, ownt_ref, ekey_ref,
+    lanes_ref, g2_ref, g1_ref, early_ref,
+    dq_ref, dkv_ref, dr_ref, chunks_ref, early_out,
+    ke_ref, qa_ref, at_ref, keys, values, kt, dmt, qms, dms, dqt,
+    recv_a, send_b, recv_b, send_c, recv_c, s0, s1, s2, s3, s4,
+    loads, sems_send, sems_recv, small_send, small_recv,
 ):
-    @pl.when(pl.program_id(0) == 0)
-    def _():
-        dr_ref[...] = jnp.zeros_like(dr_ref)
-
-    keys[0:ROWS] = kv_ref[0, 0]
-    keys[ROWS : ROWS + MROWS] = m1_ref[0, 0]
-    keys[ROWS + MROWS :] = m2_ref[0, 0]
-    values[0:ROWS] = kv_ref[0, 1]
-    values[ROWS : ROWS + MROWS] = m1_ref[0, 1]
-    values[ROWS + MROWS :] = m2_ref[0, 1]
-    kt[0:LW] = keys[...].T
-    kt[LW:] = ekey_ref[...]
-    dmt[...] = dm_ref[0].astype(F32).T
-    dqt[...] = jnp.zeros_like(dqt)
-    deltas = []
-    for head in range(LH):
-        first = window_of(head)
-        win = slice(first, first + WIN)
-        span = slice(head * HEAD_DIM, (head + 1) * HEAD_DIM)
-        qms[head] = q_ref[0, 0, :, win] * lanes_ref[head]
-        dms[head] = dm_ref[0, :, win] * lanes_ref[head]
-        deltas.append(jnp.sum(dmt[span] * at_ref[0, span], axis=0, keepdims=True))
-
-    def step(number, _):
-        rows = pl.ds(pl.multiple_of(number * BLOCK, BLOCK), BLOCK)
-        dk_parts, dv_parts = [], []
+    place = Place(groups)
+    clips = q_ref.shape[0]
+    lead = [
+        [local(src.at[clip], dst.at[clip], loads.at[3 * clip + n])
+         for n, (src, dst) in enumerate(((ke_hbm, ke_ref), (qa_hbm, qa_ref), (at_hbm, at_ref)))]
+        for clip in range(clips)
+    ]
+    place.greet()
+    total = g1_ref.shape[0]
+
+    def view(number):
+        if number < 4:
+            base, col = (number // 2) * total, (number % 2) * LW
+            return lambda first, n: g2_ref.at[pl.ds(base + first, n), col : col + LW]
+        col = (number - 4) * LW
+        return lambda first, n: g1_ref.at[pl.ds(first, n), col : col + LW]
+
+    pieces = [
+        Piece(
+            place, total, view(number), None,
+            [ref.at[number] for ref in (recv_a, send_b, recv_b, send_c, recv_c)],
+            sems_send.at[number], sems_recv.at[number],
+        )
+        for number in range(8)
+    ]
+    small = Small(place, s0, (s1, s2, s3, s4), HEAD_EARLY, small_send, small_recv, 0)
+    s0[0] = early_ref[...]
+    small.one()
+    for number in range(3):
+        pieces[number].a()
+    moves = []
+    for slot in range(9):
+        moves.append([])
+        if slot < 8:
+            moves[-1].append(pieces[slot].b)
+        if slot + 3 < 8:
+            moves[-1].append(pieces[slot + 3].a)
+        if slot > 0:
+            moves[-1].append(pieces[slot - 1].c)
+    moves[1].append(small.two)
+    moves[2].append(small.three)
+    moves[3].append(small.four)
+    moves[6].append(partial(small.five, early_out))
+
+    def pump():
+        if moves:
+            for move in moves.pop(0):
+                move()
+
+    dr_ref[...] = jnp.zeros_like(dr_ref)
+    for clip in range(clips):
+        near, far = mem_ref.at[clip + 1], mem_ref.at[clip]
+        keys[0:ROWS] = kv_ref[clip, 0]
+        keys[ROWS : ROWS + MROWS] = near[0]
+        keys[ROWS + MROWS :] = far[0]
+        values[0:ROWS] = kv_ref[clip, 1]
+        values[ROWS : ROWS + MROWS] = near[1]
+        values[ROWS + MROWS :] = far[1]
+        kt[0:LW] = keys[...].T
+        kt[LW:] = ekey_ref[...]
+        dmt[...] = dm_ref[clip].astype(F32).T
+        dqt[...] = jnp.zeros_like(dqt)
+        for made in lead[clip]:
+            made.wait()
+        deltas = []
         for head in range(LH):
             first = window_of(head)
-            variant = head // 2
             win = slice(first, first + WIN)
-            ka = keys[rows, win] * lanes_ref[head, 0:BLOCK] + ke_ref[0, variant, rows]
-            s = nt(ka, qa_ref[0, head])
-            p = jnp.exp2(s * (SCALE * LOG2E) - lse_ref[0, head : head + 1])
-            dp = nt(values[rows, win], dms[head])
-            ds = (p * (dp - deltas[head])).astype(BF16)
-            dv_parts.append(nn(p.astype(BF16), dms[head]))
-            dk_parts.append(nn(ds, qms[head]) * SCALE)
-            kts = jnp.concatenate(
-                [kt[head * HEAD_DIM : (head + 1) * HEAD_DIM, rows], kt[LW:, rows]], axis=0
-            )
-            dqt[head] += nn(kts, ds)
-        for which, parts in ((0, dk_parts), (1, dv_parts)):
-            full = jnp.concatenate(
-                [
-                    parts[0][:, 0:128] + parts[1][:, 0:128],
-                    parts[1][:, 128:256] + parts[2][:, 0:128],
-                    parts[2][:, 128:256] + parts[3][:, 128:256],
-                ],
-                axis=1,
-            )
-            both[which, rows] = full
-        return 0
-
-    both = dkv_ref.at[0]
-    lax.fori_loop(0, NBLOCK, step, 0)
-    for head in range(LH):
-        first = window_of(head)
-        span = slice(head * HEAD_DIM, (head + 1) * HEAD_DIM)
-        total = dqt[head]
-        grown = nn(grow_ref[...], total[HEAD_DIM:].astype(BF16)) * ownt_ref[...]
-        grown = grown.astype(BF16)
-        dmt[span] = dmt[span] + total[0:HEAD_DIM] * SCALE + nn(rt_ref[...], grown)
-        dr_ref[:, first : first + WIN] += nn(grown, qms[head])
-    dq_ref[0] = dmt[...].T
-
-
-def call_attention_backward(q, kv, memory, keys_extra, qa, dmix, at, lse, rt, consts):
-    clips = q.shape[0]
+            span = slice(head * HEAD_DIM, (head + 1) * HEAD_DIM)
+            qms[head] = q_ref[clip, 0, :, win] * lanes_ref[head]
+            dms[head] = dm_ref[clip, :, win] * lanes_ref[head]
+            deltas.append(jnp.sum(dmt[span] * at_ref[clip, span], axis=0, keepdims=True))
+
+        def step(number, _):
+            rows = pl.ds(pl.multiple_of(number * BLOCK, BLOCK), BLOCK)
+            dk_parts, dv_parts = [], []
+            for head in range(LH):
+                first = window_of(head)
+                variant = head // 2
+                win = slice(first, first + WIN)
+                ka = keys[rows, win] * lanes_ref[head, 0:BLOCK] + ke_ref[clip, variant, rows]
+                s = nt(ka, qa_ref[clip, head])
+                p = jnp.exp2(s * (SCALE * LOG2E) - lse_ref[clip, head : head + 1])
+                dp = nt(values[rows, win], dms[head])
+                ds = (p * (dp - deltas[head])).astype(BF16)
+                dv_parts.append(nn(p.astype(BF16), dms[head]))
+                dk_parts.append(nn(ds, qms[head]) * SCALE)
+                kts = jnp.concatenate(
+                    [kt[head * HEAD_DIM : (head + 1) * HEAD_DIM, rows], kt[LW:, rows]], axis=0
+                )
+                dqt[head] += nn(kts, ds)
+            for which, parts in ((0, dk_parts), (1, dv_parts)):
+                dkv_ref[clip, which, rows] = jnp.concatenate(
+                    [
+                        parts[0][:, 0:128] + parts[1][:, 0:128],
+                        parts[1][:, 128:256] + parts[2][:, 0:128],
+                        parts[2][:, 128:256] + parts[3][:, 128:256],
+                    ],
+                    axis=1,
+                )
+            return 0
+
+        for begin, end in ((0, 2), (2, 4), (4, 6), (6, 7)):
+            pump()
+            lax.fori_loop(begin, end, step, 0)
+        for head in range(LH):
+            first = window_of(head)
+            span = slice(head * HEAD_DIM, (head + 1) * HEAD_DIM)
+            total_t = dqt[head]
+            grown = nn(grow_ref[...], total_t[HEAD_DIM:].astype(BF16)) * ownt_ref[...]
+            grown = grown.astype(BF16)
+            dmt[span] = dmt[span] + total_t[0:HEAD_DIM] * SCALE + nn(rt_ref[...], grown)
+            dr_ref[:, first : first + WIN] += nn(grown, qms[head])
+        dq_ref[clip] = dmt[...].T
+    while moves:
+        pump()
+    for number in range(8):
+        chunks_ref[number] = pieces[number].total().astype(BF16)
+
+
+def padded_rows(width, groups):
+    return -(-width // (4 * groups) // 16) * 16 * 4 * groups
+
+
+def call_attention_backward(q, kv, memory, keys_extra, qa, dmix, at, lse, rt, g2, g1, early, consts):
+    clips, width = q.shape[0], early.shape[1]
+    groups = lax.axis_size("dp") // 4
+    total = padded_rows(width, groups)
+    if total != width:
+        g1 = jnp.pad(g1, ((0, total - width), (0, 0)))
+        g2 = jnp.pad(g2.reshape(2, width, width), ((0, 0), (0, total - width), (0, 0))).reshape(-1, width)
+    vmem = pl.BlockSpec(memory_space=pltpu.VMEM)
+    hbm = pl.BlockSpec(memory_space=pl.ANY)
     return pl.pallas_call(
-        attention_backward,
-        grid=(clips,),
-        in_specs=[
-            clip_block(1, ROWS, LW),
-            clip_block(2, ROWS, LW),
-            pl.BlockSpec((1, 2, MROWS, LW), lambda i: (i + 1, 0, 0, 0)),
-            pl.BlockSpec((1, 2, MROWS, LW), lambda i: (i, 0, 0, 0)),
-            clip_block(2, KEYS, WIN),
-            clip_block(LH, ROWS, WIN),
-            clip_block(ROWS, LW),
-            clip_block(LW, ROWS),
-            clip_block(8, ROWS),
-            whole((HEAD_DIM, 256)),
-            whole((256, 32)),
-            whole((256, ROWS)),
-            whole((32, KEYS)),
-            whole((LH, ROWS, WIN)),
-        ],
-        out_specs=[
-            clip_block(ROWS, LW),
-            clip_block(2, KEYS, LW),
-            whole((256, LW)),
-        ],
+        partial(attention_backward, groups),
+        in_specs=[vmem] * 3 + [hbm] * 2 + [vmem, hbm] + [vmem] * 9,
+        out_specs=[vmem] * 5,
         out_shape=[
             jax.ShapeDtypeStruct((clips, ROWS, LW), F32),
             jax.ShapeDtypeStruct((clips, 2, KEYS, LW), F32),
             jax.ShapeDtypeStruct((256, LW), F32),
+            jax.ShapeDtypeStruct((8, total // 4 // groups, LW), BF16),
+            jax.ShapeDtypeStruct((EARLY, width), F32),
         ],
         scratch_shapes=[
+            pltpu.VMEM(keys_extra.shape, BF16),
+            pltpu.VMEM(qa.shape, BF16),
+            pltpu.VMEM(at.shape, F32),
             pltpu.VMEM((KEYS, LW), BF16),
             pltpu.VMEM((KEYS, LW), BF16),
             pltpu.VMEM((LW + 32, KEYS), BF16),
@@ -549,15 +674,406 @@
             pltpu.VMEM((LH, ROWS, WIN), BF16),
             pltpu.VMEM((LH, ROWS, WIN), BF16),
             pltpu.VMEM((LH, HEAD_DIM + 32, ROWS), F32),
+            *piece_scratch(total, groups, LW, BF16, 8),
+            *small_scratch(EARLY, HEAD_EARLY, groups, width),
+            pltpu.SemaphoreType.DMA((3 * clips,)),
+            pltpu.SemaphoreType.DMA((8, groups + 1)),
+            pltpu.SemaphoreType.DMA((8, groups + 1)),
+            pltpu.SemaphoreType.DMA((groups + 2,)),
+            pltpu.SemaphoreType.DMA((groups + 2,)),
         ],
-        compiler_params=params(),
+        compiler_params=params(collective_id=0, has_side_effects=True),
         cost_estimate=pl.CostEstimate(
             flops=40_000_000_000, bytes_accessed=20_000_000, transcendentals=3_000_000
         ),
     )(
-        q, kv, memory, memory, keys_extra, qa, dmix, at, lse, rt,
-        consts["grow"], consts["ownt"], consts["ekey"], consts["lanes"],
+        q, kv, memory, keys_extra, qa, dmix, at, lse, rt,
+        consts["grow"], consts["ownt"], consts["ekey"], consts["lanes"], g2, g1, early,
     )
+
+
+SMALL_ROWS = 256
+REL_ROWS = 48
+
+
+def finish_kernel(
+    groups, width,
+    dq_hbm, dkv_hbm, x0q_hbm, x0kv_hbm, kvf_hbm, taps_hbm, rows_a_hbm, rows_x_hbm, branch_hbm, w_hbm,
+    tokens_hbm, middle_hbm, chunks_ref, dr_ref, gain, foldl_ref, pick_ref,
+    grad, out2, out1, outp, outq, small_out, late_out,
+    dq, dkv, x0q, x0kv, kvf, taps_ref, rows_a, rows_x, branch, w_ref, tokens, middle,
+    us, ms, kacc, dx, dmem_send, dmem_recv, res2, res1, resp, grads, stage, stage_t,
+    recv_a, send_b, recv_b, send_c, recv_c, sm_raw, sm, sm_y, sm_res, fa, fb, fc, fd, fe,
+    send_y, recv_y, l0, l1, l2, l3, l4,
+    loads, stores, sems_send, sems_recv, small_send, small_recv, mem_sems,
+):
+    place = Place(groups)
+    clips = dq.shape[0]
+    total = rows_a.shape[1]
+    names = ("dkv", "dq", "x0q", "taps", "rows_x", "branch", "x0kv", "kvf", "rows_a", "w", "tokens", "middle")
+    pairs = (
+        (dkv_hbm, dkv), (dq_hbm, dq), (x0q_hbm, x0q), (taps_hbm, taps_ref), (rows_x_hbm, rows_x),
+        (branch_hbm, branch), (x0kv_hbm, x0kv), (kvf_hbm, kvf), (rows_a_hbm, rows_a), (w_hbm, w_ref),
+        (tokens_hbm, tokens), (middle_hbm, middle),
+    )
+    lead = {
+        name: local(src, dst, loads.at[n]) for n, (name, (src, dst)) in enumerate(zip(names, pairs))
+    }
+    count = groups * 4
+    behind = (lax.rem(place.dp + count - 1, count), place.head)
+    ahead = (lax.rem(place.dp + 1, count), place.head)
+    place.greet((behind, ahead))
+
+    def view2(number):
+        if number < 4:
+            base, col = (number // 2) * total, (number % 2) * LW
+            return lambda first, n: res2.at[pl.ds(base + first, n), col : col + LW]
+        col = (number - 4) * LW
+        return lambda first, n: res1.at[pl.ds(first, n), col : col + LW]
+
+    ffn = [
+        Piece(place, total, None, view2(number), None, sems_send.at[number], sems_recv.at[number])
+        for number in range(8)
+    ]
+
+    def rows_of(ref):
+        return lambda first, n: ref.at[pl.ds(first, n)]
+
+    late = [
+        Piece(
+            place, total, rows_of(grads.at[number]), rows_of(resp.at[number]),
+            [ref.at[number] for ref in (recv_a, send_b, recv_b, send_c, recv_c)],
+            sems_send.at[8 + number], sems_recv.at[8 + number],
+        )
+        for number in range(4)
+    ]
+    tiny = Piece(
+        place, sm.shape[0], rows_of(sm), rows_of(sm_res),
+        [ref.at[0] for ref in (fa, fb, fc, fd, fe)], sems_send.at[12], sems_recv.at[12],
+    )
+    ends = Small(place, l0, (l1, l2, l3, l4), LATE, small_send, small_recv, 0)
+
+    stored = []
+
+    def flush(source, target):
+        slot = len(stored) % 2
+        if len(stored) > 1:
+            stored[-2].wait()
+        stage[slot] = source[...].astype(F32)
+        stored.append(local(stage.at[slot], target, stores.at[slot]))
+
+    def store2(number):
+        ffn[number].g()
+        if number < 4:
+            base, col = (number // 2) * total, (number % 2) * LW
+            target = out2.at[base : base + total, col : col + LW]
+        else:
+            col = (number - 4) * LW
+            target = out1.at[:, col : col + LW]
+        flush(view2(number)(0, total), target)
+
+    def step(k):
+        if k < 8:
+            ffn[k].d(chunks_ref[k])
+        if 1 <= k < 9:
+            ffn[k - 1].e()
+        if 2 <= k < 10:
+            ffn[k - 2].f()
+        if 3 <= k < 11:
+            store2(k - 3)
+
+    def product(number):
+        left, right = (
+            (rows_x, branch), (rows_a, dx.at[0]), (rows_a, dx.at[1]), (rows_a, dx.at[2])
+        )[number]
+        for first in range(0, total, total // 2):
+            grads[number, first : first + total // 2] = lax.dot_general(
+                left[:, first : first + total // 2], right[...], (((0,), (0,)), ((), ())),
+                preferred_element_type=F32,
+            ).astype(BF16)
+        late[number].a()
+
+    def shifted_store(dst, first, both, lanes):
+        both = both.reshape(2 * HGT, PADW, 128)
+        for c, shift in ((0, 1), (1, 0), (2, PADW - 1)):
+            moved = pltpu.roll(both, shift, axis=1) if shift else both
+            dst[c, pl.ds(first, 2), 1 : HGT + 1, :, lanes] = moved.reshape(2, HGT, PADW, 128)
+
+    def pooled(which, clip):
+        field = x0q.at[clip, 0] if which == 0 else x0kv.at[clip, which - 1]
+        upstream = dq.at[clip] if which == 0 else dkv.at[clip, which - 1]
+        if which:
+            memory = dmem_recv[clip, which - 1].astype(F32)
+            memory = jnp.where(place.dp == count - 1, 0.0, memory)
+            for later in range(clip + 1, clips):
+                if later == clip + 1:
+                    memory = memory + dkv[later, which - 1, ROWS : ROWS + MROWS]
+                if later == clip + 2:
+                    memory = memory + dkv[later, which - 1, ROWS + MROWS :]
+            spread(ms, 0, memory.reshape(TM, HGT, PADW, LW))
+        else:
+            spread(us, 1, upstream[...].reshape(T_LEN, HGT, PADW, LW))
+
+        def tile_loop(tile, _):
+            lanes = pl.ds(pl.multiple_of(tile * 128, 128), 128)
+            if which:
+
+                def squeeze_step(pair, _):
+                    rows = pl.ds(pl.multiple_of(pair * 112, 112), 112)
+                    own = upstream[rows, lanes].reshape(2, HGT, PADW, 128)
+                    fields = kvf[clip, which - 1, rows, lanes].astype(F32).reshape(2, HGT, PADW, 128)
+                    acc = [own[0], own[1]]
+                    for a, d, frame in ((1, 0, 0), (0, 1, 1), (2, 1, 0)):
+                        for c in range(3):
+                            block = ms[2 - c, pair + frame, :, :, lanes]
+                            for b in range(3):
+                                at = block[2 - b : 2 - b + HGT]
+                                number = a * 9 + b * 3 + c
+                                acc[d] = acc[d] + taps_ref[2 + which, number, :, lanes][None] * at
+                                kacc[2 + which, number, :, lanes] += jnp.sum(fields[d] * at, axis=0)
+                    shifted_store(us, 2 * pair + 1, keep_rows(jnp.stack(acc)), lanes)
+                    return 0
+
+                lax.fori_loop(0, TM, squeeze_step, 0)
+
+            def pair_step(pair, _):
+                rows = pl.ds(pl.multiple_of(pair * 112, 112), 112)
+                fields = field[rows, lanes].astype(F32).reshape(2, HGT, PADW, 128)
+                acc = [jnp.zeros((HGT, PADW, 128), F32) for _ in range(2)]
+                for a in range(3):
+                    for c in range(3):
+                        sums = [jnp.zeros((PADW, 128), F32) for _ in range(3)]
+                        for d in range(2):
+                            block = us[2 - c, 2 * pair + d + 2 - a, :, :, lanes]
+                            for b in range(3):
+                                at = block[2 - b : 2 - b + HGT]
+                                acc[d] = acc[d] + taps_ref[which, a * 9 + b * 3 + c, :, lanes][None] * at
+                                sums[b] = sums[b] + jnp.sum(fields[d] * at, axis=0)
+                        for b in range(3):
+                            kacc[which, a * 9 + b * 3 + c, :, lanes] += sums[b]
+                both = keep_rows(jnp.stack(acc))
+                out_rows = pl.ds(pl.multiple_of(clip * ROWS + pair * 112, 16), 112)
+                dx[which, out_rows, lanes] = both.reshape(112, 128).astype(BF16)
+                return 0
+
+            lax.fori_loop(0, T_LEN // 2, pair_step, 0)
+            return 0
+
+        lax.fori_loop(0, LW // 128, tile_loop, 0)
+
+    side_rows = ROWS // 2
+
+    def input_gradient(clip, side):
+        rows = pl.ds(pl.multiple_of(clip * ROWS + side * side_rows, 16), side_rows)
+        return nt(dx[0, rows], w_ref[0]) + nt(dx[1, rows], w_ref[1]) + nt(dx[2, rows], w_ref[2])
+
+    crossing = {}
+
+    def cross(clip):
+        send_y[clip] = input_gradient(clip, 1 - place.head).astype(BF16)
+        number = groups + 2 + clip
+        crossing[clip] = remote(
+            send_y.at[clip], recv_y.at[clip], small_send.at[number], small_recv.at[number], place.to_y
+        )
+
+    def normed_gradient(clip):
+        mine = input_gradient(clip, place.head)
+        crossing[clip].wait()
+        u = mine + recv_y[clip].astype(F32)
+        v = tokens[clip].astype(F32)
+        centred = v - jnp.mean(v, axis=-1, keepdims=True)
+        scale = lax.rsqrt(jnp.mean(centred * centred, axis=-1, keepdims=True) + EPSILON)
+        xhat = centred * scale
+        w = u * gain[0:1]
+        dv = scale * (
+            w - jnp.mean(w, axis=-1, keepdims=True) - xhat * jnp.mean(w * xhat, axis=-1, keepdims=True)
+        )
+        grad[clip] = middle[clip] + dv
+        l0[0, 0:1] += jnp.sum(u * xhat, axis=0, keepdims=True)
+        l0[0, 1:2] += jnp.sum(u, axis=0, keepdims=True)
+
+    def exact(a, b):
+        return jnp.dot(a, b, precision=HIGHEST, preferred_element_type=F32)
+
+    def small_start():
+        folded = exact(dr_ref[...], foldl_ref[...])
+        sm_raw[0:REL_ROWS] = exact(pick_ref[...], folded)
+        for which in range(5):
+            first = REL_ROWS + 32 * which
+            sums = jnp.sum(kacc[which], axis=1)
+            sums = jnp.concatenate([sums, jnp.zeros((5, LW), F32)], axis=0)
+            sm_raw[first : first + 32] = exact(sums, foldl_ref[...])
+        number = groups + 2 + clips
+        crossing["small"] = remote(
+            sm_raw, sm_y, small_send.at[number], small_recv.at[number], place.to_y
+        )
+
+    def small_next():
+        crossing["small"].wait()
+        sm[...] = sm_raw[...] + sm_y[...]
+        tiny.a()
+
+    us[...] = jnp.zeros_like(us)
+    ms[...] = jnp.zeros_like(ms)
+    kacc[...] = jnp.zeros_like(kacc)
+    l0[0] = jnp.zeros_like(l0[0])
+    sm_raw[...] = jnp.zeros_like(sm_raw)
+    step(0)
+    lead["dkv"].wait()
+    for which in range(2):
+        dmem_send[0, which] = dkv[0, which, ROWS + MROWS :].astype(BF16)
+        dmem_send[1, which] = (
+            dkv[0, which, ROWS : ROWS + MROWS] + dkv[1, which, ROWS + MROWS :]
+        ).astype(BF16)
+    memory_flight = remote(dmem_send, dmem_recv, mem_sems.at[0], mem_sems.at[1], behind)
+    for name in ("dq", "x0q", "taps"):
+        lead[name].wait()
+    pooled(0, 0)
+    step(1)
+    lead["rows_x"].wait()
+    lead["branch"].wait()
+    product(0)
+    pooled(0, 1)
+    step(2)
+    late[0].b()
+    lead["rows_a"].wait()
+    product(1)
+    step(3)
+    late[0].c()
+    memory_flight.wait()
+    lead["x0kv"].wait()
+    lead["kvf"].wait()
+    pooled(1, 0)
+    step(4)
+    late[1].b()
+    late[0].d()
+    pooled(2, 0)
+    step(5)
+    late[1].c()
+    late[0].e()
+    lead["w"].wait()
+    cross(0)
+    pooled(1, 1)
+    step(6)
+    late[1].d()
+    late[0].f()
+    product(2)
+    step(7)
+    late[1].e()
+    pooled(2, 1)
+    late[2].b()
+    product(3)
+    step(8)
+    late[1].f()
+    cross(1)
+    late[2].c()
+    late[3].b()
+    small_start()
+    step(9)
+    late[0].g()
+    stage_t[...] = resp[0].astype(F32).T
+    turned = local(stage_t, outp, stores.at[2])
+    lead["tokens"].wait()
+    lead["middle"].wait()
+    normed_gradient(0)
+    late[2].d()
+    late[3].c()
+    step(10)
+    small_next()
+    late[2].e()
+    late[3].d()
+    normed_gradient(1)
+    ends.one()
+    tiny.b()
+    late[1].g()
+    sent_q = local(resp.at[1], outq.at[0], stores.at[3])
+    late[2].f()
+    late[3].e()
+    ends.two()
+    tiny.c()
+    late[3].f()
+    ends.three()
+    tiny.d()
+    late[2].g()
+    sent_k = local(resp.at[2], outq.at[1], stores.at[4])
+    ends.four()
+    tiny.e()
+    late[3].g()
+    sent_v = local(resp.at[3], outq.at[2], stores.at[5])
+    tiny.f()
+    ends.five(late_out)
+    tiny.g()
+    small_out[...] = sm_res[...]
+    for made in [turned, sent_q, sent_k, sent_v] + stored[-2:]:
+        made.wait()
+
+
+def call_finish(dq, dkv, x0q, x0kv, kvf, all_taps, rows_a, rows_x, branch, weights, tokens, middle, chunks, dr, gain):
+    groups = lax.axis_size("dp") // 4
+    width = tokens.shape[2]
+    total = padded_rows(width, groups)
+    clips, side = tokens.shape[:2]
+    if total != width:
+        extra = ((0, 0), (0, total - width))
+        rows_a, rows_x = jnp.pad(rows_a, extra), jnp.pad(rows_x, extra)
+    small_rows = -(-SMALL_ROWS // (32 * groups)) * 32 * groups
+    foldl = np.zeros((LW, 128), np.float32)
+    foldl[np.arange(LW), np.arange(LW) % HEAD_DIM] = 1
+    pick = np.zeros((REL_ROWS, 256), np.float32)
+    pick[:NREL] = PICK.T
+    vmem = pl.BlockSpec(memory_space=pltpu.VMEM)
+    hbm = pl.BlockSpec(memory_space=pl.ANY)
+    streamed = [dq, dkv, x0q, x0kv, kvf, all_taps, rows_a, rows_x, branch, weights, tokens, middle]
+    frame = pltpu.VMEM((3, T_LEN + 2, HGT + 2, PADW, LW), F32)
+    return pl.pallas_call(
+        partial(finish_kernel, groups, width),
+        in_specs=[hbm] * 12 + [vmem] * 5,
+        out_specs=[vmem, hbm, hbm, hbm, hbm, vmem, vmem],
+        out_shape=[
+            jax.ShapeDtypeStruct(tokens.shape, F32),
+            jax.ShapeDtypeStruct((2 * total, width), F32),
+            jax.ShapeDtypeStruct((total, 4 * LW), F32),
+            jax.ShapeDtypeStruct((LW, total), F32),
+            jax.ShapeDtypeStruct((3, total, LW), BF16),
+            jax.ShapeDtypeStruct((small_rows, 128), F32),
+            jax.ShapeDtypeStruct((LATE, width), F32),
+        ],
+        scratch_shapes=[pltpu.VMEM(array.shape, array.dtype) for array in streamed]
+        + [
+            frame,
+            pltpu.VMEM((3, TM + 1, HGT + 2, PADW, LW), F32),
+            pltpu.VMEM((5, 27, 8, LW), F32),
+            pltpu.VMEM((3, clips * ROWS, LW), BF16),
+            pltpu.VMEM((2, 2, MROWS, LW), BF16),
+            pltpu.VMEM((2, 2, MROWS, LW), BF16),
+            pltpu.VMEM((2 * total, width), BF16),
+            pltpu.VMEM((total, 4 * LW), BF16),
+            pltpu.VMEM((4, total, LW), BF16),
+            pltpu.VMEM((4, total, LW), BF16),
+            pltpu.VMEM((2, total, LW), F32),
+            pltpu.VMEM((LW, total), F32),
+            *piece_scratch(total, groups, LW, BF16, 4),
+            pltpu.VMEM((small_rows, 128), F32),
+            pltpu.VMEM((small_rows, 128), F32),
+            pltpu.VMEM((small_rows, 128), F32),
+            pltpu.VMEM((small_rows, 128), F32),
+            *piece_scratch(small_rows, groups, 128, F32, 1),
+            pltpu.VMEM((clips, side, width), BF16),
+            pltpu.VMEM((clips, side, width), BF16),
+            *small_scratch(LATE, LATE, groups, width),
+            pltpu.SemaphoreType.DMA((12,)),
+            pltpu.SemaphoreType.DMA((6,)),
+            pltpu.SemaphoreType.DMA((13, 2 * groups + 2)),
+            pltpu.SemaphoreType.DMA((13, 2 * groups + 2)),
+            pltpu.SemaphoreType.DMA((groups + 3 + clips,)),
+            pltpu.SemaphoreType.DMA((groups + 3 + clips,)),
+            pltpu.SemaphoreType.DMA((2,)),
+        ],
+        compiler_params=params(collective_id=1, has_side_effects=True),
+        cost_estimate=pl.CostEstimate(
+            flops=60_000_000_000, bytes_accessed=40_000_000, transcendentals=0
+        ),
+    )(*streamed, chunks, dr, gain, jnp.asarray(foldl), jnp.asarray(pick))
 
 
 def from_behind(x, axis, by):
@@ -593,7 +1109,10 @@
 
 
 def gather_rows(x):
-    return lax.all_gather(x, "head", axis=1, tiled=True)
+    half = x.shape[1]
+    mine = lax.axis_index("head") * half
+    both = jnp.concatenate([x, x], axis=1)
+    return lax.dynamic_update_slice_in_dim(both, swap(x), half - mine, axis=1)
 
 
 def scatter_sum(x):
@@ -670,12 +1189,14 @@
     tap_q, tap_kv = taps(pool_q)[None], jnp.stack([taps(pool_k), taps(pool_v)])
     tap_s = jnp.stack([taps(squeeze_k), taps(squeeze_v)])
 
-    inputs = pad_rows(tokens).astype(F32)
+    inputs_low = pad_rows(tokens)
+    inputs = inputs_low.astype(F32)
     upstream_low = pad_rows(cotangent)
     real = (jnp.arange(inputs.shape[1]) % PADW < WID)[None, :, None]
-    first_normed, first_pull = jax.vjp(layer_norm, inputs, ln1_gain, ln1_bias)
+    first_normed = layer_norm(inputs, ln1_gain, ln1_bias)
     first_rows = gather_rows(jnp.where(real, first_normed, 0.0).astype(BF16))
     w_heads = w_qkv.transpose(1, 0, 2)
+    upstream_rows = gather_rows(lax.optimization_barrier((upstream_low, first_rows))[0])
     kv0, kv, kvf, mem = call_pool_forward(first_rows, w_heads[1:], tap_kv, tap_s)
     before = from_behind(mem[-2:], "dp", 1)
     q0, q = call_pool_forward(first_rows, w_heads[:1], tap_q)
@@ -692,7 +1213,6 @@
     output = drop_rows((middle + scatter_sum(partial_m) + fc2_bias).astype(BF16))
     upstream = upstream_low.astype(F32)
     fc2_bias_grad = jnp.sum(upstream, axis=(0, 1))
-    upstream_rows = gather_rows(upstream_low)
     w_fc2_grad = jnp.einsum("alf,ald->fd", active_low, upstream_rows, preferred_element_type=F32)
     (hidden_grad,) = gelu_pull(
         jnp.einsum("ald,fd->alf", upstream_rows, w_fc2, preferred_element_type=F32)
@@ -705,63 +1225,55 @@
     middle_grad = middle_part + upstream
     proj_bias_grad = jnp.sum(middle_grad, axis=(0, 1))
     middle_rows = gather_rows(middle_grad.astype(BF16))
-    w_proj_grad = jnp.einsum("ale,alf->ef", branch, middle_rows, preferred_element_type=F32)
     dmix = jnp.einsum("alf,ef->ale", middle_rows, w_proj, preferred_element_type=F32).astype(BF16)
 
-    w_fc2_grad, w_fc1_grad, w_proj_grad = lax.psum(
-        (w_fc2_grad.astype(BF16), w_fc1_grad.astype(BF16), w_proj_grad.astype(BF16)), "dp"
+    width = tokens.shape[2]
+    early = jnp.concatenate(
+        [
+            jnp.stack([proj_bias_grad, ln2_gain_grad, ln2_bias_grad, fc2_bias_grad]),
+            jnp.zeros((HEAD_EARLY - 4, width), F32),
+            fc1_bias_grad.reshape(-1, width),
+        ]
     )
-    dq, dkv, dr = call_attention_backward(
-        q, kv, memory, keys_extra, qa, dmix, at, lse, rel_rows, consts
+    early = jnp.pad(early, ((0, EARLY - early.shape[0]), (0, 0)))
+    dq, dkv, dr, chunks, early = call_attention_backward(
+        q, kv, memory, keys_extra, qa, dmix, at, lse, rel_rows,
+        w_fc2_grad.astype(BF16), w_fc1_grad.astype(BF16), early, consts,
     )
-    slots = dkv[:, :, ROWS:]
-    near, far = slots[:, :, :MROWS], slots[:, :, MROWS:]
-    zero = jnp.zeros((1,) + near.shape[1:], F32)
-    spread_out = jnp.concatenate([zero, near, zero], axis=0) + jnp.concatenate([far, zero, zero], axis=0)
-    later = from_behind(spread_out[:2].astype(BF16), "dp", -1).astype(F32)
-    dq0, pool_q_grad = call_pool_backward(dq, q0, tap_q)
-    leading = jnp.zeros((clip_count - 2,) + near.shape[1:], F32)
-    dmem = spread_out[2:] + jnp.concatenate([leading, later], axis=0)
-    own = dkv[:, :, :ROWS].transpose(0, 2, 1, 3).reshape(clip_count, ROWS, 2 * LW)
-    dkv0, pool_kv_grad, squeeze_grad = call_pool_backward(own, kv0, tap_kv, dmem, kvf, tap_s)
-    qkv_grad = jnp.concatenate([dq0, dkv0], axis=1)
-    w_qkv_grad = jnp.einsum("ald,akle->dke", first_rows, qkv_grad, preferred_element_type=F32)
-    w_qkv_grad = lax.psum(w_qkv_grad.astype(BF16), "dp")
-    partial_first = jnp.einsum("akle,dke->ald", qkv_grad, w_qkv, preferred_element_type=F32)
-    input_part, ln1_gain_grad, ln1_bias_grad = first_pull(scatter_sum(partial_first))
-    input_grad = drop_rows(middle_grad + input_part)
-
-    def tap_grad(g):
-        return jnp.sum(jnp.sum(g, axis=1).reshape(27, LH, HEAD_DIM), axis=1)
-
-    pair_grad = jnp.sum(dr.reshape(256, LH, HEAD_DIM), axis=1)
-    rel_grad = jnp.dot(jnp.asarray(PICK.T), pair_grad, precision=HIGHEST)
-    shared = lax.psum(
-        (
-            ln1_gain_grad,
-            ln1_bias_grad,
-            tap_grad(pool_q_grad[0]),
-            tap_grad(pool_kv_grad[0]),
-            tap_grad(pool_kv_grad[1]),
-            tap_grad(squeeze_grad[0]),
-            tap_grad(squeeze_grad[1]),
-            rel_grad[: 2 * T_LEN - 1],
-            rel_grad[2 * T_LEN - 1 : 2 * T_LEN + 2 * HGT - 2],
-            rel_grad[2 * T_LEN + 2 * HGT - 2 :],
-            proj_bias_grad,
-            ln2_gain_grad,
-            ln2_bias_grad,
-            fc2_bias_grad,
-        ),
-        ("dp", "head"),
+    input_grad, w_fc2_grad, w_fc1_grad, w_proj_grad, tail, small, late = call_finish(
+        dq, dkv, q0, kv0, kvf, jnp.concatenate([tap_q, tap_kv, tap_s]),
+        first_rows.reshape(-1, width),
+        middle_rows.reshape(-1, width),
+        branch.reshape(-1, LW),
+        w_heads,
+        inputs_low,
+        middle_grad,
+        chunks,
+        dr,
+        ln1_gain.reshape(1, -1),
     )
-    fc1_bias_grad = lax.psum(fc1_bias_grad, "dp")
+    input_grad = drop_rows(input_grad)
+    total = w_fc1_grad.shape[0]
+    if total != width:
+        w_fc2_grad = w_fc2_grad.reshape(2, total, width)[:, :width].reshape(2 * width, width)
+        w_fc1_grad, w_proj_grad, tail = w_fc1_grad[:width], w_proj_grad[:, :width], tail[:, :width]
+    w_qkv_grad = tail.astype(F32).transpose(1, 0, 2)
+    fc1_bias_grad = early[HEAD_EARLY : HEAD_EARLY + fc1_bias_grad.size // width].reshape(-1)
+    small = small[:, :HEAD_DIM]
+    shared = [late[0], late[1]]
+    shared += [small[REL_ROWS + 32 * n : REL_ROWS + 32 * n + 27] for n in range(5)]
+    shared += [
+        small[: 2 * T_LEN - 1],
+        small[2 * T_LEN - 1 : 2 * T_LEN + 2 * HGT - 2],
+        small[2 * T_LEN + 2 * HGT - 2 : NREL],
+    ]
+    shared += [early[0], early[1], early[2], early[3]]
     return (
         output,
         input_grad,
         shared[0],
         shared[1],
-        w_qkv_grad.astype(F32),
+        w_qkv_grad,
         shared[2],
         shared[3],
         shared[4],
@@ -770,13 +1282,13 @@
         shared[7],
         shared[8],
         shared[9],
-        w_proj_grad.astype(F32),
+        w_proj_grad,
         shared[10],
         shared[11],
         shared[12],
-        w_fc1_grad.astype(F32),
+        w_fc1_grad,
         fc1_bias_grad,
-        w_fc2_grad.astype(F32),
+        w_fc2_grad,
         shared[13],
     )
 

time: 666 us -> 382 us (0.57)
  waiting for transfers between devices: 344 us -> 63.6 us
  Pallas kernels: 105 us -> 195 us
  blocking collectives: 38.1 us -> 0 us
  matrix products: 55.1 us -> 34.7 us
  other arithmetic: 38.7 us -> 19.1 us
  between operations: 15.2 us -> 1.66 us
    psum x2 -> x0, waiting for transfers between devices: 231 us -> none  [the longest x1 150 us: on_device(): lax.psum((ln1_gain_grad, ln1_bias_grad, tap_grad(pool_q_grad[0]), tap_gra...]
    pallas_call x3 -> x2, Pallas kernels: 56.4 us -> 147 us  [the longest x1 97.1 us: call_finish(): pl.pallas_call(partial(finish_kernel, groups, width), in_specs=[hbm] * 12...]
    all_gather x4 -> x0, waiting for transfers between devices: 66.3 us -> none  [gather_rows(): return lax.all_gather(x, 'head', axis=1, tiled=True)]
    psum x1 -> x0, blocking collectives: 38.1 us -> none  [on_device(): fc1_bias_grad = lax.psum(fc1_bias_grad, 'dp')]
    ppermute x4 -> x7, waiting for transfers between devices: 45.8 us -> 63.6 us  [swap(): return lax.ppermute(x, 'head', [(0, 1), (1, 0)])]
    dot_general x4 -> x0, matrix products: 11 us -> none  [the longest x1 5.72 us: on_device(): jnp.einsum('akle,dke->ald', qkv_grad, w_qkv, preferred_element_type=F32)]
    unnamed x145 -> x124, local copies, waits for them, and re-layouts: 30.9 us -> 20.8 us
    convert_element_type x4 -> x2, other arithmetic: 9.68 us -> 1.66 us  [the longest x1 1.59 us: on_device(): first_rows = gather_rows(jnp.where(real, first_normed, 0.0).astype(BF16))]
  transfers between devices with their start and end apart: 12 -> 8, of which waited for: 10 -> 5; matrix products, arithmetic and copies ran while one was open for 13% -> 13% of each run, Pallas kernels for 2% -> 2%
where the time goes in v3:
time: 382 us; the launch traced here: 376 us
  Pallas kernels  195 us (51%)
  waiting for transfers between devices  63.6 us (17%)
  local copies, waits for them, and re-layouts  52.5 us (14%)
  matrix products  34.7 us (9%)
  other arithmetic  19.1 us (5%)
  starting transfers between devices  9.38 us (2%)
    pallas_call x1, Pallas kernels, call_finish(): pl.pallas_call(partial(finish_kernel, groups, width), in_specs=[hbm] * 12...  97.1 us
    ppermute x7, waiting for transfers between devices, swap(): return lax.ppermute(x, 'head', [(0, 1), (1, 0)])  63.6 us
    pallas_call x1, Pallas kernels, call_attention_backward(): pl.pallas_call(partial(attention_backward, groups), in_specs=[vmem] * 3 +...  50.3 us
    pallas_call x1, Pallas kernels, call_attention_forward(): pl.pallas_call(attention_forward, grid=(clips,), in_specs=[clip_block(1,...  26.9 us
    pallas_call x2, Pallas kernels, call_pool_forward(): pl.pallas_call(partial(pool_forward, squeeze), grid=(count, clips), in_sp...  21.2 us
    unnamed x124, local copies, waits for them, and re-layouts  20.8 us
  transfers between devices with their start and end apart: 8, of which 5 were waited for; matrix products, arithmetic and copies ran while one was open for 13% of the time, Pallas kernels for 2%

profile of v3, /device:TPU:0, one launch (start us, length us, event | category | flops | bytes accessed | tf_op | source)
XLA Modules:
  0.0 376.4 jit_solution(2168535135896770845)
XLA Ops:
  5.3 3.0 collective-permute-start
  8.4 2.0 slice.88.refs_1_
  30.1 14.6 %shard_map.491 = (bf16[2,2,448,384]{3,2,1,0:T(8,128)(2,1)}, bf16[2,2,448,384]{3,2,1,0:T(8,128)(2,1)}, bf16[2,2,448,384]{3,2,1,0:T(8,128)(2,1)}, bf16[2,2,224,384]{3,2,1,0:T(8,128)(2,1)}) custom-call(bf16[2,448,768]{2,1,0:T(8,128)(2,1)} %copy-done.12, bf16[2,768,384]{2,1,0:T(8,128)(2,1)} %slice.89.refs_1_, f32[2,27,8,384]{3,2,1,0:T(8,128)} %get-tuple-element.102.refs_2_, ...), custom_call_target="tpu_custom_call" | custom-call | flops 12000000000 | bytes 8000000 | tf_op jit(solution)/shard_map/pallas_call | solution.py:217
  48.4 6.6 %shard_map.490 = (bf16[2,1,448,384]{3,2,1,0:T(8,128)(2,1)}, bf16[2,1,448,384]{3,2,1,0:T(8,128)(2,1)}) custom-call(bf16[2,448,768]{2,1,0:T(8,128)(2,1)} %copy-done.12, bf16[1,768,384]{2,1,0:T(8,128)(2,1)} %slice.88.refs_1_, f32[1,27,8,384]{3,2,1,0:T(8,128)} %broadcast_in_dim_broadcast_in_dim.2.refs_2_), custom_call_target="tpu_custom_call" | custom-call | flops 6000000000 | bytes 4000000 | tf_op jit(solution)/shard_map/pallas_call | solution.py:217
  57.3 26.9 %shard_map.492 = (bf16[2,448,384]{2,1,0:T(8,128)(2,1)}, bf16[2,4,448,256]{3,2,1,0:T(8,128)(2,1)}, f32[2,384,448]{2,1,0:T(8,128)}, f32[2,8,448]{2,1,0:T(8,128)}) custom-call(bf16[2,1,448,384]{3,2,1,0:T(8,128)(2,1)} %get-tuple-element.44.q_ref, bf16[2,2,448,384]{3,2,1,0:T(8,128)(2,1)} %get-tuple-element.45.kv_ref, bf16[4,2,224,384]{3,2,1,0:T(8,128)(2,1)} %copy-done.30, ...), custom_call_target="tpu_custom_call" | custom-call | flops 20000000000 | bytes 10000000 | tf_op jit(solution)/shard_map/pallas_call | solution.py:293
  90.7 13.0 %collective-permute-done.2 = bf16[2,224,768]{2,1,0:T(8,128)(2,1)S(1)} collective-permute-done((bf16[2,224,768]{2,1,0:T(8,128)(2,1)S(1)}, bf16[2,224,768]{2,1,0:T(8,128)(2,1)S(1)}, u32[]{:S(2)}, u32[]{:S(2)}) %collective-permute-start.2) | collective-permute-done | bytes 688160 | tf_op jit(solution)/shard_map/ppermute | solution.py:1108
  112.7 5.7 %collective-permute-done.5 = bf16[2,224,768]{2,1,0:T(8,128)(2,1)S(1)} collective-permute-done((bf16[2,224,768]{2,1,0:T(8,128)(2,1)}, bf16[2,224,768]{2,1,0:T(8,128)(2,1)S(1)}, u32[]{:S(2)}, u32[]{:S(2)}) %collective-permute-start.5) | collective-permute-done | bytes 688160 | tf_op jit(solution)/shard_map/ppermute | solution.py:1108
  118.6 14.6 %collective-permute-done.3 = bf16[2,224,768]{2,1,0:T(8,128)(2,1)S(1)} collective-permute-done((bf16[2,224,768]{2,1,0:T(8,128)(2,1)S(1)}, bf16[2,224,768]{2,1,0:T(8,128)(2,1)S(1)}, u32[]{:S(2)}, u32[]{:S(2)}) %collective-permute-start.3) | collective-permute-done | bytes 688160 | tf_op jit(solution)/shard_map/ppermute | solution.py:1108
  134.3 2.3 fusion.11
  136.6 5.0 %fusion.7 = f32[2,448,768]{2,1,0:T(8,128)} fusion(bf16[1536,768]{1,0:T(8,128)(2,1)S(1)} %copy-done, f32[2,448,1536]{2,1,0:T(8,128)S(1)} %fusion.11, f32[1536]{0:T(1024)S(1)} %copy-done.48), kind=kOutput, calls=%fused_computation.14 | convolution fusion | flops 2127691776 | bytes 10622976 | tf_op jit(solution)/shard_map/alf,fd->ald/dot_general | solution.py:1212
  141.6 6.7 %fusion.34 = (f32[1536]{0:T(1024)S(1)}, bf16[2,448,1536]{2,1,0:T(8,128)(2,1)}) fusion(f32[2,448,1536]{2,1,0:T(8,128)S(1)} %fusion.11, f32[1536]{0:T(1024)S(1)} %copy-done.48, bf16[2,448,768]{2,1,0:T(8,128)(2,1)S(1)} %constant_dynamic-update-slice_fusion.3, bf16[1536,768]{1,0:T(8,128)(2,1)S(1)} %copy-done), kind=kOutput, calls=%fused_computation.108 | convolution fusion | flops 2144205312 | bytes 12005376 | tf_op jit(solution)/shard_map/ald,fd->alf/dot_general | solution.py:1218
  150.0 5.0 %fusion.9 = f32[2,448,768]{2,1,0:T(8,128)S(1)} fusion(bf16[768,1536]{1,0:T(8,128)(2,1)} %param.51, bf16[2,448,1536]{2,1,0:T(8,128)(2,1)} %get-tuple-element.101), kind=kOutput, calls=%fused_computation.16 | convolution fusion | flops 2113929216 | bytes 7864320 | tf_op jit(solution)/shard_map/alf,df->ald/dot_general | solution.py:1223
  155.1 2.0 collective-permute-start.6
  157.1 4.8 %bitcast_convert_fusion.1.g2_ref = bf16[1536,768]{1,0:T(8,128)(2,1)} fusion(bf16[2,448,768]{2,1,0:T(8,128)(2,1)S(1)} %copy-done.17, f32[2,448,1536]{2,1,0:T(8,128)S(1)} %bitcast.106, f32[1536]{0:T(1024)S(1)} %copy-done.48), kind=kOutput, calls=%fused_computation.10 | convolution fusion | flops 2128871424 | bytes 9246720 | tf_op jit(solution)/shard_map/alf,ald->fd/dot_general | solution.py:1216
  162.0 20.9 %collective-permute-done.6 = bf16[2,224,768]{2,1,0:T(8,128)(2,1)S(1)} collective-permute-done((bf16[2,224,768]{2,1,0:T(8,128)(2,1)S(1)}, bf16[2,224,768]{2,1,0:T(8,128)(2,1)S(1)}, u32[]{:S(2)}, u32[]{:S(2)}) %collective-permute-start.6) | collective-permute-done | bytes 688160 | tf_op jit(solution)/shard_map/ppermute | solution.py:1108
  188.9 3.9 %bitcast_convert_fusion.g1_ref = bf16[768,1536]{1,0:T(8,128)(2,1)} fusion(bf16[2,448,768]{2,1,0:T(8,128)(2,1)S(1)} %copy-done.15, bf16[2,448,1536]{2,1,0:T(8,128)(2,1)S(1)} %copy-done.51), kind=kOutput, calls=%fused_computation.9 | convolution fusion | flops 2115108864 | bytes 6488064 | tf_op jit(solution)/shard_map/ald,alf->df/dot_general | solution.py:1222
  195.1 9.4 %collective-permute-done.7 = bf16[2,224,768]{2,1,0:T(8,128)(2,1)S(1)} collective-permute-done((bf16[2,224,768]{2,1,0:T(8,128)(2,1)S(1)}, bf16[2,224,768]{2,1,0:T(8,128)(2,1)S(1)}, u32[]{:S(2)}, u32[]{:S(2)}) %collective-permute-start.7) | collective-permute-done | bytes 688160 | tf_op jit(solution)/shard_map/ppermute | solution.py:1108
  206.4 50.3 %shard_map.493 = (f32[2,448,384]{2,1,0:T(8,128)}, f32[2,2,896,384]{3,2,1,0:T(8,128)}, f32[256,384]{1,0:T(8,128)}, bf16[8,48,384]{2,1,0:T(8,128)(2,1)}, f32[16,768]{1,0:T(8,128)}) custom-call(bf16[2,1,448,384]{3,2,1,0:T(8,128)(2,1)} %get-tuple-element.44.q_ref, bf16[2,2,448,384]{3,2,1,0:T(8,128)(2,1)} %get-tuple-element.45.kv_ref, ...), custom_call_target="tpu_custom_call" | custom-call | flops 40000000000 | bytes 20000000 | tf_op jit(solution)/shard_map/pallas_call | solution.py:655
  259.0 97.1 %shard_map.494 = (f32[2,224,768]{2,1,0:T(8,128)}, f32[1536,768]{1,0:T(8,128)}, f32[768,1536]{1,0:T(8,128)}, f32[384,768]{1,0:T(8,128)}, bf16[3,768,384]{2,1,0:T(...) custom-call(f32[2,448,384]{2,1,0:T(8,128)} %get-tuple-element.52.dq_hbm, ...), custom_call_target="tpu_custom_call" | custom-call | flops 60000002048 | bytes 40000000 | tf_op jit(solution)/shard_map/pallas_call | solution.py:1028
  360.3 3.3 copy.63
  365.7 2.0 convert_bitcast_fusion
  367.7 2.9 copy.76
  370.6 2.2 copy.77
  372.8 2.4 copy.78
  (221 shorter events, 68.1 us)
Async XLA Ops:
  0.7 135.9 %copy-start = (bf16[1536,768]{1,0:T(8,128)(2,1)S(1)}, bf16[1536,768]{1,0:T(8,128)(2,1)}, u32[]{:S(2)}) copy-start(bf16[1536,768]{1,0:T(8,128)(2,1)} %param.53) | copy-start | bytes 7077892
  3.7 6.6 %copy-start.9 = (bf16[768,3,384]{2,0,1:T(8,128)(2,1)S(1)}, bf16[768,3,384]{2,0,1:T(8,128)(2,1)}, u32[]{:S(2)}) copy-start(bf16[768,3,384]{2,0,1:T(8,128)(2,1)} %param.38) | copy-start | bytes 5308420
  5.3 22.5 %collective-permute-start = (bf16[2,224,768]{2,1,0:T(8,128)(2,1)S(1)}, bf16[2,224,768]{2,1,0:T(8,128)(2,1)}, u32[]{:S(2)}, u32[]{:S(2)}) collective-permute-start(bf16[2,224,768]{2,1,0:T(8,128)(2,1)S(1)} %fusion.17), channel_id=1, source_target_pairs={{0,1},{1,0},{2,3},{3,2},{4,5},{5,4},{6,7},{7,6},{8,9},{9,8},{10,11... | collective-permute-start | bytes 2064392 | tf_op jit(solution)/shard_map/ppermute | solution.py:1108
  10.4 5.9 %copy-start.40 = (f32[13,96]{1,0:T(8,128)S(1)}, f32[13,96]{1,0:T(8,128)}, u32[]{:S(2)}) copy-start(f32[13,96]{1,0:T(8,128)} %param.46) | copy-start | bytes 14980
  44.7 10.3 %collective-permute-start.1 = (bf16[2,2,224,384]{3,2,1,0:T(8,128)(2,1)}, bf16[2,2,224,384]{3,2,1,0:T(8,128)(2,1)S(1)}, u32[]{:S(2)}, u32[]{:S(2)}) collective-permute-start(bf16[2,2,224,384]{3,2,1,0:T(8,128)(2,1)} %get-tuple-element.46), channel_id=1, source_target_pairs={{0,2},{2,4},{4,6},{6,8},{8,10},{10,12},{12,14},{14,16},{16,18},{18... | collective-permute-start | bytes 2064392 | tf_op jit(solution)/shard_map/ppermute | solution.py:1082
  57.3 26.9 %copy-start.20 = (bf16[384,768]{1,0:T(8,128)(2,1)S(1)}, bf16[384,768]{1,0:T(8,128)(2,1)}, u32[]{:S(2)}) copy-start(bf16[384,768]{1,0:T(8,128)(2,1)} %param.47) | copy-start | bytes 1769476
  86.2 17.4 %copy-start.4 = (bf16[2,4,7,8,768]{4,3,2,1,0:T(8,128)(2,1)S(1)}, bf16[2,4,7,8,768]{4,3,2,1,0:T(8,128)(2,1)}, u32[]{:S(2)}) copy-start(bf16[2,4,7,8,768]{4,3,2,1,0:T(8,128)(2,1)} %pad.40) | copy-start | bytes 2064388
  86.2 17.4 %copy-start.43 = (f32[768]{0:T(1024)S(1)}, f32[768]{0:T(1024)}, u32[]{:S(2)}) copy-start(f32[768]{0:T(1024)} %param.48) | copy-start | bytes 9220
  86.3 17.3 %collective-permute-start.2 = (bf16[2,224,768]{2,1,0:T(8,128)(2,1)S(1)}, bf16[2,224,768]{2,1,0:T(8,128)(2,1)S(1)}, u32[]{:S(2)}, u32[]{:S(2)}) collective-permute-start(bf16[2,224,768]{2,1,0:T(8,128)(2,1)S(1)} %dynamic-slice_convert_fusion.2), channel_id=1, source_target_pairs={{0,1},{1,0},{2,3},{3,2},{4,5},{5,4},{6,7},{7,6},{8,9},{9,8},{10,11... | collective-permute-start | bytes 2064392 | tf_op jit(solution)/shard_map/ppermute | solution.py:1108
  89.0 29.4 %collective-permute-start.5 = (bf16[2,224,768]{2,1,0:T(8,128)(2,1)}, bf16[2,224,768]{2,1,0:T(8,128)(2,1)S(1)}, u32[]{:S(2)}, u32[]{:S(2)}) collective-permute-start(bf16[2,224,768]{2,1,0:T(8,128)(2,1)} %bitcast.22), channel_id=1, source_target_pairs={{0,1},{1,0},{2,3},{3,2},{4,5},{5,4},{6,7},{7,6},{8,9},{9,8},{10,11... | collective-permute-start | bytes 2064392 | tf_op jit(solution)/shard_map/ppermute | solution.py:1108
  108.7 24.5 %collective-permute-start.3 = (bf16[2,224,768]{2,1,0:T(8,128)(2,1)S(1)}, bf16[2,224,768]{2,1,0:T(8,128)(2,1)S(1)}, u32[]{:S(2)}, u32[]{:S(2)}) collective-permute-start(bf16[2,224,768]{2,1,0:T(8,128)(2,1)S(1)} %add_convert_fusion.2), channel_id=1, source_target_pairs={{0,1},{1,0},{2,3},{3,2},{4,5},{5,4},{6,7},{7,6},{8,9},{9,8},{10,11... | collective-permute-start | bytes 2064392 | tf_op jit(solution)/shard_map/ppermute | solution.py:1108
  118.4 23.2 %copy-start.16 = (bf16[2,448,768]{2,1,0:T(8,128)(2,1)}, bf16[2,448,768]{2,1,0:T(8,128)(2,1)S(1)}, u32[]{:S(2)}) copy-start(bf16[2,448,768]{2,1,0:T(8,128)(2,1)S(1)} %constant_dynamic-update-slice_fusion.3) | copy-start | bytes 4128772
  118.4 15.8 %copy-start.47 = (bf16[768,1536]{1,0:T(8,128)(2,1)S(1)}, bf16[768,1536]{1,0:T(8,128)(2,1)}, u32[]{:S(2)}) copy-start(bf16[768,1536]{1,0:T(8,128)(2,1)} %param.51) | copy-start | bytes 7077892
  148.3 8.8 %slice-start.4 = ((s8[5505024]{0:T(1024)(128)(4,1)}), s8[4194304]{0:T(1024)(128)(4,1)S(1)}, s32[]{:S(2)}) async-start(s8[5505024]{0:T(1024)(128)(4,1)} %bitcast.105), calls=%async_computation.4 | async-start | bytes 8388608
  149.9 34.1 %collective-permute-start.4 = (bf16[2,224,768]{2,1,0:T(8,128)(2,1)S(1)}, bf16[2,224,768]{2,1,0:T(8,128)(2,1)S(1)}, u32[]{:S(2)}, u32[]{:S(2)}) collective-permute-start(bf16[2,224,768]{2,1,0:T(8,128)(2,1)S(1)} %dynamic-slice_convert_fusion.1), channel_id=1, source_target_pairs={{0,1},{1,0},{2,3},{3,2},{4,5},{5,4},{6,7},{7,6},{8,9},{9,8},{10,11... | collective-permute-start | bytes 2064392 | tf_op jit(solution)/shard_map/ppermute | solution.py:1108
  150.0 7.1 %copy-start.17 = (bf16[2,448,768]{2,1,0:T(8,128)(2,1)S(1)}, bf16[2,448,768]{2,1,0:T(8,128)(2,1)}, u32[]{:S(2)}) copy-start(bf16[2,448,768]{2,1,0:T(8,128)(2,1)} %copy-done.16) | copy-start | bytes 4128772
  150.0 7.1 %slice-start.5 = ((s8[5505024]{0:T(1024)(128)(4,1)}), s8[1310720]{0:T(1024)(128)(4,1)S(1)}, s32[]{:S(2)}) async-start(s8[5505024]{0:T(1024)(128)(4,1)} %bitcast.105), calls=%async_computation.5 | async-start | bytes 2621440
  155.1 27.8 %copy-start.3 = (f32[2,224,768]{2,1,0:T(8,128)S(1)}, f32[2,224,768]{2,1,0:T(8,128)}, u32[]{:S(2)}) copy-start(f32[2,224,768]{2,1,0:T(8,128)} %fusion.18) | copy-start | bytes 4128772
  155.1 27.8 %collective-permute-start.6 = (bf16[2,224,768]{2,1,0:T(8,128)(2,1)S(1)}, bf16[2,224,768]{2,1,0:T(8,128)(2,1)S(1)}, u32[]{:S(2)}, u32[]{:S(2)}) collective-permute-start(bf16[2,224,768]{2,1,0:T(8,128)(2,1)S(1)} %dynamic-slice_convert_fusion), channel_id=1, source_target_pairs={{0,1},{1,0},{2,3},{3,2},{4,5},{5,4},{6,7},{7,6},{8,9},{9,8},{10,11... | collective-permute-start | bytes 2064392 | tf_op jit(solution)/shard_map/ppermute | solution.py:1108
  187.2 17.4 %collective-permute-start.7 = (bf16[2,224,768]{2,1,0:T(8,128)(2,1)S(1)}, bf16[2,224,768]{2,1,0:T(8,128)(2,1)S(1)}, u32[]{:S(2)}, u32[]{:S(2)}) collective-permute-start(bf16[2,224,768]{2,1,0:T(8,128)(2,1)S(1)} %convert_element_type.109), channel_id=1, source_target_pairs={{0,1},{1,0},{2,3},{3,2},{4,5},{5,4},{6,7},{7,6},{8,9},{9,8},{10,11... | collective-permute-start | bytes 2064392 | tf_op jit(solution)/shard_map/ppermute | solution.py:1108
  195.0 9.6 %copy-start.21 = (bf16[384,768]{1,0:T(8,128)(2,1)S(1)}, bf16[384,768]{1,0:T(8,128)(2,1)}, u32[]{:S(2)}) copy-start(bf16[384,768]{1,0:T(8,128)(2,1)} %param.47) | copy-start | bytes 1769476
  204.6 52.1 %copy-start.13 = (bf16[2,448,768]{2,1,0:T(8,128)(2,1)}, bf16[2,448,768]{2,1,0:T(8,128)(2,1)S(1)}, u32[]{:S(2)}) copy-start(bf16[2,448,768]{2,1,0:T(8,128)(2,1)S(1)} %constant_dynamic-update-slice_fusion.2) | copy-start | bytes 4128772
  356.1 9.6 %copy-start.10 = (bf16[3,768,384]{2,1,0:T(8,128)(2,1)S(1)}, bf16[3,768,384]{2,1,0:T(8,128)(2,1)}, u32[]{:S(2)}) copy-start(bf16[3,768,384]{2,1,0:T(8,128)(2,1)} %get-tuple-element.61) | copy-start | bytes 5308420
  360.3 10.3 %slice-start.2 = ((s8[4718592]{0:T(1024)(128)(4,1)}), s8[524288]{0:T(1024)(128)(4,1)S(1)}, s32[]{:S(2)}) async-start(s8[4718592]{0:T(1024)(128)(4,1)} %bitcast.91), calls=%async_computation.2 | async-start | bytes 1048576
  (42 other events, 115.2 us)

commit v4 on v3

--- a/solution.py
+++ b/solution.py
@@ -193,9 +193,8 @@
             lax.fori_loop(0, TM // 2, squeeze_step, 0)
 
 
-def call_pool_forward(rows, weights, kernels, squeezes=None):
+def call_pool_forward(rows, weights, first, count, kernels, squeezes=None):
     clips = rows.shape[0]
-    count = weights.shape[0]
     squeeze = squeezes is not None
     tap = pl.BlockSpec((1, 27, 8, LW), lambda j, i: (j, 0, 0, 0))
 
@@ -219,7 +218,7 @@
         grid=(count, clips),
         in_specs=[
             pl.BlockSpec((1, ROWS, rows.shape[2]), lambda j, i: (i, 0, 0)),
-            pl.BlockSpec((1, weights.shape[1], LW), lambda j, i: (j, 0, 0)),
+            pl.BlockSpec((1, weights.shape[1], LW), lambda j, i: (j + first, 0, 0)),
             tap,
         ]
         + ([tap] if squeeze else []),
@@ -288,17 +287,19 @@
     return pl.BlockSpec((1,) + shape, lambda i: (i,) + (0,) * len(shape))
 
 
-def call_attention_forward(q, kv, memory, keys_extra, tables, consts):
-    clips = q.shape[0]
+def call_attention_forward(clip, q, kv, memory, keys_extra, tables, consts):
+    def block(*shape, at=clip):
+        return pl.BlockSpec((1,) + shape, lambda i: (at,) + (0,) * len(shape))
+
     return pl.pallas_call(
         attention_forward,
-        grid=(clips,),
+        grid=(1,),
         in_specs=[
-            clip_block(1, ROWS, LW),
-            clip_block(2, ROWS, LW),
-            pl.BlockSpec((1, 2, MROWS, LW), lambda i: (i + 1, 0, 0, 0)),
-            pl.BlockSpec((1, 2, MROWS, LW), lambda i: (i, 0, 0, 0)),
-            clip_block(2, KEYS, WIN),
+            block(1, ROWS, LW),
+            block(2, ROWS, LW),
+            block(2, MROWS, LW, at=clip + 1),
+            block(2, MROWS, LW, at=clip),
+            block(2, KEYS, WIN),
             whole((LH, 2, WIN, 256)),
             whole((2, 2, 256, WIN)),
             whole((2, 8, WIN)),
@@ -312,10 +313,10 @@
             clip_block(8, ROWS),
         ],
         out_shape=[
-            jax.ShapeDtypeStruct((clips, ROWS, LW), BF16),
-            jax.ShapeDtypeStruct((clips, LH, ROWS, WIN), BF16),
-            jax.ShapeDtypeStruct((clips, LW, ROWS), F32),
-            jax.ShapeDtypeStruct((clips, 8, ROWS), F32),
+            jax.ShapeDtypeStruct((1, ROWS, LW), BF16),
+            jax.ShapeDtypeStruct((1, LH, ROWS, WIN), BF16),
+            jax.ShapeDtypeStruct((1, LW, ROWS), F32),
+            jax.ShapeDtypeStruct((1, 8, ROWS), F32),
         ],
         scratch_shapes=[
             pltpu.VMEM((KEYS, LW), BF16),
@@ -325,9 +326,147 @@
         ],
         compiler_params=params(),
         cost_estimate=pl.CostEstimate(
-            flops=20_000_000_000, bytes_accessed=10_000_000, transcendentals=3_000_000
+            flops=13_000_000_000, bytes_accessed=5_000_000, transcendentals=1_500_000
         ),
     )(q, kv, memory, memory, keys_extra, tables, consts["fold"], consts["one"], consts["own"], consts["lanes"])
+
+
+HALF = ROWS // 2
+
+
+def simple_call(kernel, out_shape, gflops, *args):
+    vmem = pl.BlockSpec(memory_space=pltpu.VMEM)
+    many = isinstance(out_shape, list)
+    return pl.pallas_call(
+        kernel,
+        in_specs=[vmem] * len(args),
+        out_specs=[vmem] * len(out_shape) if many else vmem,
+        out_shape=out_shape,
+        compiler_params=params(),
+        cost_estimate=pl.CostEstimate(
+            flops=int(gflops * 1e9), bytes_accessed=2_000_000, transcendentals=0
+        ),
+    )(*args)
+
+
+def half_rows(side):
+    return pl.ds(pl.multiple_of(side * HALF, 16), HALF)
+
+
+def project_kernel(branch, w, kept, sent):
+    head = lax.axis_index("head")
+    sent[...] = nn(branch[half_rows(1 - head)], w[...]).astype(BF16)
+    kept[...] = nn(branch[half_rows(head)], w[...])
+
+
+def middle_kernel(tokens, kept, recv, vectors, x1_ref, a2_ref):
+    x1 = tokens[...].astype(F32) + kept[...] + recv[...].astype(F32) + vectors[0:1]
+    x1_ref[...] = x1
+    centred = x1 - jnp.mean(x1, axis=-1, keepdims=True)
+    scale = lax.rsqrt(jnp.mean(centred * centred, axis=-1, keepdims=True) + EPSILON)
+    a2_ref[...] = (centred * scale * vectors[1:2] + vectors[2:3]).astype(BF16)
+
+
+FFN_BLOCK = 512
+GELU_A = 0.7978845608028654
+GELU_B = 0.044715
+
+
+def ffn_kernel(a2, g, w1, b1, w2, act_ref, dpre_ref, da2_ref, out_ref, sums_ref):
+    da2 = jnp.zeros(da2_ref.shape, F32)
+    out = jnp.zeros(out_ref.shape, F32)
+    for first in range(0, w1.shape[1], FFN_BLOCK):
+        cols = slice(first, first + FFN_BLOCK)
+        pre = nn(a2[...], w1[:, cols]) + b1[0:1, cols]
+        square = pre * pre
+        bent = jnp.tanh(GELU_A * (pre + GELU_B * (pre * square)))
+        gate = 0.5 + 0.5 * bent
+        act = (pre * gate).astype(BF16)
+        slope = gate + 0.5 * pre * (1.0 - bent * bent) * (GELU_A * (1.0 + 3.0 * GELU_B * square))
+        dpre = nt(g[...], w2[cols]) * slope
+        low = dpre.astype(BF16)
+        sums_ref[0:1, cols] = jnp.sum(dpre, axis=0, keepdims=True)
+        act_ref[:, cols] = act
+        dpre_ref[:, cols] = low
+        da2 = da2 + nt(low, w1[:, cols])
+        out = out + nn(act, w2[cols])
+    da2_ref[...] = da2.astype(da2_ref.dtype)
+    out_ref[...] = out.astype(out_ref.dtype)
+
+
+def call_ffn(a2, g, w1, b1, w2, dtype):
+    hidden = w1.shape[1]
+    return simple_call(
+        ffn_kernel,
+        [
+            jax.ShapeDtypeStruct((HALF, hidden), BF16),
+            jax.ShapeDtypeStruct((HALF, hidden), BF16),
+            jax.ShapeDtypeStruct(a2.shape, dtype),
+            jax.ShapeDtypeStruct(a2.shape, dtype),
+            jax.ShapeDtypeStruct((1, hidden), F32),
+        ],
+        5, a2, g, w1, b1, w2,
+    )
+
+
+def tn(a, b):
+    return lax.dot_general(a, b, (((0,), (0,)), ((), ())), preferred_element_type=F32)
+
+
+def weight_kernel(count, *refs):
+    acts, dpres, a2s, gs = (refs[n * count : (n + 1) * count] for n in range(4))
+    g2, g1 = refs[4 * count :]
+    g2[...] = sum(tn(a[...], b[...]) for a, b in zip(acts, gs)).astype(BF16)
+    g1[...] = sum(tn(a[...], b[...]) for a, b in zip(a2s, dpres)).astype(BF16)
+
+
+def call_weights(acts, dpres, a2s, gs):
+    hidden, width = acts[0].shape[1], gs[0].shape[1]
+    count = len(acts)
+    piece = pl.BlockSpec((HALF, LW), lambda i: (0, i))
+    full = pl.BlockSpec((HALF, width), lambda i: (0, 0))
+    return pl.pallas_call(
+        partial(weight_kernel, count),
+        grid=(hidden // LW,),
+        in_specs=[piece] * (2 * count) + [full] * (2 * count),
+        out_specs=[
+            pl.BlockSpec((LW, width), lambda i: (i, 0)),
+            pl.BlockSpec((width, LW), lambda i: (0, i)),
+        ],
+        out_shape=[
+            jax.ShapeDtypeStruct((hidden, width), BF16),
+            jax.ShapeDtypeStruct((width, hidden), BF16),
+        ],
+        compiler_params=params(),
+        cost_estimate=pl.CostEstimate(flops=8_000_000_000, bytes_accessed=15_000_000, transcendentals=0),
+    )(*acts, *dpres, *a2s, *gs)
+
+
+def norm_back_kernel(kept, recv, x1_ref, g, vectors, dx_ref, low_ref, sums):
+    u = kept[...] + recv[...].astype(F32)
+    x1 = x1_ref[...]
+    centred = x1 - jnp.mean(x1, axis=-1, keepdims=True)
+    scale = lax.rsqrt(jnp.mean(centred * centred, axis=-1, keepdims=True) + EPSILON)
+    xhat = centred * scale
+    w = u * vectors[1:2]
+    up = g[...].astype(F32)
+    dx = up + scale * (
+        w - jnp.mean(w, axis=-1, keepdims=True) - xhat * jnp.mean(w * xhat, axis=-1, keepdims=True)
+    )
+    dx_ref[...] = dx
+    low_ref[...] = dx.astype(BF16)
+    sums[0:1] = jnp.sum(dx, axis=0, keepdims=True)
+    sums[1:2] = jnp.sum(u * xhat, axis=0, keepdims=True)
+    sums[2:3] = jnp.sum(u, axis=0, keepdims=True)
+    sums[3:4] = jnp.sum(up, axis=0, keepdims=True)
+    sums[4:8] = jnp.zeros((4, u.shape[1]), F32)
+
+
+def mix_kernel(mine, theirs, w, rows_ref, dmix_ref):
+    head = lax.axis_index("head")
+    for side, part in ((head, mine), (1 - head, theirs)):
+        rows_ref[half_rows(side)] = part[...]
+        dmix_ref[half_rows(side)] = nt(part[...], w[...]).astype(BF16)
 
 
 EARLY = 16
@@ -512,8 +651,9 @@
 
 def attention_backward(
     groups,
-    q_ref, kv_ref, mem_ref, ke_hbm, qa_hbm, dm_ref, at_hbm, lse_ref, rt_ref, grow_ref, ownt_ref, ekey_ref,
-    lanes_ref, g2_ref, g1_ref, early_ref,
+    q_ref, kv_ref, mem_ref, ke_hbm, qa_hbm0, qa_hbm1, dm_ref0, dm_ref1, at_hbm0, at_hbm1, lse_ref0, lse_ref1,
+    rt_ref, grow_ref, ownt_ref, ekey_ref,
+    lanes_ref, g2_ref, g1_ref, sums0, sums1, hidden0, hidden1, hidden2, hidden3,
     dq_ref, dkv_ref, dr_ref, chunks_ref, early_out,
     ke_ref, qa_ref, at_ref, keys, values, kt, dmt, qms, dms, dqt,
     recv_a, send_b, recv_b, send_c, recv_c, s0, s1, s2, s3, s4,
@@ -521,9 +661,13 @@
 ):
     place = Place(groups)
     clips = q_ref.shape[0]
+    dm_refs, lse_refs = (dm_ref0, dm_ref1), (lse_ref0, lse_ref1)
     lead = [
-        [local(src.at[clip], dst.at[clip], loads.at[3 * clip + n])
-         for n, (src, dst) in enumerate(((ke_hbm, ke_ref), (qa_hbm, qa_ref), (at_hbm, at_ref)))]
+        [
+            local(ke_hbm.at[clip], ke_ref.at[clip], loads.at[3 * clip]),
+            local((qa_hbm0, qa_hbm1)[clip].at[0], qa_ref.at[clip], loads.at[3 * clip + 1]),
+            local((at_hbm0, at_hbm1)[clip].at[0], at_ref.at[clip], loads.at[3 * clip + 2]),
+        ]
         for clip in range(clips)
     ]
     place.greet()
@@ -545,23 +689,28 @@
         for number in range(8)
     ]
     small = Small(place, s0, (s1, s2, s3, s4), HEAD_EARLY, small_send, small_recv, 0)
-    s0[0] = early_ref[...]
+    s0[0, 0:HEAD_EARLY] = sums0[...] + sums1[...]
+    hidden = hidden0[...] + hidden1[...] + hidden2[...] + hidden3[...]
+    width = s0.shape[2]
+    s0[0, HEAD_EARLY:EARLY] = jnp.zeros((EARLY - HEAD_EARLY, width), F32)
+    for n in range(hidden.shape[1] // width):
+        s0[0, HEAD_EARLY + n : HEAD_EARLY + n + 1] = hidden[:, n * width : (n + 1) * width]
     small.one()
-    for number in range(3):
-        pieces[number].a()
-    moves = []
-    for slot in range(9):
-        moves.append([])
-        if slot < 8:
-            moves[-1].append(pieces[slot].b)
-        if slot + 3 < 8:
-            moves[-1].append(pieces[slot + 3].a)
-        if slot > 0:
-            moves[-1].append(pieces[slot - 1].c)
-    moves[1].append(small.two)
-    moves[2].append(small.three)
-    moves[3].append(small.four)
-    moves[6].append(partial(small.five, early_out))
+    for piece in pieces:
+        piece.a()
+    moves = [
+        [pieces[0].b, pieces[1].b],
+        [pieces[2].b, small.two],
+        [pieces[3].b, pieces[0].c],
+        [pieces[4].b, pieces[1].c, small.three],
+        [pieces[5].b, pieces[2].c],
+        [pieces[6].b, pieces[3].c],
+        [pieces[7].b, pieces[4].c],
+        [pieces[5].c, small.four],
+        [pieces[6].c],
+        [pieces[7].c],
+        [partial(small.five, early_out)],
+    ]
 
     def pump():
         if moves:
@@ -579,7 +728,7 @@
         values[ROWS + MROWS :] = far[1]
         kt[0:LW] = keys[...].T
         kt[LW:] = ekey_ref[...]
-        dmt[...] = dm_ref[clip].astype(F32).T
+        dmt[...] = dm_refs[clip][...].astype(F32).T
         dqt[...] = jnp.zeros_like(dqt)
         for made in lead[clip]:
             made.wait()
@@ -589,7 +738,7 @@
             win = slice(first, first + WIN)
             span = slice(head * HEAD_DIM, (head + 1) * HEAD_DIM)
             qms[head] = q_ref[clip, 0, :, win] * lanes_ref[head]
-            dms[head] = dm_ref[clip, :, win] * lanes_ref[head]
+            dms[head] = dm_refs[clip][:, win] * lanes_ref[head]
             deltas.append(jnp.sum(dmt[span] * at_ref[clip, span], axis=0, keepdims=True))
 
         def step(number, _):
@@ -601,7 +750,7 @@
                 win = slice(first, first + WIN)
                 ka = keys[rows, win] * lanes_ref[head, 0:BLOCK] + ke_ref[clip, variant, rows]
                 s = nt(ka, qa_ref[clip, head])
-                p = jnp.exp2(s * (SCALE * LOG2E) - lse_ref[clip, head : head + 1])
+                p = jnp.exp2(s * (SCALE * LOG2E) - lse_refs[clip][0, head : head + 1])
                 dp = nt(values[rows, win], dms[head])
                 ds = (p * (dp - deltas[head])).astype(BF16)
                 dv_parts.append(nn(p.astype(BF16), dms[head]))
@@ -643,8 +792,8 @@
     return -(-width // (4 * groups) // 16) * 16 * 4 * groups
 
 
-def call_attention_backward(q, kv, memory, keys_extra, qa, dmix, at, lse, rt, g2, g1, early, consts):
-    clips, width = q.shape[0], early.shape[1]
+def call_attention_backward(q, kv, memory, keys_extra, qa, dmix, at, lse, rt, g2, g1, sums, hidden, consts):
+    clips, width = q.shape[0], sums[0].shape[1]
     groups = lax.axis_size("dp") // 4
     total = padded_rows(width, groups)
     if total != width:
@@ -654,7 +803,7 @@
     hbm = pl.BlockSpec(memory_space=pl.ANY)
     return pl.pallas_call(
         partial(attention_backward, groups),
-        in_specs=[vmem] * 3 + [hbm] * 2 + [vmem, hbm] + [vmem] * 9,
+        in_specs=[vmem] * 3 + [hbm] * 3 + [vmem] * 2 + [hbm] * 2 + [vmem] * 15,
         out_specs=[vmem] * 5,
         out_shape=[
             jax.ShapeDtypeStruct((clips, ROWS, LW), F32),
@@ -665,8 +814,8 @@
         ],
         scratch_shapes=[
             pltpu.VMEM(keys_extra.shape, BF16),
-            pltpu.VMEM(qa.shape, BF16),
-            pltpu.VMEM(at.shape, F32),
+            pltpu.VMEM((clips, LH, ROWS, WIN), BF16),
+            pltpu.VMEM((clips, LW, ROWS), F32),
             pltpu.VMEM((KEYS, LW), BF16),
             pltpu.VMEM((KEYS, LW), BF16),
             pltpu.VMEM((LW + 32, KEYS), BF16),
@@ -687,8 +836,8 @@
             flops=40_000_000_000, bytes_accessed=20_000_000, transcendentals=3_000_000
         ),
     )(
-        q, kv, memory, keys_extra, qa, dmix, at, lse, rt,
-        consts["grow"], consts["ownt"], consts["ekey"], consts["lanes"], g2, g1, early,
+        q, kv, memory, keys_extra, *qa, *dmix, *at, *lse, rt,
+        consts["grow"], consts["ownt"], consts["ekey"], consts["lanes"], g2, g1, *sums, *hidden,
     )
 
 
@@ -698,8 +847,8 @@
 
 def finish_kernel(
     groups, width,
-    dq_hbm, dkv_hbm, x0q_hbm, x0kv_hbm, kvf_hbm, taps_hbm, rows_a_hbm, rows_x_hbm, branch_hbm, w_hbm,
-    tokens_hbm, middle_hbm, chunks_ref, dr_ref, gain, foldl_ref, pick_ref,
+    dq_hbm, dkv_hbm, x0q_hbm, x0kv_hbm, kvf_hbm, taps_hbm, rows_a_hbm, rows_x0, rows_x1, branch0, branch1,
+    w_hbm, tokens_hbm, middle0, middle1, chunks_ref, dr_ref, gain, foldl_ref, pick_ref,
     grad, out2, out1, outp, outq, small_out, late_out,
     dq, dkv, x0q, x0kv, kvf, taps_ref, rows_a, rows_x, branch, w_ref, tokens, middle,
     us, ms, kacc, dx, dmem_send, dmem_recv, res2, res1, resp, grads, stage, stage_t,
@@ -710,11 +859,15 @@
     place = Place(groups)
     clips = dq.shape[0]
     total = rows_a.shape[1]
-    names = ("dkv", "dq", "x0q", "taps", "rows_x", "branch", "x0kv", "kvf", "rows_a", "w", "tokens", "middle")
+    names = (
+        "dkv", "dq", "x0q", "taps", "rows_x0", "rows_x1", "branch0", "branch1", "x0kv", "kvf", "rows_a", "w",
+        "tokens", "middle0", "middle1",
+    )
     pairs = (
-        (dkv_hbm, dkv), (dq_hbm, dq), (x0q_hbm, x0q), (taps_hbm, taps_ref), (rows_x_hbm, rows_x),
-        (branch_hbm, branch), (x0kv_hbm, x0kv), (kvf_hbm, kvf), (rows_a_hbm, rows_a), (w_hbm, w_ref),
-        (tokens_hbm, tokens), (middle_hbm, middle),
+        (dkv_hbm, dkv), (dq_hbm, dq), (x0q_hbm, x0q), (taps_hbm, taps_ref),
+        (rows_x0, rows_x.at[0:ROWS]), (rows_x1, rows_x.at[ROWS:]), (branch0, branch.at[0:ROWS]),
+        (branch1, branch.at[ROWS:]), (x0kv_hbm, x0kv), (kvf_hbm, kvf), (rows_a_hbm, rows_a), (w_hbm, w_ref),
+        (tokens_hbm, tokens), (middle0, middle.at[0]), (middle1, middle.at[1]),
     )
     lead = {
         name: local(src, dst, loads.at[n]) for n, (name, (src, dst)) in enumerate(zip(names, pairs))
@@ -771,16 +924,6 @@
             col = (number - 4) * LW
             target = out1.at[:, col : col + LW]
         flush(view2(number)(0, total), target)
-
-    def step(k):
-        if k < 8:
-            ffn[k].d(chunks_ref[k])
-        if 1 <= k < 9:
-            ffn[k - 1].e()
-        if 2 <= k < 10:
-            ffn[k - 2].f()
-        if 3 <= k < 11:
-            store2(k - 3)
 
     def product(number):
         left, right = (
@@ -913,12 +1056,13 @@
         sm[...] = sm_raw[...] + sm_y[...]
         tiny.a()
 
+    ffn[0].d(chunks_ref[0])
+    ffn[1].d(chunks_ref[1])
     us[...] = jnp.zeros_like(us)
     ms[...] = jnp.zeros_like(ms)
     kacc[...] = jnp.zeros_like(kacc)
     l0[0] = jnp.zeros_like(l0[0])
     sm_raw[...] = jnp.zeros_like(sm_raw)
-    step(0)
     lead["dkv"].wait()
     for which in range(2):
         dmem_send[0, which] = dkv[0, which, ROWS + MROWS :].astype(BF16)
@@ -926,83 +1070,104 @@
             dkv[0, which, ROWS : ROWS + MROWS] + dkv[1, which, ROWS + MROWS :]
         ).astype(BF16)
     memory_flight = remote(dmem_send, dmem_recv, mem_sems.at[0], mem_sems.at[1], behind)
+    for name in ("rows_x0", "rows_x1", "branch0", "branch1"):
+        lead[name].wait()
+    product(0)
     for name in ("dq", "x0q", "taps"):
         lead[name].wait()
+    late[0].b()
+    ffn[2].d(chunks_ref[2])
     pooled(0, 0)
-    step(1)
-    lead["rows_x"].wait()
-    lead["branch"].wait()
-    product(0)
+    ffn[0].e()
+    ffn[3].d(chunks_ref[3])
+    ffn[1].e()
     pooled(0, 1)
-    step(2)
-    late[0].b()
+    ffn[4].d(chunks_ref[4])
+    ffn[2].e()
+    ffn[0].f()
     lead["rows_a"].wait()
     product(1)
-    step(3)
     late[0].c()
     memory_flight.wait()
     lead["x0kv"].wait()
     lead["kvf"].wait()
+    late[1].b()
     pooled(1, 0)
-    step(4)
-    late[1].b()
+    ffn[5].d(chunks_ref[5])
+    ffn[3].e()
+    ffn[1].f()
     late[0].d()
+    ffn[4].e()
     pooled(2, 0)
-    step(5)
     late[1].c()
+    ffn[6].d(chunks_ref[6])
     late[0].e()
+    ffn[2].f()
+    store2(0)
     lead["w"].wait()
     cross(0)
+    ffn[5].e()
     pooled(1, 1)
-    step(6)
     late[1].d()
-    late[0].f()
+    ffn[7].d(chunks_ref[7])
     product(2)
-    step(7)
-    late[1].e()
+    late[2].b()
+    ffn[6].e()
+    ffn[3].f()
+    store2(1)
     pooled(2, 1)
-    late[2].b()
     product(3)
-    step(8)
-    late[1].f()
     cross(1)
     late[2].c()
     late[3].b()
     small_start()
-    step(9)
+    ffn[4].f()
+    late[0].f()
+    store2(2)
+    lead["tokens"].wait()
+    lead["middle0"].wait()
+    lead["middle1"].wait()
+    normed_gradient(0)
+    small_next()
+    late[2].d()
+    late[3].c()
+    late[1].e()
+    ffn[5].f()
+    store2(3)
+    tiny.b()
+    normed_gradient(1)
+    ends.one()
+    late[3].d()
+    tiny.c()
+    late[2].e()
+    ffn[7].e()
+    ends.two()
+    ffn[6].f()
+    store2(4)
+    late[1].f()
+    tiny.d()
+    ends.three()
     late[0].g()
     stage_t[...] = resp[0].astype(F32).T
     turned = local(stage_t, outp, stores.at[2])
-    lead["tokens"].wait()
-    lead["middle"].wait()
-    normed_gradient(0)
-    late[2].d()
-    late[3].c()
-    step(10)
-    small_next()
-    late[2].e()
-    late[3].d()
-    normed_gradient(1)
-    ends.one()
-    tiny.b()
+    late[3].e()
+    ends.four()
+    tiny.e()
+    store2(5)
+    late[2].f()
+    ffn[7].f()
+    store2(6)
     late[1].g()
     sent_q = local(resp.at[1], outq.at[0], stores.at[3])
-    late[2].f()
-    late[3].e()
-    ends.two()
-    tiny.c()
-    late[3].f()
-    ends.three()
-    tiny.d()
+    tiny.f()
+    ends.five(late_out)
+    store2(7)
     late[2].g()
     sent_k = local(resp.at[2], outq.at[1], stores.at[4])
-    ends.four()
-    tiny.e()
+    late[3].f()
+    tiny.g()
     late[3].g()
     sent_v = local(resp.at[3], outq.at[2], stores.at[5])
-    tiny.f()
-    ends.five(late_out)
-    tiny.g()
     small_out[...] = sm_res[...]
     for made in [turned, sent_q, sent_k, sent_v] + stored[-2:]:
         made.wait()
@@ -1015,7 +1180,7 @@
     clips, side = tokens.shape[:2]
     if total != width:
         extra = ((0, 0), (0, total - width))
-        rows_a, rows_x = jnp.pad(rows_a, extra), jnp.pad(rows_x, extra)
+        rows_a, rows_x = jnp.pad(rows_a, extra), [jnp.pad(x, extra) for x in rows_x]
     small_rows = -(-SMALL_ROWS // (32 * groups)) * 32 * groups
     foldl = np.zeros((LW, 128), np.float32)
     foldl[np.arange(LW), np.arange(LW) % HEAD_DIM] = 1
@@ -1023,11 +1188,18 @@
     pick[:NREL] = PICK.T
     vmem = pl.BlockSpec(memory_space=pltpu.VMEM)
     hbm = pl.BlockSpec(memory_space=pl.ANY)
-    streamed = [dq, dkv, x0q, x0kv, kvf, all_taps, rows_a, rows_x, branch, weights, tokens, middle]
+    streamed = [dq, dkv, x0q, x0kv, kvf, all_taps, rows_a, *rows_x, *branch, weights, tokens, *middle]
+    held = [
+        (array.shape, array.dtype)
+        for array in (dq, dkv, x0q, x0kv, kvf, all_taps, rows_a)
+    ] + [
+        ((clips * ROWS, total), BF16), ((clips * ROWS, LW), BF16), (weights.shape, BF16), (tokens.shape, BF16),
+        (tokens.shape, F32),
+    ]
     frame = pltpu.VMEM((3, T_LEN + 2, HGT + 2, PADW, LW), F32)
     return pl.pallas_call(
         partial(finish_kernel, groups, width),
-        in_specs=[hbm] * 12 + [vmem] * 5,
+        in_specs=[hbm] * len(streamed) + [vmem] * 5,
         out_specs=[vmem, hbm, hbm, hbm, hbm, vmem, vmem],
         out_shape=[
             jax.ShapeDtypeStruct(tokens.shape, F32),
@@ -1038,7 +1210,7 @@
             jax.ShapeDtypeStruct((small_rows, 128), F32),
             jax.ShapeDtypeStruct((LATE, width), F32),
         ],
-        scratch_shapes=[pltpu.VMEM(array.shape, array.dtype) for array in streamed]
+        scratch_shapes=[pltpu.VMEM(shape, dtype) for shape, dtype in held]
         + [
             frame,
             pltpu.VMEM((3, TM + 1, HGT + 2, PADW, LW), F32),
@@ -1061,7 +1233,7 @@
             pltpu.VMEM((clips, side, width), BF16),
             pltpu.VMEM((clips, side, width), BF16),
             *small_scratch(LATE, LATE, groups, width),
-            pltpu.SemaphoreType.DMA((12,)),
+            pltpu.SemaphoreType.DMA((15,)),
             pltpu.SemaphoreType.DMA((6,)),
             pltpu.SemaphoreType.DMA((13, 2 * groups + 2)),
             pltpu.SemaphoreType.DMA((13, 2 * groups + 2)),
@@ -1113,15 +1285,6 @@
     mine = lax.axis_index("head") * half
     both = jnp.concatenate([x, x], axis=1)
     return lax.dynamic_update_slice_in_dim(both, swap(x), half - mine, axis=1)
-
-
-def scatter_sum(x):
-    half = x.shape[1] // 2
-    mine = lax.axis_index("head") * half
-    theirs = half - mine
-    sent = lax.dynamic_slice_in_dim(x, theirs, half, axis=1).astype(BF16)
-    kept = lax.dynamic_slice_in_dim(x, mine, half, axis=1)
-    return kept + swap(sent).astype(F32)
 
 
 def taps(kernel):
@@ -1189,65 +1352,93 @@
     tap_q, tap_kv = taps(pool_q)[None], jnp.stack([taps(pool_k), taps(pool_v)])
     tap_s = jnp.stack([taps(squeeze_k), taps(squeeze_v)])
 
+    width = tokens.shape[2]
     inputs_low = pad_rows(tokens)
     inputs = inputs_low.astype(F32)
-    upstream_low = pad_rows(cotangent)
+    upstream = pad_rows(cotangent)
     real = (jnp.arange(inputs.shape[1]) % PADW < WID)[None, :, None]
     first_normed = layer_norm(inputs, ln1_gain, ln1_bias)
     first_rows = gather_rows(jnp.where(real, first_normed, 0.0).astype(BF16))
     w_heads = w_qkv.transpose(1, 0, 2)
-    upstream_rows = gather_rows(lax.optimization_barrier((upstream_low, first_rows))[0])
-    kv0, kv, kvf, mem = call_pool_forward(first_rows, w_heads[1:], tap_kv, tap_s)
+    upstream_other = swap(lax.optimization_barrier((upstream, first_rows))[0])
+    kv0, kv, kvf, mem = call_pool_forward(first_rows, w_heads, 1, 2, tap_kv, tap_s)
     before = from_behind(mem[-2:], "dp", 1)
-    q0, q = call_pool_forward(first_rows, w_heads[:1], tap_q)
+    q0, q = call_pool_forward(first_rows, w_heads, 0, 1, tap_q)
     memory = jnp.concatenate([before, mem], axis=0)
-    branch, qa, at, lse = call_attention_forward(q, kv, memory, keys_extra, tables, consts)
-    partial_z = jnp.einsum("ale,ef->alf", branch, w_proj, preferred_element_type=F32)
-    middle = inputs + scatter_sum(partial_z) + proj_bias
-    second_normed, second_pull = jax.vjp(layer_norm, middle, ln2_gain, ln2_bias)
-    second_rows = gather_rows(second_normed.astype(BF16))
-    hidden = jnp.einsum("ald,df->alf", second_rows, w_fc1, preferred_element_type=F32) + fc1_bias
-    active, gelu_pull = jax.vjp(partial(jax.nn.gelu, approximate=True), hidden)
-    active_low = active.astype(BF16)
-    partial_m = jnp.einsum("alf,fd->ald", active_low, w_fc2, preferred_element_type=F32)
-    output = drop_rows((middle + scatter_sum(partial_m) + fc2_bias).astype(BF16))
-    upstream = upstream_low.astype(F32)
-    fc2_bias_grad = jnp.sum(upstream, axis=(0, 1))
-    w_fc2_grad = jnp.einsum("alf,ald->fd", active_low, upstream_rows, preferred_element_type=F32)
-    (hidden_grad,) = gelu_pull(
-        jnp.einsum("ald,fd->alf", upstream_rows, w_fc2, preferred_element_type=F32)
+    vectors = jnp.stack([proj_bias, ln2_gain, ln2_bias])
+    hidden_bias = fc1_bias.reshape(1, -1)
+    rows32 = jax.ShapeDtypeStruct((HALF, width), F32)
+    rows16 = jax.ShapeDtypeStruct((HALF, width), BF16)
+    clips = range(clip_count)
+    branch, qa, at, lse, kept, recv = [], [], [], [], [], []
+    for clip in clips:
+        made = call_attention_forward(clip, q, kv, memory, keys_extra, tables, consts)
+        for store, value in zip((branch, qa, at, lse), made):
+            store.append(value)
+        own, sent = simple_call(project_kernel, [rows32, rows16], 1, branch[-1][0], w_proj)
+        kept.append(own)
+        recv.append(swap(sent))
+    middle, mine, theirs = [], [], []
+    for clip in clips:
+        x1, a2 = simple_call(
+            middle_kernel, [rows32, rows16], 1, inputs_low[clip], kept[clip], recv[clip], vectors
+        )
+        middle.append(x1)
+        mine.append(a2)
+        theirs.append(swap(a2))
+    own_parts = [call_ffn(mine[c], upstream[c], w_fc1, hidden_bias, w_fc2, F32) for c in clips]
+    other_parts = [call_ffn(theirs[c], upstream_other[c], w_fc1, hidden_bias, w_fc2, BF16) for c in clips]
+    second = [swap(other_parts[c][2]) for c in clips]
+    dmiddle, low, sums, rows_x, dmix = [], [], [], [], []
+    for clip in clips:
+        dx, dx_low, total = simple_call(
+            norm_back_kernel,
+            [rows32, rows16, jax.ShapeDtypeStruct((HEAD_EARLY, width), F32)],
+            1,
+            own_parts[clip][2], second[clip], middle[clip], upstream[clip], vectors,
+        )
+        dmiddle.append(dx)
+        sums.append(total)
+        low.append((dx_low, swap(dx_low)))
+    parts = own_parts + other_parts
+    w_fc2_grad, w_fc1_grad = call_weights(
+        [p[0] for p in parts],
+        [p[1] for p in parts],
+        mine + theirs,
+        [upstream[c] for c in clips] + [upstream_other[c] for c in clips],
     )
-    fc1_bias_grad = jnp.sum(hidden_grad, axis=(0, 1))
-    hidden_low = hidden_grad.astype(BF16)
-    w_fc1_grad = jnp.einsum("ald,alf->df", second_rows, hidden_low, preferred_element_type=F32)
-    partial_second = jnp.einsum("alf,df->ald", hidden_low, w_fc1, preferred_element_type=F32)
-    middle_part, ln2_gain_grad, ln2_bias_grad = second_pull(scatter_sum(partial_second))
-    middle_grad = middle_part + upstream
-    proj_bias_grad = jnp.sum(middle_grad, axis=(0, 1))
-    middle_rows = gather_rows(middle_grad.astype(BF16))
-    dmix = jnp.einsum("alf,ef->ale", middle_rows, w_proj, preferred_element_type=F32).astype(BF16)
-
-    width = tokens.shape[2]
-    early = jnp.concatenate(
-        [
-            jnp.stack([proj_bias_grad, ln2_gain_grad, ln2_bias_grad, fc2_bias_grad]),
-            jnp.zeros((HEAD_EARLY - 4, width), F32),
-            fc1_bias_grad.reshape(-1, width),
-        ]
-    )
-    early = jnp.pad(early, ((0, EARLY - early.shape[0]), (0, 0)))
+    for clip in clips:
+        rows, mix = simple_call(
+            mix_kernel,
+            [jax.ShapeDtypeStruct((ROWS, width), BF16), jax.ShapeDtypeStruct((ROWS, LW), BF16)],
+            1,
+            *low[clip], w_proj,
+        )
+        rows_x.append(rows)
+        dmix.append(mix)
+    last = [lax.optimization_barrier((other_parts[c][3], low[-1][1]))[0] for c in clips]
+    last = [swap(x) for x in last]
     dq, dkv, dr, chunks, early = call_attention_backward(
         q, kv, memory, keys_extra, qa, dmix, at, lse, rel_rows,
-        w_fc2_grad.astype(BF16), w_fc1_grad.astype(BF16), early, consts,
+        w_fc2_grad, w_fc1_grad, sums, [p[4] for p in parts], consts,
+    )
+    *last, dq = lax.optimization_barrier((*last, dq))
+    output = drop_rows(
+        jnp.stack(
+            [
+                (middle[c] + own_parts[c][3] + last[c].astype(F32) + fc2_bias).astype(BF16)
+                for c in clips
+            ]
+        )
     )
     input_grad, w_fc2_grad, w_fc1_grad, w_proj_grad, tail, small, late = call_finish(
         dq, dkv, q0, kv0, kvf, jnp.concatenate([tap_q, tap_kv, tap_s]),
         first_rows.reshape(-1, width),
-        middle_rows.reshape(-1, width),
-        branch.reshape(-1, LW),
+        rows_x,
+        [b[0] for b in branch],
         w_heads,
         inputs_low,
-        middle_grad,
+        dmiddle,
         chunks,
         dr,
         ln1_gain.reshape(1, -1),
@@ -1258,7 +1449,7 @@
         w_fc2_grad = w_fc2_grad.reshape(2, total, width)[:, :width].reshape(2 * width, width)
         w_fc1_grad, w_proj_grad, tail = w_fc1_grad[:width], w_proj_grad[:, :width], tail[:, :width]
     w_qkv_grad = tail.astype(F32).transpose(1, 0, 2)
-    fc1_bias_grad = early[HEAD_EARLY : HEAD_EARLY + fc1_bias_grad.size // width].reshape(-1)
+    fc1_bias_grad = early[HEAD_EARLY : HEAD_EARLY + fc1_bias.size // width].reshape(-1)
     small = small[:, :HEAD_DIM]
     shared = [late[0], late[1]]
     shared += [small[REL_ROWS + 32 * n : REL_ROWS + 32 * n + 27] for n in range(5)]

time: 382 us -> 348 us (0.911)
  Pallas kernels: 195 us -> 260 us
  waiting for transfers between devices: 63.6 us -> 9.97 us
  matrix products: 34.7 us -> 0.91 us
  other arithmetic: 19.1 us -> 8.64 us
  local copies, waits for them, and re-layouts: 52.5 us -> 44.3 us
  starting transfers between devices: 9.38 us -> 17 us
    pallas_call x2 -> x16, Pallas kernels: 124 us -> 186 us  [the longest x1 97.2 us: call_finish(): pl.pallas_call(partial(finish_kernel, groups, width), in_specs=[hbm] * le...]
    ppermute x7 -> x12, waiting for transfers between devices: 63.6 us -> 9.96 us  [swap(): return lax.ppermute(x, 'head', [(0, 1), (1, 0)])]
    dot_general x8 -> x0, matrix products: 31.5 us -> none  [the longest x1 6.68 us: on_device(): jnp.einsum('ald,fd->alf', upstream_rows, w_fc2, preferred_element_type=F32)]
    ppermute x7 -> x12, starting transfers between devices: 7.58 us -> 15.3 us  [swap(): return lax.ppermute(x, 'head', [(0, 1), (1, 0)])]
    unnamed x124 -> x128, local copies, waits for them, and re-layouts: 20.8 us -> 19.5 us
  transfers between devices with their start and end apart: 8 -> 13, of which waited for: 5 -> 3; matrix products, arithmetic and copies ran while one was open for 13% -> 7% of each run, Pallas kernels for 2% -> 43%
where the time goes in v4:
time: 348 us; the launch traced here: 342 us
  Pallas kernels  260 us (75%)
  local copies, waits for them, and re-layouts  44.3 us (13%)
  starting transfers between devices  17 us (5%)
  waiting for transfers between devices  9.97 us (3%)
  other arithmetic  8.64 us (2%)
    pallas_call x1, Pallas kernels, call_finish(): pl.pallas_call(partial(finish_kernel, groups, width), in_specs=[hbm] * le...  97.2 us
    pallas_call x1, Pallas kernels, call_attention_backward(): pl.pallas_call(partial(attention_backward, groups), in_specs=[vmem] * 3 +...  52.1 us
    pallas_call x12, Pallas kernels, simple_call(): pl.pallas_call(kernel, in_specs=[vmem] * len(args), out_specs=[vmem] * le...  48.7 us
    pallas_call x2, Pallas kernels, call_attention_forward(): pl.pallas_call(attention_forward, grid=(1,), in_specs=[block(1, ROWS, LW)...  30.4 us
    pallas_call x2, Pallas kernels, call_pool_forward(): pl.pallas_call(partial(pool_forward, squeeze), grid=(count, clips), in_sp...  21 us
    unnamed x128, local copies, waits for them, and re-layouts  19.5 us
    ppermute x12, starting transfers between devices, swap(): return lax.ppermute(x, 'head', [(0, 1), (1, 0)])  15.3 us
    pallas_call x1, Pallas kernels, call_weights(): pl.pallas_call(partial(weight_kernel, count), grid=(hidden // LW,), in_sp...  10.1 us
  transfers between devices with their start and end apart: 13, of which 3 were waited for; matrix products, arithmetic and copies ran while one was open for 7% of the time, Pallas kernels for 43%

profile of v4, /device:TPU:0, one launch (start us, length us, event | category | flops | bytes accessed | tf_op | source)
XLA Modules:
  0.0 342.0 jit_solution(2291144887901792408)
XLA Ops:
  3.2 3.0 collective-permute-start
  27.0 14.4 %shard_map.491 = (bf16[2,2,448,384]{3,2,1,0:T(8,128)(2,1)}, bf16[2,2,448,384]{3,2,1,0:T(8,128)(2,1)}, bf16[2,2,448,384]{3,2,1,0:T(8,128)(2,1)}, bf16[2,2,224,384]{3,2,1,0:T(8,128)(2,1)}) custom-call(bf16[2,448,768]{2,1,0:T(8,128)(2,1)} %copy-done.6, bf16[3,768,384]{2,1,0:T(8,128)(2,1)} %bitcast.86, f32[2,27,8,384]{3,2,1,0:T(8,128)} %get-tuple-element.198.refs_2_, ...), custom_call_target="tpu_custom_call" | custom-call | flops 12000000000 | bytes 8000000 | tf_op jit(solution)/shard_map/pallas_call | solution.py:216
  45.2 6.6 %shard_map.490 = (bf16[2,1,448,384]{3,2,1,0:T(8,128)(2,1)}, bf16[2,1,448,384]{3,2,1,0:T(8,128)(2,1)}) custom-call(bf16[2,448,768]{2,1,0:T(8,128)(2,1)} %copy-done.6, bf16[3,768,384]{2,1,0:T(8,128)(2,1)} %bitcast.87, f32[1,27,8,384]{3,2,1,0:T(8,128)} %broadcast_in_dim_broadcast_in_dim.2.refs_2_), custom_call_target="tpu_custom_call" | custom-call | flops 6000000000 | bytes 4000000 | tf_op jit(solution)/shard_map/pallas_call | solution.py:216
  54.2 15.1 %shard_map.492 = (bf16[1,448,384]{2,1,0:T(8,128)(2,1)}, bf16[1,4,448,256]{3,2,1,0:T(8,128)(2,1)}, f32[1,384,448]{2,1,0:T(8,128)}, f32[1,8,448]{2,1,0:T(8,128)}) custom-call(bf16[2,1,448,384]{3,2,1,0:T(8,128)(2,1)} %get-tuple-element.93.q_ref, bf16[2,2,448,384]{3,2,1,0:T(8,128)(2,1)} %get-tuple-element.94.kv_ref, bf16[4,2,224,384]{3,2,1,0:T(8,128)(2,1)} %copy-done.25, ...), custom_call_target="tpu_custom_call" | custom-call | flops 12999999488 | bytes 5000000 | tf_op jit(solution)/shard_map/pallas_call | solution.py:294
  69.3 15.3 %shard_map.497 = (bf16[1,448,384]{2,1,0:T(8,128)(2,1)}, bf16[1,4,448,256]{3,2,1,0:T(8,128)(2,1)}, f32[1,384,448]{2,1,0:T(8,128)}, f32[1,8,448]{2,1,0:T(8,128)}) custom-call(bf16[2,1,448,384]{3,2,1,0:T(8,128)(2,1)} %get-tuple-element.93.q_ref, bf16[2,2,448,384]{3,2,1,0:T(8,128)(2,1)} %get-tuple-element.94.kv_ref, bf16[4,2,224,384]{3,2,1,0:T(8,128)(2,1)} %copy-done.25, ...), custom_call_target="tpu_custom_call" | custom-call | flops 12999999488 | bytes 5000000 | tf_op jit(solution)/shard_map/pallas_call | solution.py:294
  84.6 2.6 shard_map.493
  88.8 2.5 shard_map.498
  92.6 4.7 %collective-permute-done.2.recv = bf16[224,768]{1,0:T(8,128)(2,1)S(1)} collective-permute-done((bf16[224,768]{1,0:T(8,128)(2,1)}, bf16[224,768]{1,0:T(8,128)(2,1)S(1)}, u32[]{:S(2)}, u32[]{:S(2)}) %collective-permute-start.2) | collective-permute-done | bytes 344096 | tf_op jit(solution)/shard_map/ppermute | solution.py:1280
  98.0 2.5 shard_map.494
  102.4 2.3 collective-permute-done.5.recv
  105.4 2.4 shard_map.499
  109.8 6.7 %shard_map.500 = (bf16[224,1536]{1,0:T(8,128)(2,1)}, bf16[224,1536]{1,0:T(8,128)(2,1)}, f32[224,768]{1,0:T(8,128)}, f32[224,768]{1,0:T(8,128)}, f32[1,1536]{1,0:T(1,128)}) custom-call(bf16[224,768]{1,0:T(8,128)(2,1)} %get-tuple-element.107.a2.refs_9_, bf16[224,768]{1,0:T(8,128)(2,1)} %bitcast.83, bf16[768,1536]{1,0:T(8,128)(2,1)} %w1.7, ...), custom_call_target="tpu_custom_call" | custom-call | flops 5000000000 | bytes 2000000 | tf_op jit(solution)/shard_map/pallas_call | solution.py:340
  116.5 2.9 collective-permute-done.6.a2.refs_11_
  120.2 6.5 %shard_map.501 = (bf16[224,1536]{1,0:T(8,128)(2,1)}, bf16[224,1536]{1,0:T(8,128)(2,1)}, bf16[224,768]{1,0:T(8,128)(2,1)}, bf16[224,768]{1,0:T(8,128)(2,1)}, f32[1,1536]{1,0:T(1,128)}) custom-call(bf16[224,768]{1,0:T(8,128)(2,1)} %copy-done.48, bf16[224,768]{1,0:T(8,128)(2,1)} %get-tuple-element.173.g.refs_15_, bf16[768,1536]{1,0:T(8,128)(2,1)} %w1.7, ...), custom_call_target="tpu_custom_call" | custom-call | flops 5000000000 | bytes 2000000 | tf_op jit(solution)/shard_map/pallas_call | solution.py:340
  129.3 6.5 %shard_map.496 = (bf16[224,1536]{1,0:T(8,128)(2,1)}, bf16[224,1536]{1,0:T(8,128)(2,1)}, bf16[224,768]{1,0:T(8,128)(2,1)}, bf16[224,768]{1,0:T(8,128)(2,1)}, f32[1,1536]{1,0:T(1,128)}) custom-call(bf16[224,768]{1,0:T(8,128)(2,1)} %copy-done.47, bf16[224,768]{1,0:T(8,128)(2,1)} %get-tuple-element.174.g.refs_14_, bf16[768,1536]{1,0:T(8,128)(2,1)} %w1.7, ...), custom_call_target="tpu_custom_call" | custom-call | flops 5000000000 | bytes 2000000 | tf_op jit(solution)/shard_map/pallas_call | solution.py:340
  135.9 7.1 %shard_map.495 = (bf16[224,1536]{1,0:T(8,128)(2,1)}, bf16[224,1536]{1,0:T(8,128)(2,1)}, f32[224,768]{1,0:T(8,128)}, f32[224,768]{1,0:T(8,128)}, f32[1,1536]{1,0:T(1,128)}) custom-call(bf16[224,768]{1,0:T(8,128)(2,1)} %get-tuple-element.100.a2.refs_8_, bf16[224,768]{1,0:T(8,128)(2,1)} %bitcast.80, bf16[768,1536]{1,0:T(8,128)(2,1)} %w1.7, ...), custom_call_target="tpu_custom_call" | custom-call | flops 5000000000 | bytes 2000000 | tf_op jit(solution)/shard_map/pallas_call | solution.py:340
  143.8 3.1 shard_map.502
  149.6 3.1 shard_map.503
  152.8 10.1 %shard_map.506 = (bf16[1536,768]{1,0:T(8,128)(2,1)}, bf16[768,1536]{1,0:T(8,128)(2,1)}) custom-call(bf16[224,1536]{1,0:T(8,128)(2,1)} %get-tuple-element.126.refs_0_, bf16[224,1536]{1,0:T(8,128)(2,1)} %get-tuple-element.127.refs_1_, bf16[224,1536]{1,0:T(8,128)(2,1)} %get-tuple-element.128.refs_2_, bf16[224,1536]{1,0:T(8,128)(2,1)} %get-tuple-element.129.refs_3_, ...), custom_call_target="tpu_custom_call" | custom-call | flops 8000000000 | bytes 15000000 | tf_op jit(solution)/shard_map/pallas_call | solution.py:428
  165.1 2.8 shard_map.505
  168.6 2.7 shard_map.504
  171.4 52.1 %shard_map.507 = (f32[2,448,384]{2,1,0:T(8,128)}, f32[2,2,896,384]{3,2,1,0:T(8,128)}, f32[256,384]{1,0:T(8,128)}, bf16[8,48,384]{2,1,0:T(8,128)(2,1)}, f32[16,768]{1,0:T(8,128)}) custom-call(bf16[2,1,448,384]{3,2,1,0:T(8,128)(2,1)} %get-tuple-element.93.q_ref, bf16[2,2,448,384]{3,2,1,0:T(8,128)(2,1)} %get-tuple-element.94.kv_ref, ...), custom_call_target="tpu_custom_call" | custom-call | flops 40000000000 | bytes 20000000 | tf_op jit(solution)/shard_map/pallas_call | solution.py:804
  226.4 97.2 %shard_map.508 = (f32[2,224,768]{2,1,0:T(8,128)}, f32[1536,768]{1,0:T(8,128)}, f32[768,1536]{1,0:T(8,128)}, f32[384,768]{1,0:T(8,128)}, bf16[3,768,384]{2,1,0:T(...) custom-call(f32[2,448,384]{2,1,0:T(8,128)} %get-tuple-element.146.dq_hbm, ...), custom_call_target="tpu_custom_call" | custom-call | flops 60000002048 | bytes 40000000 | tf_op jit(solution)/shard_map/pallas_call | solution.py:1200
  336.0 2.4 copy.74
  (218 shorter events, 65.5 us)
Async XLA Ops:
  0.7 10.0 %copy-start = (f32[13,96]{1,0:T(8,128)S(1)}, f32[13,96]{1,0:T(8,128)}, u32[]{:S(2)}) copy-start(f32[13,96]{1,0:T(8,128)} %param.46) | copy-start | bytes 14980
  3.2 21.6 %collective-permute-start = (bf16[2,224,768]{2,1,0:T(8,128)(2,1)S(1)}, bf16[2,224,768]{2,1,0:T(8,128)(2,1)}, u32[]{:S(2)}, u32[]{:S(2)}) collective-permute-start(bf16[2,224,768]{2,1,0:T(8,128)(2,1)S(1)} %select_convert_fusion), channel_id=1, source_target_pairs={{0,1},{1,0},{2,3},{3,2},{4,5},{5,4},{6,7},{7,6},{8,9},{9,8},{10,11... | collective-permute-start | bytes 2064392 | tf_op jit(solution)/shard_map/ppermute | solution.py:1280
  13.5 6.1 %copy-start.23 = (f32[27,384]{1,0:T(8,128)S(1)}, f32[27,384]{1,0:T(8,128)}, u32[]{:S(2)}) copy-start(f32[27,384]{1,0:T(8,128)} %tile.43) | copy-start | bytes 124420
  27.0 17.1 %copy-start.12 = (bf16[2,4,7,8,768]{4,3,2,1,0:T(8,128)(2,1)S(1)}, bf16[2,4,7,8,768]{4,3,2,1,0:T(8,128)(2,1)}, u32[]{:S(2)}) copy-start(bf16[2,4,7,8,768]{4,3,2,1,0:T(8,128)(2,1)} %pad.45) | copy-start | bytes 2064388
  41.4 10.3 %collective-permute-start.1 = (bf16[2,2,224,384]{3,2,1,0:T(8,128)(2,1)}, bf16[2,2,224,384]{3,2,1,0:T(8,128)(2,1)S(1)}, u32[]{:S(2)}, u32[]{:S(2)}) collective-permute-start(bf16[2,2,224,384]{3,2,1,0:T(8,128)(2,1)} %get-tuple-element.95), channel_id=1, source_target_pairs={{0,2},{2,4},{4,6},{6,8},{8,10},{10,12},{12,14},{14,16},{16,18},{18... | collective-permute-start | bytes 2064392 | tf_op jit(solution)/shard_map/ppermute | solution.py:1254
  44.1 47.6 %collective-permute-start.4 = (bf16[2,224,768]{2,1,0:T(8,128)(2,1)S(1)}, bf16[2,224,768]{2,1,0:T(8,128)(2,1)S(1)}, u32[]{:S(2)}, u32[]{:S(2)}) collective-permute-start(bf16[2,224,768]{2,1,0:T(8,128)(2,1)S(1)} %bitcast.74), channel_id=1, source_target_pairs={{0,1},{1,0},{2,3},{3,2},{4,5},{5,4},{6,7},{7,6},{8,9},{9,8},{10,11... | collective-permute-start | bytes 2064392 | tf_op jit(solution)/shard_map/ppermute | solution.py:1280
  87.1 10.2 %collective-permute-start.2 = (bf16[224,768]{1,0:T(8,128)(2,1)}, bf16[224,768]{1,0:T(8,128)(2,1)S(1)}, u32[]{:S(2)}, u32[]{:S(2)}) collective-permute-start(bf16[224,768]{1,0:T(8,128)(2,1)} %get-tuple-element.98), channel_id=1, source_target_pairs={{0,1},{1,0},{2,3},{3,2},{4,5},{5,4},{6,7},{7,6},{8,9},{9,8},{10,11... | collective-permute-start | bytes 1032200 | tf_op jit(solution)/shard_map/ppermute | solution.py:1280
  91.4 13.3 %collective-permute-start.5 = (bf16[224,768]{1,0:T(8,128)(2,1)}, bf16[224,768]{1,0:T(8,128)(2,1)S(1)}, u32[]{:S(2)}, u32[]{:S(2)}) collective-permute-start(bf16[224,768]{1,0:T(8,128)(2,1)} %get-tuple-element.106), channel_id=1, source_target_pairs={{0,1},{1,0},{2,3},{3,2},{4,5},{5,4},{6,7},{7,6},{8,9},{9,8},{10,11... | collective-permute-start | bytes 1032200 | tf_op jit(solution)/shard_map/ppermute | solution.py:1280
  100.5 28.1 %collective-permute-start.3 = (bf16[224,768]{1,0:T(8,128)(2,1)}, bf16[224,768]{1,0:T(8,128)(2,1)S(1)}, u32[]{:S(2)}, u32[]{:S(2)}) collective-permute-start(bf16[224,768]{1,0:T(8,128)(2,1)} %get-tuple-element.100.a2.refs_8_), channel_id=1, source_target_pairs={{0,1},{1,0},{2,3},{3,2},{4,5},{5,4},{6,7},{7,6},{8,9},{9,8},{10,11... | collective-permute-start | bytes 1032200 | tf_op jit(solution)/shard_map/ppermute | solution.py:1280
  107.8 11.6 %collective-permute-start.6 = (bf16[224,768]{1,0:T(8,128)(2,1)}, bf16[224,768]{1,0:T(8,128)(2,1)S(1)}, u32[]{:S(2)}, u32[]{:S(2)}) collective-permute-start(bf16[224,768]{1,0:T(8,128)(2,1)} %get-tuple-element.107.a2.refs_9_), channel_id=1, source_target_pairs={{0,1},{1,0},{2,3},{3,2},{4,5},{5,4},{6,7},{7,6},{8,9},{9,8},{10,11... | collective-permute-start | bytes 1032200 | tf_op jit(solution)/shard_map/ppermute | solution.py:1280
  126.7 16.4 %collective-permute-start.7 = (bf16[224,768]{1,0:T(8,128)(2,1)}, bf16[224,768]{1,0:T(8,128)(2,1)S(1)}, u32[]{:S(2)}, u32[]{:S(2)}) collective-permute-start(bf16[224,768]{1,0:T(8,128)(2,1)} %get-tuple-element.109), channel_id=1, source_target_pairs={{0,1},{1,0},{2,3},{3,2},{4,5},{5,4},{6,7},{7,6},{8,9},{9,8},{10,11... | collective-permute-start | bytes 1032200 | tf_op jit(solution)/shard_map/ppermute | solution.py:1280
  135.8 13.0 %collective-permute-start.11 = (bf16[224,768]{1,0:T(8,128)(2,1)}, bf16[224,768]{1,0:T(8,128)(2,1)S(1)}, u32[]{:S(2)}, u32[]{:S(2)}) collective-permute-start(bf16[224,768]{1,0:T(8,128)(2,1)} %get-tuple-element.118), channel_id=1, source_target_pairs={{0,1},{1,0},{2,3},{3,2},{4,5},{5,4},{6,7},{7,6},{8,9},{9,8},{10,11... | collective-permute-start | bytes 1032200 | tf_op jit(solution)/shard_map/ppermute | solution.py:1280
  146.9 16.0 %collective-permute-start.8 = (bf16[224,768]{1,0:T(8,128)(2,1)}, bf16[224,768]{1,0:T(8,128)(2,1)S(1)}, u32[]{:S(2)}, u32[]{:S(2)}) collective-permute-start(bf16[224,768]{1,0:T(8,128)(2,1)} %get-tuple-element.111.mine), channel_id=1, source_target_pairs={{0,1},{1,0},{2,3},{3,2},{4,5},{5,4},{6,7},{7,6},{8,9},{9,8},{10,11... | collective-permute-start | bytes 1032200 | tf_op jit(solution)/shard_map/ppermute | solution.py:1280
  152.7 15.2 %collective-permute-start.12 = (bf16[224,768]{1,0:T(8,128)(2,1)}, bf16[224,768]{1,0:T(8,128)(2,1)S(1)}, u32[]{:S(2)}, u32[]{:S(2)}) collective-permute-start(bf16[224,768]{1,0:T(8,128)(2,1)} %get-tuple-element.119.mine), channel_id=1, source_target_pairs={{0,1},{1,0},{2,3},{3,2},{4,5},{5,4},{6,7},{7,6},{8,9},{9,8},{10,11... | collective-permute-start | bytes 1032200 | tf_op jit(solution)/shard_map/ppermute | solution.py:1280
  152.8 10.2 %copy-start.46 = (bf16[224,768]{1,0:T(8,128)(2,1)S(1)}, bf16[224,768]{1,0:T(8,128)(2,1)}, u32[]{:S(2)}) copy-start(bf16[224,768]{1,0:T(8,128)(2,1)} %get-tuple-element.112) | copy-start | bytes 1032196
  152.8 12.2 %copy-start.45 = (bf16[224,768]{1,0:T(8,128)(2,1)S(1)}, bf16[224,768]{1,0:T(8,128)(2,1)}, u32[]{:S(2)}) copy-start(bf16[224,768]{1,0:T(8,128)(2,1)} %get-tuple-element.114) | copy-start | bytes 1032196
  163.0 63.4 %collective-permute-start.9 = (bf16[224,768]{1,0:T(8,128)(2,1)S(1)}, bf16[224,768]{1,0:T(8,128)(2,1)S(1)}, u32[]{:S(2)}, u32[]{:S(2)}) collective-permute-start(bf16[224,768]{1,0:T(8,128)(2,1)S(1)} %copy-done.46), channel_id=1, source_target_pairs={{0,1},{1,0},{2,3},{3,2},{4,5},{5,4},{6,7},{7,6},{8,9},{9,8},{10,11... | collective-permute-start | bytes 1032200 | tf_op jit(solution)/shard_map/ppermute | solution.py:1280
  165.0 61.4 %collective-permute-start.10 = (bf16[224,768]{1,0:T(8,128)(2,1)S(1)}, bf16[224,768]{1,0:T(8,128)(2,1)S(1)}, u32[]{:S(2)}, u32[]{:S(2)}) collective-permute-start(bf16[224,768]{1,0:T(8,128)(2,1)S(1)} %copy-done.45), channel_id=1, source_target_pairs={{0,1},{1,0},{2,3},{3,2},{4,5},{5,4},{6,7},{7,6},{8,9},{9,8},{10,11... | collective-permute-start | bytes 1032200 | tf_op jit(solution)/shard_map/ppermute | solution.py:1280
  226.4 101.4 %copy-start.8 = (f32[224,768]{1,0:T(8,128)S(1)}, f32[224,768]{1,0:T(8,128)}, u32[]{:S(2)}) copy-start(f32[224,768]{1,0:T(8,128)} %get-tuple-element.99.x1_ref) | copy-start | bytes 2064388
  226.4 101.4 %copy-start.9 = (f32[224,768]{1,0:T(8,128)S(1)}, f32[224,768]{1,0:T(8,128)}, u32[]{:S(2)}) copy-start(f32[224,768]{1,0:T(8,128)} %get-tuple-element.110.x1_ref) | copy-start | bytes 2064388
  226.4 101.4 %copy-start.10 = (f32[224,768]{1,0:T(8,128)S(1)}, f32[224,768]{1,0:T(8,128)}, u32[]{:S(2)}) copy-start(f32[224,768]{1,0:T(8,128)} %get-tuple-element.144) | copy-start | bytes 2064388
  226.4 101.4 %copy-start.11 = (f32[224,768]{1,0:T(8,128)S(1)}, f32[224,768]{1,0:T(8,128)}, u32[]{:S(2)}) copy-start(f32[224,768]{1,0:T(8,128)} %get-tuple-element.101) | copy-start | bytes 2064388
  226.4 101.4 %copy-start.39 = (f32[768]{0:T(1024)S(1)}, f32[768]{0:T(1024)}, u32[]{:S(2)}) copy-start(f32[768]{0:T(1024)} %param.54) | copy-start | bytes 9220
  329.6 6.4 %slice-start.2 = ((s8[4718592]{0:T(1024)(128)(4,1)}), s8[4194304]{0:T(1024)(128)(4,1)S(1)}, s32[]{:S(2)}) async-start(s8[4718592]{0:T(1024)(128)(4,1)} %bitcast.66), calls=%async_computation.2 | async-start | bytes 8388608
  (49 other events, 126.5 us)

commit v5 on v4

--- a/solution.py
+++ b/solution.py
@@ -469,9 +469,7 @@
         dmix_ref[half_rows(side)] = nt(part[...], w[...]).astype(BF16)
 
 
-EARLY = 16
 HEAD_EARLY = 8
-LATE = 8
 MESH = pl.DeviceIdType.MESH
 
 
@@ -504,10 +502,16 @@
         self.peers = [
             (lax.rem(self.group + o, groups) * 4 + lax.rem(dp, 4), head) for o in range(1, groups)
         ]
+        self.number = (head * groups + self.group) * 2 + self.xbit
+
+    def device(self, number):
+        side = lax.div(number, 2 * self.groups)
+        group = lax.rem(lax.div(number, 2), self.groups)
+        return (group * 4 + lax.rem(number, 2) * 2 + self.core, side)
 
     def greet(self, more=()):
         barrier = pltpu.get_barrier_semaphore()
-        signalled = [self.to_core, self.to_x, self.to_y] + self.peers + list(more)
+        signalled = [self.to_core, self.to_x] + self.peers + list(more)
         for peer in signalled:
             pl.semaphore_signal(barrier, inc=1, device_id=peer, device_id_type=MESH)
         pl.semaphore_wait(barrier, len(signalled))
@@ -599,65 +603,65 @@
     ]
 
 
-class Small:
-    def __init__(self, place, buffer, slots, rows_y, send, recv, base):
-        self.at, self.buffer, self.slots, self.rows_y = place, buffer, slots, rows_y
-        self.send, self.recv, self.base = send, recv, base
+class Tiny:
+    def __init__(self, place, source, result, refs, send, recv):
+        self.at, self.source, self.result = place, source, result
+        self.recv_core, self.summed, self.slots = refs
+        self.send, self.recv = send, recv
+        count = 4 * place.groups
+        self.half, self.chunk = source.shape[0] // 2, source.shape[0] // 2 // count
+        self.mine = place.number
+        self.others = [lax.rem(place.number + o, count) for o in range(1, count)]
         self.flights = {}
 
-    def start(self, number, src, dst, peer):
-        self.flights[number] = remote(
-            src, dst, self.send.at[self.base + number], self.recv.at[self.base + number], peer
-        )
-
-    def one(self):
-        self.start(0, self.buffer.at[0, 0 : self.rows_y], self.slots[0], self.at.to_y)
-
-    def two(self):
-        self.flights[0].wait()
-        if self.rows_y < self.buffer.shape[1]:
-            self.buffer[1, self.rows_y :] = self.buffer[0, self.rows_y :]
-        self.buffer[1, 0 : self.rows_y] = self.buffer[0, 0 : self.rows_y] + self.slots[0][...]
-        self.start(1, self.buffer.at[1], self.slots[1], self.at.to_core)
-
-    def three(self):
-        self.flights[1].wait()
-        self.buffer[2] = self.buffer[1] + self.slots[1][...]
-        self.start(2, self.buffer.at[2], self.slots[2], self.at.to_x)
-
-    def four(self):
-        self.flights[2].wait()
-        self.buffer[3] = self.buffer[2] + self.slots[2][...]
-        for o in range(1, self.at.groups):
-            self.start(2 + o, self.buffer.at[3], self.slots[3].at[o - 1], self.at.peers[o - 1])
-
-    def five(self, target):
-        added = self.buffer[3]
-        for o in range(1, self.at.groups):
-            self.flights[2 + o].wait()
-            added = added + self.slots[3][o - 1]
-        target[...] = added
-
-
-def small_scratch(rows, rows_y, groups, width):
-    return [
-        pltpu.VMEM((4, rows, width), F32),
-        pltpu.VMEM((rows_y, width), F32),
-        pltpu.VMEM((rows, width), F32),
-        pltpu.VMEM((rows, width), F32),
-        pltpu.VMEM((groups - 1, rows, width), F32),
-    ]
+    def rows(self, number):
+        return pl.ds(pl.multiple_of(number * self.chunk, 8), self.chunk)
+
+    def halves(self, core):
+        return pl.ds(pl.multiple_of(core * self.half, 8), self.half)
+
+    def start(self, key, src, dst, peer):
+        number = len(self.flights)
+        self.flights[key] = remote(src, dst, self.send.at[number], self.recv.at[number], peer)
+
+    def a(self):
+        self.start("a", self.source.at[self.halves(1 - self.at.core)], self.recv_core, self.at.to_core)
+
+    def b(self):
+        self.flights["a"].wait()
+        self.summed[...] = self.source[self.halves(self.at.core)] + self.recv_core[...]
+        for o, number in enumerate(self.others):
+            self.start(("b", o), self.summed.at[self.rows(number)], self.slots.at[o], self.at.device(number))
+
+    def c(self):
+        total = self.summed[self.rows(self.mine)]
+        for o, number in enumerate(self.others):
+            self.flights["b", o].wait()
+            total = total + self.slots[o]
+        rows = pl.ds(pl.multiple_of(self.at.core * self.half + self.mine * self.chunk, 8), self.chunk)
+        self.result[rows] = total
+        for o, number in enumerate(self.others):
+            self.start(("c", o), self.result.at[rows], self.result.at[rows], self.at.device(number))
+
+    def d(self):
+        for o in range(len(self.others)):
+            self.flights["c", o].wait()
+        rows = self.halves(self.at.core)
+        self.start("d", self.result.at[rows], self.result.at[rows], self.at.to_core)
+
+    def e(self):
+        self.flights["d"].wait()
 
 
 def attention_backward(
     groups,
     q_ref, kv_ref, mem_ref, ke_hbm, qa_hbm0, qa_hbm1, dm_ref0, dm_ref1, at_hbm0, at_hbm1, lse_ref0, lse_ref1,
     rt_ref, grow_ref, ownt_ref, ekey_ref,
-    lanes_ref, g2_ref, g1_ref, sums0, sums1, hidden0, hidden1, hidden2, hidden3,
-    dq_ref, dkv_ref, dr_ref, chunks_ref, early_out,
+    lanes_ref, g2_ref, g1_ref,
+    dq_ref, dkv_ref, dr_ref, chunks_ref, out2,
     ke_ref, qa_ref, at_ref, keys, values, kt, dmt, qms, dms, dqt,
-    recv_a, send_b, recv_b, send_c, recv_c, s0, s1, s2, s3, s4,
-    loads, sems_send, sems_recv, small_send, small_recv,
+    recv_a, send_b, recv_b, send_c, recv_c,
+    loads, sems_send, sems_recv,
 ):
     place = Place(groups)
     clips = q_ref.shape[0]
@@ -673,43 +677,41 @@
     place.greet()
     total = g1_ref.shape[0]
 
-    def view(number):
+    def view(number, ref):
         if number < 4:
             base, col = (number // 2) * total, (number % 2) * LW
-            return lambda first, n: g2_ref.at[pl.ds(base + first, n), col : col + LW]
+            return lambda first, n: ref.at[pl.ds(base + first, n), col : col + LW]
         col = (number - 4) * LW
         return lambda first, n: g1_ref.at[pl.ds(first, n), col : col + LW]
 
     pieces = [
         Piece(
-            place, total, view(number), None,
+            place, total, view(number, g2_ref), view(number, out2) if number < 4 else None,
             [ref.at[number] for ref in (recv_a, send_b, recv_b, send_c, recv_c)],
             sems_send.at[number], sems_recv.at[number],
         )
         for number in range(8)
     ]
-    small = Small(place, s0, (s1, s2, s3, s4), HEAD_EARLY, small_send, small_recv, 0)
-    s0[0, 0:HEAD_EARLY] = sums0[...] + sums1[...]
-    hidden = hidden0[...] + hidden1[...] + hidden2[...] + hidden3[...]
-    width = s0.shape[2]
-    s0[0, HEAD_EARLY:EARLY] = jnp.zeros((EARLY - HEAD_EARLY, width), F32)
-    for n in range(hidden.shape[1] // width):
-        s0[0, HEAD_EARLY + n : HEAD_EARLY + n + 1] = hidden[:, n * width : (n + 1) * width]
-    small.one()
-    for piece in pieces:
-        piece.a()
     moves = [
-        [pieces[0].b, pieces[1].b],
-        [pieces[2].b, small.two],
-        [pieces[3].b, pieces[0].c],
-        [pieces[4].b, pieces[1].c, small.three],
-        [pieces[5].b, pieces[2].c],
-        [pieces[6].b, pieces[3].c],
-        [pieces[7].b, pieces[4].c],
-        [pieces[5].c, small.four],
-        [pieces[6].c],
-        [pieces[7].c],
-        [partial(small.five, early_out)],
+        [pieces[0].a],
+        [pieces[0].b, pieces[1].a],
+        [pieces[2].a],
+        [pieces[1].b, pieces[3].a],
+        [pieces[4].a],
+        [pieces[0].c, pieces[2].b, pieces[5].a],
+        [pieces[6].a],
+        [pieces[1].c, pieces[3].b, pieces[7].a],
+        [],
+        [pieces[0].d, pieces[4].b],
+        [],
+        [pieces[1].d, pieces[5].b],
+        [],
+        [pieces[0].e, pieces[2].c],
+        [],
+        [pieces[1].e, pieces[3].c],
+        [],
+        [pieces[0].f, pieces[2].d, pieces[6].b],
+        [pieces[1].f, pieces[3].d, pieces[7].b, pieces[2].e, pieces[4].c, pieces[5].c, pieces[3].e, pieces[2].f, pieces[6].c, pieces[3].f, pieces[7].c],
     ]
 
     def pump():
@@ -719,6 +721,7 @@
 
     dr_ref[...] = jnp.zeros_like(dr_ref)
     for clip in range(clips):
+        pump()
         near, far = mem_ref.at[clip + 1], mem_ref.at[clip]
         keys[0:ROWS] = kv_ref[clip, 0]
         keys[ROWS : ROWS + MROWS] = near[0]
@@ -742,7 +745,7 @@
             deltas.append(jnp.sum(dmt[span] * at_ref[clip, span], axis=0, keepdims=True))
 
         def step(number, _):
-            rows = pl.ds(pl.multiple_of(number * BLOCK, BLOCK), BLOCK)
+            rows = slice(number * BLOCK, number * BLOCK + BLOCK)
             dk_parts, dv_parts = [], []
             for head in range(LH):
                 first = window_of(head)
@@ -770,9 +773,10 @@
                 )
             return 0
 
-        for begin, end in ((0, 2), (2, 4), (4, 6), (6, 7)):
+        for number in range(NBLOCK):
             pump()
-            lax.fori_loop(begin, end, step, 0)
+            step(number, 0)
+        pump()
         for head in range(LH):
             first = window_of(head)
             span = slice(head * HEAD_DIM, (head + 1) * HEAD_DIM)
@@ -784,16 +788,17 @@
         dq_ref[clip] = dmt[...].T
     while moves:
         pump()
-    for number in range(8):
-        chunks_ref[number] = pieces[number].total().astype(BF16)
+    for number in range(4):
+        pieces[number].g()
+        chunks_ref[number] = pieces[4 + number].total().astype(BF16)
 
 
 def padded_rows(width, groups):
     return -(-width // (4 * groups) // 16) * 16 * 4 * groups
 
 
-def call_attention_backward(q, kv, memory, keys_extra, qa, dmix, at, lse, rt, g2, g1, sums, hidden, consts):
-    clips, width = q.shape[0], sums[0].shape[1]
+def call_attention_backward(q, kv, memory, keys_extra, qa, dmix, at, lse, rt, g2, g1, consts):
+    clips, width = q.shape[0], g2.shape[1]
     groups = lax.axis_size("dp") // 4
     total = padded_rows(width, groups)
     if total != width:
@@ -803,14 +808,14 @@
     hbm = pl.BlockSpec(memory_space=pl.ANY)
     return pl.pallas_call(
         partial(attention_backward, groups),
-        in_specs=[vmem] * 3 + [hbm] * 3 + [vmem] * 2 + [hbm] * 2 + [vmem] * 15,
+        in_specs=[vmem] * 3 + [hbm] * 3 + [vmem] * 2 + [hbm] * 2 + [vmem] * 9,
         out_specs=[vmem] * 5,
         out_shape=[
             jax.ShapeDtypeStruct((clips, ROWS, LW), F32),
             jax.ShapeDtypeStruct((clips, 2, KEYS, LW), F32),
             jax.ShapeDtypeStruct((256, LW), F32),
-            jax.ShapeDtypeStruct((8, total // 4 // groups, LW), BF16),
-            jax.ShapeDtypeStruct((EARLY, width), F32),
+            jax.ShapeDtypeStruct((4, total // 4 // groups, LW), BF16),
+            jax.ShapeDtypeStruct(g2.shape, BF16),
         ],
         scratch_shapes=[
             pltpu.VMEM(keys_extra.shape, BF16),
@@ -824,12 +829,9 @@
             pltpu.VMEM((LH, ROWS, WIN), BF16),
             pltpu.VMEM((LH, HEAD_DIM + 32, ROWS), F32),
             *piece_scratch(total, groups, LW, BF16, 8),
-            *small_scratch(EARLY, HEAD_EARLY, groups, width),
             pltpu.SemaphoreType.DMA((3 * clips,)),
-            pltpu.SemaphoreType.DMA((8, groups + 1)),
-            pltpu.SemaphoreType.DMA((8, groups + 1)),
-            pltpu.SemaphoreType.DMA((groups + 2,)),
-            pltpu.SemaphoreType.DMA((groups + 2,)),
+            pltpu.SemaphoreType.DMA((8, 2 * groups + 2)),
+            pltpu.SemaphoreType.DMA((8, 2 * groups + 2)),
         ],
         compiler_params=params(collective_id=0, has_side_effects=True),
         cost_estimate=pl.CostEstimate(
@@ -837,24 +839,30 @@
         ),
     )(
         q, kv, memory, keys_extra, *qa, *dmix, *at, *lse, rt,
-        consts["grow"], consts["ownt"], consts["ekey"], consts["lanes"], g2, g1, *sums, *hidden,
+        consts["grow"], consts["ownt"], consts["ekey"], consts["lanes"], g2, g1,
     )
 
 
-SMALL_ROWS = 256
 REL_ROWS = 48
+TAP_ROW = NREL
+NORM_ROW = TAP_ROW + 5 * 27
+EARLY_ROW = NORM_ROW + 12
+HIDDEN_ROW = EARLY_ROW + 24
+SMALL_ROWS = HIDDEN_ROW + 24
 
 
 def finish_kernel(
     groups, width,
     dq_hbm, dkv_hbm, x0q_hbm, x0kv_hbm, kvf_hbm, taps_hbm, rows_a_hbm, rows_x0, rows_x1, branch0, branch1,
     w_hbm, tokens_hbm, middle0, middle1, chunks_ref, dr_ref, gain, foldl_ref, pick_ref,
-    grad, out2, out1, outp, outq, small_out, late_out,
+    sums0, sums1, hidden0, hidden1, hidden2, hidden3,
+    grad, out1, outp, outq, small_out,
     dq, dkv, x0q, x0kv, kvf, taps_ref, rows_a, rows_x, branch, w_ref, tokens, middle,
-    us, ms, kacc, dx, dmem_send, dmem_recv, res2, res1, resp, grads, stage, stage_t,
-    recv_a, send_b, recv_b, send_c, recv_c, sm_raw, sm, sm_y, sm_res, fa, fb, fc, fd, fe,
-    send_y, recv_y, l0, l1, l2, l3, l4,
-    loads, stores, sems_send, sems_recv, small_send, small_recv, mem_sems,
+    us, ms, kacc, dx, dmem_send, dmem_recv, res1, resp, grads, stage, stage_t,
+    recv_a, send_b, recv_b, send_c, recv_c,
+    strips, strip_res, strip_a, strip_b, strip_bb, strip_c, strip_cc,
+    sm, sm_res, sm_core, sm_sum, sm_slots, send_y, recv_y,
+    loads, stores, sems_send, sems_recv, tiny_send, tiny_recv, cross_send, cross_recv, mem_sems,
 ):
     place = Place(groups)
     clips = dq.shape[0]
@@ -875,18 +883,18 @@
     count = groups * 4
     behind = (lax.rem(place.dp + count - 1, count), place.head)
     ahead = (lax.rem(place.dp + 1, count), place.head)
-    place.greet((behind, ahead))
-
-    def view2(number):
-        if number < 4:
-            base, col = (number // 2) * total, (number % 2) * LW
-            return lambda first, n: res2.at[pl.ds(base + first, n), col : col + LW]
-        col = (number - 4) * LW
-        return lambda first, n: res1.at[pl.ds(first, n), col : col + LW]
+    others = [place.device(lax.rem(place.number + o, count)) for o in range(1, count)]
+    barrier = pltpu.get_barrier_semaphore()
+    for peer in [place.to_core, behind, ahead] + others:
+        pl.semaphore_signal(barrier, inc=1, device_id=peer, device_id_type=MESH)
+    pl.semaphore_wait(barrier, 3 + len(others))
+
+    def strip_of(number):
+        return lambda first, n: res1.at[pl.ds(first, n), number * LW : number * LW + LW]
 
     ffn = [
-        Piece(place, total, None, view2(number), None, sems_send.at[number], sems_recv.at[number])
-        for number in range(8)
+        Piece(place, total, None, strip_of(number), None, sems_send.at[number], sems_recv.at[number])
+        for number in range(4)
     ]
 
     def rows_of(ref):
@@ -896,15 +904,18 @@
         Piece(
             place, total, rows_of(grads.at[number]), rows_of(resp.at[number]),
             [ref.at[number] for ref in (recv_a, send_b, recv_b, send_c, recv_c)],
-            sems_send.at[8 + number], sems_recv.at[8 + number],
+            sems_send.at[4 + number], sems_recv.at[4 + number],
         )
-        for number in range(4)
+        for number in range(2)
+    ] + [
+        Piece(
+            place, total, rows_of(strips.at[number]), rows_of(strip_res.at[number]),
+            [ref.at[number] for ref in (strip_a, strip_b, strip_bb, strip_c, strip_cc)],
+            sems_send.at[6 + number], sems_recv.at[6 + number],
+        )
+        for number in range(6)
     ]
-    tiny = Piece(
-        place, sm.shape[0], rows_of(sm), rows_of(sm_res),
-        [ref.at[0] for ref in (fa, fb, fc, fd, fe)], sems_send.at[12], sems_recv.at[12],
-    )
-    ends = Small(place, l0, (l1, l2, l3, l4), LATE, small_send, small_recv, 0)
+    tiny = Tiny(place, sm, sm_res, (sm_core, sm_sum, sm_slots), tiny_send, tiny_recv)
 
     stored = []
 
@@ -915,24 +926,20 @@
         stage[slot] = source[...].astype(F32)
         stored.append(local(stage.at[slot], target, stores.at[slot]))
 
-    def store2(number):
+    def store1(number):
         ffn[number].g()
-        if number < 4:
-            base, col = (number // 2) * total, (number % 2) * LW
-            target = out2.at[base : base + total, col : col + LW]
+        flush(strip_of(number)(0, total), out1.at[:, number * LW : number * LW + LW])
+
+    def product(number):
+        if number < 2:
+            left, right, target = (rows_x, branch, grads.at[0]) if number == 0 else (rows_a, dx.at[0], grads.at[1])
+            lanes = slice(0, LW)
         else:
-            col = (number - 4) * LW
-            target = out1.at[:, col : col + LW]
-        flush(view2(number)(0, total), target)
-
-    def product(number):
-        left, right = (
-            (rows_x, branch), (rows_a, dx.at[0]), (rows_a, dx.at[1]), (rows_a, dx.at[2])
-        )[number]
+            left, right, target = rows_a, dx.at[1 + (number - 2) // 3], strips.at[number - 2]
+            lanes = slice((number - 2) % 3 * 128, (number - 2) % 3 * 128 + 128)
         for first in range(0, total, total // 2):
-            grads[number, first : first + total // 2] = lax.dot_general(
-                left[:, first : first + total // 2], right[...], (((0,), (0,)), ((), ())),
-                preferred_element_type=F32,
+            target[first : first + total // 2] = tn(
+                left[:, first : first + total // 2], right[:, lanes]
             ).astype(BF16)
         late[number].a()
 
@@ -942,9 +949,7 @@
             moved = pltpu.roll(both, shift, axis=1) if shift else both
             dst[c, pl.ds(first, 2), 1 : HGT + 1, :, lanes] = moved.reshape(2, HGT, PADW, 128)
 
-    def pooled(which, clip):
-        field = x0q.at[clip, 0] if which == 0 else x0kv.at[clip, which - 1]
-        upstream = dq.at[clip] if which == 0 else dkv.at[clip, which - 1]
+    def prepare(which, clip):
         if which:
             memory = dmem_recv[clip, which - 1].astype(F32)
             memory = jnp.where(place.dp == count - 1, 0.0, memory)
@@ -955,54 +960,55 @@
                     memory = memory + dkv[later, which - 1, ROWS + MROWS :]
             spread(ms, 0, memory.reshape(TM, HGT, PADW, LW))
         else:
-            spread(us, 1, upstream[...].reshape(T_LEN, HGT, PADW, LW))
-
-        def tile_loop(tile, _):
-            lanes = pl.ds(pl.multiple_of(tile * 128, 128), 128)
-            if which:
-
-                def squeeze_step(pair, _):
-                    rows = pl.ds(pl.multiple_of(pair * 112, 112), 112)
-                    own = upstream[rows, lanes].reshape(2, HGT, PADW, 128)
-                    fields = kvf[clip, which - 1, rows, lanes].astype(F32).reshape(2, HGT, PADW, 128)
-                    acc = [own[0], own[1]]
-                    for a, d, frame in ((1, 0, 0), (0, 1, 1), (2, 1, 0)):
-                        for c in range(3):
-                            block = ms[2 - c, pair + frame, :, :, lanes]
-                            for b in range(3):
-                                at = block[2 - b : 2 - b + HGT]
-                                number = a * 9 + b * 3 + c
-                                acc[d] = acc[d] + taps_ref[2 + which, number, :, lanes][None] * at
-                                kacc[2 + which, number, :, lanes] += jnp.sum(fields[d] * at, axis=0)
-                    shifted_store(us, 2 * pair + 1, keep_rows(jnp.stack(acc)), lanes)
-                    return 0
-
-                lax.fori_loop(0, TM, squeeze_step, 0)
-
-            def pair_step(pair, _):
+            spread(us, 1, dq[clip].reshape(T_LEN, HGT, PADW, LW))
+
+    def pooled(which, clip, tile):
+        field = x0q.at[clip, 0] if which == 0 else x0kv.at[clip, which - 1]
+        upstream = dq.at[clip] if which == 0 else dkv.at[clip, which - 1]
+        if tile == 0:
+            prepare(which, clip)
+        lanes = slice(tile * 128, tile * 128 + 128)
+        if which:
+
+            def squeeze_step(pair, _):
                 rows = pl.ds(pl.multiple_of(pair * 112, 112), 112)
-                fields = field[rows, lanes].astype(F32).reshape(2, HGT, PADW, 128)
-                acc = [jnp.zeros((HGT, PADW, 128), F32) for _ in range(2)]
-                for a in range(3):
+                own = upstream[rows, lanes].reshape(2, HGT, PADW, 128)
+                fields = kvf[clip, which - 1, rows, lanes].astype(F32).reshape(2, HGT, PADW, 128)
+                acc = [own[0], own[1]]
+                for a, d, frame in ((1, 0, 0), (0, 1, 1), (2, 1, 0)):
                     for c in range(3):
-                        sums = [jnp.zeros((PADW, 128), F32) for _ in range(3)]
-                        for d in range(2):
-                            block = us[2 - c, 2 * pair + d + 2 - a, :, :, lanes]
-                            for b in range(3):
-                                at = block[2 - b : 2 - b + HGT]
-                                acc[d] = acc[d] + taps_ref[which, a * 9 + b * 3 + c, :, lanes][None] * at
-                                sums[b] = sums[b] + jnp.sum(fields[d] * at, axis=0)
+                        block = ms[2 - c, pair + frame, :, :, lanes]
                         for b in range(3):
-                            kacc[which, a * 9 + b * 3 + c, :, lanes] += sums[b]
-                both = keep_rows(jnp.stack(acc))
-                out_rows = pl.ds(pl.multiple_of(clip * ROWS + pair * 112, 16), 112)
-                dx[which, out_rows, lanes] = both.reshape(112, 128).astype(BF16)
+                            at = block[2 - b : 2 - b + HGT]
+                            number = a * 9 + b * 3 + c
+                            acc[d] = acc[d] + taps_ref[2 + which, number, :, lanes][None] * at
+                            kacc[2 + which, number, :, lanes] += jnp.sum(fields[d] * at, axis=0)
+                shifted_store(us, 2 * pair + 1, keep_rows(jnp.stack(acc)), lanes)
                 return 0
 
-            lax.fori_loop(0, T_LEN // 2, pair_step, 0)
+            lax.fori_loop(0, TM, squeeze_step, 0)
+
+        def pair_step(pair, _):
+            rows = pl.ds(pl.multiple_of(pair * 112, 112), 112)
+            fields = field[rows, lanes].astype(F32).reshape(2, HGT, PADW, 128)
+            acc = [jnp.zeros((HGT, PADW, 128), F32) for _ in range(2)]
+            for a in range(3):
+                for c in range(3):
+                    sums = [jnp.zeros((PADW, 128), F32) for _ in range(3)]
+                    for d in range(2):
+                        block = us[2 - c, 2 * pair + d + 2 - a, :, :, lanes]
+                        for b in range(3):
+                            at = block[2 - b : 2 - b + HGT]
+                            acc[d] = acc[d] + taps_ref[which, a * 9 + b * 3 + c, :, lanes][None] * at
+                            sums[b] = sums[b] + jnp.sum(fields[d] * at, axis=0)
+                    for b in range(3):
+                        kacc[which, a * 9 + b * 3 + c, :, lanes] += sums[b]
+            both = keep_rows(jnp.stack(acc))
+            out_rows = pl.ds(pl.multiple_of(clip * ROWS + pair * 112, 16), 112)
+            dx[which, out_rows, lanes] = both.reshape(112, 128).astype(BF16)
             return 0
 
-        lax.fori_loop(0, LW // 128, tile_loop, 0)
+        lax.fori_loop(0, T_LEN // 2, pair_step, 0)
 
     side_rows = ROWS // 2
 
@@ -1014,9 +1020,8 @@
 
     def cross(clip):
         send_y[clip] = input_gradient(clip, 1 - place.head).astype(BF16)
-        number = groups + 2 + clip
         crossing[clip] = remote(
-            send_y.at[clip], recv_y.at[clip], small_send.at[number], small_recv.at[number], place.to_y
+            send_y.at[clip], recv_y.at[clip], cross_send.at[clip], cross_recv.at[clip], place.to_y
         )
 
     def normed_gradient(clip):
@@ -1032,37 +1037,44 @@
             w - jnp.mean(w, axis=-1, keepdims=True) - xhat * jnp.mean(w * xhat, axis=-1, keepdims=True)
         )
         grad[clip] = middle[clip] + dv
-        l0[0, 0:1] += jnp.sum(u * xhat, axis=0, keepdims=True)
-        l0[0, 1:2] += jnp.sum(u, axis=0, keepdims=True)
+        for which, value in enumerate((u * xhat, u)):
+            value = jnp.sum(value, axis=0, keepdims=True)
+            for n in range(width // 128):
+                row = NORM_ROW + which * (width // 128) + n
+                sm[row : row + 1] += value[:, n * 128 : n * 128 + 128]
 
     def exact(a, b):
         return jnp.dot(a, b, precision=HIGHEST, preferred_element_type=F32)
 
-    def small_start():
+    def small_first():
+        sm[...] = jnp.zeros_like(sm)
         folded = exact(dr_ref[...], foldl_ref[...])
-        sm_raw[0:REL_ROWS] = exact(pick_ref[...], folded)
-        for which in range(5):
-            first = REL_ROWS + 32 * which
-            sums = jnp.sum(kacc[which], axis=1)
-            sums = jnp.concatenate([sums, jnp.zeros((5, LW), F32)], axis=0)
-            sm_raw[first : first + 32] = exact(sums, foldl_ref[...])
-        number = groups + 2 + clips
-        crossing["small"] = remote(
-            sm_raw, sm_y, small_send.at[number], small_recv.at[number], place.to_y
-        )
-
-    def small_next():
-        crossing["small"].wait()
-        sm[...] = sm_raw[...] + sm_y[...]
-        tiny.a()
+        sm[0:NREL] = exact(pick_ref[...], folded)[0:NREL]
+        early = sums0[...] + sums1[...]
+        hidden = hidden0[...] + hidden1[...] + hidden2[...] + hidden3[...]
+        strip = width // 128
+        for which in range(4):
+            for n in range(strip):
+                row = EARLY_ROW + which * strip + n
+                sm[row : row + 1] = early[which : which + 1, n * 128 : n * 128 + 128]
+        count_h = hidden.shape[1] // 128
+        for side in range(2):
+            for n in range(count_h):
+                row = HIDDEN_ROW + side * count_h + n
+                part = hidden[:, n * 128 : n * 128 + 128]
+                sm[row : row + 1] = jnp.where(place.head == side, part, 0.0)
+
+    def small_taps(which):
+        first = TAP_ROW + 27 * which
+        sums = jnp.sum(kacc[which], axis=1)
+        sums = jnp.concatenate([sums, jnp.zeros((5, LW), F32)], axis=0)
+        sm[first : first + 27] = exact(sums, foldl_ref[...])[0:27]
 
     ffn[0].d(chunks_ref[0])
-    ffn[1].d(chunks_ref[1])
     us[...] = jnp.zeros_like(us)
     ms[...] = jnp.zeros_like(ms)
     kacc[...] = jnp.zeros_like(kacc)
-    l0[0] = jnp.zeros_like(l0[0])
-    sm_raw[...] = jnp.zeros_like(sm_raw)
+    small_first()
     lead["dkv"].wait()
     for which in range(2):
         dmem_send[0, which] = dkv[0, which, ROWS + MROWS :].astype(BF16)
@@ -1075,105 +1087,131 @@
     product(0)
     for name in ("dq", "x0q", "taps"):
         lead[name].wait()
+    pooled(0, 0, 0)
+    pooled(0, 0, 1)
     late[0].b()
+    pooled(0, 0, 2)
+    ffn[1].d(chunks_ref[1])
+    pooled(0, 1, 0)
+    pooled(0, 1, 1)
+    ffn[0].e()
+    pooled(0, 1, 2)
     ffn[2].d(chunks_ref[2])
-    pooled(0, 0)
-    ffn[0].e()
-    ffn[3].d(chunks_ref[3])
-    ffn[1].e()
-    pooled(0, 1)
-    ffn[4].d(chunks_ref[4])
-    ffn[2].e()
-    ffn[0].f()
     lead["rows_a"].wait()
     product(1)
-    late[0].c()
+    small_taps(0)
     memory_flight.wait()
     lead["x0kv"].wait()
     lead["kvf"].wait()
+    pooled(1, 0, 0)
     late[1].b()
-    pooled(1, 0)
-    ffn[5].d(chunks_ref[5])
-    ffn[3].e()
-    ffn[1].f()
+    late[0].c()
+    pooled(1, 0, 1)
+    ffn[0].f()
+    pooled(1, 0, 2)
+    ffn[1].e()
+    ffn[3].d(chunks_ref[3])
+    pooled(2, 0, 0)
+    store1(0)
+    pooled(2, 0, 1)
     late[0].d()
-    ffn[4].e()
-    pooled(2, 0)
-    late[1].c()
-    ffn[6].d(chunks_ref[6])
-    late[0].e()
-    ffn[2].f()
-    store2(0)
+    ffn[2].e()
+    pooled(2, 0, 2)
     lead["w"].wait()
     cross(0)
-    ffn[5].e()
-    pooled(1, 1)
+    ffn[1].f()
+    pooled(1, 1, 0)
+    late[1].c()
+    store1(1)
+    ffn[3].e()
+    product(2)
+    pooled(1, 1, 1)
+    ffn[2].f()
+    product(3)
+    pooled(1, 1, 2)
+    late[2].b()
+    store1(2)
+    product(4)
+    late[3].b()
     late[1].d()
-    ffn[7].d(chunks_ref[7])
-    product(2)
-    late[2].b()
-    ffn[6].e()
+    small_taps(1)
+    small_taps(3)
+    late[0].e()
     ffn[3].f()
-    store2(1)
-    pooled(2, 1)
-    product(3)
+    pooled(2, 1, 0)
+    store1(3)
+    product(5)
+    late[2].c()
+    pooled(2, 1, 1)
+    late[3].c()
+    late[4].b()
+    product(6)
+    late[5].b()
+    pooled(2, 1, 2)
+    late[2].d()
+    late[6].b()
+    late[0].f()
+    product(7)
+    late[3].d()
+    late[1].e()
     cross(1)
-    late[2].c()
-    late[3].b()
-    small_start()
-    ffn[4].f()
-    late[0].f()
-    store2(2)
-    lead["tokens"].wait()
-    lead["middle0"].wait()
-    lead["middle1"].wait()
-    normed_gradient(0)
-    small_next()
-    late[2].d()
-    late[3].c()
-    late[1].e()
-    ffn[5].f()
-    store2(3)
-    tiny.b()
-    normed_gradient(1)
-    ends.one()
-    late[3].d()
-    tiny.c()
-    late[2].e()
-    ffn[7].e()
-    ends.two()
-    ffn[6].f()
-    store2(4)
-    late[1].f()
-    tiny.d()
-    ends.three()
+    late[4].c()
     late[0].g()
     stage_t[...] = resp[0].astype(F32).T
-    turned = local(stage_t, outp, stores.at[2])
+    sent = [local(stage_t, outp, stores.at[2])]
+    small_taps(2)
+    small_taps(4)
+    for name in ("tokens", "middle0", "middle1"):
+        lead[name].wait()
+    normed_gradient(0)
+    late[2].e()
+    late[5].c()
     late[3].e()
-    ends.four()
+    late[6].c()
+    late[4].d()
+    late[7].b()
+    late[1].f()
+    late[5].d()
+    late[2].f()
+    late[1].g()
+    sent.append(local(resp.at[1], outq.at[0], stores.at[3]))
+    late[6].d()
+    late[2].g()
+    sent.append(local(strip_res.at[0], outq.at[1, :, 0 : 128], stores.at[4]))
+    late[3].f()
+    late[4].e()
+    late[7].c()
+    late[3].g()
+    sent.append(local(strip_res.at[1], outq.at[1, :, 128 : 256], stores.at[5]))
+    late[5].e()
+    normed_gradient(1)
+    tiny.a()
+    late[4].f()
+    late[6].e()
+    late[7].d()
+    late[4].g()
+    sent.append(local(strip_res.at[2], outq.at[1, :, 256 : 384], stores.at[6]))
+    late[5].f()
+    tiny.b()
+    late[5].g()
+    sent.append(local(strip_res.at[3], outq.at[2, :, 0 : 128], stores.at[7]))
+    late[6].f()
+    late[7].e()
+    late[6].g()
+    sent.append(local(strip_res.at[4], outq.at[2, :, 128 : 256], stores.at[8]))
+    tiny.c()
+    late[7].f()
+    late[7].g()
+    sent.append(local(strip_res.at[5], outq.at[2, :, 256 : 384], stores.at[9]))
+    tiny.d()
     tiny.e()
-    store2(5)
-    late[2].f()
-    ffn[7].f()
-    store2(6)
-    late[1].g()
-    sent_q = local(resp.at[1], outq.at[0], stores.at[3])
-    tiny.f()
-    ends.five(late_out)
-    store2(7)
-    late[2].g()
-    sent_k = local(resp.at[2], outq.at[1], stores.at[4])
-    late[3].f()
-    tiny.g()
-    late[3].g()
-    sent_v = local(resp.at[3], outq.at[2], stores.at[5])
     small_out[...] = sm_res[...]
-    for made in [turned, sent_q, sent_k, sent_v] + stored[-2:]:
+    for made in sent + stored[-2:]:
         made.wait()
 
-
-def call_finish(dq, dkv, x0q, x0kv, kvf, all_taps, rows_a, rows_x, branch, weights, tokens, middle, chunks, dr, gain):
+def call_finish(
+    dq, dkv, x0q, x0kv, kvf, all_taps, rows_a, rows_x, branch, weights, tokens, middle, chunks, dr, gain, sums, hidden
+):
     groups = lax.axis_size("dp") // 4
     width = tokens.shape[2]
     total = padded_rows(width, groups)
@@ -1181,7 +1219,7 @@
     if total != width:
         extra = ((0, 0), (0, total - width))
         rows_a, rows_x = jnp.pad(rows_a, extra), [jnp.pad(x, extra) for x in rows_x]
-    small_rows = -(-SMALL_ROWS // (32 * groups)) * 32 * groups
+    small_rows = -(-SMALL_ROWS // (64 * groups)) * 64 * groups
     foldl = np.zeros((LW, 128), np.float32)
     foldl[np.arange(LW), np.arange(LW) % HEAD_DIM] = 1
     pick = np.zeros((REL_ROWS, 256), np.float32)
@@ -1199,16 +1237,14 @@
     frame = pltpu.VMEM((3, T_LEN + 2, HGT + 2, PADW, LW), F32)
     return pl.pallas_call(
         partial(finish_kernel, groups, width),
-        in_specs=[hbm] * len(streamed) + [vmem] * 5,
-        out_specs=[vmem, hbm, hbm, hbm, hbm, vmem, vmem],
+        in_specs=[hbm] * len(streamed) + [vmem] * 11,
+        out_specs=[vmem, hbm, hbm, hbm, vmem],
         out_shape=[
             jax.ShapeDtypeStruct(tokens.shape, F32),
-            jax.ShapeDtypeStruct((2 * total, width), F32),
             jax.ShapeDtypeStruct((total, 4 * LW), F32),
             jax.ShapeDtypeStruct((LW, total), F32),
             jax.ShapeDtypeStruct((3, total, LW), BF16),
             jax.ShapeDtypeStruct((small_rows, 128), F32),
-            jax.ShapeDtypeStruct((LATE, width), F32),
         ],
         scratch_shapes=[pltpu.VMEM(shape, dtype) for shape, dtype in held]
         + [
@@ -1218,34 +1254,37 @@
             pltpu.VMEM((3, clips * ROWS, LW), BF16),
             pltpu.VMEM((2, 2, MROWS, LW), BF16),
             pltpu.VMEM((2, 2, MROWS, LW), BF16),
-            pltpu.VMEM((2 * total, width), BF16),
             pltpu.VMEM((total, 4 * LW), BF16),
-            pltpu.VMEM((4, total, LW), BF16),
-            pltpu.VMEM((4, total, LW), BF16),
+            pltpu.VMEM((2, total, LW), BF16),
+            pltpu.VMEM((2, total, LW), BF16),
             pltpu.VMEM((2, total, LW), F32),
             pltpu.VMEM((LW, total), F32),
-            *piece_scratch(total, groups, LW, BF16, 4),
+            *piece_scratch(total, groups, LW, BF16, 2),
+            pltpu.VMEM((6, total, 128), BF16),
+            pltpu.VMEM((6, total, 128), BF16),
+            *piece_scratch(total, groups, 128, BF16, 6),
             pltpu.VMEM((small_rows, 128), F32),
             pltpu.VMEM((small_rows, 128), F32),
-            pltpu.VMEM((small_rows, 128), F32),
-            pltpu.VMEM((small_rows, 128), F32),
-            *piece_scratch(small_rows, groups, 128, F32, 1),
+            pltpu.VMEM((small_rows // 2, 128), F32),
+            pltpu.VMEM((small_rows // 2, 128), F32),
+            pltpu.VMEM((4 * groups - 1, small_rows // 8 // groups, 128), F32),
             pltpu.VMEM((clips, side, width), BF16),
             pltpu.VMEM((clips, side, width), BF16),
-            *small_scratch(LATE, LATE, groups, width),
             pltpu.SemaphoreType.DMA((15,)),
-            pltpu.SemaphoreType.DMA((6,)),
-            pltpu.SemaphoreType.DMA((13, 2 * groups + 2)),
-            pltpu.SemaphoreType.DMA((13, 2 * groups + 2)),
-            pltpu.SemaphoreType.DMA((groups + 3 + clips,)),
-            pltpu.SemaphoreType.DMA((groups + 3 + clips,)),
+            pltpu.SemaphoreType.DMA((10,)),
+            pltpu.SemaphoreType.DMA((12, 2 * groups + 2)),
+            pltpu.SemaphoreType.DMA((12, 2 * groups + 2)),
+            pltpu.SemaphoreType.DMA((8 * groups,)),
+            pltpu.SemaphoreType.DMA((8 * groups,)),
+            pltpu.SemaphoreType.DMA((clips,)),
+            pltpu.SemaphoreType.DMA((clips,)),
             pltpu.SemaphoreType.DMA((2,)),
         ],
         compiler_params=params(collective_id=1, has_side_effects=True),
         cost_estimate=pl.CostEstimate(
             flops=60_000_000_000, bytes_accessed=40_000_000, transcendentals=0
         ),
-    )(*streamed, chunks, dr, gain, jnp.asarray(foldl), jnp.asarray(pick))
+    )(*streamed, chunks, dr, gain, jnp.asarray(foldl), jnp.asarray(pick), *sums, *hidden)
 
 
 def from_behind(x, axis, by):
@@ -1376,6 +1415,7 @@
         for store, value in zip((branch, qa, at, lse), made):
             store.append(value)
         own, sent = simple_call(project_kernel, [rows32, rows16], 1, branch[-1][0], w_proj)
+        sent, q = lax.optimization_barrier((sent, q)) if clip + 1 < clip_count else (sent, q)
         kept.append(own)
         recv.append(swap(sent))
     middle, mine, theirs = [], [], []
@@ -1418,9 +1458,9 @@
         dmix.append(mix)
     last = [lax.optimization_barrier((other_parts[c][3], low[-1][1]))[0] for c in clips]
     last = [swap(x) for x in last]
-    dq, dkv, dr, chunks, early = call_attention_backward(
+    dq, dkv, dr, chunks, w_fc2_grad = call_attention_backward(
         q, kv, memory, keys_extra, qa, dmix, at, lse, rel_rows,
-        w_fc2_grad, w_fc1_grad, sums, [p[4] for p in parts], consts,
+        w_fc2_grad, w_fc1_grad, consts,
     )
     *last, dq = lax.optimization_barrier((*last, dq))
     output = drop_rows(
@@ -1431,7 +1471,8 @@
             ]
         )
     )
-    input_grad, w_fc2_grad, w_fc1_grad, w_proj_grad, tail, small, late = call_finish(
+    w_fc2_grad = w_fc2_grad.astype(F32)
+    input_grad, w_fc1_grad, w_proj_grad, tail, small = call_finish(
         dq, dkv, q0, kv0, kvf, jnp.concatenate([tap_q, tap_kv, tap_s]),
         first_rows.reshape(-1, width),
         rows_x,
@@ -1442,6 +1483,8 @@
         chunks,
         dr,
         ln1_gain.reshape(1, -1),
+        sums,
+        [p[4] for p in parts],
     )
     input_grad = drop_rows(input_grad)
     total = w_fc1_grad.shape[0]
@@ -1449,10 +1492,14 @@
         w_fc2_grad = w_fc2_grad.reshape(2, total, width)[:, :width].reshape(2 * width, width)
         w_fc1_grad, w_proj_grad, tail = w_fc1_grad[:width], w_proj_grad[:, :width], tail[:, :width]
     w_qkv_grad = tail.astype(F32).transpose(1, 0, 2)
-    fc1_bias_grad = early[HEAD_EARLY : HEAD_EARLY + fc1_bias.size // width].reshape(-1)
+    norms = small[NORM_ROW:EARLY_ROW].reshape(2, width)
+    early = small[EARLY_ROW:HIDDEN_ROW].reshape(4, width)
+    fc1_bias_grad = lax.dynamic_index_in_dim(
+        small[HIDDEN_ROW:SMALL_ROWS].reshape(2, fc1_bias.size), lax.axis_index("head"), 0, keepdims=False
+    )
     small = small[:, :HEAD_DIM]
-    shared = [late[0], late[1]]
-    shared += [small[REL_ROWS + 32 * n : REL_ROWS + 32 * n + 27] for n in range(5)]
+    shared = [norms[0], norms[1]]
+    shared += [small[TAP_ROW + 27 * n : TAP_ROW + 27 * n + 27] for n in range(5)]
     shared += [
         small[: 2 * T_LEN - 1],
         small[2 * T_LEN - 1 : 2 * T_LEN + 2 * HGT - 2],

time: 348 us -> 336 us (0.966); the launches traced: 342 us -> 336 us
  Pallas kernels: 260 us -> 254 us
  other arithmetic: 8.64 us -> 12.9 us
    pallas_call x1, Pallas kernels: 97.2 us -> 73.2 us  [call_finish(): pl.pallas_call(partial(finish_kernel, groups, width), in_specs=[hbm] * le...]
    pallas_call x12, Pallas kernels: 48.7 us -> 58.8 us  [simple_call(): pl.pallas_call(kernel, in_specs=[vmem] * len(args), out_specs=[vmem] * le...]
    pallas_call x1, Pallas kernels: 52.1 us -> 60.3 us  [call_attention_backward(): pl.pallas_call(partial(attention_backward, groups), in_specs=[vmem] * 3 +...]
    convert_element_type x0 -> x1, other arithmetic: none -> 4.21 us  [on_device(): w_fc2_grad = w_fc2_grad.astype(F32)]
    unnamed x128 -> x119, local copies, waits for them, and re-layouts: 19.5 us -> 18.5 us
  transfers between devices with their start and end apart: 13 -> 13, of which waited for: 3 -> 2; matrix products, arithmetic and copies ran while one was open for 7% -> 7% of each run, Pallas kernels for 43% -> 50%
where the time goes in v5:
time: 336 us
  Pallas kernels  254 us (76%)
  local copies, waits for them, and re-layouts  41.8 us (12%)
  starting transfers between devices  15 us (4%)
  other arithmetic  12.9 us (4%)
  waiting for transfers between devices  9.47 us (3%)
    pallas_call x1, Pallas kernels, call_finish(): pl.pallas_call(partial(finish_kernel, groups, width), in_specs=[hbm] * le...  73.2 us
    pallas_call x1, Pallas kernels, call_attention_backward(): pl.pallas_call(partial(attention_backward, groups), in_specs=[vmem] * 3 +...  60.3 us
    pallas_call x12, Pallas kernels, simple_call(): pl.pallas_call(kernel, in_specs=[vmem] * len(args), out_specs=[vmem] * le...  58.8 us
    pallas_call x2, Pallas kernels, call_attention_forward(): pl.pallas_call(attention_forward, grid=(1,), in_specs=[block(1, ROWS, LW)...  30.5 us
    pallas_call x2, Pallas kernels, call_pool_forward(): pl.pallas_call(partial(pool_forward, squeeze), grid=(count, clips), in_sp...  21 us
    unnamed x119, local copies, waits for them, and re-layouts  18.5 us
    ppermute x12, starting transfers between devices, swap(): return lax.ppermute(x, 'head', [(0, 1), (1, 0)])  13.3 us
    pallas_call x1, Pallas kernels, call_weights(): pl.pallas_call(partial(weight_kernel, count), grid=(hidden // LW,), in_sp...  10.1 us
  transfers between devices with their start and end apart: 13, of which 2 were waited for; matrix products, arithmetic and copies ran while one was open for 7% of the time, Pallas kernels for 50%

profile of v5, /device:TPU:0, one launch (start us, length us, event | category | flops | bytes accessed | tf_op | source)
XLA Modules:
  0.0 335.5 jit_solution(3313781474173575581)
XLA Ops:
  3.2 3.0 collective-permute-start
  27.0 14.4 %shard_map.491 = (bf16[2,2,448,384]{3,2,1,0:T(8,128)(2,1)}, bf16[2,2,448,384]{3,2,1,0:T(8,128)(2,1)}, bf16[2,2,448,384]{3,2,1,0:T(8,128)(2,1)}, bf16[2,2,224,384]{3,2,1,0:T(8,128)(2,1)}) custom-call(bf16[2,448,768]{2,1,0:T(8,128)(2,1)} %copy-done.6, bf16[3,768,384]{2,1,0:T(8,128)(2,1)} %bitcast.94, f32[2,27,8,384]{3,2,1,0:T(8,128)} %get-tuple-element.198.refs_2_, ...), custom_call_target="tpu_custom_call" | custom-call | flops 12000000000 | bytes 8000000 | tf_op jit(solution)/shard_map/pallas_call | solution.py:216
  45.1 6.6 %shard_map.490 = (bf16[2,1,448,384]{3,2,1,0:T(8,128)(2,1)}, bf16[2,1,448,384]{3,2,1,0:T(8,128)(2,1)}) custom-call(bf16[2,448,768]{2,1,0:T(8,128)(2,1)} %copy-done.6, bf16[3,768,384]{2,1,0:T(8,128)(2,1)} %bitcast.95, f32[1,27,8,384]{3,2,1,0:T(8,128)} %broadcast_in_dim_broadcast_in_dim.2.refs_2_), custom_call_target="tpu_custom_call" | custom-call | flops 6000000000 | bytes 4000000 | tf_op jit(solution)/shard_map/pallas_call | solution.py:216
  54.0 15.1 %shard_map.492 = (bf16[1,448,384]{2,1,0:T(8,128)(2,1)}, bf16[1,4,448,256]{3,2,1,0:T(8,128)(2,1)}, f32[1,384,448]{2,1,0:T(8,128)}, f32[1,8,448]{2,1,0:T(8,128)}) custom-call(bf16[2,1,448,384]{3,2,1,0:T(8,128)(2,1)} %get-tuple-element.105.q_ref, bf16[2,2,448,384]{3,2,1,0:T(8,128)(2,1)} %get-tuple-element.94.kv_ref, bf16[4,2,224,384]{3,2,1,0:T(8,128)(2,1)} %copy-done.25, ...), custom_call_target="tpu_custom_call" | custom-call | flops 12999999488 | bytes 5000000 | tf_op jit(solution)/shard_map/pallas_call | solution.py:294
  69.1 2.5 shard_map.493
  73.4 15.4 %shard_map.497 = (bf16[1,448,384]{2,1,0:T(8,128)(2,1)}, bf16[1,4,448,256]{3,2,1,0:T(8,128)(2,1)}, f32[1,384,448]{2,1,0:T(8,128)}, f32[1,8,448]{2,1,0:T(8,128)}) custom-call(bf16[2,1,448,384]{3,2,1,0:T(8,128)(2,1)} %get-tuple-element.105.q_ref, bf16[2,2,448,384]{3,2,1,0:T(8,128)(2,1)} %get-tuple-element.94.kv_ref, bf16[4,2,224,384]{3,2,1,0:T(8,128)(2,1)} %copy-done.25, ...), custom_call_target="tpu_custom_call" | custom-call | flops 12999999488 | bytes 5000000 | tf_op jit(solution)/shard_map/pallas_call | solution.py:294
  88.8 2.5 shard_map.498
  93.3 2.4 shard_map.494
  97.4 4.7 %collective-permute-done.5.recv = bf16[224,768]{1,0:T(8,128)(2,1)S(1)} collective-permute-done((bf16[224,768]{1,0:T(8,128)(2,1)}, bf16[224,768]{1,0:T(8,128)(2,1)S(1)}, u32[]{:S(2)}, u32[]{:S(2)}) %collective-permute-start.5) | collective-permute-done | bytes 344096 | tf_op jit(solution)/shard_map/ppermute | solution.py:1319
  102.8 2.5 shard_map.499
  105.4 6.7 %shard_map.500 = (bf16[224,1536]{1,0:T(8,128)(2,1)}, bf16[224,1536]{1,0:T(8,128)(2,1)}, f32[224,768]{1,0:T(8,128)}, f32[224,768]{1,0:T(8,128)}, f32[1,1536]{1,0:T(1,128)}) custom-call(bf16[224,768]{1,0:T(8,128)(2,1)} %get-tuple-element.109.a2.refs_9_, bf16[224,768]{1,0:T(8,128)(2,1)} %bitcast.91, bf16[768,1536]{1,0:T(8,128)(2,1)} %w1.7, ...), custom_call_target="tpu_custom_call" | custom-call | flops 5000000000 | bytes 2000000 | tf_op jit(solution)/shard_map/pallas_call | solution.py:340
  112.1 4.8 %collective-permute-done.6.a2.refs_11_ = bf16[224,768]{1,0:T(8,128)(2,1)S(1)} collective-permute-done((bf16[224,768]{1,0:T(8,128)(2,1)}, bf16[224,768]{1,0:T(8,128)(2,1)S(1)}, u32[]{:S(2)}, u32[]{:S(2)}) %collective-permute-start.6) | collective-permute-done | bytes 344096 | tf_op jit(solution)/shard_map/ppermute | solution.py:1319
  117.6 6.5 %shard_map.501 = (bf16[224,1536]{1,0:T(8,128)(2,1)}, bf16[224,1536]{1,0:T(8,128)(2,1)}, bf16[224,768]{1,0:T(8,128)(2,1)}, bf16[224,768]{1,0:T(8,128)(2,1)}, f32[1,1536]{1,0:T(1,128)}) custom-call(bf16[224,768]{1,0:T(8,128)(2,1)} %copy-done.48, bf16[224,768]{1,0:T(8,128)(2,1)} %get-tuple-element.167.g.refs_15_, bf16[768,1536]{1,0:T(8,128)(2,1)} %w1.7, ...), custom_call_target="tpu_custom_call" | custom-call | flops 5000000000 | bytes 2000000 | tf_op jit(solution)/shard_map/pallas_call | solution.py:340
  124.9 6.5 %shard_map.496 = (bf16[224,1536]{1,0:T(8,128)(2,1)}, bf16[224,1536]{1,0:T(8,128)(2,1)}, bf16[224,768]{1,0:T(8,128)(2,1)}, bf16[224,768]{1,0:T(8,128)(2,1)}, f32[1,1536]{1,0:T(1,128)}) custom-call(bf16[224,768]{1,0:T(8,128)(2,1)} %copy-done.47, bf16[224,768]{1,0:T(8,128)(2,1)} %get-tuple-element.168.g.refs_14_, bf16[768,1536]{1,0:T(8,128)(2,1)} %w1.7, ...), custom_call_target="tpu_custom_call" | custom-call | flops 5000000000 | bytes 2000000 | tf_op jit(solution)/shard_map/pallas_call | solution.py:340
  133.3 17.3 %shard_map.495 = (bf16[224,1536]{1,0:T(8,128)(2,1)}, bf16[224,1536]{1,0:T(8,128)(2,1)}, f32[224,768]{1,0:T(8,128)}, f32[224,768]{1,0:T(8,128)}, f32[1,1536]{1,0:T(1,128)}) custom-call(bf16[224,768]{1,0:T(8,128)(2,1)} %get-tuple-element.101.a2.refs_8_, bf16[224,768]{1,0:T(8,128)(2,1)} %bitcast.88, bf16[768,1536]{1,0:T(8,128)(2,1)} %w1.7, ...), custom_call_target="tpu_custom_call" | custom-call | flops 5000000000 | bytes 2000000 | tf_op jit(solution)/shard_map/pallas_call | solution.py:340
  151.4 3.1 shard_map.502
  155.3 3.1 shard_map.503
  160.4 10.1 %shard_map.506 = (bf16[1536,768]{1,0:T(8,128)(2,1)}, bf16[768,1536]{1,0:T(8,128)(2,1)}) custom-call(bf16[224,1536]{1,0:T(8,128)(2,1)} %get-tuple-element.128.refs_0_, bf16[224,1536]{1,0:T(8,128)(2,1)} %get-tuple-element.129.refs_1_, bf16[224,1536]{1,0:T(8,128)(2,1)} %get-tuple-element.130.refs_2_, bf16[224,1536]{1,0:T(8,128)(2,1)} %get-tuple-element.131.refs_3_, ...), custom_call_target="tpu_custom_call" | custom-call | flops 8000000000 | bytes 15000000 | tf_op jit(solution)/shard_map/pallas_call | solution.py:428
  172.7 2.8 shard_map.505
  176.2 2.8 shard_map.504
  179.0 60.3 %shard_map.507 = (f32[2,448,384]{2,1,0:T(8,128)}, f32[2,2,896,384]{3,2,1,0:T(8,128)}, f32[256,384]{1,0:T(8,128)}, bf16[4,48,384]{2,1,0:T(8,128)(2,1)}, bf16[1536,768]{1,0:T(8,128)(2,1)}) custom-call(bf16[2,1,448,384]{3,2,1,0:T(8,128)(2,1)} %get-tuple-element.105.q_ref, bf16[2,2,448,384]{3,2,1,0:T(8,128)(2,1)} %get-tuple-element.94.kv_ref, ...), custom_call_target="tpu_custom_call" | custom-call | flops 40000000000 | bytes 20000000 | tf_op jit(solution)/shard_map/pallas_call | solution.py:809
  239.3 4.2 %convert_element_type.68 = f32[1536,768]{1,0:T(8,128)} convert(bf16[1536,768]{1,0:T(8,128)(2,1)} %get-tuple-element.164) | non-fusion elementwise | flops 1179648 | bytes 7077888 | tf_op jit(solution)/shard_map/convert_element_type | solution.py:1474
  243.5 73.2 %shard_map.508 = (f32[2,224,768]{2,1,0:T(8,128)}, f32[768,1536]{1,0:T(8,128)}, f32[384,768]{1,0:T(8,128)}, bf16[3,768,384]{2,1,0:T(8,128)(2,1)}, f32[256,128]{1,0:T(8,128)}) custom-call(f32[2,448,384]{2,1,0:T(8,128)} %get-tuple-element.142.dq_hbm, f32[2,2,896,384]{3,2,1,0:T(8,128)} %get-tuple-element.143.dkv_hbm, ...), custom_call_target="tpu_custom_call" | custom-call | flops 60000002048 | bytes 40000000 | tf_op jit(solution)/shard_map/pallas_call | solution.py:1238
  330.4 4.9 %copy.73 = f32[768,1536]{1,0:T(8,128)} copy(f32[768,1536]{1,0:T(8,128)} %get-tuple-element.242) | data formatting | bytes 9437184
  (208 shorter events, 58.5 us)
Async XLA Ops:
  0.7 10.0 %copy-start = (f32[13,96]{1,0:T(8,128)S(1)}, f32[13,96]{1,0:T(8,128)}, u32[]{:S(2)}) copy-start(f32[13,96]{1,0:T(8,128)} %param.46) | copy-start | bytes 14980
  3.2 21.6 %collective-permute-start = (bf16[2,224,768]{2,1,0:T(8,128)(2,1)S(1)}, bf16[2,224,768]{2,1,0:T(8,128)(2,1)}, u32[]{:S(2)}, u32[]{:S(2)}) collective-permute-start(bf16[2,224,768]{2,1,0:T(8,128)(2,1)S(1)} %select_convert_fusion), channel_id=1, source_target_pairs={{0,1},{1,0},{2,3},{3,2},{4,5},{5,4},{6,7},{7,6},{8,9},{9,8},{10,11... | collective-permute-start | bytes 2064392 | tf_op jit(solution)/shard_map/ppermute | solution.py:1319
  7.4 5.9 %copy-start.14 = (bf16[2,196,768]{2,0,1:T(2,128)(2,1)S(1)}, bf16[2,196,768]{2,0,1:T(2,128)(2,1)}, u32[]{:S(2)}) copy-start(bf16[2,196,768]{2,0,1:T(2,128)(2,1)} %param.56) | copy-start | bytes 1806340
  13.4 6.1 %copy-start.23 = (f32[27,384]{1,0:T(8,128)S(1)}, f32[27,384]{1,0:T(8,128)}, u32[]{:S(2)}) copy-start(f32[27,384]{1,0:T(8,128)} %tile.43) | copy-start | bytes 124420
  27.0 17.1 %copy-start.12 = (bf16[2,4,7,8,768]{4,3,2,1,0:T(8,128)(2,1)S(1)}, bf16[2,4,7,8,768]{4,3,2,1,0:T(8,128)(2,1)}, u32[]{:S(2)}) copy-start(bf16[2,4,7,8,768]{4,3,2,1,0:T(8,128)(2,1)} %pad.45) | copy-start | bytes 2064388
  41.4 10.3 %collective-permute-start.1 = (bf16[2,2,224,384]{3,2,1,0:T(8,128)(2,1)}, bf16[2,2,224,384]{3,2,1,0:T(8,128)(2,1)S(1)}, u32[]{:S(2)}, u32[]{:S(2)}) collective-permute-start(bf16[2,2,224,384]{3,2,1,0:T(8,128)(2,1)} %get-tuple-element.95), channel_id=1, source_target_pairs={{0,2},{2,4},{4,6},{6,8},{8,10},{10,12},{12,14},{14,16},{16,18},{18... | collective-permute-start | bytes 2064392 | tf_op jit(solution)/shard_map/ppermute | solution.py:1293
  44.1 47.6 %collective-permute-start.4 = (bf16[2,224,768]{2,1,0:T(8,128)(2,1)S(1)}, bf16[2,224,768]{2,1,0:T(8,128)(2,1)S(1)}, u32[]{:S(2)}, u32[]{:S(2)}) collective-permute-start(bf16[2,224,768]{2,1,0:T(8,128)(2,1)S(1)} %bitcast.82), channel_id=1, source_target_pairs={{0,1},{1,0},{2,3},{3,2},{4,5},{5,4},{6,7},{7,6},{8,9},{9,8},{10,11... | collective-permute-start | bytes 2064392 | tf_op jit(solution)/shard_map/ppermute | solution.py:1319
  71.7 20.9 %collective-permute-start.2 = (bf16[224,768]{1,0:T(8,128)(2,1)}, bf16[224,768]{1,0:T(8,128)(2,1)S(1)}, u32[]{:S(2)}, u32[]{:S(2)}) collective-permute-start(bf16[224,768]{1,0:T(8,128)(2,1)} %get-tuple-element.99), channel_id=1, source_target_pairs={{0,1},{1,0},{2,3},{3,2},{4,5},{5,4},{6,7},{7,6},{8,9},{9,8},{10,11... | collective-permute-start | bytes 1032200 | tf_op jit(solution)/shard_map/ppermute | solution.py:1319
  91.4 10.7 %collective-permute-start.5 = (bf16[224,768]{1,0:T(8,128)(2,1)}, bf16[224,768]{1,0:T(8,128)(2,1)S(1)}, u32[]{:S(2)}, u32[]{:S(2)}) collective-permute-start(bf16[224,768]{1,0:T(8,128)(2,1)} %get-tuple-element.108), channel_id=1, source_target_pairs={{0,1},{1,0},{2,3},{3,2},{4,5},{5,4},{6,7},{7,6},{8,9},{9,8},{10,11... | collective-permute-start | bytes 1032200 | tf_op jit(solution)/shard_map/ppermute | solution.py:1319
  95.7 28.4 %collective-permute-start.3 = (bf16[224,768]{1,0:T(8,128)(2,1)}, bf16[224,768]{1,0:T(8,128)(2,1)S(1)}, u32[]{:S(2)}, u32[]{:S(2)}) collective-permute-start(bf16[224,768]{1,0:T(8,128)(2,1)} %get-tuple-element.101.a2.refs_8_), channel_id=1, source_target_pairs={{0,1},{1,0},{2,3},{3,2},{4,5},{5,4},{6,7},{7,6},{8,9},{9,8},{10,11... | collective-permute-start | bytes 1032200 | tf_op jit(solution)/shard_map/ppermute | solution.py:1319
  105.3 11.5 %collective-permute-start.6 = (bf16[224,768]{1,0:T(8,128)(2,1)}, bf16[224,768]{1,0:T(8,128)(2,1)S(1)}, u32[]{:S(2)}, u32[]{:S(2)}) collective-permute-start(bf16[224,768]{1,0:T(8,128)(2,1)} %get-tuple-element.109.a2.refs_9_), channel_id=1, source_target_pairs={{0,1},{1,0},{2,3},{3,2},{4,5},{5,4},{6,7},{7,6},{8,9},{9,8},{10,11... | collective-permute-start | bytes 1032200 | tf_op jit(solution)/shard_map/ppermute | solution.py:1319
  124.1 26.6 %collective-permute-start.7 = (bf16[224,768]{1,0:T(8,128)(2,1)}, bf16[224,768]{1,0:T(8,128)(2,1)S(1)}, u32[]{:S(2)}, u32[]{:S(2)}) collective-permute-start(bf16[224,768]{1,0:T(8,128)(2,1)} %get-tuple-element.111), channel_id=1, source_target_pairs={{0,1},{1,0},{2,3},{3,2},{4,5},{5,4},{6,7},{7,6},{8,9},{9,8},{10,11... | collective-permute-start | bytes 1032200 | tf_op jit(solution)/shard_map/ppermute | solution.py:1319
  131.4 23.2 %collective-permute-start.11 = (bf16[224,768]{1,0:T(8,128)(2,1)}, bf16[224,768]{1,0:T(8,128)(2,1)S(1)}, u32[]{:S(2)}, u32[]{:S(2)}) collective-permute-start(bf16[224,768]{1,0:T(8,128)(2,1)} %get-tuple-element.120), channel_id=1, source_target_pairs={{0,1},{1,0},{2,3},{3,2},{4,5},{5,4},{6,7},{7,6},{8,9},{9,8},{10,11... | collective-permute-start | bytes 1032200 | tf_op jit(solution)/shard_map/ppermute | solution.py:1319
  154.5 16.0 %collective-permute-start.8 = (bf16[224,768]{1,0:T(8,128)(2,1)}, bf16[224,768]{1,0:T(8,128)(2,1)S(1)}, u32[]{:S(2)}, u32[]{:S(2)}) collective-permute-start(bf16[224,768]{1,0:T(8,128)(2,1)} %get-tuple-element.113.mine), channel_id=1, source_target_pairs={{0,1},{1,0},{2,3},{3,2},{4,5},{5,4},{6,7},{7,6},{8,9},{9,8},{10,11... | collective-permute-start | bytes 1032200 | tf_op jit(solution)/shard_map/ppermute | solution.py:1319
  158.4 17.0 %collective-permute-start.12 = (bf16[224,768]{1,0:T(8,128)(2,1)}, bf16[224,768]{1,0:T(8,128)(2,1)S(1)}, u32[]{:S(2)}, u32[]{:S(2)}) collective-permute-start(bf16[224,768]{1,0:T(8,128)(2,1)} %get-tuple-element.121.mine), channel_id=1, source_target_pairs={{0,1},{1,0},{2,3},{3,2},{4,5},{5,4},{6,7},{7,6},{8,9},{9,8},{10,11... | collective-permute-start | bytes 1032200 | tf_op jit(solution)/shard_map/ppermute | solution.py:1319
  160.4 10.2 %copy-start.46 = (bf16[224,768]{1,0:T(8,128)(2,1)S(1)}, bf16[224,768]{1,0:T(8,128)(2,1)}, u32[]{:S(2)}) copy-start(bf16[224,768]{1,0:T(8,128)(2,1)} %get-tuple-element.114) | copy-start | bytes 1032196
  160.4 10.3 %copy-start.45 = (bf16[224,768]{1,0:T(8,128)(2,1)S(1)}, bf16[224,768]{1,0:T(8,128)(2,1)}, u32[]{:S(2)}) copy-start(bf16[224,768]{1,0:T(8,128)(2,1)} %get-tuple-element.116) | copy-start | bytes 1032196
  170.6 72.9 %collective-permute-start.9 = (bf16[224,768]{1,0:T(8,128)(2,1)S(1)}, bf16[224,768]{1,0:T(8,128)(2,1)S(1)}, u32[]{:S(2)}, u32[]{:S(2)}) collective-permute-start(bf16[224,768]{1,0:T(8,128)(2,1)S(1)} %copy-done.46), channel_id=1, source_target_pairs={{0,1},{1,0},{2,3},{3,2},{4,5},{5,4},{6,7},{7,6},{8,9},{9,8},{10,11... | collective-permute-start | bytes 1032200 | tf_op jit(solution)/shard_map/ppermute | solution.py:1319
  170.7 72.8 %collective-permute-start.10 = (bf16[224,768]{1,0:T(8,128)(2,1)S(1)}, bf16[224,768]{1,0:T(8,128)(2,1)S(1)}, u32[]{:S(2)}, u32[]{:S(2)}) collective-permute-start(bf16[224,768]{1,0:T(8,128)(2,1)S(1)} %copy-done.45), channel_id=1, source_target_pairs={{0,1},{1,0},{2,3},{3,2},{4,5},{5,4},{6,7},{7,6},{8,9},{9,8},{10,11... | collective-permute-start | bytes 1032200 | tf_op jit(solution)/shard_map/ppermute | solution.py:1319
  243.5 79.5 %copy-start.8 = (f32[224,768]{1,0:T(8,128)S(1)}, f32[224,768]{1,0:T(8,128)}, u32[]{:S(2)}) copy-start(f32[224,768]{1,0:T(8,128)} %get-tuple-element.100.x1_ref) | copy-start | bytes 2064388
  243.5 79.5 %copy-start.9 = (f32[224,768]{1,0:T(8,128)S(1)}, f32[224,768]{1,0:T(8,128)}, u32[]{:S(2)}) copy-start(f32[224,768]{1,0:T(8,128)} %get-tuple-element.112.x1_ref) | copy-start | bytes 2064388
  243.5 79.5 %copy-start.10 = (f32[224,768]{1,0:T(8,128)S(1)}, f32[224,768]{1,0:T(8,128)}, u32[]{:S(2)}) copy-start(f32[224,768]{1,0:T(8,128)} %get-tuple-element.140) | copy-start | bytes 2064388
  243.5 79.5 %copy-start.11 = (f32[224,768]{1,0:T(8,128)S(1)}, f32[224,768]{1,0:T(8,128)}, u32[]{:S(2)}) copy-start(f32[224,768]{1,0:T(8,128)} %get-tuple-element.102) | copy-start | bytes 2064388
  243.5 79.5 %copy-start.39 = (f32[768]{0:T(1024)S(1)}, f32[768]{0:T(1024)}, u32[]{:S(2)}) copy-start(f32[768]{0:T(1024)} %param.54) | copy-start | bytes 9220
  (45 other events, 111.5 us)

commit v6 on v5

--- a/solution.py
+++ b/solution.py
@@ -137,17 +137,27 @@
     dst[2, pl.ds(first, n), 1 : HGT + 1] = pltpu.roll(flat, PADW - 1, axis=1).reshape(n, HGT, PADW, c)
 
 
+def widened(rows):
+    return jnp.broadcast_to(rows[:, None, :], (rows.shape[0], 8, rows.shape[1]))
+
+
 def pool_forward(squeeze, *refs):
     if squeeze:
-        a_ref, w_ref, k_ref, s_ref, x0_ref, xp_ref, xf_ref, m_ref, xs, ys = refs
+        a_ref, w_ref, rows_k, rows_s, x0_ref, xp_ref, xf_ref, m_ref, xs, k_ref, ys, s_ref = refs
     else:
-        a_ref, w_ref, k_ref, x0_ref, xp_ref, xs = refs
+        a_ref, w_ref, rows_k, x0_ref, xp_ref, xs, k_ref = refs
 
     @pl.when((pl.program_id(0) == 0) & (pl.program_id(1) == 0))
     def _():
         xs[...] = jnp.zeros_like(xs)
         if squeeze:
             ys[...] = jnp.zeros_like(ys)
+
+    @pl.when(pl.program_id(1) == 0)
+    def _():
+        k_ref[0] = widened(rows_k[0])
+        if squeeze:
+            s_ref[0] = widened(rows_s[0])
 
     x = nn(a_ref[0], w_ref[0])
     x0_ref[0, 0] = x.astype(BF16)
@@ -193,10 +203,11 @@
             lax.fori_loop(0, TM // 2, squeeze_step, 0)
 
 
-def call_pool_forward(rows, weights, first, count, kernels, squeezes=None):
+def call_pool_forward(rows, weights, first, count, kernels, squeeze):
     clips = rows.shape[0]
-    squeeze = squeezes is not None
-    tap = pl.BlockSpec((1, 27, 8, LW), lambda j, i: (j, 0, 0, 0))
+    tap = pl.BlockSpec((1, 27, LW), lambda j, i: (j + first, 0, 0))
+    tap_squeeze = pl.BlockSpec((1, 27, LW), lambda j, i: (j + first + 2, 0, 0))
+    wide = pltpu.VMEM((1, 27, 8, LW), F32)
 
     def out(n):
         return pl.BlockSpec((1, 1, n, LW), lambda j, i: (i, j, 0, 0))
@@ -221,20 +232,20 @@
             pl.BlockSpec((1, weights.shape[1], LW), lambda j, i: (j + first, 0, 0)),
             tap,
         ]
-        + ([tap] if squeeze else []),
+        + ([tap_squeeze] if squeeze else []),
         out_specs=specs,
         out_shape=shapes,
-        scratch_shapes=[frame] * (2 if squeeze else 1),
+        scratch_shapes=[frame, wide] * (2 if squeeze else 1),
         compiler_params=params(),
         cost_estimate=pl.CostEstimate(
             flops=60_000_000_000 * count // 10, bytes_accessed=4_000_000 * count, transcendentals=0
         ),
-    )(rows, weights, kernels, *([squeezes] if squeeze else []))
+    )(rows, weights, kernels, *([kernels] if squeeze else []))
 
 
 def attention_forward(
-    q_ref, kv_ref, m1_ref, m2_ref, ke_ref, tab_ref, fold_ref, one_ref, own_ref, lanes_ref,
-    branch_ref, qa_ref, at_ref, lse_ref, keys, vt, scores, expo,
+    q_ref, kv_ref, m1_ref, m2_ref, ke_ref, tab_ref, fold_ref, one_ref, own_ref, lanes_ref, w_ref,
+    branch_ref, qa_ref, at_ref, lse_ref, kept_ref, sent_ref, keys, vt, scores, expo, table,
 ):
     keys[0:ROWS] = kv_ref[0, 0]
     keys[ROWS : ROWS + MROWS] = m1_ref[0, 0]
@@ -248,7 +259,10 @@
         win = slice(first, first + WIN)
         heads = lanes_ref[head]
         qm = q_ref[0, 0, :, win] * heads
-        raw = nn(qm, tab_ref[head, 0]) + nn(qm, tab_ref[head, 1])
+        table[...] = jnp.zeros_like(table)
+        for part in range(2):
+            table[part, head * HEAD_DIM - first : (head + 1) * HEAD_DIM - first] = tab_ref[part]
+        raw = nn(qm, table[0]) + nn(qm, table[1])
         raw = raw * own_ref[...]
         high = raw.astype(BF16)
         rest = (raw - high.astype(F32)).astype(BF16)
@@ -277,6 +291,9 @@
         at_ref[0, head * HEAD_DIM : (head + 1) * HEAD_DIM] = out
         lse_ref[0, head : head + 1] = shift + jnp.log2(total)
     branch_ref[0] = (at_ref[0].T + q_ref[0, 0].astype(F32)).astype(BF16)
+    side = lax.axis_index("head")
+    sent_ref[...] = nn(branch_ref[0, half_rows(1 - side)], w_ref[...]).astype(BF16)
+    kept_ref[...] = nn(branch_ref[0, half_rows(side)], w_ref[...])
 
 
 def whole(shape):
@@ -287,7 +304,7 @@
     return pl.BlockSpec((1,) + shape, lambda i: (i,) + (0,) * len(shape))
 
 
-def call_attention_forward(clip, q, kv, memory, keys_extra, tables, consts):
+def call_attention_forward(clip, q, kv, memory, keys_extra, tables, w_proj, consts):
     def block(*shape, at=clip):
         return pl.BlockSpec((1,) + shape, lambda i: (at,) + (0,) * len(shape))
 
@@ -300,35 +317,41 @@
             block(2, MROWS, LW, at=clip + 1),
             block(2, MROWS, LW, at=clip),
             block(2, KEYS, WIN),
-            whole((LH, 2, WIN, 256)),
+            whole((2, HEAD_DIM, 256)),
             whole((2, 2, 256, WIN)),
             whole((2, 8, WIN)),
             whole((ROWS, 256)),
             whole((LH, ROWS, WIN)),
+            whole(w_proj.shape),
         ],
         out_specs=[
             clip_block(ROWS, LW),
             clip_block(LH, ROWS, WIN),
             clip_block(LW, ROWS),
             clip_block(8, ROWS),
+            whole((HALF, w_proj.shape[1])),
+            whole((HALF, w_proj.shape[1])),
         ],
         out_shape=[
             jax.ShapeDtypeStruct((1, ROWS, LW), BF16),
             jax.ShapeDtypeStruct((1, LH, ROWS, WIN), BF16),
             jax.ShapeDtypeStruct((1, LW, ROWS), F32),
             jax.ShapeDtypeStruct((1, 8, ROWS), F32),
+            jax.ShapeDtypeStruct((HALF, w_proj.shape[1]), F32),
+            jax.ShapeDtypeStruct((HALF, w_proj.shape[1]), BF16),
         ],
         scratch_shapes=[
             pltpu.VMEM((KEYS, LW), BF16),
             pltpu.VMEM((LW, KEYS), BF16),
             pltpu.VMEM((KEYS, ROWS), F32),
             pltpu.VMEM((KEYS, ROWS), BF16),
+            pltpu.VMEM((2, WIN, 256), BF16),
         ],
         compiler_params=params(),
         cost_estimate=pl.CostEstimate(
-            flops=13_000_000_000, bytes_accessed=5_000_000, transcendentals=1_500_000
+            flops=1_300_000_000, bytes_accessed=500_000, transcendentals=0
         ),
-    )(q, kv, memory, memory, keys_extra, tables, consts["fold"], consts["one"], consts["own"], consts["lanes"])
+    )(q, kv, memory, memory, keys_extra, tables, consts["fold"], consts["one"], consts["own"], consts["lanes"], w_proj)
 
 
 HALF = ROWS // 2
@@ -344,19 +367,13 @@
         out_shape=out_shape,
         compiler_params=params(),
         cost_estimate=pl.CostEstimate(
-            flops=int(gflops * 1e9), bytes_accessed=2_000_000, transcendentals=0
+            flops=int(gflops * 1e8), bytes_accessed=200_000, transcendentals=0
         ),
     )(*args)
 
 
 def half_rows(side):
     return pl.ds(pl.multiple_of(side * HALF, 16), HALF)
-
-
-def project_kernel(branch, w, kept, sent):
-    head = lax.axis_index("head")
-    sent[...] = nn(branch[half_rows(1 - head)], w[...]).astype(BF16)
-    kept[...] = nn(branch[half_rows(head)], w[...])
 
 
 def middle_kernel(tokens, kept, recv, vectors, x1_ref, a2_ref):
@@ -372,41 +389,54 @@
 GELU_B = 0.044715
 
 
-def ffn_kernel(a2, g, w1, b1, w2, act_ref, dpre_ref, da2_ref, out_ref, sums_ref):
-    da2 = jnp.zeros(da2_ref.shape, F32)
-    out = jnp.zeros(out_ref.shape, F32)
+def joined(refs):
+    return jnp.concatenate([ref[...] for ref in refs], axis=0) if len(refs) > 1 else refs[0][...]
+
+
+def ffn_kernel(count, *refs):
+    a2 = joined(refs[:count])
+    g = joined(refs[count : 2 * count])
+    w1, b1, w2 = refs[2 * count : 2 * count + 3]
+    outs = refs[2 * count + 3 :]
+    act_refs, dpre_refs, da2_refs, out_refs = (outs[n * count : (n + 1) * count] for n in range(4))
+    sums_ref = outs[4 * count]
+    da2 = jnp.zeros(a2.shape, F32)
+    out = jnp.zeros(a2.shape, F32)
     for first in range(0, w1.shape[1], FFN_BLOCK):
         cols = slice(first, first + FFN_BLOCK)
-        pre = nn(a2[...], w1[:, cols]) + b1[0:1, cols]
+        pre = nn(a2, w1[:, cols]) + b1[0:1, cols]
         square = pre * pre
         bent = jnp.tanh(GELU_A * (pre + GELU_B * (pre * square)))
         gate = 0.5 + 0.5 * bent
         act = (pre * gate).astype(BF16)
         slope = gate + 0.5 * pre * (1.0 - bent * bent) * (GELU_A * (1.0 + 3.0 * GELU_B * square))
-        dpre = nt(g[...], w2[cols]) * slope
+        dpre = nt(g, w2[cols]) * slope
         low = dpre.astype(BF16)
         sums_ref[0:1, cols] = jnp.sum(dpre, axis=0, keepdims=True)
-        act_ref[:, cols] = act
-        dpre_ref[:, cols] = low
+        for n in range(count):
+            act_refs[n][:, cols] = act[n * HALF : (n + 1) * HALF]
+            dpre_refs[n][:, cols] = low[n * HALF : (n + 1) * HALF]
         da2 = da2 + nt(low, w1[:, cols])
         out = out + nn(act, w2[cols])
-    da2_ref[...] = da2.astype(da2_ref.dtype)
-    out_ref[...] = out.astype(out_ref.dtype)
-
-
-def call_ffn(a2, g, w1, b1, w2, dtype):
-    hidden = w1.shape[1]
-    return simple_call(
-        ffn_kernel,
-        [
-            jax.ShapeDtypeStruct((HALF, hidden), BF16),
-            jax.ShapeDtypeStruct((HALF, hidden), BF16),
-            jax.ShapeDtypeStruct(a2.shape, dtype),
-            jax.ShapeDtypeStruct(a2.shape, dtype),
-            jax.ShapeDtypeStruct((1, hidden), F32),
-        ],
-        5, a2, g, w1, b1, w2,
+    for n in range(count):
+        da2_refs[n][...] = da2[n * HALF : (n + 1) * HALF].astype(da2_refs[n].dtype)
+        out_refs[n][...] = out[n * HALF : (n + 1) * HALF].astype(out_refs[n].dtype)
+
+
+def call_ffn(parts, w1, b1, w2):
+    hidden, width = w2.shape
+    count = len(parts)
+    made = simple_call(
+        partial(ffn_kernel, count),
+        [jax.ShapeDtypeStruct((HALF, hidden), BF16)] * (2 * count)
+        + [jax.ShapeDtypeStruct((HALF, width), dtype) for _, _, dtype in parts] * 2
+        + [jax.ShapeDtypeStruct((1, hidden), F32)],
+        5,
+        *[part[0] for part in parts],
+        *[part[1] for part in parts],
+        w1, b1, w2,
     )
+    return [tuple(made[n :: count][:4]) for n in range(count)], made[-1]
 
 
 def tn(a, b):
@@ -416,8 +446,8 @@
 def weight_kernel(count, *refs):
     acts, dpres, a2s, gs = (refs[n * count : (n + 1) * count] for n in range(4))
     g2, g1 = refs[4 * count :]
-    g2[...] = sum(tn(a[...], b[...]) for a, b in zip(acts, gs)).astype(BF16)
-    g1[...] = sum(tn(a[...], b[...]) for a, b in zip(a2s, dpres)).astype(BF16)
+    g2[...] = tn(joined(acts), joined(gs)).astype(BF16)
+    g1[...] = tn(joined(a2s), joined(dpres)).astype(BF16)
 
 
 def call_weights(acts, dpres, a2s, gs):
@@ -438,7 +468,7 @@
             jax.ShapeDtypeStruct((width, hidden), BF16),
         ],
         compiler_params=params(),
-        cost_estimate=pl.CostEstimate(flops=8_000_000_000, bytes_accessed=15_000_000, transcendentals=0),
+        cost_estimate=pl.CostEstimate(flops=800_000_000, bytes_accessed=1_500_000, transcendentals=0),
     )(*acts, *dpres, *a2s, *gs)
 
 
@@ -853,12 +883,12 @@
 
 def finish_kernel(
     groups, width,
-    dq_hbm, dkv_hbm, x0q_hbm, x0kv_hbm, kvf_hbm, taps_hbm, rows_a_hbm, rows_x0, rows_x1, branch0, branch1,
+    dq_hbm, dkv_hbm, x0q_hbm, x0kv_hbm, kvf_hbm, rows_taps, rows_a_hbm, rows_x0, rows_x1, branch0, branch1,
     w_hbm, tokens_hbm, middle0, middle1, chunks_ref, dr_ref, gain, foldl_ref, pick_ref,
-    sums0, sums1, hidden0, hidden1, hidden2, hidden3,
+    sums0, sums1, hidden0, hidden1, hidden2,
     grad, out1, outp, outq, small_out,
     dq, dkv, x0q, x0kv, kvf, taps_ref, rows_a, rows_x, branch, w_ref, tokens, middle,
-    us, ms, kacc, dx, dmem_send, dmem_recv, res1, resp, grads, stage, stage_t,
+    us, ms, kacc, dx, dmem_send, dmem_recv, resp, grads, stage_t,
     recv_a, send_b, recv_b, send_c, recv_c,
     strips, strip_res, strip_a, strip_b, strip_bb, strip_c, strip_cc,
     sm, sm_res, sm_core, sm_sum, sm_slots, send_y, recv_y,
@@ -868,11 +898,11 @@
     clips = dq.shape[0]
     total = rows_a.shape[1]
     names = (
-        "dkv", "dq", "x0q", "taps", "rows_x0", "rows_x1", "branch0", "branch1", "x0kv", "kvf", "rows_a", "w",
+        "dkv", "dq", "x0q", "rows_x0", "rows_x1", "branch0", "branch1", "x0kv", "kvf", "rows_a", "w",
         "tokens", "middle0", "middle1",
     )
     pairs = (
-        (dkv_hbm, dkv), (dq_hbm, dq), (x0q_hbm, x0q), (taps_hbm, taps_ref),
+        (dkv_hbm, dkv), (dq_hbm, dq), (x0q_hbm, x0q),
         (rows_x0, rows_x.at[0:ROWS]), (rows_x1, rows_x.at[ROWS:]), (branch0, branch.at[0:ROWS]),
         (branch1, branch.at[ROWS:]), (x0kv_hbm, x0kv), (kvf_hbm, kvf), (rows_a_hbm, rows_a), (w_hbm, w_ref),
         (tokens_hbm, tokens), (middle0, middle.at[0]), (middle1, middle.at[1]),
@@ -890,7 +920,7 @@
     pl.semaphore_wait(barrier, 3 + len(others))
 
     def strip_of(number):
-        return lambda first, n: res1.at[pl.ds(first, n), number * LW : number * LW + LW]
+        return lambda first, n: out1.at[pl.ds(first, n), number * LW : number * LW + LW]
 
     ffn = [
         Piece(place, total, None, strip_of(number), None, sems_send.at[number], sems_recv.at[number])
@@ -916,19 +946,6 @@
         for number in range(6)
     ]
     tiny = Tiny(place, sm, sm_res, (sm_core, sm_sum, sm_slots), tiny_send, tiny_recv)
-
-    stored = []
-
-    def flush(source, target):
-        slot = len(stored) % 2
-        if len(stored) > 1:
-            stored[-2].wait()
-        stage[slot] = source[...].astype(F32)
-        stored.append(local(stage.at[slot], target, stores.at[slot]))
-
-    def store1(number):
-        ffn[number].g()
-        flush(strip_of(number)(0, total), out1.at[:, number * LW : number * LW + LW])
 
     def product(number):
         if number < 2:
@@ -1051,7 +1068,7 @@
         folded = exact(dr_ref[...], foldl_ref[...])
         sm[0:NREL] = exact(pick_ref[...], folded)[0:NREL]
         early = sums0[...] + sums1[...]
-        hidden = hidden0[...] + hidden1[...] + hidden2[...] + hidden3[...]
+        hidden = hidden0[...] + hidden1[...] + hidden2[...]
         strip = width // 128
         for which in range(4):
             for n in range(strip):
@@ -1074,6 +1091,8 @@
     us[...] = jnp.zeros_like(us)
     ms[...] = jnp.zeros_like(ms)
     kacc[...] = jnp.zeros_like(kacc)
+    for which in range(5):
+        taps_ref[which] = widened(rows_taps[which])
     small_first()
     lead["dkv"].wait()
     for which in range(2):
@@ -1085,7 +1104,7 @@
     for name in ("rows_x0", "rows_x1", "branch0", "branch1"):
         lead[name].wait()
     product(0)
-    for name in ("dq", "x0q", "taps"):
+    for name in ("dq", "x0q"):
         lead[name].wait()
     pooled(0, 0, 0)
     pooled(0, 0, 1)
@@ -1112,7 +1131,7 @@
     ffn[1].e()
     ffn[3].d(chunks_ref[3])
     pooled(2, 0, 0)
-    store1(0)
+    ffn[0].g()
     pooled(2, 0, 1)
     late[0].d()
     ffn[2].e()
@@ -1122,7 +1141,7 @@
     ffn[1].f()
     pooled(1, 1, 0)
     late[1].c()
-    store1(1)
+    ffn[1].g()
     ffn[3].e()
     product(2)
     pooled(1, 1, 1)
@@ -1130,7 +1149,7 @@
     product(3)
     pooled(1, 1, 2)
     late[2].b()
-    store1(2)
+    ffn[2].g()
     product(4)
     late[3].b()
     late[1].d()
@@ -1139,7 +1158,7 @@
     late[0].e()
     ffn[3].f()
     pooled(2, 1, 0)
-    store1(3)
+    ffn[3].g()
     product(5)
     late[2].c()
     pooled(2, 1, 1)
@@ -1206,7 +1225,7 @@
     tiny.d()
     tiny.e()
     small_out[...] = sm_res[...]
-    for made in sent + stored[-2:]:
+    for made in sent:
         made.wait()
 
 def call_finish(
@@ -1229,19 +1248,20 @@
     streamed = [dq, dkv, x0q, x0kv, kvf, all_taps, rows_a, *rows_x, *branch, weights, tokens, *middle]
     held = [
         (array.shape, array.dtype)
-        for array in (dq, dkv, x0q, x0kv, kvf, all_taps, rows_a)
+        for array in (dq, dkv, x0q, x0kv, kvf)
     ] + [
+        ((5, 27, 8, LW), F32), (rows_a.shape, BF16),
         ((clips * ROWS, total), BF16), ((clips * ROWS, LW), BF16), (weights.shape, BF16), (tokens.shape, BF16),
         (tokens.shape, F32),
     ]
     frame = pltpu.VMEM((3, T_LEN + 2, HGT + 2, PADW, LW), F32)
     return pl.pallas_call(
         partial(finish_kernel, groups, width),
-        in_specs=[hbm] * len(streamed) + [vmem] * 11,
-        out_specs=[vmem, hbm, hbm, hbm, vmem],
+        in_specs=[hbm] * 5 + [vmem] + [hbm] * (len(streamed) - 6) + [vmem] * 10,
+        out_specs=[vmem, vmem, hbm, hbm, vmem],
         out_shape=[
             jax.ShapeDtypeStruct(tokens.shape, F32),
-            jax.ShapeDtypeStruct((total, 4 * LW), F32),
+            jax.ShapeDtypeStruct((total, 4 * LW), BF16),
             jax.ShapeDtypeStruct((LW, total), F32),
             jax.ShapeDtypeStruct((3, total, LW), BF16),
             jax.ShapeDtypeStruct((small_rows, 128), F32),
@@ -1254,10 +1274,8 @@
             pltpu.VMEM((3, clips * ROWS, LW), BF16),
             pltpu.VMEM((2, 2, MROWS, LW), BF16),
             pltpu.VMEM((2, 2, MROWS, LW), BF16),
-            pltpu.VMEM((total, 4 * LW), BF16),
             pltpu.VMEM((2, total, LW), BF16),
             pltpu.VMEM((2, total, LW), BF16),
-            pltpu.VMEM((2, total, LW), F32),
             pltpu.VMEM((LW, total), F32),
             *piece_scratch(total, groups, LW, BF16, 2),
             pltpu.VMEM((6, total, 128), BF16),
@@ -1326,8 +1344,8 @@
     return lax.dynamic_update_slice_in_dim(both, swap(x), half - mine, axis=1)
 
 
-def taps(kernel):
-    return jnp.broadcast_to(jnp.tile(kernel, (1, LH))[:, None, :], (27, 8, LW))
+def taps(*kernels):
+    return jnp.tile(jnp.stack(kernels), (1, 1, LH))
 
 
 def on_device(
@@ -1370,26 +1388,9 @@
     pair_table = (pairs * HEAD_DIM**0.5).T
     table_high = pair_table.astype(BF16)
     table_rest = (pair_table - table_high.astype(F32)).astype(BF16)
-    tables = jnp.stack(
-        [
-            jnp.stack(
-                [
-                    jnp.pad(
-                        part,
-                        (
-                            (head * HEAD_DIM - window_of(head), WIN - HEAD_DIM - head * HEAD_DIM + window_of(head)),
-                            (0, 0),
-                        ),
-                    )
-                    for part in (table_high, table_rest)
-                ]
-            )
-            for head in range(LH)
-        ]
-    )
+    tables = jnp.stack([table_high, table_rest])
     rel_rows = pairs.T.astype(BF16)
-    tap_q, tap_kv = taps(pool_q)[None], jnp.stack([taps(pool_k), taps(pool_v)])
-    tap_s = jnp.stack([taps(squeeze_k), taps(squeeze_v)])
+    all_taps = taps(pool_q, pool_k, pool_v, squeeze_k, squeeze_v)
 
     width = tokens.shape[2]
     inputs_low = pad_rows(tokens)
@@ -1400,9 +1401,9 @@
     first_rows = gather_rows(jnp.where(real, first_normed, 0.0).astype(BF16))
     w_heads = w_qkv.transpose(1, 0, 2)
     upstream_other = swap(lax.optimization_barrier((upstream, first_rows))[0])
-    kv0, kv, kvf, mem = call_pool_forward(first_rows, w_heads, 1, 2, tap_kv, tap_s)
+    kv0, kv, kvf, mem = call_pool_forward(first_rows, w_heads, 1, 2, all_taps, True)
     before = from_behind(mem[-2:], "dp", 1)
-    q0, q = call_pool_forward(first_rows, w_heads, 0, 1, tap_q)
+    q0, q = call_pool_forward(first_rows, w_heads, 0, 1, all_taps, False)
     memory = jnp.concatenate([before, mem], axis=0)
     vectors = jnp.stack([proj_bias, ln2_gain, ln2_bias])
     hidden_bias = fc1_bias.reshape(1, -1)
@@ -1411,52 +1412,82 @@
     clips = range(clip_count)
     branch, qa, at, lse, kept, recv = [], [], [], [], [], []
     for clip in clips:
-        made = call_attention_forward(clip, q, kv, memory, keys_extra, tables, consts)
+        *made, own, sent = call_attention_forward(clip, q, kv, memory, keys_extra, tables, w_proj, consts)
         for store, value in zip((branch, qa, at, lse), made):
             store.append(value)
-        own, sent = simple_call(project_kernel, [rows32, rows16], 1, branch[-1][0], w_proj)
         sent, q = lax.optimization_barrier((sent, q)) if clip + 1 < clip_count else (sent, q)
         kept.append(own)
         recv.append(swap(sent))
+
+    def after(value, *earlier):
+        return lax.optimization_barrier((value, *earlier))[0]
+
     middle, mine, theirs = [], [], []
+    own_parts, other_parts, second = [None] * clip_count, [None] * clip_count, [None] * clip_count
+
+    hidden_sums = []
+
+    def through(*rows):
+        made, total = call_ffn(
+            [
+                (mine[clip], upstream[clip], F32) if own else (theirs[clip], upstream_other[clip], BF16)
+                for clip, own in rows
+            ],
+            w_fc1, hidden_bias, w_fc2,
+        )
+        hidden_sums.append(total)
+        for (clip, own), part in zip(rows, made):
+            if own:
+                own_parts[clip] = part
+            else:
+                other_parts[clip] = part
+                second[clip] = swap(part[2])
+
     for clip in clips:
-        x1, a2 = simple_call(
-            middle_kernel, [rows32, rows16], 1, inputs_low[clip], kept[clip], recv[clip], vectors
-        )
+        landed = after(recv[clip], own_parts[clip - 1][2]) if clip else recv[clip]
+        x1, a2 = simple_call(middle_kernel, [rows32, rows16], 1, inputs_low[clip], kept[clip], landed, vectors)
         middle.append(x1)
         mine.append(a2)
         theirs.append(swap(a2))
-    own_parts = [call_ffn(mine[c], upstream[c], w_fc1, hidden_bias, w_fc2, F32) for c in clips]
-    other_parts = [call_ffn(theirs[c], upstream_other[c], w_fc1, hidden_bias, w_fc2, BF16) for c in clips]
-    second = [swap(other_parts[c][2]) for c in clips]
+        if clip == 0:
+            through((0, True))
+        else:
+            through((clip, True), (clip - 1, False))
+    theirs[-1] = after(theirs[-1], own_parts[-1][2])
+    through((clip_count - 1, False))
     dmiddle, low, sums, rows_x, dmix = [], [], [], [], []
+    parts = own_parts + other_parts
     for clip in clips:
+        if clip + 1 == clip_count:
+            w_fc2_grad, w_fc1_grad = call_weights(
+                [p[0] for p in parts],
+                [p[1] for p in parts],
+                mine + theirs,
+                [after(upstream[0], low[0][0])]
+                + [upstream[c] for c in clips[1:]]
+                + [upstream_other[c] for c in clips],
+            )
+        landed = after(second[clip], w_fc2_grad if clip + 1 == clip_count else other_parts[-1][2])
         dx, dx_low, total = simple_call(
             norm_back_kernel,
             [rows32, rows16, jax.ShapeDtypeStruct((HEAD_EARLY, width), F32)],
             1,
-            own_parts[clip][2], second[clip], middle[clip], upstream[clip], vectors,
+            own_parts[clip][2], landed, middle[clip], upstream[clip], vectors,
         )
         dmiddle.append(dx)
         sums.append(total)
         low.append((dx_low, swap(dx_low)))
-    parts = own_parts + other_parts
-    w_fc2_grad, w_fc1_grad = call_weights(
-        [p[0] for p in parts],
-        [p[1] for p in parts],
-        mine + theirs,
-        [upstream[c] for c in clips] + [upstream_other[c] for c in clips],
-    )
     for clip in clips:
+        received = after(low[clip][1], low[-1][0])
         rows, mix = simple_call(
             mix_kernel,
             [jax.ShapeDtypeStruct((ROWS, width), BF16), jax.ShapeDtypeStruct((ROWS, LW), BF16)],
             1,
-            *low[clip], w_proj,
+            low[clip][0], received, w_proj,
         )
         rows_x.append(rows)
         dmix.append(mix)
-    last = [lax.optimization_barrier((other_parts[c][3], low[-1][1]))[0] for c in clips]
+    last = [lax.optimization_barrier((other_parts[c][3], dmix[-1]))[0] for c in clips]
     last = [swap(x) for x in last]
     dq, dkv, dr, chunks, w_fc2_grad = call_attention_backward(
         q, kv, memory, keys_extra, qa, dmix, at, lse, rel_rows,
@@ -1473,7 +1504,7 @@
     )
     w_fc2_grad = w_fc2_grad.astype(F32)
     input_grad, w_fc1_grad, w_proj_grad, tail, small = call_finish(
-        dq, dkv, q0, kv0, kvf, jnp.concatenate([tap_q, tap_kv, tap_s]),
+        dq, dkv, q0, kv0, kvf, all_taps,
         first_rows.reshape(-1, width),
         rows_x,
         [b[0] for b in branch],
@@ -1484,9 +1515,10 @@
         dr,
         ln1_gain.reshape(1, -1),
         sums,
-        [p[4] for p in parts],
+        hidden_sums,
     )
     input_grad = drop_rows(input_grad)
+    w_fc1_grad = w_fc1_grad.astype(F32)
     total = w_fc1_grad.shape[0]
     if total != width:
         w_fc2_grad = w_fc2_grad.reshape(2, total, width)[:, :width].reshape(2 * width, width)

time: 336 us -> 325 us (0.967)
  local copies, waits for them, and re-layouts: 41.8 us -> 29.2 us
  Pallas kernels: 254 us -> 244 us
  waiting for transfers between devices: 9.47 us -> 16.5 us
    pallas_call x12 -> x9, Pallas kernels: 58.8 us -> 49.6 us  [simple_call(): pl.pallas_call(kernel, in_specs=[vmem] * len(args), out_specs=[vmem] * le...]
    unnamed x119 -> x96, local copies, waits for them, and re-layouts: 18.5 us -> 10.8 us
    ppermute x12, waiting for transfers between devices: 9.47 us -> 16.5 us  [swap(): return lax.ppermute(x, 'head', [(0, 1), (1, 0)])]
    convert_element_type x0 -> x1, other arithmetic: none -> 4.63 us  [on_device(): w_fc1_grad = w_fc1_grad.astype(F32)]
  transfers between devices with their start and end apart: 13 -> 13, of which waited for: 2 -> 3; matrix products, arithmetic and copies ran while one was open for 7% -> 4% of each run, Pallas kernels for 50% -> 47%
where the time goes in v6:
time: 325 us
  Pallas kernels  244 us (75%)
  local copies, waits for them, and re-layouts  29.2 us (9%)
  waiting for transfers between devices  16.5 us (5%)
  starting transfers between devices  16.4 us (5%)
  other arithmetic  15.9 us (5%)
    pallas_call x1, Pallas kernels, call_finish(): pl.pallas_call(partial(finish_kernel, groups, width), in_specs=[hbm] * 5...  74.9 us
    pallas_call x1, Pallas kernels, call_attention_backward(): pl.pallas_call(partial(attention_backward, groups), in_specs=[vmem] * 3 +...  57.9 us
    pallas_call x9, Pallas kernels, simple_call(): pl.pallas_call(kernel, in_specs=[vmem] * len(args), out_specs=[vmem] * le...  49.6 us
    pallas_call x2, Pallas kernels, call_attention_forward(): pl.pallas_call(attention_forward, grid=(1,), in_specs=[block(1, ROWS, LW)...  30.7 us
    pallas_call x2, Pallas kernels, call_pool_forward(): pl.pallas_call(partial(pool_forward, squeeze), grid=(count, clips), in_sp...  21.6 us
    ppermute x12, waiting for transfers between devices, swap(): return lax.ppermute(x, 'head', [(0, 1), (1, 0)])  16.5 us
    ppermute x12, starting transfers between devices, swap(): return lax.ppermute(x, 'head', [(0, 1), (1, 0)])  14.9 us
    unnamed x96, local copies, waits for them, and re-layouts  10.8 us
  transfers between devices with their start and end apart: 13, of which 3 were waited for; matrix products, arithmetic and copies ran while one was open for 4% of the time, Pallas kernels for 47%

profile of v6, /device:TPU:0, one launch (start us, length us, event | category | flops | bytes accessed | tf_op | source)
XLA Modules:
  0.0 324.9 jit_solution(3940219740482795479)
XLA Ops:
  3.3 3.0 collective-permute-start
  11.4 10.5 %collective-permute-done = bf16[2,224,768]{2,1,0:T(8,128)(2,1)} collective-permute-done((bf16[2,224,768]{2,1,0:T(8,128)(2,1)S(1)}, bf16[2,224,768]{2,1,0:T(8,128)(2,1)}, u32[]{:S(2)}, u32[]{:S(2)}) %collective-permute-start) | collective-permute-done | bytes 688160 | tf_op jit(solution)/shard_map/ppermute | solution.py:1337
  24.1 14.9 %shard_map.491 = (bf16[2,2,448,384]{3,2,1,0:T(8,128)(2,1)}, bf16[2,2,448,384]{3,2,1,0:T(8,128)(2,1)}, bf16[2,2,448,384]{3,2,1,0:T(8,128)(2,1)}, bf16[2,2,224,384]{3,2,1,0:T(8,128)(2,1)}) custom-call(bf16[2,448,768]{2,1,0:T(8,128)(2,1)} %copy-done.11, bf16[3,768,384]{2,1,0:T(8,128)(2,1)} %bitcast.88, f32[5,27,384]{2,1,0:T(8,128)} %tile.10.refs_2_.refs_3_.rows_taps, ...), custom_call_target="tpu_custom_call" | custom-call | flops 12000000000 | bytes 8000000 | tf_op jit(solution)/shard_map/pallas_call | solution.py:227
  43.3 6.7 %shard_map.490 = (bf16[2,1,448,384]{3,2,1,0:T(8,128)(2,1)}, bf16[2,1,448,384]{3,2,1,0:T(8,128)(2,1)}) custom-call(bf16[2,448,768]{2,1,0:T(8,128)(2,1)} %copy-done.11, bf16[3,768,384]{2,1,0:T(8,128)(2,1)} %bitcast.89, f32[5,27,384]{2,1,0:T(8,128)} %tile.10.refs_2_.refs_3_.rows_taps), custom_call_target="tpu_custom_call" | custom-call | flops 6000000000 | bytes 4000000 | tf_op jit(solution)/shard_map/pallas_call | solution.py:227
  52.3 15.2 %shard_map.492 = (bf16[1,448,384]{2,1,0:T(8,128)(2,1)}, bf16[1,4,448,256]{3,2,1,0:T(8,128)(2,1)}, f32[1,384,448]{2,1,0:T(8,128)}, f32[1,8,448]{2,1,0:T(8,128)}, ...) custom-call(bf16[2,1,448,384]{3,2,1,0:T(8,128)(2,1)} %get-tuple-element.108.q_ref, ...), custom_call_target="tpu_custom_call" | custom-call | flops 1300000000 | bytes 500000 | tf_op jit(solution)/shard_map/pallas_call | solution.py:311
  67.8 15.5 %shard_map.495 = (bf16[1,448,384]{2,1,0:T(8,128)(2,1)}, bf16[1,4,448,256]{3,2,1,0:T(8,128)(2,1)}, f32[1,384,448]{2,1,0:T(8,128)}, f32[1,8,448]{2,1,0:T(8,128)}, ...) custom-call(bf16[2,1,448,384]{3,2,1,0:T(8,128)(2,1)} %get-tuple-element.108.q_ref, ...), custom_call_target="tpu_custom_call" | custom-call | flops 1300000000 | bytes 500000 | tf_op jit(solution)/shard_map/pallas_call | solution.py:311
  87.3 2.5 shard_map.493
  91.7 6.7 %shard_map.494 = (bf16[224,1536]{1,0:T(8,128)(2,1)}, bf16[224,1536]{1,0:T(8,128)(2,1)}, f32[224,768]{1,0:T(8,128)}, f32[224,768]{1,0:T(8,128)}, f32[1,1536]{1,0:T(1,128)}) custom-call(bf16[224,768]{1,0:T(8,128)(2,1)} %get-tuple-element.106.refs_0_.refs_8_, bf16[224,768]{1,0:T(8,128)(2,1)} %bitcast.73, bf16[768,1536]{1,0:T(8,128)(2,1)} %refs_2_.3, ...), custom_call_target="tpu_custom_call" | custom-call | flops 500000000 | bytes 200000 | tf_op jit(solution)/shard_map/pallas_call | solution.py:363
  99.1 2.4 shard_map.496
  105.0 9.7 %shard_map.497 = (bf16[224,1536]{1,0:T(8,128)(2,1)}, bf16[224,1536]{1,0:T(8,128)(2,1)}, bf16[224,1536]{1,0:T(8,128)(2,1)}, bf16[224,1536]{1,0:T(8,128)(2,1)}, f3...) custom-call(bf16[224,768]{1,0:T(8,128)(2,1)} %get-tuple-element.113., ...), custom_call_target="tpu_custom_call" | custom-call | flops 500000000 | bytes 200000 | tf_op jit(solution)/shard_map/pallas_call | solution.py:363
  115.7 6.5 %shard_map.498 = (bf16[224,1536]{1,0:T(8,128)(2,1)}, bf16[224,1536]{1,0:T(8,128)(2,1)}, bf16[224,768]{1,0:T(8,128)(2,1)}, bf16[224,768]{1,0:T(8,128)(2,1)}, f32[1,1536]{1,0:T(1,128)}) custom-call(bf16[224,768]{1,0:T(8,128)(2,1)} %copy-done.9, bf16[224,768]{1,0:T(8,128)(2,1)} %get-tuple-element.177.refs_1_.refs_15_, bf16[768,1536]{1,0:T(8,128)(2,1)} %refs_2_.3, ...), custom_call_target="tpu_custom_call" | custom-call | flops 500000000 | bytes 200000 | tf_op jit(solution)/shard_map/pallas_call | solution.py:363
  122.2 1.7 collective-permute-start.7
  126.3 13.1 %shard_map.499 = (f32[224,768]{1,0:T(8,128)}, bf16[224,768]{1,0:T(8,128)(2,1)}, f32[8,768]{1,0:T(8,128)}) custom-call(f32[224,768]{1,0:T(8,128)} %get-tuple-element.111.kept, bf16[224,768]{1,0:T(8,128)(2,1)} %copy-done.22, f32[224,768]{1,0:T(8,128)} %get-tuple-element.105.x1_ref, bf16[224,768]{1,0:T(8,128)(2,1)} %bitcast.74, f32[3,768]{1,0:T(4,128)} %pad_maximum_fusion.3.vectors), custom_call_target="tpu_custom_call" | custom-call | flops 100000000 | bytes 200000 | tf_op jit(solution)/shard_map/pallas_call | solution.py:363
  139.9 9.8 %shard_map.500 = (bf16[1536,768]{1,0:T(8,128)(2,1)}, bf16[768,1536]{1,0:T(8,128)(2,1)}) custom-call(bf16[224,1536]{1,0:T(8,128)(2,1)} %get-tuple-element.119.refs_0_, bf16[224,1536]{1,0:T(8,128)(2,1)} %get-tuple-element.120.refs_1_, bf16[224,1536]{1,0:T(8,128)(2,1)} %get-tuple-element.121.refs_2_, bf16[224,1536]{1,0:T(8,128)(2,1)} %get-tuple-element.122.refs_3_, ...), custom_call_target="tpu_custom_call" | custom-call | flops 800000000 | bytes 1500000 | tf_op jit(solution)/shard_map/pallas_call | solution.py:458
  150.4 3.2 shard_map.501
  156.4 2.8 shard_map.503
  159.3 4.3 %collective-permute-done.9.theirs = bf16[224,768]{1,0:T(8,128)(2,1)S(1)} collective-permute-done((bf16[224,768]{1,0:T(8,128)(2,1)}, bf16[224,768]{1,0:T(8,128)(2,1)S(1)}, u32[]{:S(2)}, u32[]{:S(2)}) %collective-permute-start.9) | collective-permute-done | bytes 344096 | tf_op jit(solution)/shard_map/ppermute | solution.py:1337
  164.3 2.8 shard_map.502
  169.2 57.9 %shard_map.504 = (f32[2,448,384]{2,1,0:T(8,128)}, f32[2,2,896,384]{3,2,1,0:T(8,128)}, f32[256,384]{1,0:T(8,128)}, bf16[4,48,384]{2,1,0:T(8,128)(2,1)}, bf16[1536,768]{1,0:T(8,128)(2,1)}) custom-call(bf16[2,1,448,384]{3,2,1,0:T(8,128)(2,1)} %get-tuple-element.108.q_ref, bf16[2,2,448,384]{3,2,1,0:T(8,128)(2,1)} %get-tuple-element.100.kv_ref, ...), custom_call_target="tpu_custom_call" | custom-call | flops 40000000000 | bytes 20000000 | tf_op jit(solution)/shard_map/pallas_call | solution.py:839
  227.1 4.4 %convert_element_type.60 = f32[1536,768]{1,0:T(8,128)} convert(bf16[1536,768]{1,0:T(8,128)(2,1)} %get-tuple-element.176) | non-fusion elementwise | flops 1179648 | bytes 7077888 | tf_op jit(solution)/shard_map/convert_element_type | solution.py:1505
  231.4 74.9 %shard_map.505 = (f32[2,224,768]{2,1,0:T(8,128)}, bf16[768,1536]{1,0:T(8,128)(2,1)}, f32[384,768]{1,0:T(8,128)}, bf16[3,768,384]{2,1,0:T(8,128)(2,1)}, f32[256,128]{1,0:T(8,128)}) custom-call(f32[2,448,384]{2,1,0:T(8,128)} %get-tuple-element.153.dq_hbm, f32[2,2,896,384]{3,2,1,0:T(8,128)} %get-tuple-element.154.dkv_hbm, ...), custom_call_target="tpu_custom_call" | custom-call | flops 60000002048 | bytes 40000000 | tf_op jit(solution)/shard_map/pallas_call | solution.py:1258
  312.6 4.6 %convert_element_type.59 = f32[768,1536]{1,0:T(8,128)} convert(bf16[768,1536]{1,0:T(8,128)(2,1)} %get-tuple-element.175) | non-fusion elementwise | flops 1179648 | bytes 7077888 | tf_op jit(solution)/shard_map/convert_element_type | solution.py:1521
  317.2 2.0 convert_bitcast_fusion
  319.3 2.0 copy.63
  (166 shorter events, 46.4 us)
Async XLA Ops:
  0.7 6.9 %copy-start = (f32[15,96]{1,0:T(8,128)S(1)}, f32[15,96]{1,0:T(8,128)}, u32[]{:S(2)}) copy-start(f32[15,96]{1,0:T(8,128)} %param.44) | copy-start | bytes 17284
  2.8 5.4 %copy-start.5 = (bf16[2,4,7,8,768]{4,3,2,1,0:T(8,128)(2,1)}, bf16[2,4,7,8,768]{4,3,2,1,0:T(8,128)(2,1)S(1)}, u32[]{:S(2)}) copy-start(bf16[2,4,7,8,768]{4,3,2,1,0:T(8,128)(2,1)S(1)} %pad.8) | copy-start | bytes 2064388
  2.9 5.1 %copy-start.25 = (f32[256,13]{1,0:T(8,128)S(1)}, f32[256,13]{1,0:T(8,128)}, u32[]{:S(2)}) copy-start(f32[256,13]{1,0:T(8,128)} %constant.99) | copy-start | bytes 39940
  2.9 5.4 %copy-start.24 = (f32[256,13]{1,0:T(8,128)S(1)}, f32[256,13]{1,0:T(8,128)}, u32[]{:S(2)}) copy-start(f32[256,13]{1,0:T(8,128)} %constant.100) | copy-start | bytes 39940
  2.9 5.4 %copy-start.34 = (f32[13,96]{1,0:T(8,128)S(1)}, f32[13,96]{1,0:T(8,128)}, u32[]{:S(2)}) copy-start(f32[13,96]{1,0:T(8,128)} %param.46) | copy-start | bytes 14980
  3.3 18.6 %collective-permute-start = (bf16[2,224,768]{2,1,0:T(8,128)(2,1)S(1)}, bf16[2,224,768]{2,1,0:T(8,128)(2,1)}, u32[]{:S(2)}, u32[]{:S(2)}) collective-permute-start(bf16[2,224,768]{2,1,0:T(8,128)(2,1)S(1)} %select_convert_fusion), channel_id=1, source_target_pairs={{0,1},{1,0},{2,3},{3,2},{4,5},{5,4},{6,7},{7,6},{8,9},{9,8},{10,11... | collective-permute-start | bytes 2064392 | tf_op jit(solution)/shard_map/ppermute | solution.py:1337
  24.1 16.5 %copy-start.37 = (f32[768]{0:T(1024)S(1)}, f32[768]{0:T(1024)}, u32[]{:S(2)}) copy-start(f32[768]{0:T(1024)} %param.48) | copy-start | bytes 9220
  24.1 16.5 %copy-start.38 = (f32[768]{0:T(1024)S(1)}, f32[768]{0:T(1024)}, u32[]{:S(2)}) copy-start(f32[768]{0:T(1024)} %param.49) | copy-start | bytes 9220
  24.1 16.5 %copy-start.39 = (f32[768]{0:T(1024)S(1)}, f32[768]{0:T(1024)}, u32[]{:S(2)}) copy-start(f32[768]{0:T(1024)} %param.50) | copy-start | bytes 9220
  24.1 16.6 %copy-start.16 = (bf16[2,196,768]{2,0,1:T(2,128)(2,1)S(1)}, bf16[2,196,768]{2,0,1:T(2,128)(2,1)}, u32[]{:S(2)}) copy-start(bf16[2,196,768]{2,0,1:T(2,128)(2,1)} %param.56) | copy-start | bytes 1806340
  39.0 10.9 %collective-permute-start.1 = (bf16[2,2,224,384]{3,2,1,0:T(8,128)(2,1)}, bf16[2,2,224,384]{3,2,1,0:T(8,128)(2,1)S(1)}, u32[]{:S(2)}, u32[]{:S(2)}) collective-permute-start(bf16[2,2,224,384]{3,2,1,0:T(8,128)(2,1)} %get-tuple-element.101), channel_id=1, source_target_pairs={{0,2},{2,4},{4,6},{6,8},{8,10},{10,12},{12,14},{14,16},{16,18},{18... | collective-permute-start | bytes 2064392 | tf_op jit(solution)/shard_map/ppermute | solution.py:1311
  41.5 61.7 %collective-permute-start.5 = (bf16[2,224,768]{2,1,0:T(8,128)(2,1)S(1)}, bf16[2,224,768]{2,1,0:T(8,128)(2,1)S(1)}, u32[]{:S(2)}, u32[]{:S(2)}) collective-permute-start(bf16[2,224,768]{2,1,0:T(8,128)(2,1)S(1)} %bitcast.84), channel_id=1, source_target_pairs={{0,1},{1,0},{2,3},{3,2},{4,5},{5,4},{6,7},{7,6},{8,9},{9,8},{10,11... | collective-permute-start | bytes 2064392 | tf_op jit(solution)/shard_map/ppermute | solution.py:1337
  67.5 19.1 %collective-permute-start.2 = (bf16[224,768]{1,0:T(8,128)(2,1)}, bf16[224,768]{1,0:T(8,128)(2,1)S(1)}, u32[]{:S(2)}, u32[]{:S(2)}) collective-permute-start(bf16[224,768]{1,0:T(8,128)(2,1)} %get-tuple-element.104), channel_id=1, source_target_pairs={{0,1},{1,0},{2,3},{3,2},{4,5},{5,4},{6,7},{7,6},{8,9},{9,8},{10,11... | collective-permute-start | bytes 1032200 | tf_op jit(solution)/shard_map/ppermute | solution.py:1337
  83.3 15.1 %collective-permute-start.3 = (bf16[224,768]{1,0:T(8,128)(2,1)}, bf16[224,768]{1,0:T(8,128)(2,1)S(1)}, u32[]{:S(2)}, u32[]{:S(2)}) collective-permute-start(bf16[224,768]{1,0:T(8,128)(2,1)} %get-tuple-element.110), channel_id=1, source_target_pairs={{0,1},{1,0},{2,3},{3,2},{4,5},{5,4},{6,7},{7,6},{8,9},{9,8},{10,11... | collective-permute-start | bytes 1032200 | tf_op jit(solution)/shard_map/ppermute | solution.py:1337
  89.8 14.5 %collective-permute-start.4 = (bf16[224,768]{1,0:T(8,128)(2,1)}, bf16[224,768]{1,0:T(8,128)(2,1)S(1)}, u32[]{:S(2)}, u32[]{:S(2)}) collective-permute-start(bf16[224,768]{1,0:T(8,128)(2,1)} %get-tuple-element.106.refs_0_.refs_8_), channel_id=1, source_target_pairs={{0,1},{1,0},{2,3},{3,2},{4,5},{5,4},{6,7},{7,6},{8,9},{9,8},{10,11... | collective-permute-start | bytes 1032200 | tf_op jit(solution)/shard_map/ppermute | solution.py:1337
  101.5 13.4 %collective-permute-start.6 = (bf16[224,768]{1,0:T(8,128)(2,1)}, bf16[224,768]{1,0:T(8,128)(2,1)S(1)}, u32[]{:S(2)}, u32[]{:S(2)}) collective-permute-start(bf16[224,768]{1,0:T(8,128)(2,1)} %get-tuple-element.113.refs_0_.refs_9_), channel_id=1, source_target_pairs={{0,1},{1,0},{2,3},{3,2},{4,5},{5,4},{6,7},{7,6},{8,9},{9,8},{10,11... | collective-permute-start | bytes 1032200 | tf_op jit(solution)/shard_map/ppermute | solution.py:1337
  114.7 10.9 %collective-permute-start.8 = (bf16[224,768]{1,0:T(8,128)(2,1)}, bf16[224,768]{1,0:T(8,128)(2,1)S(1)}, u32[]{:S(2)}, u32[]{:S(2)}) collective-permute-start(bf16[224,768]{1,0:T(8,128)(2,1)} %get-tuple-element.127), channel_id=1, source_target_pairs={{0,1},{1,0},{2,3},{3,2},{4,5},{5,4},{6,7},{7,6},{8,9},{9,8},{10,11... | collective-permute-start | bytes 1032200 | tf_op jit(solution)/shard_map/ppermute | solution.py:1337
  122.2 27.5 %collective-permute-start.7 = (bf16[224,768]{1,0:T(8,128)(2,1)}, bf16[224,768]{1,0:T(8,128)(2,1)S(1)}, u32[]{:S(2)}, u32[]{:S(2)}) collective-permute-start(bf16[224,768]{1,0:T(8,128)(2,1)} %get-tuple-element.118), channel_id=1, source_target_pairs={{0,1},{1,0},{2,3},{3,2},{4,5},{5,4},{6,7},{7,6},{8,9},{9,8},{10,11... | collective-permute-start | bytes 1032200 | tf_op jit(solution)/shard_map/ppermute | solution.py:1337
  139.4 16.3 %collective-permute-start.12 = (bf16[224,768]{1,0:T(8,128)(2,1)}, bf16[224,768]{1,0:T(8,128)(2,1)S(1)}, u32[]{:S(2)}, u32[]{:S(2)}) collective-permute-start(bf16[224,768]{1,0:T(8,128)(2,1)} %get-tuple-element.129.mine), channel_id=1, source_target_pairs={{0,1},{1,0},{2,3},{3,2},{4,5},{5,4},{6,7},{7,6},{8,9},{9,8},{10,11... | collective-permute-start | bytes 1032200 | tf_op jit(solution)/shard_map/ppermute | solution.py:1337
  153.6 13.5 %copy-start.43 = (bf16[224,768]{1,0:T(8,128)(2,1)S(1)}, bf16[224,768]{1,0:T(8,128)(2,1)}, u32[]{:S(2)}) copy-start(bf16[224,768]{1,0:T(8,128)(2,1)} %get-tuple-element.139) | copy-start | bytes 1032196
  153.6 14.8 %copy-start.42 = (bf16[224,768]{1,0:T(8,128)(2,1)S(1)}, bf16[224,768]{1,0:T(8,128)(2,1)}, u32[]{:S(2)}) copy-start(bf16[224,768]{1,0:T(8,128)(2,1)} %get-tuple-element.137) | copy-start | bytes 1032196
  153.6 10.0 %collective-permute-start.9 = (bf16[224,768]{1,0:T(8,128)(2,1)}, bf16[224,768]{1,0:T(8,128)(2,1)S(1)}, u32[]{:S(2)}, u32[]{:S(2)}) collective-permute-start(bf16[224,768]{1,0:T(8,128)(2,1)} %get-tuple-element.134.mine), channel_id=1, source_target_pairs={{0,1},{1,0},{2,3},{3,2},{4,5},{5,4},{6,7},{7,6},{8,9},{9,8},{10,11... | collective-permute-start | bytes 1032200 | tf_op jit(solution)/shard_map/ppermute | solution.py:1337
  167.1 64.3 %collective-permute-start.11 = (bf16[224,768]{1,0:T(8,128)(2,1)S(1)}, bf16[224,768]{1,0:T(8,128)(2,1)S(1)}, u32[]{:S(2)}, u32[]{:S(2)}) collective-permute-start(bf16[224,768]{1,0:T(8,128)(2,1)S(1)} %copy-done.43), channel_id=1, source_target_pairs={{0,1},{1,0},{2,3},{3,2},{4,5},{5,4},{6,7},{7,6},{8,9},{9,8},{10,11... | collective-permute-start | bytes 1032200 | tf_op jit(solution)/shard_map/ppermute | solution.py:1337
  168.4 63.0 %collective-permute-start.10 = (bf16[224,768]{1,0:T(8,128)(2,1)S(1)}, bf16[224,768]{1,0:T(8,128)(2,1)S(1)}, u32[]{:S(2)}, u32[]{:S(2)}) collective-permute-start(bf16[224,768]{1,0:T(8,128)(2,1)S(1)} %copy-done.42), channel_id=1, source_target_pairs={{0,1},{1,0},{2,3},{3,2},{4,5},{5,4},{6,7},{7,6},{8,9},{9,8},{10,11... | collective-permute-start | bytes 1032200 | tf_op jit(solution)/shard_map/ppermute | solution.py:1337
  (34 other events, 79.7 us)
